TPU v7x, 128 devices: a whole 4x4x4 slice. The times are simulated.
128 devices in a mesh: expert: 32 (over z, x, y_hi), tensor: 4 (over y_lo, core).
Axes of the slice: x: 4, y: 4 (y_hi: 2, y_lo: 2; y = y_hi * 2 + y_lo), z: 4, core: 2. Of those that a mesh axis runs over, the one named last changes fastest.
Arguments:
- layer_input: bfloat16 [16384, 768], P('expert'), may hold values from -6 to 6
- attn_gain: float32 [768], replicated, may hold values from 0.1 to 1.9
- query_weight: bfloat16 [768, 768], P(None, 'tensor'), may hold values from -0.21875 to 0.21875
- key_weight: bfloat16 [768, 768], P(None, 'tensor'), may hold values from -0.21875 to 0.21875
- value_weight: bfloat16 [768, 768], P(None, 'tensor'), may hold values from -0.21875 to 0.21875
- output_weight: bfloat16 [768, 768], P('tensor'), may hold values from -1.75 to 1.75
- position_bias: float32 [32, 12], P(None, 'tensor'), may hold values from -4 to 4
- moe_gain: float32 [768], replicated, may hold values from 0.1 to 1.9
- router_weight: bfloat16 [768, 64], replicated, may hold values from -0.107910156 to 0.107910156
- expert_in: bfloat16 [64, 768, 3072], P('expert', None, 'tensor'), may hold values from -0.21875 to 0.21875
- expert_out: bfloat16 [64, 3072, 768], P('expert', 'tensor'), may hold values from -12.75 to 12.75
- route_expert: int32 [16384], P('expert'), may hold values from 0 to 63, as said below
- route_slot: int32 [16384], P('expert'), may hold values from 0 to 9
- route_drop: int32 [16384], P('expert'), may hold values from 0 to 1
- out_grad: bfloat16 [16384, 768], P('expert'), may hold values from -6 to 6
Outputs:
- layer_output: bfloat16 [16384, 768], P('expert')
- input_grad: float32 [16384, 768], P('expert')
- attn_gain_grad: float32 [768], replicated
- query_grad: float32 [768, 768], P(None, 'tensor')
- key_grad: float32 [768, 768], P(None, 'tensor')
- value_grad: float32 [768, 768], P(None, 'tensor')
- output_grad: float32 [768, 768], P('tensor')
- bias_grad: float32 [32, 12], P(None, 'tensor')
- moe_gain_grad: float32 [768], replicated
- router_grad: float32 [768, 64], replicated
- expert_in_grad: float32 [64, 768, 3072], P('expert', None, 'tensor')
- expert_out_grad: float32 [64, 3072, 768], P('expert', 'tensor')
Inputs may be any that keep to these rules, and one draw needn't show every extreme that they name: On each index of expert, the kept tokens (route_drop 0) hold distinct pairs of route_expert and route_slot, and 64 tokens are dropped; some expert is given all 10 slots by every index of expert, and the dropped tokens name that expert and slot 0.
All inputs are finite; a program needn't handle non-finite values.
Results may differ from a plain program's by a relative error of at most 0.029.
Values may be sent and summed in bfloat16 or wider, within the bound.
No kernel may reach another device: no remote copies, remote signals or barrier semaphores. Data moves between devices by JAX's collectives and lax.ppermute only.
A program may use at most 128 MiB of HBM per device.

v0:
```python
import jax
import jax.numpy as jnp
import numpy as np
from jax import lax
from jax.sharding import PartitionSpec as P

BUCKETS = 32
SEQ_LEN = 512


EPSILON = 1e-06
HIGHEST_PRECISION = lax.Precision.HIGHEST


def offset_selector(length, buckets):
    period = 2 * length + 1
    offsets = np.arange(period) - (length - 1)
    half_count = buckets // 2
    exact_count = half_count // 2
    upper_side = (offsets > 0).astype(np.int64) * half_count
    distance = np.abs(offsets)
    ratio = np.log(np.maximum(distance, 1) / exact_count) / np.log(128.0 / exact_count)
    far_bucket = np.minimum(
        exact_count + (ratio * (half_count - exact_count)).astype(np.int64), half_count - 1
    )
    bucket_ids = upper_side + np.where(distance < exact_count, distance, far_bucket)
    valid = (np.arange(period) < 2 * length - 1).astype(np.float32)
    selector = (bucket_ids[:, None] == np.arange(buckets)[None, :]).astype(np.float32) * valid[
        :, None
    ]
    return selector


def norm_forward(values, gain_vector):
    norm_scale = lax.rsqrt(jnp.mean(values * values, axis=-1, keepdims=True) + EPSILON)
    return (values * norm_scale * gain_vector, norm_scale)


def norm_backward(values, norm_scale, gain_vector, upstream):
    weighted = upstream * gain_vector
    inner_sum = jnp.mean(weighted * values, axis=-1, keepdims=True)
    result = norm_scale * weighted - values * norm_scale**3 * inner_sum
    return (result, jnp.sum(upstream * values * norm_scale, axis=0))


def shards(
    layer_input,
    attn_gain,
    query_weight,
    key_weight,
    value_weight,
    output_weight,
    position_bias,
    moe_gain,
    router_weight,
    expert_in,
    expert_out,
    route_expert,
    route_slot,
    route_drop,
    out_grad,
):
    tokens = layer_input.shape[0]
    model_width = layer_input.shape[1]
    groups = lax.axis_size("expert")
    local_experts = expert_in.shape[0]
    experts = groups * local_experts
    capacity = 5 * tokens // (4 * experts)
    heads_here = position_bias.shape[1]
    head_size = query_weight.shape[1] // heads_here
    seq_count = tokens // SEQ_LEN
    score_scale = head_size ** (-0.5)
    selector = jnp.asarray(offset_selector(SEQ_LEN, BUCKETS))

    def bias_of(table):
        line = jnp.transpose(jnp.dot(selector, table, precision=HIGHEST_PRECISION))
        flat = jnp.tile(line, (1, SEQ_LEN))[:, : SEQ_LEN * 2 * SEQ_LEN]
        return flat.reshape(heads_here, SEQ_LEN, 2 * SEQ_LEN)[:, :, SEQ_LEN - 1 : 2 * SEQ_LEN - 1]

    bias, bias_back = jax.vjp(bias_of, position_bias)

    def split_heads(matrix):
        return matrix.reshape(seq_count, SEQ_LEN, heads_here, head_size)

    def merge_heads(blocks):
        return blocks.reshape(tokens, heads_here * head_size).astype(jnp.bfloat16)

    hidden = layer_input.astype(jnp.float32)
    normed_full, scale_one = norm_forward(hidden, attn_gain)
    normed = normed_full.astype(jnp.bfloat16)
    queries = jnp.dot(normed, query_weight, preferred_element_type=jnp.float32).astype(jnp.bfloat16)
    keys_all = jnp.dot(normed, key_weight, preferred_element_type=jnp.float32).astype(jnp.bfloat16)
    values_all = jnp.dot(normed, value_weight, preferred_element_type=jnp.float32).astype(
        jnp.bfloat16
    )
    query_blocks = split_heads(queries)
    key_blocks = split_heads(keys_all)
    value_blocks = split_heads(values_all)

    def score_of(query_block, key_block):
        return (
            jnp.einsum("qhc,khc->hqk", query_block, key_block, preferred_element_type=jnp.float32)
            * score_scale
            + bias
        )

    def attend(pieces):
        query_block, key_block, value_block = pieces
        scores = score_of(query_block, key_block)
        row_max = jnp.max(scores, axis=-1, keepdims=True)
        exponent_term = jnp.exp(scores - row_max)
        row_total = jnp.sum(exponent_term, axis=-1, keepdims=True)
        weights_low = (exponent_term / row_total).astype(jnp.bfloat16)
        context_block = jnp.einsum(
            "hqk,khc->qhc", weights_low, value_block, preferred_element_type=jnp.float32
        )
        return (context_block, (row_max + jnp.log(row_total))[..., 0])

    context_full, log_total = lax.map(attend, (query_blocks, key_blocks, value_blocks))
    context = merge_heads(context_full)
    attended = lax.psum(
        jnp.dot(context, output_weight, preferred_element_type=jnp.float32), "tensor"
    )
    middle = hidden + attended
    mixed_full, scale_two = norm_forward(middle, moe_gain)
    mixed = mixed_full.astype(jnp.bfloat16)
    logits = jnp.dot(mixed, router_weight, preferred_element_type=jnp.float32)
    router_probs = jax.nn.softmax(logits, axis=-1)
    kept_mask = (1 - route_drop).astype(jnp.float32)
    one_hot = (route_expert[:, None] == jnp.arange(experts, dtype=jnp.int32)[None, :]).astype(
        jnp.float32
    )
    chosen_prob = jnp.sum(router_probs * one_hot, axis=-1)
    gate_value = chosen_prob * kept_mask
    slot_total = experts * capacity
    target = jnp.where(route_drop > 0, slot_total, route_expert * capacity + route_slot)
    placement = target[None, :] == jnp.arange(slot_total, dtype=jnp.int32)[:, None]
    place_low = placement.astype(jnp.bfloat16)
    place_full = placement.astype(jnp.float32)

    def to_slots(rows):
        slots = jnp.dot(place_low, rows, preferred_element_type=jnp.float32).astype(jnp.bfloat16)
        return slots.reshape(groups, local_experts, capacity, model_width)

    def from_slots(slots):
        flat_slots = slots.reshape(slot_total, slots.shape[-1])
        if flat_slots.dtype == jnp.bfloat16:
            return jnp.einsum(
                "st,sd->td", place_low, flat_slots, preferred_element_type=jnp.float32
            )
        return jnp.einsum("st,sd->td", place_full, flat_slots, precision=HIGHEST_PRECISION)

    received = lax.all_to_all(to_slots(mixed), "expert", split_axis=0, concat_axis=0, tiled=True)
    pre_act = jnp.einsum("secd,edf->secf", received, expert_in, preferred_element_type=jnp.float32)
    activated, gelu_back = jax.vjp(jax.nn.gelu, pre_act)
    act_low = activated.astype(jnp.bfloat16)
    partial_out = jnp.einsum(
        "secf,efd->secd", act_low, expert_out, preferred_element_type=jnp.float32
    )
    summed = lax.psum(partial_out, "tensor").astype(jnp.bfloat16)
    expert_rows = from_slots(
        lax.all_to_all(summed, "expert", split_axis=0, concat_axis=0, tiled=True)
    )
    layer_output = (middle + gate_value[:, None] * expert_rows).astype(jnp.bfloat16)
    upstream = out_grad.astype(jnp.float32)
    gate_grad = jnp.sum(upstream * expert_rows, axis=-1) * kept_mask
    row_grad = (upstream * gate_value[:, None]).astype(jnp.bfloat16)
    grad_received = lax.all_to_all(
        to_slots(row_grad), "expert", split_axis=0, concat_axis=0, tiled=True
    )
    act_grad = jnp.einsum(
        "secd,efd->secf", grad_received, expert_out, preferred_element_type=jnp.float32
    )
    pre_grad = gelu_back(act_grad)[0].astype(jnp.bfloat16)
    expert_out_grad = jnp.einsum(
        "secf,secd->efd", act_low, grad_received, preferred_element_type=jnp.float32
    )
    expert_in_grad = jnp.einsum(
        "secd,secf->edf", received, pre_grad, preferred_element_type=jnp.float32
    )
    input_part = jnp.einsum(
        "secf,edf->secd", pre_grad, expert_in, preferred_element_type=jnp.float32
    )
    input_sum = lax.psum(input_part, "tensor")
    mixed_grad = from_slots(
        lax.all_to_all(input_sum, "expert", split_axis=0, concat_axis=0, tiled=True)
    )
    logit_grad = (router_probs * (one_hot - chosen_prob[:, None]) * gate_grad[:, None]).astype(
        jnp.bfloat16
    )
    router_grad = jnp.einsum("td,te->de", mixed, logit_grad, preferred_element_type=jnp.float32)
    mixed_grad = mixed_grad + jnp.einsum(
        "te,de->td", logit_grad, router_weight, preferred_element_type=jnp.float32
    )
    middle_back, moe_gain_grad = norm_backward(middle, scale_two, moe_gain, mixed_grad)
    middle_grad = upstream + middle_back
    middle_low = middle_grad.astype(jnp.bfloat16)
    output_grad = jnp.einsum("td,te->de", context, middle_low, preferred_element_type=jnp.float32)
    context_grad = jnp.einsum(
        "te,de->td", middle_low, output_weight, preferred_element_type=jnp.float32
    ).astype(jnp.bfloat16)

    def attend_back(running, pieces):
        query_block, key_block, value_block, context_block, log_block = pieces
        weights = jnp.exp(score_of(query_block, key_block) - log_block[..., None])
        weights_low = weights.astype(jnp.bfloat16)
        value_grad_block = jnp.einsum(
            "hqk,qhc->khc", weights_low, context_block, preferred_element_type=jnp.float32
        )
        weight_grad = jnp.einsum(
            "qhc,khc->hqk", context_block, value_block, preferred_element_type=jnp.float32
        )
        inner_sum = jnp.sum(weights * weight_grad, axis=-1, keepdims=True)
        score_grad = (weights * (weight_grad - inner_sum)).astype(jnp.bfloat16)
        query_grad_block = (
            jnp.einsum("hqk,khc->qhc", score_grad, key_block, preferred_element_type=jnp.float32)
            * score_scale
        )
        key_grad_block = (
            jnp.einsum("hqk,qhc->khc", score_grad, query_block, preferred_element_type=jnp.float32)
            * score_scale
        )
        return (
            running + score_grad.astype(jnp.float32),
            (query_grad_block, key_grad_block, value_grad_block),
        )

    bias_sum, grad_blocks = lax.scan(
        attend_back,
        jnp.zeros((heads_here, SEQ_LEN, SEQ_LEN), jnp.float32),
        (query_blocks, key_blocks, value_blocks, split_heads(context_grad), log_total),
    )
    queries_low = merge_heads(grad_blocks[0])
    keys_low = merge_heads(grad_blocks[1])
    values_low = merge_heads(grad_blocks[2])
    query_grad = jnp.einsum("td,te->de", normed, queries_low, preferred_element_type=jnp.float32)
    key_grad = jnp.einsum("td,te->de", normed, keys_low, preferred_element_type=jnp.float32)
    value_grad = jnp.einsum("td,te->de", normed, values_low, preferred_element_type=jnp.float32)
    normed_part = jnp.einsum(
        "te,de->td", queries_low, query_weight, preferred_element_type=jnp.float32
    )
    normed_part = normed_part + jnp.einsum(
        "te,de->td", keys_low, key_weight, preferred_element_type=jnp.float32
    )
    normed_part = normed_part + jnp.einsum(
        "te,de->td", values_low, value_weight, preferred_element_type=jnp.float32
    )
    normed_grad = lax.psum(normed_part.astype(jnp.bfloat16), "tensor").astype(jnp.float32)
    hidden_back, attn_gain_grad = norm_backward(hidden, scale_one, attn_gain, normed_grad)
    input_grad = middle_grad + hidden_back
    bias_grad = bias_back(bias_sum)[0]
    summed_grads = (
        lax.psum(attn_gain_grad.astype(jnp.bfloat16), "expert").astype(jnp.float32),
        lax.psum(query_grad.astype(jnp.bfloat16), "expert").astype(jnp.float32),
        lax.psum(key_grad.astype(jnp.bfloat16), "expert").astype(jnp.float32),
        lax.psum(value_grad.astype(jnp.bfloat16), "expert").astype(jnp.float32),
        lax.psum(output_grad.astype(jnp.bfloat16), "expert").astype(jnp.float32),
        lax.psum(bias_grad.astype(jnp.bfloat16), "expert").astype(jnp.float32),
        lax.psum(moe_gain_grad.astype(jnp.bfloat16), "expert").astype(jnp.float32),
        lax.psum(router_grad.astype(jnp.bfloat16), "expert").astype(jnp.float32),
    )
    return (
        layer_output,
        input_grad,
        summed_grads[0],
        summed_grads[1],
        summed_grads[2],
        summed_grads[3],
        summed_grads[4],
        summed_grads[5],
        summed_grads[6],
        summed_grads[7],
        expert_in_grad,
        expert_out_grad,
    )


def solution(mesh):
    in_specs = (
        P("expert", None),
        P(),
        P(None, "tensor"),
        P(None, "tensor"),
        P(None, "tensor"),
        P("tensor", None),
        P(None, "tensor"),
        P(),
        P(),
        P("expert", None, "tensor"),
        P("expert", "tensor", None),
        P("expert"),
        P("expert"),
        P("expert"),
        P("expert", None),
    )
    out_specs = (
        P("expert", None),
        P("expert", None),
        P(),
        P(None, "tensor"),
        P(None, "tensor"),
        P(None, "tensor"),
        P("tensor", None),
        P(None, "tensor"),
        P(),
        P(),
        P("expert", None, "tensor"),
        P("expert", "tensor", None),
    )
    return jax.shard_map(shards, mesh=mesh, in_specs=in_specs, out_specs=out_specs, check_vma=False)
```

profile of v0, /device:TPU:0, one launch (start us, length us, event | category | flops | bytes accessed | tf_op | source)
XLA Modules:
  0.0 777.4 jit_solution(9643858291279352101)
XLA Ops:
  10.4 3.4 tile.4
  13.8 13.9 %tile.10 = f32[3,524800]{1,0:T(4,128)} reshape(f32[3,512,1025]{2,1,0:T(8,128)} %tile.4) | data formatting | bytes 12595200 | tf_op jit(solution)/shard_map/jvp()/tile | solution.py:77
  27.7 3.4 slice-done
  31.1 3.9 copy.93
  37.5 3.6 copy.80
  48.7 51.4 %all-reduce.10.cloned.1.call-done = f32[512,768]{1,0:T(8,128)} async-done(((f32[512,768]{1,0:T(8,128)}), f32[512,768]{1,0:T(8,128)}) %all-reduce.10.cloned.1.call-update) | async-done | bytes 1572880 | tf_op jit(solution)/shard_map/psum | solution.py:121
  110.9 28.2 %all_to_all.20 = bf16[32,2,10,768]{3,1,2,0:T(2,128)(2,1)S(1)} all-to-all(bf16[32,2,10,768]{3,1,2,0:T(2,128)(2,1)S(1)} %copy.58), channel_id=1, replica_groups=mesh['expert'=32,'tensor'=4] {'expert'}, dimensions={0} | all-to-all | bytes 1966080 | tf_op jit(solution)/shard_map/all_to_all | solution.py:153
  144.7 39.2 %all-reduce.17 = bf16[32,2,10,768]{3,0,2,1:T(8,128)(2,1)} all-reduce(f32[32,2,10,768]{3,0,2,1:T(8,128)} %fusion.22), channel_id=1, replica_groups=mesh['expert'=32,'tensor'=4] {'tensor'}, use_global_device_ids=true, to_apply=%region_8.9 | all-reduce | flops 491520 | bytes 2949120 | tf_op jit(solution)/shard_map/psum | solution.py:160
  187.0 4.6 all-to-all-start.1
  193.7 17.3 %all-to-all-done.1 = bf16[32,2,10,768]{3,1,2,0:T(2,128)(2,1)} async-done(((bf16[32,2,10,768]{3,1,2,0:T(2,128)(2,1)}), bf16[32,2,10,768]{3,1,2,0:T(2,128)(2,1)}, u32[]{:S(2)}, u32[]{:S(2)}) %all-to-all-start.1) | async-done | bytes 983072 | tf_op jit(solution)/shard_map/all_to_all | solution.py:162
  216.7 3.6 fusion.31
  227.4 21.7 %all_to_all.21 = bf16[32,2,10,768]{3,1,2,0:T(2,128)(2,1)S(1)} all-to-all(bf16[32,2,10,768]{3,1,2,0:T(2,128)(2,1)S(1)} %copy.62), channel_id=1, replica_groups=mesh['expert'=32,'tensor'=4] {'expert'}, dimensions={0} | all-to-all | bytes 1966080 | tf_op jit(solution)/shard_map/all_to_all | solution.py:168
  254.3 50.8 %all-reduce.12.cloned.1.call-done = f32[32,2,10,768]{3,0,2,1:T(8,128)} async-done(((f32[32,2,10,768]{3,0,2,1:T(8,128)}), f32[32,2,10,768]{3,0,2,1:T(8,128)}) %all-reduce.12.cloned.1.call-update) | async-done | bytes 1966096 | tf_op jit(solution)/shard_map/psum | solution.py:184
  305.1 4.4 copy.64
  309.4 9.4 %all-to-all-start.3 = ((f32[32,2,10,768]{3,1,2,0:T(2,128)}), f32[32,2,10,768]{3,1,2,0:T(2,128)S(1)}, u32[]{:S(2)}, u32[]{:S(2)}) async-start(f32[32,2,10,768]{3,1,2,0:T(2,128)} %copy.64), calls=%async_computation.3 | async-start | bytes 3932160 | tf_op jit(solution)/shard_map/all_to_all | solution.py:186
  321.1 5.3 convolution_bitcast_fusion.1
  326.4 3.8 convolution_bitcast_fusion
  330.2 19.1 %all-to-all-done.3 = f32[32,2,10,768]{3,1,2,0:T(2,128)S(1)} async-done(((f32[32,2,10,768]{3,1,2,0:T(2,128)}), f32[32,2,10,768]{3,1,2,0:T(2,128)S(1)}, u32[]{:S(2)}, u32[]{:S(2)}) %all-to-all-start.3) | async-done | bytes 1966112 | tf_op jit(solution)/shard_map/all_to_all | solution.py:186
  372.7 4.7 copy.83
  380.8 7.1 pad_convert_fusion
  387.9 14.7 %reshape.144 = f32[3,512,1025]{2,1,0:T(8,128)} reshape(f32[3,524800]{1,0:T(4,128)} %pad_convert_fusion) | data formatting | bytes 12595200 | tf_op jit(solution)/shard_map/transpose(jvp())/reshape | solution.py:77
  402.6 3.4 reduce_sum.120
  408.3 95.9 %all-reduce.2 = (bf16[768]{0:T(1024)(128)(2,1)S(1)}, bf16[32,3]{0,1:T(4,128)(2,1)S(1)}, bf16[768]{0:T(1024)(128)(2,1)S(1)}) all-reduce(bf16[768]{0:T(1024)(128)(2,1)S(1)} %get-tuple-element.57, bf16[32,3]{0,1:T(4,128)(2,1)S(1)} %fusion.53, bf16[768]{0:T(1024)(128)(2,1)S(1)} %get-tuple-element.55), channel_id=1, replica_groups=mesh['expert'=32,'tensor'=4] {'expert'}, use_global_device_ids=true, to_apply=%region_16.17 | all-reduce | flops 1632 | bytes 6528 | tf_op jit(solution)/shard_map/psum | solution.py:253
  509.4 255.0 %all-reduce.16.cloned.1.call-done = (bf16[768,192]{0,1:T(8,128)(2,1)}, bf16[768,192]{0,1:T(8,128)(2,1)}, bf16[768,192]{0,1:T(8,128)(2,1)}, bf16[192,768]{1,0:T(8,128)(2,1)}, bf16[768,64]{0,1:T(8,128)(2,1)}) async-done(((bf16[768,192]{0,1:T(8,128)(2,1)}, bf16[768,192]{0,1:T(8,128)(2,1)}, bf16[768,192]{0,1:T(8,128)(2,1)}, bf16[192,768]{1,0:T(8,128)(2,1)}, bf16[768,64]{0,1:T(8,128)(2,1)}), ...) | async-done | bytes 1277968 | tf_op jit(solution)/shard_map/psum | solution.py:254
  (171 shorter events, 95.0 us)
Async XLA Ops:
  7.2 135.1 %copy-start = (bf16[2,768,768]{2,1,0:T(8,128)(2,1)S(1)}, bf16[2,768,768]{2,1,0:T(8,128)(2,1)}, u32[]{:S(2)}) copy-start(bf16[2,768,768]{2,1,0:T(8,128)(2,1)} %param.26) | copy-start | bytes 7077892
  7.2 92.9 %all-reduce.10.cloned.1.call-start = ((), (), s32[]{:S(2)}) async-start(), calls=%async_computation.4 | async-start | bytes 3145728 | tf_op jit(solution)/shard_map/psum | solution.py:121
  27.7 3.4 slice-start
  37.5 3.6 copy-start.9
  37.5 3.6 copy-start.31
  37.5 3.6 copy-start.44
  42.1 3.1 copy-start.39
  48.7 54.2 %copy-start.42 = (f32[768]{0:T(1024)S(1)}, f32[768]{0:T(1024)}, u32[]{:S(2)}) copy-start(f32[768]{0:T(1024)} %param.23) | copy-start | bytes 9220
  108.6 31.6 %copy-start.10 = (bf16[2,768,768]{2,1,0:T(8,128)(2,1)S(1)}, bf16[2,768,768]{2,1,0:T(8,128)(2,1)}, u32[]{:S(2)}) copy-start(bf16[2,768,768]{2,1,0:T(8,128)(2,1)} %param.25) | copy-start | bytes 7077892
  187.0 24.1 %all-to-all-start.1 = ((bf16[32,2,10,768]{3,1,2,0:T(2,128)(2,1)}), bf16[32,2,10,768]{3,1,2,0:T(2,128)(2,1)}, u32[]{:S(2)}, u32[]{:S(2)}) async-start(bf16[32,2,10,768]{3,1,2,0:T(2,128)(2,1)} %copy.60), calls=%async_computation.1 | async-start | bytes 1966080 | tf_op jit(solution)/shard_map/all_to_all | solution.py:162
  191.7 113.4 %all-reduce.12.cloned.1.call-start = ((), (), s32[]{:S(2)}) async-start(), calls=%async_computation.5 | async-start | bytes 3932160 | tf_op jit(solution)/shard_map/psum | solution.py:184
  216.7 3.6 copy-start.24
  225.1 24.1 %copy-start.16 = (f32[2,32,10,768]{3,1,2,0:T(8,128)S(1)}, f32[2,32,10,768]{3,1,2,0:T(8,128)}, u32[]{:S(2)}) copy-start(f32[2,32,10,768]{3,1,2,0:T(8,128)} %copy-done.15) | copy-start | bytes 5898244
  309.4 39.8 %all-to-all-start.3 = ((f32[32,2,10,768]{3,1,2,0:T(2,128)}), f32[32,2,10,768]{3,1,2,0:T(2,128)S(1)}, u32[]{:S(2)}, u32[]{:S(2)}) async-start(f32[32,2,10,768]{3,1,2,0:T(2,128)} %copy.64), calls=%async_computation.3 | async-start | bytes 3932160 | tf_op jit(solution)/shard_map/all_to_all | solution.py:186
  318.8 87.6 %all-reduce.14.cloned.1.call-start = ((), (), s32[]{:S(2)}) async-start(), calls=%async_computation.6 | async-start | bytes 1572864 | tf_op jit(solution)/shard_map/psum | solution.py:248
  321.1 5.3 copy-start.17
  321.1 5.3 copy-start.22
  359.3 20.4 %copy-start.6 = (f32[512,768]{1,0:T(8,128)}, f32[512,768]{1,0:T(8,128)S(1)}, u32[]{:S(2)}) copy-start(f32[512,768]{1,0:T(8,128)S(1)} %get-tuple-element.80) | copy-start | bytes 4718596
  369.9 394.5 %all-reduce.16.cloned.1.call-start = ((), (), s32[]{:S(2)}) async-start(), calls=%async_computation.7 | async-start | bytes 2555904 | tf_op jit(solution)/shard_map/psum | solution.py:254
  402.6 3.4 copy-start.14
  506.0 264.5 %copy-start.1 = (bf16[2,768,768]{2,1,0:T(8,128)(2,1)S(1)}, bf16[2,768,768]{2,1,0:T(8,128)(2,1)}, u32[]{:S(2)}) copy-start(bf16[2,768,768]{2,1,0:T(8,128)(2,1)} %param.26) | copy-start | bytes 7077892
  764.4 3.7 copy-start.34
  764.4 4.6 copy-start.33
  764.4 5.4 copy-start.41
  (30 other events, 49.9 us)
Sparse Core Ops, SparseCore 0:
  48.7 51.2 all-reduce.9
  254.4 50.6 all-reduce.11
  370.1 34.7 all-reduce.13
  408.1 356.2 all-reduce.15
where the time goes:
time: 787 us; the launch traced here: 777 us
  waiting for transfers between devices  394 us (50%)
  blocking collectives  185 us (24%)
  local copies, waits for them, and re-layouts  93.3 us (12%)
  matrix products  45.9 us (6%)
  other arithmetic  29.9 us (4%)
  starting transfers between devices  15 us (2%)
  between operations  14.6 us (2%)
    psum x1, waiting for transfers between devices, shards(): lax.psum(query_grad.astype(jnp.bfloat16), 'expert').astype(jnp.float32)  255 us
    psum x1, blocking collectives, shards(): lax.psum(attn_gain_grad.astype(jnp.bfloat16), 'expert').astype(jnp.float32)  95.9 us
    psum x1, waiting for transfers between devices, shards(): lax.psum(jnp.dot(context, output_weight, preferred_element_type=jnp.float...  51.4 us
    psum x1, waiting for transfers between devices, shards(): input_sum = lax.psum(input_part, 'tensor')  50.8 us
    psum x1, blocking collectives, shards(): summed = lax.psum(partial_out, 'tensor').astype(jnp.bfloat16)  39.2 us
    all_to_all x1, blocking collectives, shards(): lax.all_to_all(to_slots(mixed), 'expert', split_axis=0, concat_axis=0, ti...  28.2 us
    unnamed x99, local copies, waits for them, and re-layouts  27.1 us
    all_to_all x1, blocking collectives, shards(): lax.all_to_all(to_slots(row_grad), 'expert', split_axis=0, concat_axis=0,...  21.7 us
  transfers between devices with their start and end apart: 6, of which 5 were waited for; matrix products, arithmetic and copies ran while one was open for 7% of the time, Pallas kernels for 0%

commit v1 on v0

v1 whole, which is shorter than its diff:
```python
import jax
import jax.numpy as jnp
import numpy as np
from jax import lax
from jax.experimental import pallas as pl
from jax.experimental.pallas import tpu as pltpu
from jax.sharding import Mesh
from jax.sharding import PartitionSpec as P

BUCKETS = 32
EPS = 1e-06
SEQ = 512
D = 768
HEAD = 64
HEADS_HERE = 3
WIDTH = HEADS_HERE * HEAD
EXPERTS = 64
CAP = 10
GROUPS = 32
CHUNK = 40
ROWS = GROUPS * CHUNK
HALF = D // 2
GRADS = 896
F32 = jnp.float32
BF16 = jnp.bfloat16
GELU_C = float(np.sqrt(2.0 / np.pi))


def bucket_of(offsets):
    half_count = BUCKETS // 2
    exact_count = half_count // 2
    upper_side = (offsets > 0).astype(np.int64) * half_count
    distance = np.abs(offsets)
    ratio = np.log(np.maximum(distance, 1) / exact_count) / np.log(128.0 / exact_count)
    far_bucket = np.minimum(
        exact_count + (ratio * (half_count - exact_count)).astype(np.int64), half_count - 1
    )
    return upper_side + np.where(distance < exact_count, distance, far_bucket)


def line_ids():
    ids = np.full((8, 256), -1, np.int32)
    for row, block in enumerate((-1, 0, 1)):
        ids[row] = bucket_of(128 * block + 128 - np.arange(256))
    ids[:3, 0] = -1
    return ids


def regroup_matrix():
    sel = np.zeros((320, 320), np.float32)
    for g in range(8):
        for half in range(2):
            for e in range(2):
                for c in range(CAP):
                    sel[half * 160 + e * 80 + g * 10 + c, g * 40 + half * 20 + e * 10 + c] = 1
    return sel


def spread_matrix(width, start, total):
    out = np.zeros((width, total), np.float32)
    out[np.arange(width), start + np.arange(width)] = 1
    return out


def dot(a, b):
    return jnp.dot(a, b, preferred_element_type=F32)


def dot_nt(a, b):
    return lax.dot_general(a, b, (((1,), (1,)), ((), ())), preferred_element_type=F32)


def dot_tn(a, b):
    return lax.dot_general(a, b, (((0,), (0,)), ((), ())), preferred_element_type=F32)


def head_mask(head, rows):
    lanes = lax.broadcasted_iota(jnp.int32, (rows, WIDTH), 1)
    return (lanes >= head * HEAD) & (lanes < (head + 1) * HEAD)


def only_head(matrix, head):
    return jnp.where(head_mask(head, matrix.shape[0]), matrix, jnp.zeros_like(matrix))


def call(body, out_shape, args, scratch=(), scalars=0, limit=40, flops=0, moved=0):
    specs = [pl.BlockSpec(memory_space=pltpu.SMEM)] * scalars
    specs += [pl.BlockSpec(memory_space=pltpu.VMEM)] * (len(args) - scalars)
    return pl.pallas_call(
        body,
        out_shape=out_shape,
        in_specs=specs,
        out_specs=jax.tree.map(lambda _: pl.BlockSpec(memory_space=pltpu.VMEM), out_shape),
        scratch_shapes=scratch,
        compiler_params=pltpu.CompilerParams(vmem_limit_bytes=limit << 20),
        cost_estimate=pl.CostEstimate(flops=flops, bytes_accessed=moved, transcendentals=0),
    )(*args)


def shape(dims, dtype):
    return jax.ShapeDtypeStruct(dims, dtype)


def bias_tile(tiles_ref, far_low, far_high, head, block):
    if block < -1:
        return far_low
    if block > 1:
        return far_high
    return tiles_ref[head * 3 + block + 1]


def scores_t(keys, query_scaled, tiles_ref, table_ref, head, part):
    raw = dot_nt(keys, query_scaled)
    far_low = table_ref[BUCKETS // 2 - 1, head]
    far_high = table_ref[BUCKETS - 1, head]
    rows = []
    for key_block in range(4):
        cols = []
        for i in range(2):
            piece = raw[key_block * 128 : key_block * 128 + 128, i * 128 : i * 128 + 128]
            block = key_block - (part * 2 + i)
            cols.append(piece + bias_tile(tiles_ref, far_low, far_high, head, block))
        rows.append(jnp.concatenate(cols, axis=1))
    return jnp.concatenate(rows, axis=0)


def attention_forward(
    table_ref, x_ref, gain_ref, wq_ref, wk_ref, wv_ref, ids_ref,
    normed_ref, q_ref, k_ref, v_ref, ctx_ref, lse_ref, tiles_ref,
):
    for i in range(4):
        rows = pl.ds(i * 128, 128)
        x = x_ref[rows, :].astype(F32)
        scale = lax.rsqrt(jnp.mean(x * x, axis=-1, keepdims=True) + EPS)
        normed_ref[rows, :] = (x * scale * gain_ref[...]).astype(BF16)
    for head in range(HEADS_HERE):
        for block in range(3):
            ids = ids_ref[block : block + 1, :]
            line = jnp.zeros((1, 256), F32)
            for b in range(BUCKETS):
                line = jnp.where(ids == b, table_ref[b, head], line)
            wide = pltpu.roll(
                jnp.broadcast_to(line, (128, 256)), 0, 1, stride=1, stride_axis=0
            )
            tiles_ref[head * 3 + block] = wide[:, 128:]
    normed = normed_ref[...]
    queries = dot(normed, wq_ref[...]).astype(BF16)
    keys = dot(normed, wk_ref[...]).astype(BF16)
    values = dot(normed, wv_ref[...]).astype(BF16)
    q_ref[...] = queries
    k_ref[...] = keys
    v_ref[...] = values
    lse_ref[...] = jnp.zeros((8, SEQ), F32)
    scaled = queries * jnp.asarray(HEAD**-0.5, BF16)
    for part in range(2):
        rows = slice(part * 256, part * 256 + 256)
        context = jnp.zeros((256, WIDTH), F32)
        for head in range(HEADS_HERE):
            scores = scores_t(
                keys, only_head(scaled[rows], head), tiles_ref, table_ref, head, part
            )
            top = jnp.max(scores, axis=0, keepdims=True)
            grown = jnp.exp(scores - top)
            total = jnp.sum(grown, axis=0, keepdims=True)
            probs = (grown * (1.0 / total)).astype(BF16)
            lse_ref[head : head + 1, rows] = top + jnp.log(total)
            context = context + dot_tn(probs, only_head(values, head))
        ctx_ref[rows, :] = context.astype(BF16)


def route_columns(route_ref):
    return jnp.transpose(route_ref[...].astype(F32))


def row_of(expert, slot, drop):
    row = (expert >> 1) * CHUNK + (expert & 1) * CAP + slot
    return jnp.where(drop > 0, -1000, row)


def middle_kernel(
    place_ref, x_ref, ctx0, ctx1, ctx2, ctx3, wo0, wo1, wo2, wo3, gain_ref, router_ref,
    route_ref, grad_ref, middle_ref, mixed_ref, probs_ref, send_ref, ctx_s, wo_s, rows_s,
):
    me = place_ref[0]
    core = place_ref[1]
    for step, (c, w) in enumerate(((ctx0, wo0), (ctx1, wo1), (ctx2, wo2), (ctx3, wo3))):
        ctx_s[me ^ step] = c[...]
        wo_s[me ^ step] = w[...]
    columns = route_columns(route_ref)
    for i in range(2):
        rows = slice(i * 256, i * 256 + 256)
        attended = dot(ctx_s[0, rows, :], wo_s[0])
        for t in range(1, 4):
            attended = attended + dot(ctx_s[t, rows, :], wo_s[t])
        middle = x_ref[rows, :].astype(F32) + attended
        scale = lax.rsqrt(jnp.mean(middle * middle, axis=-1, keepdims=True) + EPS)
        mixed = (middle * scale * gain_ref[...]).astype(BF16)
        middle_ref[rows, :] = middle
        mixed_ref[rows, :] = mixed
        logits = dot(mixed, router_ref[...])
        grown = jnp.exp(logits - jnp.max(logits, axis=-1, keepdims=True))
        probs = grown / jnp.sum(grown, axis=-1, keepdims=True)
        probs_ref[rows, :] = probs
        expert = columns[rows, 0:1].astype(jnp.int32)
        lanes = lax.broadcasted_iota(jnp.int32, (256, EXPERTS), 1)
        chosen = jnp.sum(jnp.where(lanes == expert, probs, 0.0), axis=-1, keepdims=True)
        gate = chosen * (1.0 - columns[rows, 2:3])
        grads = (grad_ref[rows, :].astype(F32) * gate).astype(BF16)
        rows_s[rows, :] = jnp.where(core == 0, mixed, grads)
    target = row_of(route_ref[0:1, :], route_ref[1:2, :], route_ref[2:3, :])
    for i in range(4):
        index = lax.broadcasted_iota(jnp.int32, (320, SEQ), 0) + 320 * i
        low = (index == target).astype(F32).astype(BF16)
        high = (index == target + 20).astype(F32).astype(BF16)
        out = dot(low, rows_s[:, :HALF]) + dot(high, rows_s[:, HALF:])
        send_ref[pl.ds(i * 320, 320), :] = out.astype(BF16)


def expert_kernel(
    place_ref, own_ref, other_ref, in_ref, out_ref, sel_ref, back_ref,
    mine_ref, theirs_ref, x_ref, s_ref, act_ref, pre_ref, o_s, i_s,
):
    core = place_ref[1]
    for b in range(4):
        rows = pl.ds(b * 320, 320)
        own = own_ref[rows, :]
        other = other_ref[rows, :]
        for dest, block in (
            (x_ref, jnp.where(core == 0, own, other)),
            (s_ref, jnp.where(core == 0, other, own)),
        ):
            sorted_rows = dot(sel_ref[...], block).astype(BF16)
            for half in range(2):
                for e in range(2):
                    dest[e, pl.ds(b * 80, 80), pl.ds(half * HALF, HALF)] = sorted_rows[
                        half * 160 + e * 80 : half * 160 + e * 80 + 80
                    ]
    for e in range(2):
        x = x_ref[e]
        s = s_ref[e]
        out = jnp.zeros((320, D), F32)
        back = jnp.zeros((320, D), F32)
        for f in range(3):
            cols = slice(f * 256, f * 256 + 256)
            w_in = in_ref[e, :, cols]
            w_out = out_ref[e, cols, :]
            pre = dot(x, w_in)
            bent = jnp.tanh(GELU_C * (pre + 0.044715 * (pre * pre * pre)))
            cdf = 0.5 * (1.0 + bent)
            act = (pre * cdf).astype(BF16)
            slope = cdf + (0.5 * GELU_C) * pre * (1.0 - bent * bent) * (
                1.0 + (3 * 0.044715) * (pre * pre)
            )
            act_ref[e, :, cols] = act
            out = out + dot(act, w_out)
            act_grad = dot_nt(s, w_out)
            pre_grad = (act_grad * slope).astype(BF16)
            pre_ref[e, :, cols] = pre_grad
            back = back + dot_nt(pre_grad, w_in)
        o_s[e] = out.astype(BF16)
        i_s[e] = back.astype(BF16)
    for b in range(4):
        rows = pl.ds(b * 80, 80)
        pieces = []
        for src in (o_s, i_s):
            stacked = jnp.concatenate(
                [
                    src[e, rows, pl.ds(half * HALF, HALF)]
                    for half in range(2)
                    for e in range(2)
                ],
                axis=0,
            )
            pieces.append(dot(back_ref[...], stacked).astype(BF16))
        mine_ref[pl.ds(b * 320, 320), :] = jnp.where(core == 0, pieces[0], pieces[1])
        theirs_ref[pl.ds(b * 320, 320), :] = jnp.where(core == 0, pieces[1], pieces[0])


def expert_grads_kernel(x_ref, s_ref, act_ref, pre_ref, in_grad_ref, out_grad_ref):
    out_grad_ref[0] = dot_tn(act_ref[0], s_ref[0])
    in_grad_ref[0] = dot_tn(x_ref[0], pre_ref[0])


def expert_grads(x, s, act, pre):
    whole = pl.BlockSpec((1, 320, D), lambda e, f: (e, 0, 0))
    part = pl.BlockSpec((1, 320, 256), lambda e, f: (e, 0, f))
    return pl.pallas_call(
        expert_grads_kernel,
        grid=(2, 3),
        out_shape=(shape((2, D, D), F32), shape((2, D, D), F32)),
        in_specs=[whole, whole, part, part],
        out_specs=(
            pl.BlockSpec((1, D, 256), lambda e, f: (e, 0, f)),
            pl.BlockSpec((1, 256, D), lambda e, f: (e, f, 0)),
        ),
        compiler_params=pltpu.CompilerParams(vmem_limit_bytes=24 << 20),
        cost_estimate=pl.CostEstimate(
            flops=8 * 320 * D * D, bytes_accessed=14_000_000, transcendentals=0
        ),
    )(x, s, act, pre)


def tokens_kernel(route_ref, recv_ref, out_ref):
    columns = route_columns(route_ref).astype(jnp.int32)
    target = row_of(columns[:, 0:1], columns[:, 1:2], columns[:, 2:3])
    slots = (
        recv_ref[pl.ds(0, ROWS), :].astype(F32) + recv_ref[pl.ds(ROWS, ROWS), :].astype(F32)
    ).astype(BF16)
    for i in range(2):
        rows = slice(i * 256, i * 256 + 256)
        index = lax.broadcasted_iota(jnp.int32, (256, ROWS), 1)
        low = (index == target[rows]).astype(F32).astype(BF16)
        high = (index == target[rows] + 20).astype(F32).astype(BF16)
        out_ref[rows, pl.ds(0, HALF)] = dot(low, slots).astype(BF16)
        out_ref[rows, pl.ds(HALF, HALF)] = dot(high, slots).astype(BF16)


def backward_kernel(
    place_ref, table_ref, x_ref, middle_ref, mixed_ref, probs_ref, route_ref, grad_ref,
    own_ref, other_ref, router_ref, gain_ref, wo_ref, ctx_ref, q_ref, k_ref, v_ref, normed_ref,
    lse_ref, tiles_ref, wq_ref, wk_ref, wv_ref, ids_ref, place_q, place_r,
    output_ref, middle_grad_ref, grads_ref, small_ref, mine_ref, theirs_ref,
    low_s, logit_s, normed_s,
):
    core = place_ref[1]
    columns = route_columns(route_ref)
    gain = gain_ref[...]
    gain_grad = jnp.zeros((1, D), F32)
    for i in range(4):
        rows = slice(i * 128, i * 128 + 128)
        own = own_ref[rows, :]
        other = other_ref[rows, :]
        expert_rows = jnp.where(core == 0, own, other).astype(F32)
        mixed_grad = jnp.where(core == 0, other, own).astype(F32)
        probs = probs_ref[rows, :]
        kept = 1.0 - columns[rows, 2:3]
        lanes = lax.broadcasted_iota(jnp.int32, (128, EXPERTS), 1)
        hot = (lanes == columns[rows, 0:1].astype(jnp.int32)).astype(F32)
        chosen = jnp.sum(probs * hot, axis=-1, keepdims=True)
        middle = middle_ref[rows, :]
        upstream = grad_ref[rows, :].astype(F32)
        output_ref[rows, :] = (middle + (chosen * kept) * expert_rows).astype(BF16)
        gate_grad = jnp.sum(upstream * expert_rows, axis=-1, keepdims=True) * kept
        logit_grad = (probs * (hot - chosen) * gate_grad).astype(BF16)
        logit_s[rows, :] = logit_grad
        mixed_grad = mixed_grad + dot_nt(logit_grad, router_ref[...])
        scale = lax.rsqrt(jnp.mean(middle * middle, axis=-1, keepdims=True) + EPS)
        weighted = mixed_grad * gain
        inner = jnp.mean(weighted * middle, axis=-1, keepdims=True)
        gain_grad = gain_grad + jnp.sum(mixed_grad * middle * scale, axis=0, keepdims=True)
        middle_grad = upstream + scale * weighted - middle * (scale * scale * scale * inner)
        middle_grad_ref[rows, :] = middle_grad
        low_s[rows, :] = middle_grad.astype(BF16)
    middle_low = low_s[...]
    output_grad = dot_tn(middle_low, ctx_ref[...])
    pad = jnp.zeros((D, 256 - WIDTH), F32)
    grads_ref[:, 640:] = jnp.concatenate([output_grad, pad], axis=1).astype(BF16)
    ctx_grad = dot_nt(middle_low, wo_ref[...]).astype(BF16)

    keys = k_ref[...]
    values = v_ref[...]
    key_scaled = keys * jnp.asarray(HEAD**-0.5, BF16)
    query_scaled = q_ref[...] * jnp.asarray(HEAD**-0.5, BF16)
    key_grad = jnp.zeros((SEQ, WIDTH), F32)
    value_grad = jnp.zeros((SEQ, WIDTH), F32)
    query_grads = [jnp.zeros((256, WIDTH), F32), jnp.zeros((256, WIDTH), F32)]
    small_ref[...] = jnp.zeros((8, D), F32)
    small_ref[0:1, :] = gain_grad
    turn = (
        lax.broadcasted_iota(jnp.int32, (128, 128), 0)
        + lax.broadcasted_iota(jnp.int32, (128, 128), 1)
        == 127
    ).astype(F32)
    for head in range(HEADS_HERE):
        near = [jnp.zeros((128, 128), F32) for _ in range(3)]
        far_low = jnp.zeros((128, 128), F32)
        far_high = jnp.zeros((128, 128), F32)
        key_head = only_head(key_scaled, head)
        for part in range(2):
            rows = slice(part * 256, part * 256 + 256)
            query_head = only_head(query_scaled[rows], head)
            ctx_head = only_head(ctx_grad[rows], head)
            scores = scores_t(keys, query_head, tiles_ref, table_ref, head, part)
            probs = jnp.exp(scores - lse_ref[head : head + 1, rows])
            value_grad = value_grad + dot(probs.astype(BF16), ctx_head)
            prob_grad = dot_nt(values, ctx_head)
            inner = jnp.sum(probs * prob_grad, axis=0, keepdims=True)
            score_grad = (probs * (prob_grad - inner)).astype(BF16)
            key_grad = key_grad + dot(score_grad, query_head)
            query_grads[part] = query_grads[part] + dot_tn(score_grad, key_head)
            for key_block in range(4):
                for i in range(2):
                    piece = score_grad[
                        key_block * 128 : key_block * 128 + 128, i * 128 : i * 128 + 128
                    ].astype(F32)
                    block = key_block - (part * 2 + i)
                    if block < -1:
                        far_low = far_low + piece
                    elif block > 1:
                        far_high = far_high + piece
                    else:
                        near[block + 1] = near[block + 1] + piece
        buckets = lax.broadcasted_iota(jnp.int32, (BUCKETS, 256), 0)
        by_bucket = jnp.zeros((BUCKETS, 256), F32)
        for block in range(3):
            turned = jnp.dot(
                turn, near[block], precision=lax.Precision.HIGHEST, preferred_element_type=F32
            )
            wide = jnp.concatenate([turned, jnp.zeros((128, 128), F32)], axis=1)
            wide = pltpu.roll(wide, 1, 1, stride=1, stride_axis=0)
            line = jnp.sum(wide, axis=0, keepdims=True)
            by_bucket = by_bucket + jnp.where(
                buckets == ids_ref[block : block + 1, :], line, 0.0
            )
        side = lax.broadcasted_iota(jnp.int32, (BUCKETS, 128), 0)
        low_line = jnp.sum(far_low, axis=0, keepdims=True)
        high_line = jnp.sum(far_high, axis=0, keepdims=True)
        ends = jnp.where(side == BUCKETS // 2 - 1, low_line, 0.0) + jnp.where(
            side == BUCKETS - 1, high_line, 0.0
        )
        by_bucket = by_bucket[:, :128] + by_bucket[:, 128:] + ends
        total = jnp.sum(by_bucket, axis=1, keepdims=True)
        total = jnp.concatenate([total, jnp.zeros((128 - BUCKETS, 1), F32)], axis=0)
        total = jnp.transpose(jnp.broadcast_to(total, (128, 128)))
        small_ref[1 + head : 2 + head, 0:128] = total[0:1, :]
    query_low = jnp.concatenate(query_grads, axis=0).astype(BF16)
    key_low = key_grad.astype(BF16)
    value_low = value_grad.astype(BF16)
    spread = (
        dot(query_low, place_q[0]) + dot(key_low, place_q[1]) + dot(value_low, place_q[2])
    ).astype(BF16)
    logit_spread = dot(logit_s[...], place_r[...]).astype(BF16)
    joined = dot_tn(normed_ref[...], spread) + dot_tn(mixed_ref[...], logit_spread)
    grads_ref[:, :640] = joined.astype(BF16)
    normed_part = (
        dot_nt(query_low, wq_ref[...])
        + dot_nt(key_low, wk_ref[...])
        + dot_nt(value_low, wv_ref[...])
    )
    normed_s[...] = normed_part.astype(BF16)
    mine_ref[...] = normed_s[pl.ds(pl.multiple_of(core * 256, 256), 256), :]
    theirs_ref[...] = normed_s[pl.ds(pl.multiple_of((1 - core) * 256, 256), 256), :]


def input_kernel(
    place_ref, own_ref, other_ref, x_ref, gain_ref, middle_grad_ref, small_in, input_ref, small_ref
):
    core = place_ref[1]
    gain = gain_ref[...]
    gain_grad = jnp.zeros((1, D), F32)
    for i in range(4):
        rows = slice(i * 128, i * 128 + 128)
        local = slice((i % 2) * 128, (i % 2) * 128 + 128)
        own = own_ref[local, :]
        other = other_ref[local, :]
        normed_grad = jnp.where(core == i // 2, own, other).astype(F32)
        hidden = x_ref[rows, :].astype(F32)
        scale = lax.rsqrt(jnp.mean(hidden * hidden, axis=-1, keepdims=True) + EPS)
        weighted = normed_grad * gain
        inner = jnp.mean(weighted * hidden, axis=-1, keepdims=True)
        gain_grad = gain_grad + jnp.sum(normed_grad * hidden * scale, axis=0, keepdims=True)
        input_ref[rows, :] = (
            middle_grad_ref[rows, :]
            + scale * weighted
            - hidden * (scale * scale * scale * inner)
        )
    small_ref[...] = small_in[...]
    small_ref[4:5, :] = gain_grad


def finish_kernel(
    recv_ref, split_ref, small_ref, q_ref, k_ref, v_ref, o_ref, router_ref, whole_s
):
    small = jnp.zeros((8, GRADS), F32)
    for j in range(GROUPS):
        block = recv_ref[pl.ds(j * 32, 32), :].astype(F32)
        whole_s[pl.ds(j * 24, 24), :] = block[:24]
        small = small + block[24:]
    small_ref[...] = small[:, :D]
    joined = whole_s[:, :640].astype(BF16)
    q_ref[...] = whole_s[:, :WIDTH]
    k_ref[...] = dot(joined, split_ref[0])
    v_ref[...] = dot(joined, split_ref[1])
    router_ref[...] = dot(joined, split_ref[2])[:, :EXPERTS]
    o_ref[...] = jnp.transpose(whole_s[:, 640:])[:WIDTH, :]


def shards(
    layer_input, attn_gain, query_weight, key_weight, value_weight, output_weight, position_bias,
    moe_gain, router_weight, expert_in, expert_out, route_expert, route_slot, route_drop, out_grad,
):
    experts_axis = ("z", "x", "h")
    pair_axis = ("l", "z", "x", "h")
    core = lax.axis_index("c")
    place = jnp.stack([lax.axis_index("l") * 2 + core, core]).astype(jnp.int32)

    def swap(array, axis):
        return lax.ppermute(array, axis, [(0, 1), (1, 0)])

    ids = jnp.asarray(line_ids())
    gain_one = attn_gain.reshape(1, D)
    gain_two = moe_gain.reshape(1, D)
    zeros = jnp.zeros_like(route_drop)
    route = jnp.stack([route_expert, route_slot, route_drop] + [zeros] * 5)
    wo_link = swap(output_weight, "l")
    wo_core = swap(output_weight, "c")
    wo_far = swap(wo_link, "c")

    tall = shape((SEQ, WIDTH), BF16)
    normed, queries, keys, values, context, lse, tiles = call(
        attention_forward,
        (shape((SEQ, D), BF16), tall, tall, tall, tall, shape((8, SEQ), F32),
         shape((9, 128, 128), F32)),
        (position_bias, layer_input, gain_one, query_weight, key_weight, value_weight, ids),
        scalars=1, limit=32, flops=900_000_000, moved=5_000_000,
    )
    ctx_link = swap(context, "l")
    ctx_core = swap(context, "c")
    ctx_far = swap(ctx_link, "c")
    middle, mixed, probs, send = call(
        middle_kernel,
        (shape((SEQ, D), F32), shape((SEQ, D), BF16), shape((SEQ, EXPERTS), F32),
         shape((ROWS, HALF), BF16)),
        (place, layer_input, context, ctx_core, ctx_link, ctx_far,
         output_weight, wo_core, wo_link, wo_far, gain_two, router_weight, route, out_grad),
        scratch=(pltpu.VMEM((4, SEQ, WIDTH), BF16), pltpu.VMEM((4, WIDTH, D), BF16),
                 pltpu.VMEM((SEQ, D), BF16)),
        scalars=1, limit=32, flops=1_700_000_000, moved=8_000_000,
    )
    received = lax.all_to_all(send, experts_axis, 0, 0, tiled=True)
    received_other = swap(received, "c")
    select = regroup_matrix()
    low = shape((2, 320, D), BF16)
    mine, theirs, slots, slot_grads, act, pre_grad = call(
        expert_kernel,
        (shape((ROWS, HALF), BF16), shape((ROWS, HALF), BF16), low, low, low, low),
        (place, received, received_other, expert_in, expert_out,
         jnp.asarray(select, BF16), jnp.asarray(select.T, BF16)),
        scratch=(pltpu.VMEM((2, 320, D), BF16), pltpu.VMEM((2, 320, D), BF16)),
        scalars=1, limit=48, flops=5_000_000_000, moved=14_000_000,
    )
    partial = (mine.astype(F32) + swap(theirs, "c").astype(F32)).astype(BF16)
    back = lax.all_to_all(
        jnp.concatenate([partial, partial], axis=0), pair_axis, 0, 0, tiled=True
    )
    expert_in_grad, expert_out_grad = expert_grads(slots, slot_grads, act, pre_grad)
    rows_own = call(
        tokens_kernel, shape((SEQ, D), BF16), (route, back),
        limit=32, flops=2_000_000_000, moved=3_000_000,
    )
    rows_other = swap(rows_own, "c")
    place_q = jnp.asarray(
        np.stack([spread_matrix(WIDTH, WIDTH * i, 640) for i in range(3)]), BF16
    )
    place_r = jnp.asarray(spread_matrix(EXPERTS, 3 * WIDTH, 640), BF16)
    layer_output, middle_grad, grads, small, norm_mine, norm_theirs = call(
        backward_kernel,
        (shape((SEQ, D), BF16), shape((SEQ, D), F32), shape((D, GRADS), BF16),
         shape((8, D), F32), shape((256, D), BF16), shape((256, D), BF16)),
        (place, position_bias, layer_input, middle, mixed, probs, route, out_grad,
         rows_own, rows_other, router_weight, gain_two, output_weight, context, queries, keys,
         values, normed, lse, tiles, query_weight, key_weight, value_weight, ids,
         place_q, place_r),
        scratch=(pltpu.VMEM((SEQ, D), BF16), pltpu.VMEM((SEQ, EXPERTS), BF16),
                 pltpu.VMEM((SEQ, D), BF16)),
        scalars=2, limit=48, flops=4_000_000_000, moved=12_000_000,
    )
    scattered = lax.all_to_all(grads, experts_axis, 0, 0, tiled=True)
    halved = (norm_mine.astype(F32) + swap(norm_theirs, "c").astype(F32)).astype(BF16)
    halved = (halved.astype(F32) + swap(halved, "l").astype(F32)).astype(BF16)
    halved_other = swap(halved, "c")
    input_grad, small = call(
        input_kernel,
        (shape((SEQ, D), F32), shape((8, D), F32)),
        (place, halved, halved_other, layer_input, gain_one, middle_grad, small),
        scalars=1, limit=32, flops=10_000_000, moved=5_000_000,
    )
    summed = jnp.sum(scattered.reshape(GROUPS, 24, GRADS).astype(F32), axis=0)
    spread = jnp.concatenate([summed, jnp.pad(small, ((0, 0), (0, GRADS - D)))], axis=0)
    spread = jnp.broadcast_to(spread.astype(BF16)[None], (GROUPS, 32, GRADS))
    gathered = lax.all_to_all(
        spread.reshape(GROUPS * 32, GRADS), experts_axis, 0, 0, tiled=True
    )
    split = np.zeros((3, 640, WIDTH), np.float32)
    split[0] = spread_matrix(WIDTH, WIDTH, 640).T
    split[1] = spread_matrix(WIDTH, 2 * WIDTH, 640).T
    split[2, :, :EXPERTS] = spread_matrix(EXPERTS, 3 * WIDTH, 640).T
    out = shape((D, WIDTH), F32)
    small, query_grad, key_grad, value_grad, output_grad, router_grad = call(
        finish_kernel,
        (shape((8, D), F32), out, out, out, shape((WIDTH, D), F32), shape((D, EXPERTS), F32)),
        (gathered, jnp.asarray(split, BF16)),
        scratch=(pltpu.VMEM((D, GRADS), F32),),
        limit=32, flops=600_000_000, moved=6_000_000,
    )
    return (
        layer_output,
        input_grad,
        small[4],
        query_grad,
        key_grad,
        value_grad,
        output_grad,
        jnp.transpose(small[1:4, :BUCKETS]),
        small[0],
        router_grad,
        expert_in_grad,
        expert_out_grad,
    )


def solution(mesh):
    fine = Mesh(mesh.devices.reshape(4, 4, 2, 2, 2), ("z", "x", "h", "l", "c"))
    ex = ("z", "x", "h")
    te = ("l", "c")
    in_specs = (
        P(ex, None), P(), P(None, te), P(None, te), P(None, te), P(te, None), P(None, te), P(),
        P(), P(ex, None, te), P(ex, te, None), P(ex), P(ex), P(ex), P(ex, None),
    )
    out_specs = (
        P(ex, None), P(ex, None), P(), P(None, te), P(None, te), P(None, te), P(te, None),
        P(None, te), P(), P(), P(ex, None, te), P(ex, te, None),
    )
    return jax.shard_map(shards, mesh=fine, in_specs=in_specs, out_specs=out_specs, check_vma=False)
```

time: 787 us -> 217 us (0.28); the launches traced: 777 us -> 217 us
  waiting for transfers between devices: 394 us -> 58.8 us
  blocking collectives: 185 us -> 61.4 us
  local copies, waits for them, and re-layouts: 93.3 us -> 28 us
  matrix products: 45.9 us -> 0 us
  Pallas kernels: 0 us -> 43.3 us
  other arithmetic: 29.9 us -> 3.27 us
  between operations: 14.6 us -> 1.04 us
    psum x4 -> x0, waiting for transfers between devices: 357 us -> none  [the longest x1 255 us: shards(): lax.psum(query_grad.astype(jnp.bfloat16), 'expert').astype(jnp.float32)]
    psum x2 -> x0, blocking collectives: 135 us -> none  [the longest x1 95.9 us: shards(): lax.psum(attn_gain_grad.astype(jnp.bfloat16), 'expert').astype(jnp.float32)]
    dot_general x33 -> x0, matrix products: 45.9 us -> none  [the longest x1 5.27 us: shards(): jnp.einsum('secd,secf->edf', received, pre_grad, preferred_element_type=j...]
    pallas_call x0 -> x8, Pallas kernels: none -> 43.3 us  [the longest x7 37.8 us: call(): pl.pallas_call(body, out_shape=out_shape, in_specs=specs, out_specs=jax.t...]
    ppermute x0 -> x12, waiting for transfers between devices: none -> 40.4 us  [swap(): return lax.ppermute(array, axis, [(0, 1), (1, 0)])]
    reshape x7 -> x2, local copies, waits for them, and re-layouts: 30.9 us -> 0.69 us  [the longest x1 0.69 us: shards(): gain_one = attn_gain.reshape(1, D)]
    all_to_all x2, waiting for transfers between devices: 36.4 us -> 18.4 us  [the longest x1 18.4 us: shards(): lax.all_to_all(spread.reshape(GROUPS * 32, GRADS), experts_axis, 0, 0, ti...]
    another operation x2 -> x3, local copies, waits for them, and re-layouts: 17.3 us -> 0.04 us  [shards(): route = jnp.stack([route_expert, route_slot, route_drop] + [zeros] * 5)]
  transfers between devices with their start and end apart: 6 -> 14, of which waited for: 5 -> 8; matrix products, arithmetic and copies ran while one was open for 7% -> 3% of each run, Pallas kernels for 0% -> 6%
where the time goes in v1:
time: 217 us
  blocking collectives  61.4 us (28%)
  waiting for transfers between devices  58.8 us (27%)
  Pallas kernels  43.3 us (20%)
  local copies, waits for them, and re-layouts  28 us (13%)
  starting transfers between devices  20.7 us (10%)
  other arithmetic  3.27 us (2%)
    ppermute x12, waiting for transfers between devices, swap(): return lax.ppermute(array, axis, [(0, 1), (1, 0)])  40.4 us
    pallas_call x7, Pallas kernels, call(): pl.pallas_call(body, out_shape=out_shape, in_specs=specs, out_specs=jax.t...  37.8 us
    all_to_all x1, blocking collectives, shards(): lax.all_to_all(jnp.concatenate([partial, partial], axis=0), pair_axis, 0,...  31.9 us
    all_to_all x1, blocking collectives, shards(): received = lax.all_to_all(send, experts_axis, 0, 0, tiled=True)  29.5 us
    unnamed x93, local copies, waits for them, and re-layouts  24.7 us
    all_to_all x1, waiting for transfers between devices, shards(): lax.all_to_all(spread.reshape(GROUPS * 32, GRADS), experts_axis, 0, 0, ti...  18.4 us
    all_to_all x1, starting transfers between devices, shards(): lax.all_to_all(spread.reshape(GROUPS * 32, GRADS), experts_axis, 0, 0, ti...  10.9 us
    pallas_call x1, Pallas kernels, expert_grads(): pl.pallas_call(expert_grads_kernel, grid=(2, 3), out_shape=(shape((2, D,...  5.52 us
  transfers between devices with their start and end apart: 14, of which 8 were waited for; matrix products, arithmetic and copies ran while one was open for 3% of the time, Pallas kernels for 6%

profile of v1, /device:TPU:0, one launch (start us, length us, event | category | flops | bytes accessed | tf_op | source)
XLA Modules:
  0.0 216.5 jit_solution(7132132465716025403)
XLA Ops:
  0.7 1.7 collective-permute-start.4
  7.4 4.1 %shard_map.292 = (bf16[512,768]{1,0:T(8,128)(2,1)S(1)}, bf16[512,192]{1,0:T(8,128)(2,1)S(1)}, bf16[512,192]{1,0:T(8,128)(2,1)S(1)}, bf16[512,192]{1,0:T(8,128)(2...) custom-call(f32[32,3]{1,0:T(8,128)S(1)} %copy.38.table_ref, ...), custom_call_target="tpu_custom_call" | custom-call | flops 900000000 | bytes 5000000 | tf_op jit(solution)/shard_map/pallas_call | solution.py:89
  16.2 7.1 %collective-permute-done.1.ctx2 = bf16[512,192]{1,0:T(8,128)(2,1)} collective-permute-done((bf16[512,192]{1,0:T(8,128)(2,1)}, bf16[512,192]{1,0:T(8,128)(2,1)}, u32[]{:S(2)}, u32[]{:S(2)}) %collective-permute-start.1) | collective-permute-done | bytes 196640 | tf_op jit(solution)/shard_map/ppermute | solution.py:498
  23.7 1.5 collective-permute-done.2.ctx3
  26.4 5.5 %shard_map.293 = (f32[512,768]{1,0:T(8,128)S(1)}, bf16[512,768]{1,0:T(8,128)(2,1)S(1)}, f32[512,64]{1,0:T(8,128)S(1)}, bf16[1280,384]{1,0:T(8,128)(2,1)S(1)}) custom-call(s32[2]{0:T(128)S(1)} %pad_add_fusion.place_ref, bf16[512,768]{1,0:T(8,128)(2,1)S(1)} %copy-done.2, bf16[512,192]{1,0:T(8,128)(2,1)} %get-tuple-element.45.ctx0.ctx_ref, ...), custom_call_target="tpu_custom_call" | custom-call | flops 1700000000 | bytes 8000000 | tf_op jit(solution)/shard_map/pallas_call | solution.py:89
  32.7 29.5 %all_to_all.39 = bf16[32,40,384]{2,1,0:T(8,128)(2,1)S(1)} all-to-all(bf16[32,40,384]{2,1,0:T(8,128)(2,1)S(1)} %bitcast.15), channel_id=1, replica_groups=mesh['z'=4,'x'=4,'h'=2,'l'=2,'c'=2] {'z','x','h'}, dimensions={0} | all-to-all | bytes 1966080 | tf_op jit(solution)/shard_map/all_to_all | solution.py:530
  62.2 2.6 %collective-permute-done.6.other_ref = bf16[1280,384]{1,0:T(8,128)(2,1)S(1)} collective-permute-done((bf16[1280,384]{1,0:T(8,128)(2,1)S(1)}, bf16[1280,384]{1,0:T(8,128)(2,1)S(1)}, u32[]{:S(2)}, u32[]{:S(2)}) %collective-permute-start.6) | collective-permute-done | bytes 983072 | tf_op jit(solution)/shard_map/ppermute | solution.py:498
  65.7 9.6 %shard_map.294 = (bf16[1280,384]{1,0:T(8,128)(2,1)S(1)}, bf16[1280,384]{1,0:T(8,128)(2,1)S(1)}, bf16[2,320,768]{2,1,0:T(8,128)(2,1)S(1)}, bf16[2,320,768]{2,1,0:...) custom-call(s32[2]{0:T(128)S(1)} %pad_add_fusion.place_ref, ...), custom_call_target="tpu_custom_call" | custom-call | flops 5000000000 | bytes 14000000 | tf_op jit(solution)/shard_map/pallas_call | solution.py:89
  75.6 2.4 %collective-permute-done.7 = bf16[1280,384]{1,0:T(8,128)(2,1)S(1)} collective-permute-done((bf16[1280,384]{1,0:T(8,128)(2,1)S(1)}, bf16[1280,384]{1,0:T(8,128)(2,1)S(1)}, u32[]{:S(2)}, u32[]{:S(2)}) %collective-permute-start.7) | collective-permute-done | bytes 983072 | tf_op jit(solution)/shard_map/ppermute | solution.py:498
  78.5 31.9 %all_to_all.40 = bf16[64,40,384]{2,1,0:T(8,128)(2,1)S(1)} all-to-all(bf16[64,40,384]{2,1,0:T(8,128)(2,1)S(1)} %bitcast.16), channel_id=1, replica_groups=mesh['z'=4,'x'=4,'h'=2,'l'=2,'c'=2] {'l','z','x','h'}, dimensions={0} | all-to-all | bytes 3932160 | tf_op jit(solution)/shard_map/all_to_all | solution.py:543
  110.4 1.9 shard_map.295.own_ref
  112.7 2.3 %collective-permute-done.8.other_ref = bf16[512,768]{1,0:T(8,128)(2,1)S(1)} collective-permute-done((bf16[512,768]{1,0:T(8,128)(2,1)S(1)}, bf16[512,768]{1,0:T(8,128)(2,1)S(1)}, u32[]{:S(2)}, u32[]{:S(2)}) %collective-permute-start.8) | collective-permute-done | bytes 786464 | tf_op jit(solution)/shard_map/ppermute | solution.py:498
  115.9 12.2 %shard_map.296 = (bf16[512,768]{1,0:T(8,128)(2,1)}, f32[512,768]{1,0:T(8,128)}, bf16[768,896]{1,0:T(8,128)(2,1)}, f32[8,768]{1,0:T(8,128)S(1)}, bf16[256,768]{1,...) custom-call(s32[2]{0:T(128)S(1)} %pad_add_fusion.place_ref, f32[32,3]{1,0:T(8,128)S(1)} %copy.38.table_ref, ...), custom_call_target="tpu_custom_call" | custom-call | flops 4000000000 | bytes 12000000 | tf_op jit(solution)/shard_map/pallas_call | solution.py:89
  128.3 5.3 %all-to-all-start.2 = ((bf16[32,24,896]{2,1,0:T(8,128)(2,1)}), bf16[32,24,896]{2,1,0:T(8,128)(2,1)}, u32[]{:S(2)}, u32[]{:S(2)}) async-start(bf16[32,24,896]{2,1,0:T(8,128)(2,1)} %bitcast.17), calls=%async_computation.2 | async-start | bytes 2752512 | tf_op jit(solution)/shard_map/all_to_all | solution.py:568
  135.7 22.8 %collective-permute-done.10 = bf16[256,768]{1,0:T(8,128)(2,1)S(1)} collective-permute-done((bf16[256,768]{1,0:T(8,128)(2,1)S(1)}, bf16[256,768]{1,0:T(8,128)(2,1)S(1)}, u32[]{:S(2)}, u32[]{:S(2)}) %collective-permute-start.10) | collective-permute-done | bytes 393248 | tf_op jit(solution)/shard_map/ppermute | solution.py:498
  158.7 1.7 collective-permute-done.11.other_ref
  160.4 2.6 %shard_map.297 = (f32[512,768]{1,0:T(8,128)}, f32[8,768]{1,0:T(8,128)S(1)}) custom-call(s32[2]{0:T(128)S(1)} %pad_add_fusion.place_ref, bf16[256,768]{1,0:T(8,128)(2,1)S(1)} %add_convert_fusion.1.own_ref, bf16[256,768]{1,0:T(8,128)(2,1)S(1)} %collective-permute-done.11.other_ref, bf16[512,768]{1,0:T(8,128)(2,1)S(1)} %copy-done.2, ...), custom_call_target="tpu_custom_call" | custom-call | flops 10000000 | bytes 5000000 | tf_op jit(solution)/shard_map/pallas_call | solution.py:89
  163.0 1.5 reduce
  164.6 1.4 broadcast_in_dim.2
  165.9 10.9 %all-to-all-start.3 = ((bf16[32,32,896]{2,1,0:T(8,128)(2,1)}), bf16[32,32,896]{2,1,0:T(8,128)(2,1)S(1)}, u32[]{:S(2)}, u32[]{:S(2)}) async-start(bf16[32,32,896]{2,1,0:T(8,128)(2,1)} %broadcast_in_dim.2), calls=%async_computation.3 | async-start | bytes 3670016 | tf_op jit(solution)/shard_map/all_to_all | solution.py:581
  181.7 5.5 %shard_map.299 = (f32[2,768,768]{2,1,0:T(8,128)}, f32[2,768,768]{2,1,0:T(8,128)}) custom-call(bf16[2,320,768]{2,1,0:T(8,128)(2,1)S(1)} %copy-done.18, bf16[2,320,768]{2,1,0:T(8,128)(2,1)S(1)} %copy-done.20, bf16[2,320,768]{2,1,0:T(8,128)(2,1)S(1)} %copy-done.22, bf16[2,320,768]{2,1,0:T(8,128)(2,1)S(1)} %copy-done.23), custom_call_target="tpu_custom_call" | custom-call | flops 1509949440 | bytes 14000000 | tf_op jit(solution)/shard_map/pallas_call | solution.py:287
  187.2 18.4 %all-to-all-done.3 = bf16[32,32,896]{2,1,0:T(8,128)(2,1)S(1)} async-done(((bf16[32,32,896]{2,1,0:T(8,128)(2,1)}), bf16[32,32,896]{2,1,0:T(8,128)(2,1)S(1)}, u32[]{:S(2)}, u32[]{:S(2)}) %all-to-all-start.3) | async-done | bytes 1835040 | tf_op jit(solution)/shard_map/all_to_all | solution.py:581
  205.5 1.9 shard_map.298
  211.3 2.2 %copy.43 = f32[768,192]{0,1:T(8,128)} copy(f32[768,192]{1,0:T(8,128)} %copy-done.7) | data formatting | bytes 1179648
  (123 shorter events, 29.0 us)
Async XLA Ops:
  0.7 15.0 %collective-permute-start.4 = (bf16[192,768]{1,0:T(8,128)(2,1)}, bf16[192,768]{1,0:T(8,128)(2,1)S(1)}, u32[]{:S(2)}, u32[]{:S(2)}) collective-permute-start(bf16[192,768]{1,0:T(8,128)(2,1)} %wo_ref.1), channel_id=1, source_target_pairs={{0,2},{2,0},{1,3},{3,1},{4,6},{6,4},{5,7},{7,5},{8,10},{10,8},{9,1... | collective-permute-start | bytes 884744 | tf_op jit(solution)/shard_map/ppermute | solution.py:498
  6.1 17.2 %copy-start.36 = (f32[768]{0:T(1024)S(1)}, f32[768]{0:T(1024)}, u32[]{:S(2)}) copy-start(f32[768]{0:T(1024)} %param.28) | copy-start | bytes 9220
  6.2 17.2 %copy-start.35 = (bf16[768,64]{0,1:T(8,128)(2,1)S(1)}, bf16[768,64]{0,1:T(8,128)(2,1)}, u32[]{:S(2)}) copy-start(bf16[768,64]{0,1:T(8,128)(2,1)} %param.29) | copy-start | bytes 294916
  7.4 16.2 %copy-start.37 = (s32[512]{0:T(512)S(1)}, s32[512]{0:T(512)}, u32[]{:S(2)}) copy-start(s32[512]{0:T(512)} %param.32) | copy-start | bytes 6148
  7.4 16.2 %copy-start.38 = (s32[512]{0:T(512)S(1)}, s32[512]{0:T(512)}, u32[]{:S(2)}) copy-start(s32[512]{0:T(512)} %param.33) | copy-start | bytes 6148
  7.4 16.2 %copy-start.39 = (s32[512]{0:T(512)S(1)}, s32[512]{0:T(512)}, u32[]{:S(2)}) copy-start(s32[512]{0:T(512)} %param.34) | copy-start | bytes 6148
  15.3 8.1 %collective-permute-start.1 = (bf16[512,192]{1,0:T(8,128)(2,1)}, bf16[512,192]{1,0:T(8,128)(2,1)}, u32[]{:S(2)}, u32[]{:S(2)}) collective-permute-start(bf16[512,192]{1,0:T(8,128)(2,1)} %get-tuple-element.45.ctx0.ctx_ref), channel_id=1, source_target_pairs={{0,2},{2,0},{1,3},{3,1},{4,6},{6,4},{5,7},{7,5},{8,10},{10,8},{9,1... | collective-permute-start | bytes 589832 | tf_op jit(solution)/shard_map/ppermute | solution.py:498
  15.6 8.1 %collective-permute-start.3 = (bf16[192,768]{1,0:T(8,128)(2,1)S(1)}, bf16[192,768]{1,0:T(8,128)(2,1)S(1)}, u32[]{:S(2)}, u32[]{:S(2)}) collective-permute-start(bf16[192,768]{1,0:T(8,128)(2,1)S(1)} %copy-done.10), channel_id=1, source_target_pairs={{0,1},{1,0},{2,3},{3,2},{4,5},{5,4},{6,7},{7,6},{8,9},{9,8},{10,11... | collective-permute-start | bytes 884744 | tf_op jit(solution)/shard_map/ppermute | solution.py:498
  15.7 9.6 %collective-permute-start.5 = (bf16[192,768]{1,0:T(8,128)(2,1)S(1)}, bf16[192,768]{1,0:T(8,128)(2,1)}, u32[]{:S(2)}, u32[]{:S(2)}) collective-permute-start(bf16[192,768]{1,0:T(8,128)(2,1)S(1)} %collective-permute-done.4.wo2), channel_id=1, source_target_pairs={{0,1},{1,0},{2,3},{3,2},{4,5},{5,4},{6,7},{7,6},{8,9},{9,8},{10,11... | collective-permute-start | bytes 884744 | tf_op jit(solution)/shard_map/ppermute | solution.py:498
  16.2 7.6 %collective-permute-start = (bf16[512,192]{1,0:T(8,128)(2,1)}, bf16[512,192]{1,0:T(8,128)(2,1)}, u32[]{:S(2)}, u32[]{:S(2)}) collective-permute-start(bf16[512,192]{1,0:T(8,128)(2,1)} %get-tuple-element.45.ctx0.ctx_ref), channel_id=1, source_target_pairs={{0,1},{1,0},{2,3},{3,2},{4,5},{5,4},{6,7},{7,6},{8,9},{9,8},{10,11... | collective-permute-start | bytes 589832 | tf_op jit(solution)/shard_map/ppermute | solution.py:498
  23.4 1.9 collective-permute-start.2
  32.7 29.5 %copy-start.26 = (f32[512,768]{1,0:T(8,128)}, f32[512,768]{1,0:T(8,128)S(1)}, u32[]{:S(2)}) copy-start(f32[512,768]{1,0:T(8,128)S(1)} %get-tuple-element.46.middle_ref) | copy-start | bytes 4718596
  32.7 33.0 %copy-start.12 = (bf16[320,320]{1,0:T(8,128)(2,1)S(1)}, bf16[320,320]{1,0:T(8,128)(2,1)}, u32[]{:S(2)}) copy-start(bf16[320,320]{1,0:T(8,128)(2,1)} %constant.31.clone.back_ref) | copy-start | bytes 614404
  32.7 33.0 %copy-start.13 = (bf16[320,320]{1,0:T(8,128)(2,1)S(1)}, bf16[320,320]{1,0:T(8,128)(2,1)}, u32[]{:S(2)}) copy-start(bf16[320,320]{1,0:T(8,128)(2,1)} %constant.30.clone.sel_ref) | copy-start | bytes 614404
  62.2 2.6 %collective-permute-start.6 = (bf16[1280,384]{1,0:T(8,128)(2,1)S(1)}, bf16[1280,384]{1,0:T(8,128)(2,1)S(1)}, u32[]{:S(2)}, u32[]{:S(2)}) collective-permute-start(bf16[1280,384]{1,0:T(8,128)(2,1)S(1)} %bitcast.18), channel_id=1, source_target_pairs={{0,1},{1,0},{2,3},{3,2},{4,5},{5,4},{6,7},{7,6},{8,9},{9,8},{10,11... | collective-permute-start | bytes 2949128 | tf_op jit(solution)/shard_map/ppermute | solution.py:498
  75.4 2.6 %collective-permute-start.7 = (bf16[1280,384]{1,0:T(8,128)(2,1)S(1)}, bf16[1280,384]{1,0:T(8,128)(2,1)S(1)}, u32[]{:S(2)}, u32[]{:S(2)}) collective-permute-start(bf16[1280,384]{1,0:T(8,128)(2,1)S(1)} %get-tuple-element.51), channel_id=1, source_target_pairs={{0,1},{1,0},{2,3},{3,2},{4,5},{5,4},{6,7},{7,6},{8,9},{9,8},{10,11... | collective-permute-start | bytes 2949128 | tf_op jit(solution)/shard_map/ppermute | solution.py:498
  112.4 2.6 %collective-permute-start.8 = (bf16[512,768]{1,0:T(8,128)(2,1)S(1)}, bf16[512,768]{1,0:T(8,128)(2,1)S(1)}, u32[]{:S(2)}, u32[]{:S(2)}) collective-permute-start(bf16[512,768]{1,0:T(8,128)(2,1)S(1)} %shard_map.295.own_ref), channel_id=1, source_target_pairs={{0,1},{1,0},{2,3},{3,2},{4,5},{5,4},{6,7},{7,6},{8,9},{9,8},{10,11... | collective-permute-start | bytes 2359304 | tf_op jit(solution)/shard_map/ppermute | solution.py:498
  128.1 5.4 %collective-permute-start.9 = (bf16[256,768]{1,0:T(8,128)(2,1)S(1)}, bf16[256,768]{1,0:T(8,128)(2,1)}, u32[]{:S(2)}, u32[]{:S(2)}) collective-permute-start(bf16[256,768]{1,0:T(8,128)(2,1)S(1)} %get-tuple-element.60), channel_id=1, source_target_pairs={{0,1},{1,0},{2,3},{3,2},{4,5},{5,4},{6,7},{7,6},{8,9},{9,8},{10,11... | collective-permute-start | bytes 1179656 | tf_op jit(solution)/shard_map/ppermute | solution.py:498
  128.3 32.2 %copy-start = (f32[512,768]{1,0:T(8,128)S(1)}, f32[512,768]{1,0:T(8,128)}, u32[]{:S(2)}) copy-start(f32[512,768]{1,0:T(8,128)} %get-tuple-element.61.middle_grad_ref) | copy-start | bytes 4718596
  128.3 34.8 %all-to-all-start.2 = ((bf16[32,24,896]{2,1,0:T(8,128)(2,1)}), bf16[32,24,896]{2,1,0:T(8,128)(2,1)}, u32[]{:S(2)}, u32[]{:S(2)}) async-start(bf16[32,24,896]{2,1,0:T(8,128)(2,1)} %bitcast.17), calls=%async_computation.2 | async-start | bytes 2752512 | tf_op jit(solution)/shard_map/all_to_all | solution.py:568
  134.6 23.9 %collective-permute-start.10 = (bf16[256,768]{1,0:T(8,128)(2,1)S(1)}, bf16[256,768]{1,0:T(8,128)(2,1)S(1)}, u32[]{:S(2)}, u32[]{:S(2)}) collective-permute-start(bf16[256,768]{1,0:T(8,128)(2,1)S(1)} %add_convert_fusion.2), channel_id=1, source_target_pairs={{0,2},{2,0},{1,3},{3,1},{4,6},{6,4},{5,7},{7,5},{8,10},{10,8},{9,1... | collective-permute-start | bytes 1179656 | tf_op jit(solution)/shard_map/ppermute | solution.py:498
  158.6 1.8 collective-permute-start.11
  165.9 39.6 %all-to-all-start.3 = ((bf16[32,32,896]{2,1,0:T(8,128)(2,1)}), bf16[32,32,896]{2,1,0:T(8,128)(2,1)S(1)}, u32[]{:S(2)}, u32[]{:S(2)}) async-start(bf16[32,32,896]{2,1,0:T(8,128)(2,1)} %broadcast_in_dim.2), calls=%async_computation.3 | async-start | bytes 3670016 | tf_op jit(solution)/shard_map/all_to_all | solution.py:581
  181.7 23.9 %copy-start.1 = (bf16[3,640,192]{2,1,0:T(8,128)(2,1)S(1)}, bf16[3,640,192]{2,1,0:T(8,128)(2,1)}, u32[]{:S(2)}) copy-start(bf16[3,640,192]{2,1,0:T(8,128)(2,1)} %constant.34.clone.split_ref) | copy-start | bytes 2211844
  (32 other events, 95.0 us)

commit v2 on v1

--- a/solution.py
+++ b/solution.py
@@ -56,12 +56,6 @@
     return sel
 
 
-def spread_matrix(width, start, total):
-    out = np.zeros((width, total), np.float32)
-    out[np.arange(width), start + np.arange(width)] = 1
-    return out
-
-
 def dot(a, b):
     return jnp.dot(a, b, preferred_element_type=F32)
 
@@ -111,8 +105,8 @@
 
 def scores_t(keys, query_scaled, tiles_ref, table_ref, head, part):
     raw = dot_nt(keys, query_scaled)
-    far_low = table_ref[BUCKETS // 2 - 1, head]
-    far_high = table_ref[BUCKETS - 1, head]
+    far_low = table_ref[head, BUCKETS // 2 - 1]
+    far_high = table_ref[head, BUCKETS - 1]
     rows = []
     for key_block in range(4):
         cols = []
@@ -138,15 +132,15 @@
             ids = ids_ref[block : block + 1, :]
             line = jnp.zeros((1, 256), F32)
             for b in range(BUCKETS):
-                line = jnp.where(ids == b, table_ref[b, head], line)
+                line = jnp.where(ids == b, table_ref[head, b], line)
             wide = pltpu.roll(
                 jnp.broadcast_to(line, (128, 256)), 0, 1, stride=1, stride_axis=0
             )
             tiles_ref[head * 3 + block] = wide[:, 128:]
     normed = normed_ref[...]
-    queries = dot(normed, wq_ref[...]).astype(BF16)
-    keys = dot(normed, wk_ref[...]).astype(BF16)
-    values = dot(normed, wv_ref[...]).astype(BF16)
+    queries = dot_nt(normed, wq_ref[...]).astype(BF16)
+    keys = dot_nt(normed, wk_ref[...]).astype(BF16)
+    values = dot_nt(normed, wv_ref[...]).astype(BF16)
     q_ref[...] = queries
     k_ref[...] = keys
     v_ref[...] = values
@@ -177,9 +171,26 @@
     return jnp.where(drop > 0, -1000, row)
 
 
+def place_kernel(route_ref, low_ref, high_ref, low_t_ref, high_t_ref):
+    target = row_of(route_ref[0:1, :], route_ref[1:2, :], route_ref[2:3, :])
+    for i in range(4):
+        rows = pl.ds(i * 320, 320)
+        index = lax.broadcasted_iota(jnp.int32, (320, SEQ), 0) + 320 * i
+        low_ref[rows, :] = (index == target).astype(F32).astype(BF16)
+        high_ref[rows, :] = (index == target + 20).astype(F32).astype(BF16)
+    columns = route_columns(route_ref).astype(jnp.int32)
+    target = row_of(columns[:, 0:1], columns[:, 1:2], columns[:, 2:3])
+    for i in range(4):
+        rows = slice(i * 128, i * 128 + 128)
+        index = lax.broadcasted_iota(jnp.int32, (128, ROWS), 1)
+        low_t_ref[rows, :] = (index == target[rows]).astype(F32).astype(BF16)
+        high_t_ref[rows, :] = (index == target[rows] + 20).astype(F32).astype(BF16)
+
+
 def middle_kernel(
     place_ref, x_ref, ctx0, ctx1, ctx2, ctx3, wo0, wo1, wo2, wo3, gain_ref, router_ref,
-    route_ref, grad_ref, middle_ref, mixed_ref, probs_ref, send_ref, ctx_s, wo_s, rows_s,
+    route_ref, low_ref, high_ref, grad_ref, middle_ref, mixed_ref, probs_ref, send_ref,
+    ctx_s, wo_s, rows_s,
 ):
     me = place_ref[0]
     core = place_ref[1]
@@ -197,23 +208,20 @@
         mixed = (middle * scale * gain_ref[...]).astype(BF16)
         middle_ref[rows, :] = middle
         mixed_ref[rows, :] = mixed
-        logits = dot(mixed, router_ref[...])
+        lanes = lax.broadcasted_iota(jnp.int32, (256, 128), 1)
+        logits = jnp.where(lanes < EXPERTS, dot_nt(mixed, router_ref[...]), -jnp.inf)
         grown = jnp.exp(logits - jnp.max(logits, axis=-1, keepdims=True))
         probs = grown / jnp.sum(grown, axis=-1, keepdims=True)
         probs_ref[rows, :] = probs
         expert = columns[rows, 0:1].astype(jnp.int32)
-        lanes = lax.broadcasted_iota(jnp.int32, (256, EXPERTS), 1)
         chosen = jnp.sum(jnp.where(lanes == expert, probs, 0.0), axis=-1, keepdims=True)
         gate = chosen * (1.0 - columns[rows, 2:3])
         grads = (grad_ref[rows, :].astype(F32) * gate).astype(BF16)
         rows_s[rows, :] = jnp.where(core == 0, mixed, grads)
-    target = row_of(route_ref[0:1, :], route_ref[1:2, :], route_ref[2:3, :])
     for i in range(4):
-        index = lax.broadcasted_iota(jnp.int32, (320, SEQ), 0) + 320 * i
-        low = (index == target).astype(F32).astype(BF16)
-        high = (index == target + 20).astype(F32).astype(BF16)
-        out = dot(low, rows_s[:, :HALF]) + dot(high, rows_s[:, HALF:])
-        send_ref[pl.ds(i * 320, 320), :] = out.astype(BF16)
+        rows = pl.ds(i * 320, 320)
+        out = dot(low_ref[rows, :], rows_s[:, :HALF]) + dot(high_ref[rows, :], rows_s[:, HALF:])
+        send_ref[rows, :] = out.astype(BF16)
 
 
 def expert_kernel(
@@ -300,26 +308,19 @@
     )(x, s, act, pre)
 
 
-def tokens_kernel(route_ref, recv_ref, out_ref):
-    columns = route_columns(route_ref).astype(jnp.int32)
-    target = row_of(columns[:, 0:1], columns[:, 1:2], columns[:, 2:3])
+def tokens_kernel(low_ref, high_ref, recv_ref, out_ref):
     slots = (
         recv_ref[pl.ds(0, ROWS), :].astype(F32) + recv_ref[pl.ds(ROWS, ROWS), :].astype(F32)
     ).astype(BF16)
-    for i in range(2):
-        rows = slice(i * 256, i * 256 + 256)
-        index = lax.broadcasted_iota(jnp.int32, (256, ROWS), 1)
-        low = (index == target[rows]).astype(F32).astype(BF16)
-        high = (index == target[rows] + 20).astype(F32).astype(BF16)
-        out_ref[rows, pl.ds(0, HALF)] = dot(low, slots).astype(BF16)
-        out_ref[rows, pl.ds(HALF, HALF)] = dot(high, slots).astype(BF16)
+    out_ref[:, pl.ds(0, HALF)] = dot(low_ref[...], slots).astype(BF16)
+    out_ref[:, pl.ds(HALF, HALF)] = dot(high_ref[...], slots).astype(BF16)
 
 
 def backward_kernel(
     place_ref, table_ref, x_ref, middle_ref, mixed_ref, probs_ref, route_ref, grad_ref,
     own_ref, other_ref, router_ref, gain_ref, wo_ref, ctx_ref, q_ref, k_ref, v_ref, normed_ref,
-    lse_ref, tiles_ref, wq_ref, wk_ref, wv_ref, ids_ref, place_q, place_r,
-    output_ref, middle_grad_ref, grads_ref, small_ref, mine_ref, theirs_ref,
+    lse_ref, tiles_ref, wq_ref, wk_ref, wv_ref, ids_ref, stretch_ref,
+    output_ref, middle_grad_ref, grads_ref, mine_ref, theirs_ref,
     low_s, logit_s, normed_s,
 ):
     core = place_ref[1]
@@ -334,7 +335,7 @@
         mixed_grad = jnp.where(core == 0, other, own).astype(F32)
         probs = probs_ref[rows, :]
         kept = 1.0 - columns[rows, 2:3]
-        lanes = lax.broadcasted_iota(jnp.int32, (128, EXPERTS), 1)
+        lanes = lax.broadcasted_iota(jnp.int32, (128, 128), 1)
         hot = (lanes == columns[rows, 0:1].astype(jnp.int32)).astype(F32)
         chosen = jnp.sum(probs * hot, axis=-1, keepdims=True)
         middle = middle_ref[rows, :]
@@ -343,7 +344,7 @@
         gate_grad = jnp.sum(upstream * expert_rows, axis=-1, keepdims=True) * kept
         logit_grad = (probs * (hot - chosen) * gate_grad).astype(BF16)
         logit_s[rows, :] = logit_grad
-        mixed_grad = mixed_grad + dot_nt(logit_grad, router_ref[...])
+        mixed_grad = mixed_grad + dot(logit_grad, router_ref[...])
         scale = lax.rsqrt(jnp.mean(middle * middle, axis=-1, keepdims=True) + EPS)
         weighted = mixed_grad * gain
         inner = jnp.mean(weighted * middle, axis=-1, keepdims=True)
@@ -352,9 +353,7 @@
         middle_grad_ref[rows, :] = middle_grad
         low_s[rows, :] = middle_grad.astype(BF16)
     middle_low = low_s[...]
-    output_grad = dot_tn(middle_low, ctx_ref[...])
-    pad = jnp.zeros((D, 256 - WIDTH), F32)
-    grads_ref[:, 640:] = jnp.concatenate([output_grad, pad], axis=1).astype(BF16)
+    grads_ref[pl.ds(3 * WIDTH, WIDTH), :D] = dot_tn(ctx_ref[...], middle_low).astype(BF16)
     ctx_grad = dot_nt(middle_low, wo_ref[...]).astype(BF16)
 
     keys = k_ref[...]
@@ -364,8 +363,8 @@
     key_grad = jnp.zeros((SEQ, WIDTH), F32)
     value_grad = jnp.zeros((SEQ, WIDTH), F32)
     query_grads = [jnp.zeros((256, WIDTH), F32), jnp.zeros((256, WIDTH), F32)]
-    small_ref[...] = jnp.zeros((8, D), F32)
-    small_ref[0:1, :] = gain_grad
+    bias_grad = jnp.zeros((BUCKETS, 128), F32)
+    bias_lanes = lax.broadcasted_iota(jnp.int32, (BUCKETS, 128), 1)
     turn = (
         lax.broadcasted_iota(jnp.int32, (128, 128), 0)
         + lax.broadcasted_iota(jnp.int32, (128, 128), 1)
@@ -420,69 +419,95 @@
         )
         by_bucket = by_bucket[:, :128] + by_bucket[:, 128:] + ends
         total = jnp.sum(by_bucket, axis=1, keepdims=True)
-        total = jnp.concatenate([total, jnp.zeros((128 - BUCKETS, 1), F32)], axis=0)
-        total = jnp.transpose(jnp.broadcast_to(total, (128, 128)))
-        small_ref[1 + head : 2 + head, 0:128] = total[0:1, :]
+        bias_grad = bias_grad + jnp.where(bias_lanes == EXPERTS + 1 + head, total, 0.0)
     query_low = jnp.concatenate(query_grads, axis=0).astype(BF16)
     key_low = key_grad.astype(BF16)
     value_low = value_grad.astype(BF16)
-    spread = (
-        dot(query_low, place_q[0]) + dot(key_low, place_q[1]) + dot(value_low, place_q[2])
-    ).astype(BF16)
-    logit_spread = dot(logit_s[...], place_r[...]).astype(BF16)
-    joined = dot_tn(normed_ref[...], spread) + dot_tn(mixed_ref[...], logit_spread)
-    grads_ref[:, :640] = joined.astype(BF16)
+    normed = normed_ref[...]
+    for i, low in enumerate((query_low, key_low, value_low)):
+        grads_ref[pl.ds(i * WIDTH, WIDTH), :D] = dot_tn(low, normed).astype(BF16)
+    rest = dot_tn(mixed_ref[...], logit_s[...]) + dot(stretch_ref[...], bias_grad.astype(BF16))
+    column = jnp.transpose(jnp.broadcast_to(gain_grad, (128, D)))
+    lanes = lax.broadcasted_iota(jnp.int32, (D, 128), 1)
+    grads_ref[:, D:] = jnp.where(lanes == EXPERTS, column, rest).astype(BF16)
     normed_part = (
-        dot_nt(query_low, wq_ref[...])
-        + dot_nt(key_low, wk_ref[...])
-        + dot_nt(value_low, wv_ref[...])
+        dot(query_low, wq_ref[...])
+        + dot(key_low, wk_ref[...])
+        + dot(value_low, wv_ref[...])
     )
     normed_s[...] = normed_part.astype(BF16)
     mine_ref[...] = normed_s[pl.ds(pl.multiple_of(core * 256, 256), 256), :]
     theirs_ref[...] = normed_s[pl.ds(pl.multiple_of((1 - core) * 256, 256), 256), :]
 
 
-def input_kernel(
-    place_ref, own_ref, other_ref, x_ref, gain_ref, middle_grad_ref, small_in, input_ref, small_ref
-):
+def halves(core, own_ref, other_ref, i):
+    local = slice((i % 2) * 128, (i % 2) * 128 + 128)
+    return jnp.where(core == i // 2, own_ref[local, :], other_ref[local, :]).astype(F32)
+
+
+def reduce_kernel(place_ref, parts_ref, own_ref, other_ref, x_ref, send_ref):
+    core = place_ref[1]
+    gain_grad = jnp.zeros((1, D), F32)
+    for i in range(4):
+        hidden = x_ref[pl.ds(i * 128, 128), :].astype(F32)
+        scale = lax.rsqrt(jnp.mean(hidden * hidden, axis=-1, keepdims=True) + EPS)
+        normed_grad = halves(core, own_ref, other_ref, i)
+        gain_grad = gain_grad + jnp.sum(normed_grad * hidden * scale, axis=0, keepdims=True)
+    total = jnp.zeros((24, GRADS), F32)
+    for j in range(GROUPS // 2):
+        pair = parts_ref[pl.ds(j * 48, 48), :].astype(F32)
+        total = total + pair[:24] + pair[24:]
+    lines = [
+        pltpu.roll(gain_grad[:, r // 4 * 128 : r // 4 * 128 + 128], (96 - r % 4 * 32) % 128, 1)
+        for r in range(24)
+    ]
+    lanes = lax.broadcasted_iota(jnp.int32, (24, 128), 1)
+    last = jnp.where(lanes < 96, total[:, D:], jnp.concatenate(lines, axis=0))
+    chunk = jnp.concatenate([total[:, :D], last], axis=1)
+    pair = jnp.concatenate([chunk, chunk], axis=0).astype(BF16)
+    for j in range(GROUPS // 2):
+        send_ref[pl.ds(j * 48, 48), :] = pair
+
+
+def input_kernel(place_ref, own_ref, other_ref, x_ref, gain_ref, middle_grad_ref, input_ref):
     core = place_ref[1]
     gain = gain_ref[...]
-    gain_grad = jnp.zeros((1, D), F32)
     for i in range(4):
         rows = slice(i * 128, i * 128 + 128)
-        local = slice((i % 2) * 128, (i % 2) * 128 + 128)
-        own = own_ref[local, :]
-        other = other_ref[local, :]
-        normed_grad = jnp.where(core == i // 2, own, other).astype(F32)
         hidden = x_ref[rows, :].astype(F32)
         scale = lax.rsqrt(jnp.mean(hidden * hidden, axis=-1, keepdims=True) + EPS)
-        weighted = normed_grad * gain
+        weighted = halves(core, own_ref, other_ref, i) * gain
         inner = jnp.mean(weighted * hidden, axis=-1, keepdims=True)
-        gain_grad = gain_grad + jnp.sum(normed_grad * hidden * scale, axis=0, keepdims=True)
         input_ref[rows, :] = (
             middle_grad_ref[rows, :]
             + scale * weighted
             - hidden * (scale * scale * scale * inner)
         )
-    small_ref[...] = small_in[...]
-    small_ref[4:5, :] = gain_grad
 
 
 def finish_kernel(
-    recv_ref, split_ref, small_ref, q_ref, k_ref, v_ref, o_ref, router_ref, whole_s
+    recv_ref, stretch_ref, gain_one_ref, gain_two_ref, bias_ref,
+    q_ref, k_ref, v_ref, o_ref, router_ref,
 ):
-    small = jnp.zeros((8, GRADS), F32)
+    for i, out in enumerate((q_ref, k_ref, v_ref, o_ref)):
+        out[...] = recv_ref[pl.ds(i * WIDTH, WIDTH), :D].astype(F32)
+    last = recv_ref[:, D:].astype(F32)
+    summed = jnp.zeros((24, 128), F32)
     for j in range(GROUPS):
-        block = recv_ref[pl.ds(j * 32, 32), :].astype(F32)
-        whole_s[pl.ds(j * 24, 24), :] = block[:24]
-        small = small + block[24:]
-    small_ref[...] = small[:, :D]
-    joined = whole_s[:, :640].astype(BF16)
-    q_ref[...] = whole_s[:, :WIDTH]
-    k_ref[...] = dot(joined, split_ref[0])
-    v_ref[...] = dot(joined, split_ref[1])
-    router_ref[...] = dot(joined, split_ref[2])[:, :EXPERTS]
-    o_ref[...] = jnp.transpose(whole_s[:, 640:])[:WIDTH, :]
+        summed = summed + last[j * 24 : j * 24 + 24]
+    lanes = lax.broadcasted_iota(jnp.int32, (1, 128), 1)
+    for block in range(6):
+        line = jnp.zeros((1, 128), F32)
+        for i in range(4):
+            r = block * 4 + i
+            piece = pltpu.roll(summed[r : r + 1], (32 + 32 * i) % 128, 1)
+            line = jnp.where((lanes >= 32 * i) & (lanes < 32 * i + 32), piece, line)
+        gain_one_ref[:, pl.ds(block * 128, 128)] = line
+    turned = jnp.transpose(last)
+    router_ref[...] = turned[:EXPERTS]
+    tail = turned[EXPERTS : EXPERTS + 8]
+    gain_two_ref[...] = tail[0:1]
+    bias_ref[...] = dot(tail.astype(BF16), stretch_ref[...])
 
 
 def shards(
@@ -502,6 +527,9 @@
     gain_two = moe_gain.reshape(1, D)
     zeros = jnp.zeros_like(route_drop)
     route = jnp.stack([route_expert, route_slot, route_drop] + [zeros] * 5)
+    table = jnp.transpose(position_bias)
+    wq, wk, wv = (jnp.transpose(w) for w in (query_weight, key_weight, value_weight))
+    router = jnp.pad(jnp.transpose(router_weight), ((0, 128 - EXPERTS), (0, 0)))
     wo_link = swap(output_weight, "l")
     wo_core = swap(output_weight, "c")
     wo_far = swap(wo_link, "c")
@@ -511,21 +539,27 @@
         attention_forward,
         (shape((SEQ, D), BF16), tall, tall, tall, tall, shape((8, SEQ), F32),
          shape((9, 128, 128), F32)),
-        (position_bias, layer_input, gain_one, query_weight, key_weight, value_weight, ids),
-        scalars=1, limit=32, flops=900_000_000, moved=5_000_000,
+        (table, layer_input, gain_one, wq, wk, wv, ids),
+        scalars=1, limit=16, flops=900_000_000, moved=5_000_000,
     )
     ctx_link = swap(context, "l")
     ctx_core = swap(context, "c")
     ctx_far = swap(ctx_link, "c")
+    flat, flat_t = shape((ROWS, SEQ), BF16), shape((SEQ, ROWS), BF16)
+    low_place, high_place, low_back, high_back = call(
+        place_kernel, (flat, flat, flat_t, flat_t), (route,),
+        limit=12, flops=10_000_000, moved=5_500_000,
+    )
     middle, mixed, probs, send = call(
         middle_kernel,
-        (shape((SEQ, D), F32), shape((SEQ, D), BF16), shape((SEQ, EXPERTS), F32),
+        (shape((SEQ, D), F32), shape((SEQ, D), BF16), shape((SEQ, 128), F32),
          shape((ROWS, HALF), BF16)),
         (place, layer_input, context, ctx_core, ctx_link, ctx_far,
-         output_weight, wo_core, wo_link, wo_far, gain_two, router_weight, route, out_grad),
+         output_weight, wo_core, wo_link, wo_far, gain_two, router, route, low_place, high_place,
+         out_grad),
         scratch=(pltpu.VMEM((4, SEQ, WIDTH), BF16), pltpu.VMEM((4, WIDTH, D), BF16),
                  pltpu.VMEM((SEQ, D), BF16)),
-        scalars=1, limit=32, flops=1_700_000_000, moved=8_000_000,
+        scalars=1, limit=16, flops=1_700_000_000, moved=8_000_000,
     )
     received = lax.all_to_all(send, experts_axis, 0, 0, tiled=True)
     received_other = swap(received, "c")
@@ -537,7 +571,7 @@
         (place, received, received_other, expert_in, expert_out,
          jnp.asarray(select, BF16), jnp.asarray(select.T, BF16)),
         scratch=(pltpu.VMEM((2, 320, D), BF16), pltpu.VMEM((2, 320, D), BF16)),
-        scalars=1, limit=48, flops=5_000_000_000, moved=14_000_000,
+        scalars=1, limit=24, flops=5_000_000_000, moved=14_000_000,
     )
     partial = (mine.astype(F32) + swap(theirs, "c").astype(F32)).astype(BF16)
     back = lax.all_to_all(
@@ -545,65 +579,58 @@
     )
     expert_in_grad, expert_out_grad = expert_grads(slots, slot_grads, act, pre_grad)
     rows_own = call(
-        tokens_kernel, shape((SEQ, D), BF16), (route, back),
-        limit=32, flops=2_000_000_000, moved=3_000_000,
+        tokens_kernel, shape((SEQ, D), BF16), (low_back, high_back, back),
+        limit=12, flops=2_000_000_000, moved=3_000_000,
     )
     rows_other = swap(rows_own, "c")
-    place_q = jnp.asarray(
-        np.stack([spread_matrix(WIDTH, WIDTH * i, 640) for i in range(3)]), BF16
-    )
-    place_r = jnp.asarray(spread_matrix(EXPERTS, 3 * WIDTH, 640), BF16)
-    layer_output, middle_grad, grads, small, norm_mine, norm_theirs = call(
+    stretch = np.zeros((D, 128), np.float32)
+    stretch[24 * np.arange(BUCKETS), np.arange(BUCKETS)] = 1
+    layer_output, middle_grad, grads, norm_mine, norm_theirs = call(
         backward_kernel,
         (shape((SEQ, D), BF16), shape((SEQ, D), F32), shape((D, GRADS), BF16),
-         shape((8, D), F32), shape((256, D), BF16), shape((256, D), BF16)),
-        (place, position_bias, layer_input, middle, mixed, probs, route, out_grad,
-         rows_own, rows_other, router_weight, gain_two, output_weight, context, queries, keys,
-         values, normed, lse, tiles, query_weight, key_weight, value_weight, ids,
-         place_q, place_r),
-        scratch=(pltpu.VMEM((SEQ, D), BF16), pltpu.VMEM((SEQ, EXPERTS), BF16),
+         shape((256, D), BF16), shape((256, D), BF16)),
+        (place, table, layer_input, middle, mixed, probs, route, out_grad,
+         rows_own, rows_other, router, gain_two, output_weight, context, queries, keys,
+         values, normed, lse, tiles, wq, wk, wv, ids, jnp.asarray(stretch[:, :BUCKETS], BF16)),
+        scratch=(pltpu.VMEM((SEQ, D), BF16), pltpu.VMEM((SEQ, 128), BF16),
                  pltpu.VMEM((SEQ, D), BF16)),
-        scalars=2, limit=48, flops=4_000_000_000, moved=12_000_000,
+        scalars=2, limit=24, flops=4_000_000_000, moved=12_000_000,
     )
     scattered = lax.all_to_all(grads, experts_axis, 0, 0, tiled=True)
     halved = (norm_mine.astype(F32) + swap(norm_theirs, "c").astype(F32)).astype(BF16)
     halved = (halved.astype(F32) + swap(halved, "l").astype(F32)).astype(BF16)
     halved_other = swap(halved, "c")
-    input_grad, small = call(
-        input_kernel,
-        (shape((SEQ, D), F32), shape((8, D), F32)),
-        (place, halved, halved_other, layer_input, gain_one, middle_grad, small),
-        scalars=1, limit=32, flops=10_000_000, moved=5_000_000,
-    )
-    summed = jnp.sum(scattered.reshape(GROUPS, 24, GRADS).astype(F32), axis=0)
-    spread = jnp.concatenate([summed, jnp.pad(small, ((0, 0), (0, GRADS - D)))], axis=0)
-    spread = jnp.broadcast_to(spread.astype(BF16)[None], (GROUPS, 32, GRADS))
-    gathered = lax.all_to_all(
-        spread.reshape(GROUPS * 32, GRADS), experts_axis, 0, 0, tiled=True
-    )
-    split = np.zeros((3, 640, WIDTH), np.float32)
-    split[0] = spread_matrix(WIDTH, WIDTH, 640).T
-    split[1] = spread_matrix(WIDTH, 2 * WIDTH, 640).T
-    split[2, :, :EXPERTS] = spread_matrix(EXPERTS, 3 * WIDTH, 640).T
-    out = shape((D, WIDTH), F32)
-    small, query_grad, key_grad, value_grad, output_grad, router_grad = call(
-        finish_kernel,
-        (shape((8, D), F32), out, out, out, shape((WIDTH, D), F32), shape((D, EXPERTS), F32)),
-        (gathered, jnp.asarray(split, BF16)),
-        scratch=(pltpu.VMEM((D, GRADS), F32),),
-        limit=32, flops=600_000_000, moved=6_000_000,
-    )
+    spread = call(
+        reduce_kernel, shape((D, GRADS), BF16),
+        (place, scattered, halved, halved_other, layer_input),
+        scalars=1, limit=12, flops=10_000_000, moved=5_000_000,
+    )
+    gathered = lax.all_to_all(spread, experts_axis, 0, 0, tiled=True)
+    input_grad = call(
+        input_kernel, shape((SEQ, D), F32),
+        (place, halved, halved_other, layer_input, gain_one, middle_grad),
+        scalars=1, limit=12, flops=10_000_000, moved=5_000_000,
+    )
+    out = shape((WIDTH, D), F32)
+    line = shape((1, D), F32)
+    gain_one_grad, gain_two_grad, bias_grad, query_grad, key_grad, value_grad, output_grad, \
+        router_grad = call(
+            finish_kernel,
+            (line, line, shape((8, 128), F32), out, out, out, out, shape((EXPERTS, D), F32)),
+            (gathered, jnp.asarray(stretch, BF16)),
+            limit=12, flops=10_000_000, moved=6_000_000,
+        )
     return (
         layer_output,
         input_grad,
-        small[4],
-        query_grad,
-        key_grad,
-        value_grad,
+        gain_one_grad.reshape(D),
+        jnp.transpose(query_grad),
+        jnp.transpose(key_grad),
+        jnp.transpose(value_grad),
         output_grad,
-        jnp.transpose(small[1:4, :BUCKETS]),
-        small[0],
-        router_grad,
+        jnp.transpose(bias_grad[1 : 1 + HEADS_HERE, :BUCKETS]),
+        gain_two_grad.reshape(D),
+        jnp.transpose(router_grad),
         expert_in_grad,
         expert_out_grad,
     )

time: 217 us -> 194 us (0.89)
  local copies, waits for them, and re-layouts: 28 us -> 17.5 us
  waiting for transfers between devices: 58.8 us -> 50.2 us
  Pallas kernels: 43.3 us -> 40.1 us
    unnamed x93 -> x88, local copies, waits for them, and re-layouts: 24.7 us -> 15.3 us
    all_to_all x1, waiting for transfers between devices: 18.4 us -> 10.5 us  [shards(): gathered = lax.all_to_all(spread, experts_axis, 0, 0, tiled=True)]
    pallas_call x7 -> x9, Pallas kernels: 37.8 us -> 34.5 us  [call(): pl.pallas_call(body, out_shape=out_shape, in_specs=specs, out_specs=jax.t...]
  transfers between devices with their start and end apart: 14 -> 14, of which waited for: 8 -> 7; matrix products, arithmetic and copies ran while one was open for 3% -> 1% of each run, Pallas kernels for 6% -> 7%
where the time goes in v2:
time: 194 us; the launch traced here: 193 us
  blocking collectives  61.8 us (32%)
  waiting for transfers between devices  50.2 us (26%)
  Pallas kernels  40.1 us (21%)
  starting transfers between devices  20.4 us (11%)
  local copies, waits for them, and re-layouts  17.5 us (9%)
    ppermute x12, waiting for transfers between devices, swap(): return lax.ppermute(array, axis, [(0, 1), (1, 0)])  39.7 us
    pallas_call x9, Pallas kernels, call(): pl.pallas_call(body, out_shape=out_shape, in_specs=specs, out_specs=jax.t...  34.5 us
    all_to_all x1, blocking collectives, shards(): lax.all_to_all(jnp.concatenate([partial, partial], axis=0), pair_axis, 0,...  32.1 us
    all_to_all x1, blocking collectives, shards(): received = lax.all_to_all(send, experts_axis, 0, 0, tiled=True)  29.7 us
    unnamed x88, local copies, waits for them, and re-layouts  15.3 us
    all_to_all x1, starting transfers between devices, shards(): gathered = lax.all_to_all(spread, experts_axis, 0, 0, tiled=True)  10.9 us
    all_to_all x1, waiting for transfers between devices, shards(): gathered = lax.all_to_all(spread, experts_axis, 0, 0, tiled=True)  10.5 us
    pallas_call x1, Pallas kernels, expert_grads(): pl.pallas_call(expert_grads_kernel, grid=(2, 3), out_shape=(shape((2, D,...  5.52 us
  transfers between devices with their start and end apart: 14, of which 7 were waited for; matrix products, arithmetic and copies ran while one was open for 1% of the time, Pallas kernels for 7%

profile of v2, /device:TPU:0, one launch (start us, length us, event | category | flops | bytes accessed | tf_op | source)
XLA Modules:
  0.0 193.1 jit_solution(2435085032037283125)
XLA Ops:
  0.7 1.7 collective-permute-start.4
  8.5 3.1 %shard_map.283 = (bf16[512,768]{1,0:T(8,128)(2,1)S(1)}, bf16[512,192]{1,0:T(8,128)(2,1)S(1)}, bf16[512,192]{1,0:T(8,128)(2,1)S(1)}, bf16[512,192]{1,0:T(8,128)(2...) custom-call(f32[3,32]{1,0:T(4,128)S(1)} %bitcast.36, ...), custom_call_target="tpu_custom_call" | custom-call | flops 900000000 | bytes 5000000 | tf_op jit(solution)/shard_map/pallas_call | solution.py:83
  16.4 6.8 %collective-permute-done.1.ctx2 = bf16[512,192]{1,0:T(8,128)(2,1)S(1)} collective-permute-done((bf16[512,192]{1,0:T(8,128)(2,1)S(1)}, bf16[512,192]{1,0:T(8,128)(2,1)S(1)}, u32[]{:S(2)}, u32[]{:S(2)}) %collective-permute-start.1) | collective-permute-done | bytes 196640 | tf_op jit(solution)/shard_map/ppermute | solution.py:523
  24.2 1.6 shard_map.284
  26.0 5.3 %shard_map.285 = (f32[512,768]{1,0:T(8,128)S(1)}, bf16[512,768]{1,0:T(8,128)(2,1)S(1)}, f32[512,128]{1,0:T(8,128)S(1)}, bf16[1280,384]{1,0:T(8,128)(2,1)S(1)}) custom-call(s32[2]{0:T(128)S(1)} %pad_add_fusion.place_ref, bf16[512,768]{1,0:T(8,128)(2,1)S(1)} %copy-done.1, bf16[512,192]{1,0:T(8,128)(2,1)S(1)} %get-tuple-element.48.ctx0.ctx_ref, ...), custom_call_target="tpu_custom_call" | custom-call | flops 1700000000 | bytes 8000000 | tf_op jit(solution)/shard_map/pallas_call | solution.py:83
  31.3 29.7 %all_to_all.44 = bf16[32,40,384]{2,1,0:T(8,128)(2,1)S(1)} all-to-all(bf16[32,40,384]{2,1,0:T(8,128)(2,1)S(1)} %bitcast.29), channel_id=1, replica_groups=mesh['z'=4,'x'=4,'h'=2,'l'=2,'c'=2] {'z','x','h'}, dimensions={0} | all-to-all | bytes 1966080 | tf_op jit(solution)/shard_map/all_to_all | solution.py:564
  61.0 2.6 %collective-permute-done.6.other_ref = bf16[1280,384]{1,0:T(8,128)(2,1)S(1)} collective-permute-done((bf16[1280,384]{1,0:T(8,128)(2,1)S(1)}, bf16[1280,384]{1,0:T(8,128)(2,1)S(1)}, u32[]{:S(2)}, u32[]{:S(2)}) %collective-permute-start.6) | collective-permute-done | bytes 983072 | tf_op jit(solution)/shard_map/ppermute | solution.py:523
  63.6 7.2 %shard_map.286 = (bf16[1280,384]{1,0:T(8,128)(2,1)S(1)}, bf16[1280,384]{1,0:T(8,128)(2,1)S(1)}, bf16[2,320,768]{2,1,0:T(8,128)(2,1)S(1)}, bf16[2,320,768]{2,1,0:...) custom-call(s32[2]{0:T(128)S(1)} %pad_add_fusion.place_ref, ...), custom_call_target="tpu_custom_call" | custom-call | flops 5000000000 | bytes 14000000 | tf_op jit(solution)/shard_map/pallas_call | solution.py:83
  71.1 2.4 %collective-permute-done.7 = bf16[1280,384]{1,0:T(8,128)(2,1)S(1)} collective-permute-done((bf16[1280,384]{1,0:T(8,128)(2,1)S(1)}, bf16[1280,384]{1,0:T(8,128)(2,1)S(1)}, u32[]{:S(2)}, u32[]{:S(2)}) %collective-permute-start.7) | collective-permute-done | bytes 983072 | tf_op jit(solution)/shard_map/ppermute | solution.py:523
  74.1 32.1 %all_to_all.45 = bf16[64,40,384]{2,1,0:T(8,128)(2,1)S(1)} all-to-all(bf16[64,40,384]{2,1,0:T(8,128)(2,1)S(1)} %bitcast.38), channel_id=1, replica_groups=mesh['z'=4,'x'=4,'h'=2,'l'=2,'c'=2] {'l','z','x','h'}, dimensions={0} | all-to-all | bytes 3932160 | tf_op jit(solution)/shard_map/all_to_all | solution.py:577
  106.3 1.6 shard_map.287.own_ref
  108.1 2.3 %collective-permute-done.8.other_ref = bf16[512,768]{1,0:T(8,128)(2,1)S(1)} collective-permute-done((bf16[512,768]{1,0:T(8,128)(2,1)S(1)}, bf16[512,768]{1,0:T(8,128)(2,1)S(1)}, u32[]{:S(2)}, u32[]{:S(2)}) %collective-permute-start.8) | collective-permute-done | bytes 786464 | tf_op jit(solution)/shard_map/ppermute | solution.py:523
  110.5 9.4 %shard_map.288 = (bf16[512,768]{1,0:T(8,128)(2,1)}, f32[512,768]{1,0:T(8,128)S(1)}, bf16[768,896]{1,0:T(8,128)(2,1)}, bf16[256,768]{1,0:T(8,128)(2,1)S(1)}, bf16[256,768]{1,0:T(8,128)(2,1)S(1)}) custom-call(s32[2]{0:T(128)S(1)} %pad_add_fusion.place_ref, f32[3,32]{1,0:T(4,128)S(1)} %bitcast.37, bf16[512,768]{1,0:T(8,128)(2,1)S(1)} %copy-done.1, ...), custom_call_target="tpu_custom_call" | custom-call | flops 4000000000 | bytes 12000000 | tf_op jit(solution)/shard_map/pallas_call | solution.py:83
  121.2 5.0 %all-to-all-start.2 = ((bf16[32,24,896]{2,1,0:T(8,128)(2,1)}), bf16[32,24,896]{2,1,0:T(8,128)(2,1)S(1)}, u32[]{:S(2)}, u32[]{:S(2)}) async-start(bf16[32,24,896]{2,1,0:T(8,128)(2,1)} %bitcast.14), calls=%async_computation.2 | async-start | bytes 2752512 | tf_op jit(solution)/shard_map/all_to_all | solution.py:599
  127.4 23.9 %collective-permute-done.10 = bf16[256,768]{1,0:T(8,128)(2,1)S(1)} collective-permute-done((bf16[256,768]{1,0:T(8,128)(2,1)S(1)}, bf16[256,768]{1,0:T(8,128)(2,1)S(1)}, u32[]{:S(2)}, u32[]{:S(2)}) %collective-permute-start.10) | collective-permute-done | bytes 393248 | tf_op jit(solution)/shard_map/ppermute | solution.py:523
  151.5 1.7 collective-permute-done.11.other_ref
  153.2 2.4 %shard_map.290 = bf16[768,896]{1,0:T(8,128)(2,1)} custom-call(s32[2]{0:T(128)S(1)} %pad_add_fusion.place_ref, bf16[768,896]{1,0:T(8,128)(2,1)S(1)} %bitcast.24, bf16[256,768]{1,0:T(8,128)(2,1)S(1)} %add_convert_fusion.1.own_ref, bf16[256,768]{1,0:T(8,128)(2,1)S(1)} %collective-permute-done.11.other_ref, bf16[512,768]{1,0:T(8,128)(2,1)S(1)} %copy-done.1), custom_call_target="tpu_custom_call" | custom-call | flops 10000000 | bytes 5000000 | tf_op jit(solution)/shard_map/pallas_call | solution.py:83
  155.5 10.9 %all-to-all-start.3 = ((bf16[32,24,896]{2,1,0:T(8,128)(2,1)}), bf16[32,24,896]{2,1,0:T(8,128)(2,1)S(1)}, u32[]{:S(2)}, u32[]{:S(2)}) async-start(bf16[32,24,896]{2,1,0:T(8,128)(2,1)} %bitcast.16), calls=%async_computation.3 | async-start | bytes 2752512 | tf_op jit(solution)/shard_map/all_to_all | solution.py:608
  168.9 1.2 copy-done.27
  170.1 1.2 copy-done.29
  171.3 5.5 %shard_map.292 = (f32[2,768,768]{2,1,0:T(8,128)}, f32[2,768,768]{2,1,0:T(8,128)}) custom-call(bf16[2,320,768]{2,1,0:T(8,128)(2,1)S(1)} %copy-done.23, bf16[2,320,768]{2,1,0:T(8,128)(2,1)S(1)} %copy-done.25, bf16[2,320,768]{2,1,0:T(8,128)(2,1)S(1)} %copy-done.27, bf16[2,320,768]{2,1,0:T(8,128)(2,1)S(1)} %copy-done.29), custom_call_target="tpu_custom_call" | custom-call | flops 1509949440 | bytes 14000000 | tf_op jit(solution)/shard_map/pallas_call | solution.py:295
  176.8 2.3 %shard_map.289 = f32[512,768]{1,0:T(8,128)} custom-call(s32[2]{0:T(128)S(1)} %pad_add_fusion.place_ref, bf16[256,768]{1,0:T(8,128)(2,1)S(1)} %add_convert_fusion.1.own_ref, bf16[256,768]{1,0:T(8,128)(2,1)S(1)} %collective-permute-done.11.other_ref, bf16[512,768]{1,0:T(8,128)(2,1)S(1)} %copy-done.1, f32[1,768]{1,0:T(1,128)S(1)} %reshape.44.gain_ref, ...), custom_call_target="tpu_custom_call" | custom-call | flops 10000000 | bytes 5000000 | tf_op jit(solution)/shard_map/pallas_call | solution.py:83
  179.1 10.5 %all-to-all-done.3 = bf16[32,24,896]{2,1,0:T(8,128)(2,1)S(1)} async-done(((bf16[32,24,896]{2,1,0:T(8,128)(2,1)}), bf16[32,24,896]{2,1,0:T(8,128)(2,1)S(1)}, u32[]{:S(2)}, u32[]{:S(2)}) %all-to-all-start.3) | async-done | bytes 1376288 | tf_op jit(solution)/shard_map/all_to_all | solution.py:608
  189.7 1.6 shard_map.291
  (118 shorter events, 19.8 us)
Async XLA Ops:
  0.6 22.6 %copy-start.40 = (f32[768]{0:T(1024)S(1)}, f32[768]{0:T(1024)}, u32[]{:S(2)}) copy-start(f32[768]{0:T(1024)} %param.27) | copy-start | bytes 9220
  0.7 23.5 %copy-start.43 = (s32[512]{0:T(512)S(1)}, s32[512]{0:T(512)}, u32[]{:S(2)}) copy-start(s32[512]{0:T(512)} %param.33) | copy-start | bytes 6148
  0.7 23.5 %copy-start.42 = (s32[512]{0:T(512)S(1)}, s32[512]{0:T(512)}, u32[]{:S(2)}) copy-start(s32[512]{0:T(512)} %param.32) | copy-start | bytes 6148
  0.7 23.5 %copy-start.41 = (s32[512]{0:T(512)S(1)}, s32[512]{0:T(512)}, u32[]{:S(2)}) copy-start(s32[512]{0:T(512)} %param.31) | copy-start | bytes 6148
  0.7 15.2 %collective-permute-start.4 = (bf16[192,768]{1,0:T(8,128)(2,1)}, bf16[192,768]{1,0:T(8,128)(2,1)S(1)}, u32[]{:S(2)}, u32[]{:S(2)}) collective-permute-start(bf16[192,768]{1,0:T(8,128)(2,1)} %wo_ref.1), channel_id=1, source_target_pairs={{0,2},{2,0},{1,3},{3,1},{4,6},{6,4},{5,7},{7,5},{8,10},{10,8},{9,1... | collective-permute-start | bytes 884744 | tf_op jit(solution)/shard_map/ppermute | solution.py:523
  8.5 17.4 %copy-start.1 = (bf16[512,768]{1,0:T(8,128)(2,1)S(1)}, bf16[512,768]{1,0:T(8,128)(2,1)}, u32[]{:S(2)}) copy-start(bf16[512,768]{1,0:T(8,128)(2,1)} %x_ref.9) | copy-start | bytes 2359300
  8.5 17.4 %copy-start.4 = (bf16[512,768]{1,0:T(8,128)(2,1)S(1)}, bf16[512,768]{1,0:T(8,128)(2,1)}, u32[]{:S(2)}) copy-start(bf16[512,768]{1,0:T(8,128)(2,1)} %grad_ref.3) | copy-start | bytes 2359300
  15.5 7.8 %collective-permute-start.1 = (bf16[512,192]{1,0:T(8,128)(2,1)S(1)}, bf16[512,192]{1,0:T(8,128)(2,1)S(1)}, u32[]{:S(2)}, u32[]{:S(2)}) collective-permute-start(bf16[512,192]{1,0:T(8,128)(2,1)S(1)} %get-tuple-element.48.ctx0.ctx_ref), channel_id=1, source_target_pairs={{0,2},{2,0},{1,3},{3,1},{4,6},{6,4},{5,7},{7,5},{8,10},{10,8},{9,1... | collective-permute-start | bytes 589832 | tf_op jit(solution)/shard_map/ppermute | solution.py:523
  15.8 10.1 %collective-permute-start.3 = (bf16[192,768]{1,0:T(8,128)(2,1)S(1)}, bf16[192,768]{1,0:T(8,128)(2,1)S(1)}, u32[]{:S(2)}, u32[]{:S(2)}) collective-permute-start(bf16[192,768]{1,0:T(8,128)(2,1)S(1)} %copy-done.5), channel_id=1, source_target_pairs={{0,1},{1,0},{2,3},{3,2},{4,5},{5,4},{6,7},{7,6},{8,9},{9,8},{10,11... | collective-permute-start | bytes 884744 | tf_op jit(solution)/shard_map/ppermute | solution.py:523
  15.8 10.1 %collective-permute-start.5 = (bf16[192,768]{1,0:T(8,128)(2,1)S(1)}, bf16[192,768]{1,0:T(8,128)(2,1)S(1)}, u32[]{:S(2)}, u32[]{:S(2)}) collective-permute-start(bf16[192,768]{1,0:T(8,128)(2,1)S(1)} %collective-permute-done.4.wo2), channel_id=1, source_target_pairs={{0,1},{1,0},{2,3},{3,2},{4,5},{5,4},{6,7},{7,6},{8,9},{9,8},{10,11... | collective-permute-start | bytes 884744 | tf_op jit(solution)/shard_map/ppermute | solution.py:523
  16.3 9.6 %collective-permute-start = (bf16[512,192]{1,0:T(8,128)(2,1)S(1)}, bf16[512,192]{1,0:T(8,128)(2,1)}, u32[]{:S(2)}, u32[]{:S(2)}) collective-permute-start(bf16[512,192]{1,0:T(8,128)(2,1)S(1)} %get-tuple-element.48.ctx0.ctx_ref), channel_id=1, source_target_pairs={{0,1},{1,0},{2,3},{3,2},{4,5},{5,4},{6,7},{7,6},{8,9},{9,8},{10,11... | collective-permute-start | bytes 589832 | tf_op jit(solution)/shard_map/ppermute | solution.py:523
  23.2 2.7 %collective-permute-start.2 = (bf16[512,192]{1,0:T(8,128)(2,1)S(1)}, bf16[512,192]{1,0:T(8,128)(2,1)}, u32[]{:S(2)}, u32[]{:S(2)}) collective-permute-start(bf16[512,192]{1,0:T(8,128)(2,1)S(1)} %collective-permute-done.1.ctx2), channel_id=1, source_target_pairs={{0,1},{1,0},{2,3},{3,2},{4,5},{5,4},{6,7},{7,6},{8,9},{9,8},{10,11... | collective-permute-start | bytes 589832 | tf_op jit(solution)/shard_map/ppermute | solution.py:523
  25.9 37.6 %copy-start.7 = (bf16[2,768,768]{2,1,0:T(8,128)(2,1)S(1)}, bf16[2,768,768]{2,1,0:T(8,128)(2,1)}, u32[]{:S(2)}) copy-start(bf16[2,768,768]{2,1,0:T(8,128)(2,1)} %in_ref.1) | copy-start | bytes 7077892
  26.0 37.6 %copy-start.8 = (bf16[2,768,768]{2,1,0:T(8,128)(2,1)S(1)}, bf16[2,768,768]{2,1,0:T(8,128)(2,1)}, u32[]{:S(2)}) copy-start(bf16[2,768,768]{2,1,0:T(8,128)(2,1)} %out_ref.1) | copy-start | bytes 7077892
  31.3 32.3 %copy-start.17 = (bf16[320,320]{1,0:T(8,128)(2,1)S(1)}, bf16[320,320]{1,0:T(8,128)(2,1)}, u32[]{:S(2)}) copy-start(bf16[320,320]{1,0:T(8,128)(2,1)} %constant.26.clone.back_ref) | copy-start | bytes 614404
  31.3 32.3 %copy-start.18 = (bf16[320,320]{1,0:T(8,128)(2,1)S(1)}, bf16[320,320]{1,0:T(8,128)(2,1)}, u32[]{:S(2)}) copy-start(bf16[320,320]{1,0:T(8,128)(2,1)} %constant.25.clone.sel_ref) | copy-start | bytes 614404
  61.0 2.6 %collective-permute-start.6 = (bf16[1280,384]{1,0:T(8,128)(2,1)S(1)}, bf16[1280,384]{1,0:T(8,128)(2,1)S(1)}, u32[]{:S(2)}, u32[]{:S(2)}) collective-permute-start(bf16[1280,384]{1,0:T(8,128)(2,1)S(1)} %bitcast.27), channel_id=1, source_target_pairs={{0,1},{1,0},{2,3},{3,2},{4,5},{5,4},{6,7},{7,6},{8,9},{9,8},{10,11... | collective-permute-start | bytes 2949128 | tf_op jit(solution)/shard_map/ppermute | solution.py:523
  70.9 2.6 %collective-permute-start.7 = (bf16[1280,384]{1,0:T(8,128)(2,1)S(1)}, bf16[1280,384]{1,0:T(8,128)(2,1)S(1)}, u32[]{:S(2)}, u32[]{:S(2)}) collective-permute-start(bf16[1280,384]{1,0:T(8,128)(2,1)S(1)} %get-tuple-element.58), channel_id=1, source_target_pairs={{0,1},{1,0},{2,3},{3,2},{4,5},{5,4},{6,7},{7,6},{8,9},{9,8},{10,11... | collective-permute-start | bytes 2949128 | tf_op jit(solution)/shard_map/ppermute | solution.py:523
  107.8 2.6 %collective-permute-start.8 = (bf16[512,768]{1,0:T(8,128)(2,1)S(1)}, bf16[512,768]{1,0:T(8,128)(2,1)S(1)}, u32[]{:S(2)}, u32[]{:S(2)}) collective-permute-start(bf16[512,768]{1,0:T(8,128)(2,1)S(1)} %shard_map.287.own_ref), channel_id=1, source_target_pairs={{0,1},{1,0},{2,3},{3,2},{4,5},{5,4},{6,7},{7,6},{8,9},{9,8},{10,11... | collective-permute-start | bytes 2359304 | tf_op jit(solution)/shard_map/ppermute | solution.py:523
  121.0 5.1 %collective-permute-start.9 = (bf16[256,768]{1,0:T(8,128)(2,1)S(1)}, bf16[256,768]{1,0:T(8,128)(2,1)S(1)}, u32[]{:S(2)}, u32[]{:S(2)}) collective-permute-start(bf16[256,768]{1,0:T(8,128)(2,1)S(1)} %get-tuple-element.67), channel_id=1, source_target_pairs={{0,1},{1,0},{2,3},{3,2},{4,5},{5,4},{6,7},{7,6},{8,9},{9,8},{10,11... | collective-permute-start | bytes 1179656 | tf_op jit(solution)/shard_map/ppermute | solution.py:523
  121.2 32.0 %all-to-all-start.2 = ((bf16[32,24,896]{2,1,0:T(8,128)(2,1)}), bf16[32,24,896]{2,1,0:T(8,128)(2,1)S(1)}, u32[]{:S(2)}, u32[]{:S(2)}) async-start(bf16[32,24,896]{2,1,0:T(8,128)(2,1)} %bitcast.14), calls=%async_computation.2 | async-start | bytes 2752512 | tf_op jit(solution)/shard_map/all_to_all | solution.py:599
  126.3 25.0 %collective-permute-start.10 = (bf16[256,768]{1,0:T(8,128)(2,1)S(1)}, bf16[256,768]{1,0:T(8,128)(2,1)S(1)}, u32[]{:S(2)}, u32[]{:S(2)}) collective-permute-start(bf16[256,768]{1,0:T(8,128)(2,1)S(1)} %add_convert_fusion.2), channel_id=1, source_target_pairs={{0,2},{2,0},{1,3},{3,1},{4,6},{6,4},{5,7},{7,5},{8,10},{10,8},{9,1... | collective-permute-start | bytes 1179656 | tf_op jit(solution)/shard_map/ppermute | solution.py:523
  151.4 1.8 collective-permute-start.11
  155.5 34.1 %all-to-all-start.3 = ((bf16[32,24,896]{2,1,0:T(8,128)(2,1)}), bf16[32,24,896]{2,1,0:T(8,128)(2,1)S(1)}, u32[]{:S(2)}, u32[]{:S(2)}) async-start(bf16[32,24,896]{2,1,0:T(8,128)(2,1)} %bitcast.16), calls=%async_computation.3 | async-start | bytes 2752512 | tf_op jit(solution)/shard_map/all_to_all | solution.py:608
  (34 other events, 100.2 us)

commit v3 on v2

--- a/solution.py
+++ b/solution.py
@@ -38,12 +38,19 @@
     return upper_side + np.where(distance < exact_count, distance, far_bucket)
 
 
-def line_ids():
-    ids = np.full((8, 256), -1, np.int32)
-    for row, block in enumerate((-1, 0, 1)):
-        ids[row] = bucket_of(128 * block + 128 - np.arange(256))
-    ids[:3, 0] = -1
-    return ids
+FAR_STARTS = [
+    int(np.argmax(bucket_of(-np.arange(256)) >= b)) for b in range(9, BUCKETS // 2)
+]
+
+
+def line_buckets(block, rows):
+    offset = 128 * block + 128 - lax.broadcasted_iota(jnp.int32, (rows, 256), 1)
+    distance = jnp.abs(offset)
+    far = jnp.full((rows, 256), 8, jnp.int32)
+    for start in FAR_STARTS:
+        far = far + (distance >= start).astype(jnp.int32)
+    bucket = jnp.where(distance < 8, distance, far)
+    return jnp.where(offset > 0, bucket + BUCKETS // 2, bucket)
 
 
 def regroup_matrix():
@@ -77,18 +84,24 @@
     return jnp.where(head_mask(head, matrix.shape[0]), matrix, jnp.zeros_like(matrix))
 
 
-def call(body, out_shape, args, scratch=(), scalars=0, limit=40, flops=0, moved=0):
-    specs = [pl.BlockSpec(memory_space=pltpu.SMEM)] * scalars
-    specs += [pl.BlockSpec(memory_space=pltpu.VMEM)] * (len(args) - scalars)
-    return pl.pallas_call(
+def call(
+    body, out_shape, args, scratch=(), scalars=0, far=(), far_out=(), limit=40, flops=0, moved=0
+):
+    spaces = [pltpu.SMEM] * scalars + [pltpu.VMEM] * (len(args) - scalars)
+    for i in far:
+        spaces[i] = pltpu.HBM
+    outs = out_shape if isinstance(out_shape, tuple) else (out_shape,)
+    out_spaces = [pltpu.HBM if i in far_out else pltpu.VMEM for i in range(len(outs))]
+    result = pl.pallas_call(
         body,
-        out_shape=out_shape,
-        in_specs=specs,
-        out_specs=jax.tree.map(lambda _: pl.BlockSpec(memory_space=pltpu.VMEM), out_shape),
+        out_shape=outs,
+        in_specs=[pl.BlockSpec(memory_space=space) for space in spaces],
+        out_specs=tuple(pl.BlockSpec(memory_space=space) for space in out_spaces),
         scratch_shapes=scratch,
         compiler_params=pltpu.CompilerParams(vmem_limit_bytes=limit << 20),
         cost_estimate=pl.CostEstimate(flops=flops, bytes_accessed=moved, transcendentals=0),
     )(*args)
+    return result if isinstance(out_shape, tuple) else result[0]
 
 
 def shape(dims, dtype):
@@ -103,10 +116,10 @@
     return tiles_ref[head * 3 + block + 1]
 
 
-def scores_t(keys, query_scaled, tiles_ref, table_ref, head, part):
+def scores_t(keys, query_scaled, tiles_ref, table, head, part):
     raw = dot_nt(keys, query_scaled)
-    far_low = table_ref[head, BUCKETS // 2 - 1]
-    far_high = table_ref[head, BUCKETS - 1]
+    far_low = table[head : head + 1, BUCKETS // 2 - 1 : BUCKETS // 2]
+    far_high = table[head : head + 1, BUCKETS - 1 : BUCKETS]
     rows = []
     for key_block in range(4):
         cols = []
@@ -119,40 +132,72 @@
 
 
 def attention_forward(
-    table_ref, x_ref, gain_ref, wq_ref, wk_ref, wv_ref, ids_ref,
-    normed_ref, q_ref, k_ref, v_ref, ctx_ref, lse_ref, tiles_ref,
+    table_hbm, x_hbm, gain_hbm, wq_hbm, wk_hbm, wv_hbm,
+    normed_hbm, q_hbm, k_hbm, v_hbm, tiles_hbm, ctx_ref, lse_ref,
+    table_ref, x_ref, gain_ref, wq_ref, wk_ref, wv_ref, normed_ref, q_ref, k_ref, v_ref,
+    tiles_ref, sems,
 ):
+    loads = [
+        pltpu.make_async_copy(src, dst, sems.at[i])
+        for i, (src, dst) in enumerate(
+            (
+                (table_hbm, table_ref), (x_hbm, x_ref), (wq_hbm, wq_ref), (wk_hbm, wk_ref),
+                (wv_hbm, wv_ref), (gain_hbm, gain_ref),
+            )
+        )
+    ]
+    for load in loads:
+        load.start()
+    stores = []
+
+    def store(src, dst):
+        copy = pltpu.make_async_copy(src, dst, sems.at[6 + len(stores)])
+        copy.start()
+        stores.append(copy)
+
+    loads[0].wait()
+    table = table_ref[...]
+    lines = []
+    for block in (-1, 0, 1):
+        buckets = lax.broadcasted_iota(jnp.int32, (BUCKETS, 256), 0)
+        hot = (buckets == line_buckets(block, BUCKETS)).astype(F32)
+        lines.append(
+            jnp.dot(table, hot, precision=lax.Precision.HIGHEST, preferred_element_type=F32)
+        )
+    for head in range(HEADS_HERE):
+        for block in range(3):
+            wide = pltpu.roll(
+                jnp.broadcast_to(lines[block][head : head + 1], (128, 256)),
+                0, 1, stride=1, stride_axis=0,
+            )
+            tiles_ref[head * 3 + block] = wide[:, 128:]
+    store(tiles_ref, tiles_hbm)
+    loads[1].wait()
+    loads[5].wait()
+    gain = gain_ref[...].reshape(1, D)
     for i in range(4):
         rows = pl.ds(i * 128, 128)
         x = x_ref[rows, :].astype(F32)
         scale = lax.rsqrt(jnp.mean(x * x, axis=-1, keepdims=True) + EPS)
-        normed_ref[rows, :] = (x * scale * gain_ref[...]).astype(BF16)
-    for head in range(HEADS_HERE):
-        for block in range(3):
-            ids = ids_ref[block : block + 1, :]
-            line = jnp.zeros((1, 256), F32)
-            for b in range(BUCKETS):
-                line = jnp.where(ids == b, table_ref[head, b], line)
-            wide = pltpu.roll(
-                jnp.broadcast_to(line, (128, 256)), 0, 1, stride=1, stride_axis=0
-            )
-            tiles_ref[head * 3 + block] = wide[:, 128:]
+        normed_ref[rows, :] = (x * scale * gain).astype(BF16)
+    store(normed_ref, normed_hbm)
     normed = normed_ref[...]
-    queries = dot_nt(normed, wq_ref[...]).astype(BF16)
-    keys = dot_nt(normed, wk_ref[...]).astype(BF16)
-    values = dot_nt(normed, wv_ref[...]).astype(BF16)
-    q_ref[...] = queries
-    k_ref[...] = keys
-    v_ref[...] = values
+    for load, weight, out, out_hbm in (
+        (loads[2], wq_ref, q_ref, q_hbm),
+        (loads[3], wk_ref, k_ref, k_hbm),
+        (loads[4], wv_ref, v_ref, v_hbm),
+    ):
+        load.wait()
+        out[...] = dot_nt(normed, weight[...]).astype(BF16)
+        store(out, out_hbm)
+    queries, keys, values = q_ref[...], k_ref[...], v_ref[...]
     lse_ref[...] = jnp.zeros((8, SEQ), F32)
     scaled = queries * jnp.asarray(HEAD**-0.5, BF16)
     for part in range(2):
         rows = slice(part * 256, part * 256 + 256)
         context = jnp.zeros((256, WIDTH), F32)
         for head in range(HEADS_HERE):
-            scores = scores_t(
-                keys, only_head(scaled[rows], head), tiles_ref, table_ref, head, part
-            )
+            scores = scores_t(keys, only_head(scaled[rows], head), tiles_ref, table, head, part)
             top = jnp.max(scores, axis=0, keepdims=True)
             grown = jnp.exp(scores - top)
             total = jnp.sum(grown, axis=0, keepdims=True)
@@ -160,6 +205,8 @@
             lse_ref[head : head + 1, rows] = top + jnp.log(total)
             context = context + dot_tn(probs, only_head(values, head))
         ctx_ref[rows, :] = context.astype(BF16)
+    for copy in stores:
+        copy.wait()
 
 
 def route_columns(route_ref):
@@ -319,7 +366,7 @@
 def backward_kernel(
     place_ref, table_ref, x_ref, middle_ref, mixed_ref, probs_ref, route_ref, grad_ref,
     own_ref, other_ref, router_ref, gain_ref, wo_ref, ctx_ref, q_ref, k_ref, v_ref, normed_ref,
-    lse_ref, tiles_ref, wq_ref, wk_ref, wv_ref, ids_ref, stretch_ref,
+    lse_ref, tiles_ref, wq_ref, wk_ref, wv_ref, stretch_ref,
     output_ref, middle_grad_ref, grads_ref, mine_ref, theirs_ref,
     low_s, logit_s, normed_s,
 ):
@@ -379,7 +426,7 @@
             rows = slice(part * 256, part * 256 + 256)
             query_head = only_head(query_scaled[rows], head)
             ctx_head = only_head(ctx_grad[rows], head)
-            scores = scores_t(keys, query_head, tiles_ref, table_ref, head, part)
+            scores = scores_t(keys, query_head, tiles_ref, table_ref[...], head, part)
             probs = jnp.exp(scores - lse_ref[head : head + 1, rows])
             value_grad = value_grad + dot(probs.astype(BF16), ctx_head)
             prob_grad = dot_nt(values, ctx_head)
@@ -409,7 +456,7 @@
             wide = pltpu.roll(wide, 1, 1, stride=1, stride_axis=0)
             line = jnp.sum(wide, axis=0, keepdims=True)
             by_bucket = by_bucket + jnp.where(
-                buckets == ids_ref[block : block + 1, :], line, 0.0
+                buckets == line_buckets(block - 1, BUCKETS), line, 0.0
             )
         side = lax.broadcasted_iota(jnp.int32, (BUCKETS, 128), 0)
         low_line = jnp.sum(far_low, axis=0, keepdims=True)
@@ -502,12 +549,12 @@
             r = block * 4 + i
             piece = pltpu.roll(summed[r : r + 1], (32 + 32 * i) % 128, 1)
             line = jnp.where((lanes >= 32 * i) & (lanes < 32 * i + 32), piece, line)
-        gain_one_ref[:, pl.ds(block * 128, 128)] = line
+        gain_one_ref[pl.ds(block * 128, 128)] = line[0]
     turned = jnp.transpose(last)
     router_ref[...] = turned[:EXPERTS]
     tail = turned[EXPERTS : EXPERTS + 8]
-    gain_two_ref[...] = tail[0:1]
-    bias_ref[...] = dot(tail.astype(BF16), stretch_ref[...])
+    gain_two_ref[...] = tail[0]
+    bias_ref[...] = dot(tail.astype(BF16), stretch_ref[...])[1 : 1 + HEADS_HERE]
 
 
 def shards(
@@ -522,7 +569,6 @@
     def swap(array, axis):
         return lax.ppermute(array, axis, [(0, 1), (1, 0)])
 
-    ids = jnp.asarray(line_ids())
     gain_one = attn_gain.reshape(1, D)
     gain_two = moe_gain.reshape(1, D)
     zeros = jnp.zeros_like(route_drop)
@@ -535,21 +581,30 @@
     wo_far = swap(wo_link, "c")
 
     tall = shape((SEQ, WIDTH), BF16)
-    normed, queries, keys, values, context, lse, tiles = call(
+    wide = shape((SEQ, D), BF16)
+    tile_shape = (3 * HEADS_HERE, 128, 128)
+    weight_vmem = pltpu.VMEM((WIDTH, D), BF16)
+    tall_vmem = pltpu.VMEM((SEQ, WIDTH), BF16)
+    normed, queries, keys, values, tiles, context, lse = call(
         attention_forward,
-        (shape((SEQ, D), BF16), tall, tall, tall, tall, shape((8, SEQ), F32),
-         shape((9, 128, 128), F32)),
-        (table, layer_input, gain_one, wq, wk, wv, ids),
-        scalars=1, limit=16, flops=900_000_000, moved=5_000_000,
-    )
-    ctx_link = swap(context, "l")
-    ctx_core = swap(context, "c")
-    ctx_far = swap(ctx_link, "c")
+        (wide, tall, tall, tall, shape(tile_shape, F32), tall, shape((8, SEQ), F32)),
+        (table, layer_input, attn_gain, wq, wk, wv),
+        far=(0, 1, 2, 3, 4, 5), far_out=(0, 1, 2, 3, 4),
+        scratch=(pltpu.VMEM((HEADS_HERE, BUCKETS), F32), pltpu.VMEM((SEQ, D), BF16),
+                 pltpu.VMEM((D,), F32), weight_vmem, weight_vmem, weight_vmem, pltpu.VMEM((SEQ, D), BF16),
+                 tall_vmem, tall_vmem, tall_vmem, pltpu.VMEM(tile_shape, F32),
+                 pltpu.SemaphoreType.DMA((11,))),
+        limit=60, flops=900_000_000, moved=5_000_000,
+    )
     flat, flat_t = shape((ROWS, SEQ), BF16), shape((SEQ, ROWS), BF16)
     low_place, high_place, low_back, high_back = call(
         place_kernel, (flat, flat, flat_t, flat_t), (route,),
         limit=12, flops=10_000_000, moved=5_500_000,
     )
+    ctx_link = swap(context, "l")
+    ctx_core = swap(context, "c")
+    ctx_link_late, low_place = lax.optimization_barrier((ctx_link, low_place))
+    ctx_far = swap(ctx_link_late, "c")
     middle, mixed, probs, send = call(
         middle_kernel,
         (shape((SEQ, D), F32), shape((SEQ, D), BF16), shape((SEQ, 128), F32),
@@ -583,7 +638,7 @@
         limit=12, flops=2_000_000_000, moved=3_000_000,
     )
     rows_other = swap(rows_own, "c")
-    stretch = np.zeros((D, 128), np.float32)
+    stretch = np.zeros((D, BUCKETS), np.float32)
     stretch[24 * np.arange(BUCKETS), np.arange(BUCKETS)] = 1
     layer_output, middle_grad, grads, norm_mine, norm_theirs = call(
         backward_kernel,
@@ -591,10 +646,10 @@
          shape((256, D), BF16), shape((256, D), BF16)),
         (place, table, layer_input, middle, mixed, probs, route, out_grad,
          rows_own, rows_other, router, gain_two, output_weight, context, queries, keys,
-         values, normed, lse, tiles, wq, wk, wv, ids, jnp.asarray(stretch[:, :BUCKETS], BF16)),
+         values, normed, lse, tiles, wq, wk, wv, jnp.asarray(stretch, BF16)),
         scratch=(pltpu.VMEM((SEQ, D), BF16), pltpu.VMEM((SEQ, 128), BF16),
                  pltpu.VMEM((SEQ, D), BF16)),
-        scalars=2, limit=24, flops=4_000_000_000, moved=12_000_000,
+        scalars=1, limit=24, flops=4_000_000_000, moved=12_000_000,
     )
     scattered = lax.all_to_all(grads, experts_axis, 0, 0, tiled=True)
     halved = (norm_mine.astype(F32) + swap(norm_theirs, "c").astype(F32)).astype(BF16)
@@ -612,24 +667,25 @@
         scalars=1, limit=12, flops=10_000_000, moved=5_000_000,
     )
     out = shape((WIDTH, D), F32)
-    line = shape((1, D), F32)
+    line = shape((D,), F32)
     gain_one_grad, gain_two_grad, bias_grad, query_grad, key_grad, value_grad, output_grad, \
         router_grad = call(
             finish_kernel,
-            (line, line, shape((8, 128), F32), out, out, out, out, shape((EXPERTS, D), F32)),
+            (line, line, shape((HEADS_HERE, BUCKETS), F32), out, out, out, out,
+             shape((EXPERTS, D), F32)),
             (gathered, jnp.asarray(stretch, BF16)),
             limit=12, flops=10_000_000, moved=6_000_000,
         )
     return (
         layer_output,
         input_grad,
-        gain_one_grad.reshape(D),
+        gain_one_grad,
         jnp.transpose(query_grad),
         jnp.transpose(key_grad),
         jnp.transpose(value_grad),
         output_grad,
-        jnp.transpose(bias_grad[1 : 1 + HEADS_HERE, :BUCKETS]),
-        gain_two_grad.reshape(D),
+        jnp.transpose(bias_grad),
+        gain_two_grad,
         jnp.transpose(router_grad),
         expert_in_grad,
         expert_out_grad,

time: 194 us -> 187 us (0.964)
  local copies, waits for them, and re-layouts: 17.5 us -> 10.3 us
  Pallas kernels: 40.1 us -> 43.5 us
  waiting for transfers between devices: 50.2 us -> 47.7 us
    unnamed x88 -> x80, local copies, waits for them, and re-layouts: 15.3 us -> 10.3 us
    pallas_call x9, Pallas kernels: 34.5 us -> 37.9 us  [call(): pl.pallas_call(body, out_shape=outs, in_specs=[pl.BlockSpec(memory_space=...]
    ppermute x12, waiting for transfers between devices: 39.7 us -> 37.2 us  [swap(): return lax.ppermute(array, axis, [(0, 1), (1, 0)])]
  transfers between devices with their start and end apart: 14 -> 14, of which waited for: 7 -> 9; matrix products, arithmetic and copies ran while one was open for 1% -> 1% of each run, Pallas kernels for 7% -> 8%
where the time goes in v3:
time: 187 us; the launch traced here: 186 us
  blocking collectives  61.4 us (33%)
  waiting for transfers between devices  47.7 us (26%)
  Pallas kernels  43.5 us (23%)
  starting transfers between devices  20.6 us (11%)
  local copies, waits for them, and re-layouts  10.3 us (6%)
    pallas_call x9, Pallas kernels, call(): pl.pallas_call(body, out_shape=outs, in_specs=[pl.BlockSpec(memory_space=...  37.9 us
    ppermute x12, waiting for transfers between devices, swap(): return lax.ppermute(array, axis, [(0, 1), (1, 0)])  37.2 us
    all_to_all x1, blocking collectives, shards(): lax.all_to_all(jnp.concatenate([partial, partial], axis=0), pair_axis, 0,...  32 us
    all_to_all x1, blocking collectives, shards(): received = lax.all_to_all(send, experts_axis, 0, 0, tiled=True)  29.4 us
    all_to_all x1, starting transfers between devices, shards(): gathered = lax.all_to_all(spread, experts_axis, 0, 0, tiled=True)  11.1 us
    all_to_all x1, waiting for transfers between devices, shards(): gathered = lax.all_to_all(spread, experts_axis, 0, 0, tiled=True)  10.5 us
    unnamed x80, local copies, waits for them, and re-layouts  10.3 us
    pallas_call x1, Pallas kernels, expert_grads(): pl.pallas_call(expert_grads_kernel, grid=(2, 3), out_shape=(shape((2, D,...  5.52 us
  transfers between devices with their start and end apart: 14, of which 9 were waited for; matrix products, arithmetic and copies ran while one was open for 1% of the time, Pallas kernels for 8%

profile of v3, /device:TPU:0, one launch (start us, length us, event | category | flops | bytes accessed | tf_op | source)
XLA Modules:
  0.0 186.3 jit_solution(5501273680673023448)
XLA Ops:
  0.7 1.7 collective-permute-start.4
  2.4 5.4 %shard_map.274 = (bf16[512,768]{1,0:T(8,128)(2,1)}, bf16[512,192]{1,0:T(8,128)(2,1)}, bf16[512,192]{1,0:T(8,128)(2,1)}, bf16[512,192]{1,0:T(8,128)(2,1)}, f32[9,...) custom-call(f32[3,32]{1,0:T(4,128)} %bitcast.35, bf16[512,768]{1,0:T(8,128)(2,1)} %x_ref.7, ...), custom_call_target="tpu_custom_call" | custom-call | flops 900000000 | bytes 5000000 | tf_op jit(solution)/shard_map/pallas_call | solution.py:95
  8.3 1.4 collective-permute-done.4.wo2
  10.3 1.6 shard_map.275
  14.0 2.0 %collective-permute-done.1.ctx2 = bf16[512,192]{1,0:T(8,128)(2,1)} collective-permute-done((bf16[512,192]{1,0:T(8,128)(2,1)}, bf16[512,192]{1,0:T(8,128)(2,1)}, u32[]{:S(2)}, u32[]{:S(2)}) %collective-permute-start.1) | collective-permute-done | bytes 196640 | tf_op jit(solution)/shard_map/ppermute | solution.py:570
  16.2 1.7 collective-permute-done.2.ctx3
  20.0 5.7 %shard_map.276 = (f32[512,768]{1,0:T(8,128)S(1)}, bf16[512,768]{1,0:T(8,128)(2,1)S(1)}, f32[512,128]{1,0:T(8,128)S(1)}, bf16[1280,384]{1,0:T(8,128)(2,1)S(1)}) custom-call(s32[2]{0:T(128)S(1)} %pad_add_fusion.place_ref, bf16[512,768]{1,0:T(8,128)(2,1)S(1)} %copy-done, bf16[512,192]{1,0:T(8,128)(2,1)S(1)} %copy-done.5, ...), custom_call_target="tpu_custom_call" | custom-call | flops 1700000000 | bytes 8000000 | tf_op jit(solution)/shard_map/pallas_call | solution.py:95
  25.8 29.4 %all_to_all.44 = bf16[32,40,384]{2,1,0:T(8,128)(2,1)S(1)} all-to-all(bf16[32,40,384]{2,1,0:T(8,128)(2,1)S(1)} %bitcast.28), channel_id=1, replica_groups=mesh['z'=4,'x'=4,'h'=2,'l'=2,'c'=2] {'z','x','h'}, dimensions={0} | all-to-all | bytes 1966080 | tf_op jit(solution)/shard_map/all_to_all | solution.py:619
  55.1 2.6 %collective-permute-done.6.other_ref = bf16[1280,384]{1,0:T(8,128)(2,1)S(1)} collective-permute-done((bf16[1280,384]{1,0:T(8,128)(2,1)S(1)}, bf16[1280,384]{1,0:T(8,128)(2,1)S(1)}, u32[]{:S(2)}, u32[]{:S(2)}) %collective-permute-start.6) | collective-permute-done | bytes 983072 | tf_op jit(solution)/shard_map/ppermute | solution.py:570
  57.7 7.2 %shard_map.277 = (bf16[1280,384]{1,0:T(8,128)(2,1)S(1)}, bf16[1280,384]{1,0:T(8,128)(2,1)S(1)}, bf16[2,320,768]{2,1,0:T(8,128)(2,1)S(1)}, bf16[2,320,768]{2,1,0:...) custom-call(s32[2]{0:T(128)S(1)} %pad_add_fusion.place_ref, ...), custom_call_target="tpu_custom_call" | custom-call | flops 5000000000 | bytes 14000000 | tf_op jit(solution)/shard_map/pallas_call | solution.py:95
  65.2 2.4 %collective-permute-done.7 = bf16[1280,384]{1,0:T(8,128)(2,1)S(1)} collective-permute-done((bf16[1280,384]{1,0:T(8,128)(2,1)S(1)}, bf16[1280,384]{1,0:T(8,128)(2,1)S(1)}, u32[]{:S(2)}, u32[]{:S(2)}) %collective-permute-start.7) | collective-permute-done | bytes 983072 | tf_op jit(solution)/shard_map/ppermute | solution.py:570
  68.2 32.0 %all_to_all.45 = bf16[64,40,384]{2,1,0:T(8,128)(2,1)S(1)} all-to-all(bf16[64,40,384]{2,1,0:T(8,128)(2,1)S(1)} %bitcast.37), channel_id=1, replica_groups=mesh['z'=4,'x'=4,'h'=2,'l'=2,'c'=2] {'l','z','x','h'}, dimensions={0} | all-to-all | bytes 3932160 | tf_op jit(solution)/shard_map/all_to_all | solution.py:632
  100.4 1.5 shard_map.278.own_ref
  102.2 2.3 %collective-permute-done.8.other_ref = bf16[512,768]{1,0:T(8,128)(2,1)S(1)} collective-permute-done((bf16[512,768]{1,0:T(8,128)(2,1)S(1)}, bf16[512,768]{1,0:T(8,128)(2,1)S(1)}, u32[]{:S(2)}, u32[]{:S(2)}) %collective-permute-start.8) | collective-permute-done | bytes 786464 | tf_op jit(solution)/shard_map/ppermute | solution.py:570
  104.6 10.1 %shard_map.279 = (bf16[512,768]{1,0:T(8,128)(2,1)}, f32[512,768]{1,0:T(8,128)S(1)}, bf16[768,896]{1,0:T(8,128)(2,1)}, bf16[256,768]{1,0:T(8,128)(2,1)S(1)}, bf16[256,768]{1,0:T(8,128)(2,1)S(1)}) custom-call(s32[2]{0:T(128)S(1)} %pad_add_fusion.place_ref, f32[3,32]{1,0:T(4,128)S(1)} %bitcast.36, bf16[512,768]{1,0:T(8,128)(2,1)S(1)} %copy-done, ...), custom_call_target="tpu_custom_call" | custom-call | flops 4000000000 | bytes 12000000 | tf_op jit(solution)/shard_map/pallas_call | solution.py:95
  116.0 5.0 %all-to-all-start.2 = ((bf16[32,24,896]{2,1,0:T(8,128)(2,1)}), bf16[32,24,896]{2,1,0:T(8,128)(2,1)S(1)}, u32[]{:S(2)}, u32[]{:S(2)}) async-start(bf16[32,24,896]{2,1,0:T(8,128)(2,1)} %bitcast.14), calls=%async_computation.2 | async-start | bytes 2752512 | tf_op jit(solution)/shard_map/all_to_all | solution.py:654
  123.2 23.0 %collective-permute-done.10 = bf16[256,768]{1,0:T(8,128)(2,1)S(1)} collective-permute-done((bf16[256,768]{1,0:T(8,128)(2,1)S(1)}, bf16[256,768]{1,0:T(8,128)(2,1)S(1)}, u32[]{:S(2)}, u32[]{:S(2)}) %collective-permute-start.10) | collective-permute-done | bytes 393248 | tf_op jit(solution)/shard_map/ppermute | solution.py:570
  146.3 1.7 collective-permute-done.11.other_ref
  148.1 2.4 %shard_map.281 = bf16[768,896]{1,0:T(8,128)(2,1)} custom-call(s32[2]{0:T(128)S(1)} %pad_add_fusion.place_ref, bf16[768,896]{1,0:T(8,128)(2,1)S(1)} %bitcast.23, bf16[256,768]{1,0:T(8,128)(2,1)S(1)} %add_convert_fusion.1.own_ref, bf16[256,768]{1,0:T(8,128)(2,1)S(1)} %collective-permute-done.11.other_ref, bf16[512,768]{1,0:T(8,128)(2,1)S(1)} %copy-done), custom_call_target="tpu_custom_call" | custom-call | flops 10000000 | bytes 5000000 | tf_op jit(solution)/shard_map/pallas_call | solution.py:95
  150.4 11.1 %all-to-all-start.3 = ((bf16[32,24,896]{2,1,0:T(8,128)(2,1)}), bf16[32,24,896]{2,1,0:T(8,128)(2,1)S(1)}, u32[]{:S(2)}, u32[]{:S(2)}) async-start(bf16[32,24,896]{2,1,0:T(8,128)(2,1)} %bitcast.16), calls=%async_computation.3 | async-start | bytes 2752512 | tf_op jit(solution)/shard_map/all_to_all | solution.py:663
  166.3 5.5 %shard_map.283 = (f32[2,768,768]{2,1,0:T(8,128)}, f32[2,768,768]{2,1,0:T(8,128)}) custom-call(bf16[2,320,768]{2,1,0:T(8,128)(2,1)S(1)} %copy-done.21, bf16[2,320,768]{2,1,0:T(8,128)(2,1)S(1)} %copy-done.23, bf16[2,320,768]{2,1,0:T(8,128)(2,1)S(1)} %copy-done.25, bf16[2,320,768]{2,1,0:T(8,128)(2,1)S(1)} %copy-done.27), custom_call_target="tpu_custom_call" | custom-call | flops 1509949440 | bytes 14000000 | tf_op jit(solution)/shard_map/pallas_call | solution.py:342
  171.9 2.3 %shard_map.280 = f32[512,768]{1,0:T(8,128)} custom-call(s32[2]{0:T(128)S(1)} %pad_add_fusion.place_ref, bf16[256,768]{1,0:T(8,128)(2,1)S(1)} %add_convert_fusion.1.own_ref, bf16[256,768]{1,0:T(8,128)(2,1)S(1)} %collective-permute-done.11.other_ref, bf16[512,768]{1,0:T(8,128)(2,1)S(1)} %copy-done, f32[1,768]{1,0:T(1,128)S(1)} %reshape.39.gain_ref, ...), custom_call_target="tpu_custom_call" | custom-call | flops 10000000 | bytes 5000000 | tf_op jit(solution)/shard_map/pallas_call | solution.py:95
  174.2 10.5 %all-to-all-done.3 = bf16[32,24,896]{2,1,0:T(8,128)(2,1)S(1)} async-done(((bf16[32,24,896]{2,1,0:T(8,128)(2,1)}), bf16[32,24,896]{2,1,0:T(8,128)(2,1)S(1)}, u32[]{:S(2)}, u32[]{:S(2)}) %all-to-all-start.3) | async-done | bytes 1376288 | tf_op jit(solution)/shard_map/all_to_all | solution.py:663
  184.7 1.6 shard_map.282
  (107 shorter events, 14.8 us)
Async XLA Ops:
  0.6 17.3 %copy-start = (bf16[512,768]{1,0:T(8,128)(2,1)S(1)}, bf16[512,768]{1,0:T(8,128)(2,1)}, u32[]{:S(2)}) copy-start(bf16[512,768]{1,0:T(8,128)(2,1)} %x_ref.7) | copy-start | bytes 2359300
  0.7 15.4 %copy-start.35 = (f32[768]{0:T(1024)S(1)}, f32[768]{0:T(1024)}, u32[]{:S(2)}) copy-start(f32[768]{0:T(1024)} %param.26) | copy-start | bytes 9220
  0.7 15.4 %copy-start.34 = (bf16[768,64]{0,1:T(8,128)(2,1)S(1)}, bf16[768,64]{0,1:T(8,128)(2,1)}, u32[]{:S(2)}) copy-start(bf16[768,64]{0,1:T(8,128)(2,1)} %param.27) | copy-start | bytes 294916
  0.7 9.1 %collective-permute-start.4 = (bf16[192,768]{1,0:T(8,128)(2,1)}, bf16[192,768]{1,0:T(8,128)(2,1)}, u32[]{:S(2)}, u32[]{:S(2)}) collective-permute-start(bf16[192,768]{1,0:T(8,128)(2,1)} %wo_ref.1), channel_id=1, source_target_pairs={{0,2},{2,0},{1,3},{3,1},{4,6},{6,4},{5,7},{7,5},{8,10},{10,8},{9,1... | collective-permute-start | bytes 884744 | tf_op jit(solution)/shard_map/ppermute | solution.py:570
  7.9 8.2 %collective-permute-start.1 = (bf16[512,192]{1,0:T(8,128)(2,1)}, bf16[512,192]{1,0:T(8,128)(2,1)}, u32[]{:S(2)}, u32[]{:S(2)}) collective-permute-start(bf16[512,192]{1,0:T(8,128)(2,1)} %get-tuple-element.50.ctx0.ctx_ref), channel_id=1, source_target_pairs={{0,2},{2,0},{1,3},{3,1},{4,6},{6,4},{5,7},{7,5},{8,10},{10,8},{9,1... | collective-permute-start | bytes 589832 | tf_op jit(solution)/shard_map/ppermute | solution.py:570
  8.3 7.9 %collective-permute-start.3 = (bf16[192,768]{1,0:T(8,128)(2,1)}, bf16[192,768]{1,0:T(8,128)(2,1)}, u32[]{:S(2)}, u32[]{:S(2)}) collective-permute-start(bf16[192,768]{1,0:T(8,128)(2,1)} %wo_ref.1), channel_id=1, source_target_pairs={{0,1},{1,0},{2,3},{3,2},{4,5},{5,4},{6,7},{7,6},{8,9},{9,8},{10,11... | collective-permute-start | bytes 884744 | tf_op jit(solution)/shard_map/ppermute | solution.py:570
  9.8 8.2 %collective-permute-start.5 = (bf16[192,768]{1,0:T(8,128)(2,1)}, bf16[192,768]{1,0:T(8,128)(2,1)}, u32[]{:S(2)}, u32[]{:S(2)}) collective-permute-start(bf16[192,768]{1,0:T(8,128)(2,1)} %collective-permute-done.4.wo2), channel_id=1, source_target_pairs={{0,1},{1,0},{2,3},{3,2},{4,5},{5,4},{6,7},{7,6},{8,9},{9,8},{10,11... | collective-permute-start | bytes 884744 | tf_op jit(solution)/shard_map/ppermute | solution.py:570
  9.8 6.4 %collective-permute-start = (bf16[512,192]{1,0:T(8,128)(2,1)}, bf16[512,192]{1,0:T(8,128)(2,1)}, u32[]{:S(2)}, u32[]{:S(2)}) collective-permute-start(bf16[512,192]{1,0:T(8,128)(2,1)} %get-tuple-element.50.ctx0.ctx_ref), channel_id=1, source_target_pairs={{0,1},{1,0},{2,3},{3,2},{4,5},{5,4},{6,7},{7,6},{8,9},{9,8},{10,11... | collective-permute-start | bytes 589832 | tf_op jit(solution)/shard_map/ppermute | solution.py:570
  16.1 1.9 %collective-permute-start.2 = (bf16[512,192]{1,0:T(8,128)(2,1)}, bf16[512,192]{1,0:T(8,128)(2,1)}, u32[]{:S(2)}, u32[]{:S(2)}) collective-permute-start(bf16[512,192]{1,0:T(8,128)(2,1)} %collective-permute-done.1.ctx2), channel_id=1, source_target_pairs={{0,1},{1,0},{2,3},{3,2},{4,5},{5,4},{6,7},{7,6},{8,9},{9,8},{10,11... | collective-permute-start | bytes 589832 | tf_op jit(solution)/shard_map/ppermute | solution.py:570
  20.0 37.7 %copy-start.8 = (bf16[2,768,768]{2,1,0:T(8,128)(2,1)S(1)}, bf16[2,768,768]{2,1,0:T(8,128)(2,1)}, u32[]{:S(2)}) copy-start(bf16[2,768,768]{2,1,0:T(8,128)(2,1)} %in_ref.1) | copy-start | bytes 7077892
  20.0 37.7 %copy-start.9 = (bf16[2,768,768]{2,1,0:T(8,128)(2,1)S(1)}, bf16[2,768,768]{2,1,0:T(8,128)(2,1)}, u32[]{:S(2)}) copy-start(bf16[2,768,768]{2,1,0:T(8,128)(2,1)} %out_ref.1) | copy-start | bytes 7077892
  25.8 32.0 %copy-start.14 = (bf16[320,320]{1,0:T(8,128)(2,1)S(1)}, bf16[320,320]{1,0:T(8,128)(2,1)}, u32[]{:S(2)}) copy-start(bf16[320,320]{1,0:T(8,128)(2,1)} %constant.21.clone.back_ref) | copy-start | bytes 614404
  25.8 32.0 %copy-start.15 = (bf16[320,320]{1,0:T(8,128)(2,1)S(1)}, bf16[320,320]{1,0:T(8,128)(2,1)}, u32[]{:S(2)}) copy-start(bf16[320,320]{1,0:T(8,128)(2,1)} %constant.20.clone.sel_ref) | copy-start | bytes 614404
  55.1 2.6 %collective-permute-start.6 = (bf16[1280,384]{1,0:T(8,128)(2,1)S(1)}, bf16[1280,384]{1,0:T(8,128)(2,1)S(1)}, u32[]{:S(2)}, u32[]{:S(2)}) collective-permute-start(bf16[1280,384]{1,0:T(8,128)(2,1)S(1)} %bitcast.26), channel_id=1, source_target_pairs={{0,1},{1,0},{2,3},{3,2},{4,5},{5,4},{6,7},{7,6},{8,9},{9,8},{10,11... | collective-permute-start | bytes 2949128 | tf_op jit(solution)/shard_map/ppermute | solution.py:570
  65.0 2.6 %collective-permute-start.7 = (bf16[1280,384]{1,0:T(8,128)(2,1)S(1)}, bf16[1280,384]{1,0:T(8,128)(2,1)S(1)}, u32[]{:S(2)}, u32[]{:S(2)}) collective-permute-start(bf16[1280,384]{1,0:T(8,128)(2,1)S(1)} %get-tuple-element.62), channel_id=1, source_target_pairs={{0,1},{1,0},{2,3},{3,2},{4,5},{5,4},{6,7},{7,6},{8,9},{9,8},{10,11... | collective-permute-start | bytes 2949128 | tf_op jit(solution)/shard_map/ppermute | solution.py:570
  68.2 32.1 %copy-start.17 = (bf16[512,1280]{1,0:T(8,128)(2,1)S(1)}, bf16[512,1280]{1,0:T(8,128)(2,1)}, u32[]{:S(2)}) copy-start(bf16[512,1280]{1,0:T(8,128)(2,1)} %copy-done.16) | copy-start | bytes 3932164
  68.2 32.0 %copy-start.19 = (bf16[512,1280]{1,0:T(8,128)(2,1)S(1)}, bf16[512,1280]{1,0:T(8,128)(2,1)}, u32[]{:S(2)}) copy-start(bf16[512,1280]{1,0:T(8,128)(2,1)} %copy-done.18) | copy-start | bytes 3932164
  101.9 2.6 %collective-permute-start.8 = (bf16[512,768]{1,0:T(8,128)(2,1)S(1)}, bf16[512,768]{1,0:T(8,128)(2,1)S(1)}, u32[]{:S(2)}, u32[]{:S(2)}) collective-permute-start(bf16[512,768]{1,0:T(8,128)(2,1)S(1)} %shard_map.278.own_ref), channel_id=1, source_target_pairs={{0,1},{1,0},{2,3},{3,2},{4,5},{5,4},{6,7},{7,6},{8,9},{9,8},{10,11... | collective-permute-start | bytes 2359304 | tf_op jit(solution)/shard_map/ppermute | solution.py:570
  115.9 5.1 %collective-permute-start.9 = (bf16[256,768]{1,0:T(8,128)(2,1)S(1)}, bf16[256,768]{1,0:T(8,128)(2,1)}, u32[]{:S(2)}, u32[]{:S(2)}) collective-permute-start(bf16[256,768]{1,0:T(8,128)(2,1)S(1)} %get-tuple-element.71), channel_id=1, source_target_pairs={{0,1},{1,0},{2,3},{3,2},{4,5},{5,4},{6,7},{7,6},{8,9},{9,8},{10,11... | collective-permute-start | bytes 1179656 | tf_op jit(solution)/shard_map/ppermute | solution.py:570
  116.0 32.0 %all-to-all-start.2 = ((bf16[32,24,896]{2,1,0:T(8,128)(2,1)}), bf16[32,24,896]{2,1,0:T(8,128)(2,1)S(1)}, u32[]{:S(2)}, u32[]{:S(2)}) async-start(bf16[32,24,896]{2,1,0:T(8,128)(2,1)} %bitcast.14), calls=%async_computation.2 | async-start | bytes 2752512 | tf_op jit(solution)/shard_map/all_to_all | solution.py:654
  122.1 24.0 %collective-permute-start.10 = (bf16[256,768]{1,0:T(8,128)(2,1)S(1)}, bf16[256,768]{1,0:T(8,128)(2,1)S(1)}, u32[]{:S(2)}, u32[]{:S(2)}) collective-permute-start(bf16[256,768]{1,0:T(8,128)(2,1)S(1)} %add_convert_fusion.2), channel_id=1, source_target_pairs={{0,2},{2,0},{1,3},{3,1},{4,6},{6,4},{5,7},{7,5},{8,10},{10,8},{9,1... | collective-permute-start | bytes 1179656 | tf_op jit(solution)/shard_map/ppermute | solution.py:570
  146.3 1.8 collective-permute-start.11
  150.4 11.1 %copy-start.36 = (f32[768]{0:T(1024)S(1)}, f32[768]{0:T(1024)}, u32[]{:S(2)}) copy-start(f32[768]{0:T(1024)} %gain_hbm.1) | copy-start | bytes 9220
  150.4 34.3 %all-to-all-start.3 = ((bf16[32,24,896]{2,1,0:T(8,128)(2,1)}), bf16[32,24,896]{2,1,0:T(8,128)(2,1)S(1)}, u32[]{:S(2)}, u32[]{:S(2)}) async-start(bf16[32,24,896]{2,1,0:T(8,128)(2,1)} %bitcast.16), calls=%async_computation.3 | async-start | bytes 2752512 | tf_op jit(solution)/shard_map/all_to_all | solution.py:663
  (30 other events, 112.6 us)

commit v4 on v3

--- a/solution.py
+++ b/solution.py
@@ -133,9 +133,9 @@
 
 def attention_forward(
     table_hbm, x_hbm, gain_hbm, wq_hbm, wk_hbm, wv_hbm,
-    normed_hbm, q_hbm, k_hbm, v_hbm, tiles_hbm, ctx_ref, lse_ref,
+    normed_hbm, q_hbm, k_hbm, v_hbm, probs_hbm, ctx_ref,
     table_ref, x_ref, gain_ref, wq_ref, wk_ref, wv_ref, normed_ref, q_ref, k_ref, v_ref,
-    tiles_ref, sems,
+    tiles_ref, probs_ref, sems,
 ):
     loads = [
         pltpu.make_async_copy(src, dst, sems.at[i])
@@ -160,7 +160,7 @@
     lines = []
     for block in (-1, 0, 1):
         buckets = lax.broadcasted_iota(jnp.int32, (BUCKETS, 256), 0)
-        hot = (buckets == line_buckets(block, BUCKETS)).astype(F32)
+        hot = (buckets == line_buckets(block, 1)).astype(F32)
         lines.append(
             jnp.dot(table, hot, precision=lax.Precision.HIGHEST, preferred_element_type=F32)
         )
@@ -171,7 +171,6 @@
                 0, 1, stride=1, stride_axis=0,
             )
             tiles_ref[head * 3 + block] = wide[:, 128:]
-    store(tiles_ref, tiles_hbm)
     loads[1].wait()
     loads[5].wait()
     gain = gain_ref[...].reshape(1, D)
@@ -191,7 +190,6 @@
         out[...] = dot_nt(normed, weight[...]).astype(BF16)
         store(out, out_hbm)
     queries, keys, values = q_ref[...], k_ref[...], v_ref[...]
-    lse_ref[...] = jnp.zeros((8, SEQ), F32)
     scaled = queries * jnp.asarray(HEAD**-0.5, BF16)
     for part in range(2):
         rows = slice(part * 256, part * 256 + 256)
@@ -202,7 +200,8 @@
             grown = jnp.exp(scores - top)
             total = jnp.sum(grown, axis=0, keepdims=True)
             probs = (grown * (1.0 / total)).astype(BF16)
-            lse_ref[head : head + 1, rows] = top + jnp.log(total)
+            probs_ref[head, part] = probs
+            store(probs_ref.at[head, part], probs_hbm.at[head, part])
             context = context + dot_tn(probs, only_head(values, head))
         ctx_ref[rows, :] = context.astype(BF16)
     for copy in stores:
@@ -235,27 +234,39 @@
 
 
 def middle_kernel(
-    place_ref, x_ref, ctx0, ctx1, ctx2, ctx3, wo0, wo1, wo2, wo3, gain_ref, router_ref,
-    route_ref, low_ref, high_ref, grad_ref, middle_ref, mixed_ref, probs_ref, send_ref,
-    ctx_s, wo_s, rows_s,
+    place_ref, x_hbm, ctx0, ctx1, ctx2, ctx3, wo0, wo1, wo2, wo3, gain_hbm, router_hbm,
+    route_hbm, low_hbm, high_hbm, grad_hbm, middle_hbm, mixed_hbm, probs_hbm, send_ref,
+    ctx_s, wo_s, x_ref, gain_ref, router_ref, route_ref, low_ref, high_ref, grad_ref,
+    middle_ref, mixed_ref, probs_ref, rows_s, sems, out_sems,
 ):
     me = place_ref[0]
     core = place_ref[1]
+    pairs = []
     for step, (c, w) in enumerate(((ctx0, wo0), (ctx1, wo1), (ctx2, wo2), (ctx3, wo3))):
-        ctx_s[me ^ step] = c[...]
-        wo_s[me ^ step] = w[...]
+        pairs += [(c, ctx_s.at[me ^ step]), (w, wo_s.at[me ^ step])]
+    pairs += [
+        (x_hbm, x_ref), (gain_hbm, gain_ref), (route_hbm, route_ref), (router_hbm, router_ref),
+        (grad_hbm, grad_ref), (low_hbm, low_ref), (high_hbm, high_ref),
+    ]
+    loads = [pltpu.make_async_copy(a, b, sems.at[i]) for i, (a, b) in enumerate(pairs)]
+    for load in loads:
+        load.start()
+    for load in loads[:13]:
+        load.wait()
+    stores = []
     columns = route_columns(route_ref)
-    for i in range(2):
-        rows = slice(i * 256, i * 256 + 256)
+    gain = gain_ref[...].reshape(1, D)
+    for i in range(4):
+        rows = slice(i * 128, i * 128 + 128)
         attended = dot(ctx_s[0, rows, :], wo_s[0])
         for t in range(1, 4):
             attended = attended + dot(ctx_s[t, rows, :], wo_s[t])
         middle = x_ref[rows, :].astype(F32) + attended
         scale = lax.rsqrt(jnp.mean(middle * middle, axis=-1, keepdims=True) + EPS)
-        mixed = (middle * scale * gain_ref[...]).astype(BF16)
+        mixed = (middle * scale * gain).astype(BF16)
         middle_ref[rows, :] = middle
         mixed_ref[rows, :] = mixed
-        lanes = lax.broadcasted_iota(jnp.int32, (256, 128), 1)
+        lanes = lax.broadcasted_iota(jnp.int32, (128, 128), 1)
         logits = jnp.where(lanes < EXPERTS, dot_nt(mixed, router_ref[...]), -jnp.inf)
         grown = jnp.exp(logits - jnp.max(logits, axis=-1, keepdims=True))
         probs = grown / jnp.sum(grown, axis=-1, keepdims=True)
@@ -265,10 +276,19 @@
         gate = chosen * (1.0 - columns[rows, 2:3])
         grads = (grad_ref[rows, :].astype(F32) * gate).astype(BF16)
         rows_s[rows, :] = jnp.where(core == 0, mixed, grads)
+        for src, dst in ((middle_ref, middle_hbm), (mixed_ref, mixed_hbm), (probs_ref, probs_hbm)):
+            part = pl.ds(i * 128, 128)
+            copy = pltpu.make_async_copy(src.at[part], dst.at[part], out_sems.at[len(stores)])
+            copy.start()
+            stores.append(copy)
+    for load in loads[13:]:
+        load.wait()
     for i in range(4):
         rows = pl.ds(i * 320, 320)
         out = dot(low_ref[rows, :], rows_s[:, :HALF]) + dot(high_ref[rows, :], rows_s[:, HALF:])
         send_ref[rows, :] = out.astype(BF16)
+    for copy in stores:
+        copy.wait()
 
 
 def expert_kernel(
@@ -364,13 +384,14 @@
 
 
 def backward_kernel(
-    place_ref, table_ref, x_ref, middle_ref, mixed_ref, probs_ref, route_ref, grad_ref,
+    place_ref, x_ref, middle_ref, mixed_ref, probs_ref, route_ref, grad_ref,
     own_ref, other_ref, router_ref, gain_ref, wo_ref, ctx_ref, q_ref, k_ref, v_ref, normed_ref,
-    lse_ref, tiles_ref, wq_ref, wk_ref, wv_ref, stretch_ref,
-    output_ref, middle_grad_ref, grads_ref, mine_ref, theirs_ref,
-    low_s, logit_s, normed_s,
+    weights_ref, wq_ref, wk_ref, wv_ref, stretch_ref,
+    output_hbm, middle_grad_hbm, grads_ref, mine_ref, theirs_ref, gain_one_ref,
+    low_s, logit_s, normed_s, output_ref, middle_grad_ref, sems,
 ):
     core = place_ref[1]
+    stores = []
     columns = route_columns(route_ref)
     gain = gain_ref[...]
     gain_grad = jnp.zeros((1, D), F32)
@@ -399,17 +420,23 @@
         middle_grad = upstream + scale * weighted - middle * (scale * scale * scale * inner)
         middle_grad_ref[rows, :] = middle_grad
         low_s[rows, :] = middle_grad.astype(BF16)
+        for src, dst in ((output_ref, output_hbm), (middle_grad_ref, middle_grad_hbm)):
+            part = pl.ds(i * 128, 128)
+            copy = pltpu.make_async_copy(src.at[part], dst.at[part], sems.at[len(stores)])
+            copy.start()
+            stores.append(copy)
     middle_low = low_s[...]
     grads_ref[pl.ds(3 * WIDTH, WIDTH), :D] = dot_tn(ctx_ref[...], middle_low).astype(BF16)
     ctx_grad = dot_nt(middle_low, wo_ref[...]).astype(BF16)
 
-    keys = k_ref[...]
     values = v_ref[...]
-    key_scaled = keys * jnp.asarray(HEAD**-0.5, BF16)
+    key_scaled = k_ref[...] * jnp.asarray(HEAD**-0.5, BF16)
     query_scaled = q_ref[...] * jnp.asarray(HEAD**-0.5, BF16)
     key_grad = jnp.zeros((SEQ, WIDTH), F32)
     value_grad = jnp.zeros((SEQ, WIDTH), F32)
     query_grads = [jnp.zeros((256, WIDTH), F32), jnp.zeros((256, WIDTH), F32)]
+    buckets = lax.broadcasted_iota(jnp.int32, (BUCKETS, 256), 0)
+    line_ids = [line_buckets(block, 1) for block in (-1, 0, 1)]
     bias_grad = jnp.zeros((BUCKETS, 128), F32)
     bias_lanes = lax.broadcasted_iota(jnp.int32, (BUCKETS, 128), 1)
     turn = (
@@ -426,9 +453,9 @@
             rows = slice(part * 256, part * 256 + 256)
             query_head = only_head(query_scaled[rows], head)
             ctx_head = only_head(ctx_grad[rows], head)
-            scores = scores_t(keys, query_head, tiles_ref, table_ref[...], head, part)
-            probs = jnp.exp(scores - lse_ref[head : head + 1, rows])
-            value_grad = value_grad + dot(probs.astype(BF16), ctx_head)
+            probs_low = weights_ref[head, part]
+            probs = probs_low.astype(F32)
+            value_grad = value_grad + dot(probs_low, ctx_head)
             prob_grad = dot_nt(values, ctx_head)
             inner = jnp.sum(probs * prob_grad, axis=0, keepdims=True)
             score_grad = (probs * (prob_grad - inner)).astype(BF16)
@@ -446,7 +473,6 @@
                         far_high = far_high + piece
                     else:
                         near[block + 1] = near[block + 1] + piece
-        buckets = lax.broadcasted_iota(jnp.int32, (BUCKETS, 256), 0)
         by_bucket = jnp.zeros((BUCKETS, 256), F32)
         for block in range(3):
             turned = jnp.dot(
@@ -456,7 +482,7 @@
             wide = pltpu.roll(wide, 1, 1, stride=1, stride_axis=0)
             line = jnp.sum(wide, axis=0, keepdims=True)
             by_bucket = by_bucket + jnp.where(
-                buckets == line_buckets(block - 1, BUCKETS), line, 0.0
+                buckets == line_ids[block], line, 0.0
             )
         side = lax.broadcasted_iota(jnp.int32, (BUCKETS, 128), 0)
         low_line = jnp.sum(far_low, axis=0, keepdims=True)
@@ -483,8 +509,14 @@
         + dot(value_low, wv_ref[...])
     )
     normed_s[...] = normed_part.astype(BF16)
+    hidden = x_ref[...].astype(F32)
+    scale = lax.rsqrt(jnp.mean(hidden * hidden, axis=-1, keepdims=True) + EPS)
+    gain_one = jnp.sum(normed_part * hidden * scale, axis=0, keepdims=True)
+    gain_one_ref[...] = jnp.broadcast_to(gain_one, (8, D))
     mine_ref[...] = normed_s[pl.ds(pl.multiple_of(core * 256, 256), 256), :]
     theirs_ref[...] = normed_s[pl.ds(pl.multiple_of((1 - core) * 256, 256), 256), :]
+    for copy in stores:
+        copy.wait()
 
 
 def halves(core, own_ref, other_ref, i):
@@ -492,14 +524,8 @@
     return jnp.where(core == i // 2, own_ref[local, :], other_ref[local, :]).astype(F32)
 
 
-def reduce_kernel(place_ref, parts_ref, own_ref, other_ref, x_ref, send_ref):
-    core = place_ref[1]
-    gain_grad = jnp.zeros((1, D), F32)
-    for i in range(4):
-        hidden = x_ref[pl.ds(i * 128, 128), :].astype(F32)
-        scale = lax.rsqrt(jnp.mean(hidden * hidden, axis=-1, keepdims=True) + EPS)
-        normed_grad = halves(core, own_ref, other_ref, i)
-        gain_grad = gain_grad + jnp.sum(normed_grad * hidden * scale, axis=0, keepdims=True)
+def reduce_kernel(parts_ref, pair_ref, link_ref, send_ref):
+    gain_grad = (pair_ref[0:1] + pair_ref[8:9]) + (link_ref[0:1] + link_ref[8:9])
     total = jnp.zeros((24, GRADS), F32)
     for j in range(GROUPS // 2):
         pair = parts_ref[pl.ds(j * 48, 48), :].astype(F32)
@@ -585,15 +611,16 @@
     tile_shape = (3 * HEADS_HERE, 128, 128)
     weight_vmem = pltpu.VMEM((WIDTH, D), BF16)
     tall_vmem = pltpu.VMEM((SEQ, WIDTH), BF16)
-    normed, queries, keys, values, tiles, context, lse = call(
+    probs_shape = (HEADS_HERE, 2, SEQ, 256)
+    normed, queries, keys, values, weights, context = call(
         attention_forward,
-        (wide, tall, tall, tall, shape(tile_shape, F32), tall, shape((8, SEQ), F32)),
+        (wide, tall, tall, tall, shape(probs_shape, BF16), tall),
         (table, layer_input, attn_gain, wq, wk, wv),
         far=(0, 1, 2, 3, 4, 5), far_out=(0, 1, 2, 3, 4),
         scratch=(pltpu.VMEM((HEADS_HERE, BUCKETS), F32), pltpu.VMEM((SEQ, D), BF16),
                  pltpu.VMEM((D,), F32), weight_vmem, weight_vmem, weight_vmem, pltpu.VMEM((SEQ, D), BF16),
                  tall_vmem, tall_vmem, tall_vmem, pltpu.VMEM(tile_shape, F32),
-                 pltpu.SemaphoreType.DMA((11,))),
+                 pltpu.VMEM(probs_shape, BF16), pltpu.SemaphoreType.DMA((16,))),
         limit=60, flops=900_000_000, moved=5_000_000,
     )
     flat, flat_t = shape((ROWS, SEQ), BF16), shape((SEQ, ROWS), BF16)
@@ -607,14 +634,19 @@
     ctx_far = swap(ctx_link_late, "c")
     middle, mixed, probs, send = call(
         middle_kernel,
-        (shape((SEQ, D), F32), shape((SEQ, D), BF16), shape((SEQ, 128), F32),
-         shape((ROWS, HALF), BF16)),
+        (shape((SEQ, D), F32), wide, shape((SEQ, 128), F32), shape((ROWS, HALF), BF16)),
         (place, layer_input, context, ctx_core, ctx_link, ctx_far,
-         output_weight, wo_core, wo_link, wo_far, gain_two, router, route, low_place, high_place,
+         output_weight, wo_core, wo_link, wo_far, moe_gain, router, route, low_place, high_place,
          out_grad),
         scratch=(pltpu.VMEM((4, SEQ, WIDTH), BF16), pltpu.VMEM((4, WIDTH, D), BF16),
-                 pltpu.VMEM((SEQ, D), BF16)),
-        scalars=1, limit=16, flops=1_700_000_000, moved=8_000_000,
+                 pltpu.VMEM((SEQ, D), BF16), pltpu.VMEM((D,), F32), pltpu.VMEM((128, D), BF16),
+                 pltpu.VMEM((8, SEQ), jnp.int32), pltpu.VMEM((ROWS, SEQ), BF16),
+                 pltpu.VMEM((ROWS, SEQ), BF16), pltpu.VMEM((SEQ, D), BF16),
+                 pltpu.VMEM((SEQ, D), F32), pltpu.VMEM((SEQ, D), BF16),
+                 pltpu.VMEM((SEQ, 128), F32), pltpu.VMEM((SEQ, D), BF16),
+                 pltpu.SemaphoreType.DMA((15,)), pltpu.SemaphoreType.DMA((12,))),
+        scalars=1, far=tuple(range(1, 16)), far_out=(0, 1, 2),
+        limit=60, flops=1_700_000_000, moved=8_000_000,
     )
     received = lax.all_to_all(send, experts_axis, 0, 0, tiled=True)
     received_other = swap(received, "c")
@@ -640,25 +672,29 @@
     rows_other = swap(rows_own, "c")
     stretch = np.zeros((D, BUCKETS), np.float32)
     stretch[24 * np.arange(BUCKETS), np.arange(BUCKETS)] = 1
-    layer_output, middle_grad, grads, norm_mine, norm_theirs = call(
+    half = shape((256, D), BF16)
+    layer_output, middle_grad, grads, norm_mine, norm_theirs, gain_part = call(
         backward_kernel,
-        (shape((SEQ, D), BF16), shape((SEQ, D), F32), shape((D, GRADS), BF16),
-         shape((256, D), BF16), shape((256, D), BF16)),
-        (place, table, layer_input, middle, mixed, probs, route, out_grad,
+        (wide, shape((SEQ, D), F32), shape((D, GRADS), BF16), half, half, shape((8, D), F32)),
+        (place, layer_input, middle, mixed, probs, route, out_grad,
          rows_own, rows_other, router, gain_two, output_weight, context, queries, keys,
-         values, normed, lse, tiles, wq, wk, wv, jnp.asarray(stretch, BF16)),
+         values, normed, weights, wq, wk, wv, jnp.asarray(stretch, BF16)),
         scratch=(pltpu.VMEM((SEQ, D), BF16), pltpu.VMEM((SEQ, 128), BF16),
-                 pltpu.VMEM((SEQ, D), BF16)),
+                 pltpu.VMEM((SEQ, D), BF16), pltpu.VMEM((SEQ, D), BF16),
+                 pltpu.VMEM((SEQ, D), F32), pltpu.SemaphoreType.DMA((8,))),
+        far_out=(0, 1),
         scalars=1, limit=24, flops=4_000_000_000, moved=12_000_000,
     )
+    gain_pair = jnp.concatenate([gain_part, swap(gain_part, "c")], axis=0)
+    halved = (norm_mine.astype(F32) + swap(norm_theirs, "c").astype(F32)).astype(BF16)
     scattered = lax.all_to_all(grads, experts_axis, 0, 0, tiled=True)
-    halved = (norm_mine.astype(F32) + swap(norm_theirs, "c").astype(F32)).astype(BF16)
+    gain_link = swap(gain_pair, "l")
     halved = (halved.astype(F32) + swap(halved, "l").astype(F32)).astype(BF16)
     halved_other = swap(halved, "c")
     spread = call(
         reduce_kernel, shape((D, GRADS), BF16),
-        (place, scattered, halved, halved_other, layer_input),
-        scalars=1, limit=12, flops=10_000_000, moved=5_000_000,
+        (scattered, gain_pair, gain_link),
+        limit=12, flops=10_000_000, moved=3_000_000,
     )
     gathered = lax.all_to_all(spread, experts_axis, 0, 0, tiled=True)
     input_grad = call(

time: 187 us -> 194 us (1.037)
  starting transfers between devices: 20.6 us -> 15.2 us
  waiting for transfers between devices: 47.7 us -> 51.9 us
  Pallas kernels: 43.5 us -> 46.9 us
    all_to_all x1, waiting for transfers between devices: 0.01 us -> 11.8 us  [shards(): scattered = lax.all_to_all(grads, experts_axis, 0, 0, tiled=True)]
    all_to_all x1, waiting for transfers between devices: 10.5 us -> 0.01 us  [shards(): gathered = lax.all_to_all(spread, experts_axis, 0, 0, tiled=True)]
    all_to_all x1, starting transfers between devices: 11.1 us -> 5.22 us  [shards(): gathered = lax.all_to_all(spread, experts_axis, 0, 0, tiled=True)]
    pallas_call x9, Pallas kernels: 37.9 us -> 41.4 us  [call(): pl.pallas_call(body, out_shape=outs, in_specs=[pl.BlockSpec(memory_space=...]
    ppermute x12 -> x14, waiting for transfers between devices: 37.2 us -> 40.1 us  [swap(): return lax.ppermute(array, axis, [(0, 1), (1, 0)])]
    unnamed x80 -> x107, local copies, waits for them, and re-layouts: 10.3 us -> 11.1 us
    ppermute x12 -> x14, starting transfers between devices: 4.48 us -> 4.96 us  [swap(): return lax.ppermute(array, axis, [(0, 1), (1, 0)])]
  transfers between devices with their start and end apart: 14 -> 16, of which waited for: 9 -> 10; matrix products, arithmetic and copies ran while one was open for 1% -> 1% of each run, Pallas kernels for 8% -> 9%
where the time goes in v4:
time: 194 us; the launch traced here: 192 us
  blocking collectives  62.1 us (32%)
  waiting for transfers between devices  51.9 us (27%)
  Pallas kernels  46.9 us (24%)
  starting transfers between devices  15.2 us (8%)
  local copies, waits for them, and re-layouts  11.9 us (6%)
  other arithmetic  2.38 us (1%)
    pallas_call x9, Pallas kernels, call(): pl.pallas_call(body, out_shape=outs, in_specs=[pl.BlockSpec(memory_space=...  41.4 us
    ppermute x14, waiting for transfers between devices, swap(): return lax.ppermute(array, axis, [(0, 1), (1, 0)])  40.1 us
    all_to_all x1, blocking collectives, shards(): lax.all_to_all(jnp.concatenate([partial, partial], axis=0), pair_axis, 0,...  32.2 us
    all_to_all x1, blocking collectives, shards(): received = lax.all_to_all(send, experts_axis, 0, 0, tiled=True)  29.8 us
    all_to_all x1, waiting for transfers between devices, shards(): scattered = lax.all_to_all(grads, experts_axis, 0, 0, tiled=True)  11.8 us
    unnamed x107, local copies, waits for them, and re-layouts  11.1 us
    pallas_call x1, Pallas kernels, expert_grads(): pl.pallas_call(expert_grads_kernel, grid=(2, 3), out_shape=(shape((2, D,...  5.55 us
    all_to_all x1, starting transfers between devices, shards(): gathered = lax.all_to_all(spread, experts_axis, 0, 0, tiled=True)  5.22 us
  transfers between devices with their start and end apart: 16, of which 10 were waited for; matrix products, arithmetic and copies ran while one was open for 1% of the time, Pallas kernels for 9%

profile of v4, /device:TPU:0, one launch (start us, length us, event | category | flops | bytes accessed | tf_op | source)
XLA Modules:
  0.0 191.7 jit_solution(5914556608068950343)
XLA Ops:
  0.7 1.7 collective-permute-start.4
  2.4 6.0 %shard_map.274 = (bf16[512,768]{1,0:T(8,128)(2,1)}, bf16[512,192]{1,0:T(8,128)(2,1)}, bf16[512,192]{1,0:T(8,128)(2,1)}, bf16[512,192]{1,0:T(8,128)(2,1)}, bf16[3...) custom-call(f32[3,32]{1,0:T(4,128)} %bitcast.44, bf16[512,768]{1,0:T(8,128)(2,1)} %x_ref.3, f32[768]{0:T(1024)} %gain_hbm.2, ...), custom_call_target="tpu_custom_call" | custom-call | flops 900000000 | bytes 5000000 | tf_op jit(solution)/shard_map/pallas_call | solution.py:95
  10.2 1.6 shard_map.275
  19.6 8.6 %shard_map.276 = (f32[512,768]{1,0:T(8,128)}, bf16[512,768]{1,0:T(8,128)(2,1)}, f32[512,128]{1,0:T(8,128)}, bf16[1280,384]{1,0:T(8,128)(2,1)}) custom-call(s32[2]{0:T(128)} %pad_add_fusion.place_ref, bf16[512,768]{1,0:T(8,128)(2,1)} %x_ref.3, bf16[512,192]{1,0:T(8,128)(2,1)} %get-tuple-element.50.ctx0.ctx_ref, bf16[512,192]{1,0:T(8,128)(2,1)} %copy-done.45, ...), custom_call_target="tpu_custom_call" | custom-call | flops 1700000000 | bytes 8000000 | tf_op jit(solution)/shard_map/pallas_call | solution.py:95
  28.2 29.8 %all_to_all.44 = bf16[32,40,384]{2,1,0:T(8,128)(2,1)S(1)} all-to-all(bf16[32,40,384]{2,1,0:T(8,128)(2,1)} %bitcast.35), channel_id=1, replica_groups=mesh['z'=4,'x'=4,'h'=2,'l'=2,'c'=2] {'z','x','h'}, dimensions={0} | all-to-all | bytes 1966080 | tf_op jit(solution)/shard_map/all_to_all | solution.py:651
  58.0 2.6 %collective-permute-done.6.other_ref = bf16[1280,384]{1,0:T(8,128)(2,1)S(1)} collective-permute-done((bf16[1280,384]{1,0:T(8,128)(2,1)S(1)}, bf16[1280,384]{1,0:T(8,128)(2,1)S(1)}, u32[]{:S(2)}, u32[]{:S(2)}) %collective-permute-start.6) | collective-permute-done | bytes 983072 | tf_op jit(solution)/shard_map/ppermute | solution.py:596
  60.6 1.7 copy-done.15
  62.3 7.2 %shard_map.277 = (bf16[1280,384]{1,0:T(8,128)(2,1)S(1)}, bf16[1280,384]{1,0:T(8,128)(2,1)S(1)}, bf16[2,320,768]{2,1,0:T(8,128)(2,1)S(1)}, bf16[2,320,768]{2,1,0:...) custom-call(s32[2]{0:T(128)S(1)} %copy-done.13, bf16[1280,384]{1,0:T(8,128)(2,1)S(1)} %bitcast.27, ...), custom_call_target="tpu_custom_call" | custom-call | flops 5000000000 | bytes 14000000 | tf_op jit(solution)/shard_map/pallas_call | solution.py:95
  69.7 2.4 %collective-permute-done.7 = bf16[1280,384]{1,0:T(8,128)(2,1)S(1)} collective-permute-done((bf16[1280,384]{1,0:T(8,128)(2,1)S(1)}, bf16[1280,384]{1,0:T(8,128)(2,1)S(1)}, u32[]{:S(2)}, u32[]{:S(2)}) %collective-permute-start.7) | collective-permute-done | bytes 983072 | tf_op jit(solution)/shard_map/ppermute | solution.py:596
  72.7 32.2 %all_to_all.45 = bf16[64,40,384]{2,1,0:T(8,128)(2,1)S(1)} all-to-all(bf16[64,40,384]{2,1,0:T(8,128)(2,1)S(1)} %bitcast.34), channel_id=1, replica_groups=mesh['z'=4,'x'=4,'h'=2,'l'=2,'c'=2] {'l','z','x','h'}, dimensions={0} | all-to-all | bytes 3932160 | tf_op jit(solution)/shard_map/all_to_all | solution.py:664
  105.1 1.5 shard_map.278.own_ref
  107.0 2.2 %collective-permute-done.8.other_ref = bf16[512,768]{1,0:T(8,128)(2,1)S(1)} collective-permute-done((bf16[512,768]{1,0:T(8,128)(2,1)S(1)}, bf16[512,768]{1,0:T(8,128)(2,1)S(1)}, u32[]{:S(2)}, u32[]{:S(2)}) %collective-permute-start.8) | collective-permute-done | bytes 786464 | tf_op jit(solution)/shard_map/ppermute | solution.py:596
  109.4 11.0 %shard_map.279 = (bf16[512,768]{1,0:T(8,128)(2,1)}, f32[512,768]{1,0:T(8,128)S(1)}, bf16[768,896]{1,0:T(8,128)(2,1)}, bf16[256,768]{1,0:T(8,128)(2,1)S(1)}, bf16...) custom-call(s32[2]{0:T(128)S(1)} %copy-done.13, bf16[512,768]{1,0:T(8,128)(2,1)S(1)} %copy-done, ...), custom_call_target="tpu_custom_call" | custom-call | flops 4000000000 | bytes 12000000 | tf_op jit(solution)/shard_map/pallas_call | solution.py:95
  121.6 5.0 %all-to-all-start.2 = ((bf16[32,24,896]{2,1,0:T(8,128)(2,1)}), bf16[32,24,896]{2,1,0:T(8,128)(2,1)S(1)}, u32[]{:S(2)}, u32[]{:S(2)}) async-start(bf16[32,24,896]{2,1,0:T(8,128)(2,1)} %bitcast.14), calls=%async_computation.2 | async-start | bytes 2752512 | tf_op jit(solution)/shard_map/all_to_all | solution.py:690
  127.2 1.2 collective-permute-done.12
  129.4 8.7 %collective-permute-done.13.link_ref = f32[16,768]{1,0:T(8,128)S(1)} collective-permute-done((f32[16,768]{1,0:T(8,128)S(1)}, f32[16,768]{1,0:T(8,128)S(1)}, u32[]{:S(2)}, u32[]{:S(2)}) %collective-permute-start.13) | collective-permute-done | bytes 49184 | tf_op jit(solution)/shard_map/ppermute | solution.py:596
  138.1 11.8 %all-to-all-done.2 = bf16[32,24,896]{2,1,0:T(8,128)(2,1)S(1)} async-done(((bf16[32,24,896]{2,1,0:T(8,128)(2,1)}), bf16[32,24,896]{2,1,0:T(8,128)(2,1)S(1)}, u32[]{:S(2)}, u32[]{:S(2)}) %all-to-all-start.2) | async-done | bytes 1376288 | tf_op jit(solution)/shard_map/all_to_all | solution.py:690
  149.9 1.4 shard_map.281
  151.3 5.2 %all-to-all-start.3 = ((bf16[32,24,896]{2,1,0:T(8,128)(2,1)}), bf16[32,24,896]{2,1,0:T(8,128)(2,1)S(1)}, u32[]{:S(2)}, u32[]{:S(2)}) async-start(bf16[32,24,896]{2,1,0:T(8,128)(2,1)} %bitcast.16), calls=%async_computation.3 | async-start | bytes 2752512 | tf_op jit(solution)/shard_map/all_to_all | solution.py:699
  156.6 1.2 add_convert_fusion.2
  157.9 21.6 %collective-permute-done.10 = bf16[256,768]{1,0:T(8,128)(2,1)S(1)} collective-permute-done((bf16[256,768]{1,0:T(8,128)(2,1)S(1)}, bf16[256,768]{1,0:T(8,128)(2,1)S(1)}, u32[]{:S(2)}, u32[]{:S(2)}) %collective-permute-start.10) | collective-permute-done | bytes 393248 | tf_op jit(solution)/shard_map/ppermute | solution.py:596
  182.1 5.5 %shard_map.283 = (f32[2,768,768]{2,1,0:T(8,128)}, f32[2,768,768]{2,1,0:T(8,128)}) custom-call(bf16[2,320,768]{2,1,0:T(8,128)(2,1)S(1)} %copy-done.30, bf16[2,320,768]{2,1,0:T(8,128)(2,1)S(1)} %copy-done.32, bf16[2,320,768]{2,1,0:T(8,128)(2,1)S(1)} %copy-done.34, bf16[2,320,768]{2,1,0:T(8,128)(2,1)S(1)} %copy-done.36), custom_call_target="tpu_custom_call" | custom-call | flops 1509949440 | bytes 14000000 | tf_op jit(solution)/shard_map/pallas_call | solution.py:362
  187.7 2.4 %shard_map.280 = f32[512,768]{1,0:T(8,128)} custom-call(s32[2]{0:T(128)S(1)} %copy-done.13, bf16[256,768]{1,0:T(8,128)(2,1)S(1)} %add_convert_fusion.1.own_ref, bf16[256,768]{1,0:T(8,128)(2,1)S(1)} %collective-permute-done.11.other_ref, bf16[512,768]{1,0:T(8,128)(2,1)S(1)} %copy-done, f32[1,768]{1,0:T(1,128)S(1)} %reshape.39.gain_ref, f32[512,768]{1,0:T(8,128)S(1)} %copy-done.2), custom_call_target="tpu_custom_call" | custom-call | flops 10000000 | bytes 5000000 | tf_op jit(solution)/shard_map/pallas_call | solution.py:95
  190.1 1.6 shard_map.282
  (139 shorter events, 16.0 us)
Async XLA Ops:
  0.7 9.0 %collective-permute-start.4 = (bf16[192,768]{1,0:T(8,128)(2,1)}, bf16[192,768]{1,0:T(8,128)(2,1)S(1)}, u32[]{:S(2)}, u32[]{:S(2)}) collective-permute-start(bf16[192,768]{1,0:T(8,128)(2,1)} %wo_ref.1), channel_id=1, source_target_pairs={{0,2},{2,0},{1,3},{3,1},{4,6},{6,4},{5,7},{7,5},{8,10},{10,8},{9,1... | collective-permute-start | bytes 884744 | tf_op jit(solution)/shard_map/ppermute | solution.py:596
  8.4 8.1 %collective-permute-start.1 = (bf16[512,192]{1,0:T(8,128)(2,1)}, bf16[512,192]{1,0:T(8,128)(2,1)S(1)}, u32[]{:S(2)}, u32[]{:S(2)}) collective-permute-start(bf16[512,192]{1,0:T(8,128)(2,1)} %get-tuple-element.50.ctx0.ctx_ref), channel_id=1, source_target_pairs={{0,2},{2,0},{1,3},{3,1},{4,6},{6,4},{5,7},{7,5},{8,10},{10,8},{9,1... | collective-permute-start | bytes 589832 | tf_op jit(solution)/shard_map/ppermute | solution.py:596
  8.9 9.0 %collective-permute-start.3 = (bf16[192,768]{1,0:T(8,128)(2,1)S(1)}, bf16[192,768]{1,0:T(8,128)(2,1)S(1)}, u32[]{:S(2)}, u32[]{:S(2)}) collective-permute-start(bf16[192,768]{1,0:T(8,128)(2,1)S(1)} %copy-done.7), channel_id=1, source_target_pairs={{0,1},{1,0},{2,3},{3,2},{4,5},{5,4},{6,7},{7,6},{8,9},{9,8},{10,11... | collective-permute-start | bytes 884744 | tf_op jit(solution)/shard_map/ppermute | solution.py:596
  9.7 8.4 %collective-permute-start.5 = (bf16[192,768]{1,0:T(8,128)(2,1)S(1)}, bf16[192,768]{1,0:T(8,128)(2,1)S(1)}, u32[]{:S(2)}, u32[]{:S(2)}) collective-permute-start(bf16[192,768]{1,0:T(8,128)(2,1)S(1)} %collective-permute-done.4.wo2), channel_id=1, source_target_pairs={{0,1},{1,0},{2,3},{3,2},{4,5},{5,4},{6,7},{7,6},{8,9},{9,8},{10,11... | collective-permute-start | bytes 884744 | tf_op jit(solution)/shard_map/ppermute | solution.py:596
  9.7 8.2 %collective-permute-start = (bf16[512,192]{1,0:T(8,128)(2,1)}, bf16[512,192]{1,0:T(8,128)(2,1)S(1)}, u32[]{:S(2)}, u32[]{:S(2)}) collective-permute-start(bf16[512,192]{1,0:T(8,128)(2,1)} %get-tuple-element.50.ctx0.ctx_ref), channel_id=1, source_target_pairs={{0,1},{1,0},{2,3},{3,2},{4,5},{5,4},{6,7},{7,6},{8,9},{9,8},{10,11... | collective-permute-start | bytes 589832 | tf_op jit(solution)/shard_map/ppermute | solution.py:596
  16.5 1.5 collective-permute-start.2
  19.5 41.1 %copy-start.14 = (bf16[2,768,768]{2,1,0:T(8,128)(2,1)S(1)}, bf16[2,768,768]{2,1,0:T(8,128)(2,1)}, u32[]{:S(2)}) copy-start(bf16[2,768,768]{2,1,0:T(8,128)(2,1)} %in_ref.1) | copy-start | bytes 7077892
  28.2 32.4 %copy-start.13 = (s32[2]{0:T(128)S(1)}, s32[2]{0:T(128)}, u32[]{:S(2)}) copy-start(s32[2]{0:T(128)} %pad_add_fusion.place_ref) | copy-start | bytes 28
  28.2 32.4 %copy-start.22 = (bf16[320,320]{1,0:T(8,128)(2,1)S(1)}, bf16[320,320]{1,0:T(8,128)(2,1)}, u32[]{:S(2)}) copy-start(bf16[320,320]{1,0:T(8,128)(2,1)} %constant.21.clone.back_ref) | copy-start | bytes 614404
  28.2 32.4 %copy-start.23 = (bf16[320,320]{1,0:T(8,128)(2,1)S(1)}, bf16[320,320]{1,0:T(8,128)(2,1)}, u32[]{:S(2)}) copy-start(bf16[320,320]{1,0:T(8,128)(2,1)} %constant.20.clone.sel_ref) | copy-start | bytes 614404
  58.0 2.6 %collective-permute-start.6 = (bf16[1280,384]{1,0:T(8,128)(2,1)S(1)}, bf16[1280,384]{1,0:T(8,128)(2,1)S(1)}, u32[]{:S(2)}, u32[]{:S(2)}) collective-permute-start(bf16[1280,384]{1,0:T(8,128)(2,1)S(1)} %bitcast.26), channel_id=1, source_target_pairs={{0,1},{1,0},{2,3},{3,2},{4,5},{5,4},{6,7},{7,6},{8,9},{9,8},{10,11... | collective-permute-start | bytes 2949128 | tf_op jit(solution)/shard_map/ppermute | solution.py:596
  69.5 2.6 %collective-permute-start.7 = (bf16[1280,384]{1,0:T(8,128)(2,1)S(1)}, bf16[1280,384]{1,0:T(8,128)(2,1)S(1)}, u32[]{:S(2)}, u32[]{:S(2)}) collective-permute-start(bf16[1280,384]{1,0:T(8,128)(2,1)S(1)} %get-tuple-element.62), channel_id=1, source_target_pairs={{0,1},{1,0},{2,3},{3,2},{4,5},{5,4},{6,7},{7,6},{8,9},{9,8},{10,11... | collective-permute-start | bytes 2949128 | tf_op jit(solution)/shard_map/ppermute | solution.py:596
  72.4 36.8 %copy-start.39 = (bf16[512,192]{1,0:T(8,128)(2,1)S(1)}, bf16[512,192]{1,0:T(8,128)(2,1)}, u32[]{:S(2)}) copy-start(bf16[512,192]{1,0:T(8,128)(2,1)} %get-tuple-element.64.k_ref) | copy-start | bytes 589828
  72.4 36.8 %copy-start.40 = (bf16[512,192]{1,0:T(8,128)(2,1)S(1)}, bf16[512,192]{1,0:T(8,128)(2,1)}, u32[]{:S(2)}) copy-start(bf16[512,192]{1,0:T(8,128)(2,1)} %get-tuple-element.65.v_ref) | copy-start | bytes 589828
  72.7 32.3 %copy-start.25 = (bf16[512,1280]{1,0:T(8,128)(2,1)S(1)}, bf16[512,1280]{1,0:T(8,128)(2,1)}, u32[]{:S(2)}) copy-start(bf16[512,1280]{1,0:T(8,128)(2,1)} %copy-done.24) | copy-start | bytes 3932164
  72.7 36.6 %copy-start.28 = (bf16[3,2,512,256]{3,2,1,0:T(8,128)(2,1)S(1)}, bf16[3,2,512,256]{3,2,1,0:T(8,128)(2,1)}, u32[]{:S(2)}) copy-start(bf16[3,2,512,256]{3,2,1,0:T(8,128)(2,1)} %get-tuple-element.67.weights_ref) | copy-start | bytes 4718596
  106.7 2.6 %collective-permute-start.8 = (bf16[512,768]{1,0:T(8,128)(2,1)S(1)}, bf16[512,768]{1,0:T(8,128)(2,1)S(1)}, u32[]{:S(2)}, u32[]{:S(2)}) collective-permute-start(bf16[512,768]{1,0:T(8,128)(2,1)S(1)} %shard_map.278.own_ref), channel_id=1, source_target_pairs={{0,1},{1,0},{2,3},{3,2},{4,5},{5,4},{6,7},{7,6},{8,9},{9,8},{10,11... | collective-permute-start | bytes 2359304 | tf_op jit(solution)/shard_map/ppermute | solution.py:596
  121.6 28.3 %all-to-all-start.2 = ((bf16[32,24,896]{2,1,0:T(8,128)(2,1)}), bf16[32,24,896]{2,1,0:T(8,128)(2,1)S(1)}, u32[]{:S(2)}, u32[]{:S(2)}) async-start(bf16[32,24,896]{2,1,0:T(8,128)(2,1)} %bitcast.14), calls=%async_computation.2 | async-start | bytes 2752512 | tf_op jit(solution)/shard_map/all_to_all | solution.py:690
  126.6 30.0 %collective-permute-start.9 = (bf16[256,768]{1,0:T(8,128)(2,1)S(1)}, bf16[256,768]{1,0:T(8,128)(2,1)}, u32[]{:S(2)}, u32[]{:S(2)}) collective-permute-start(bf16[256,768]{1,0:T(8,128)(2,1)S(1)} %get-tuple-element.70), channel_id=1, source_target_pairs={{0,1},{1,0},{2,3},{3,2},{4,5},{5,4},{6,7},{7,6},{8,9},{9,8},{10,11... | collective-permute-start | bytes 1179656 | tf_op jit(solution)/shard_map/ppermute | solution.py:596
  126.7 1.7 collective-permute-start.12
  128.4 9.7 %collective-permute-start.13 = (f32[16,768]{1,0:T(8,128)S(1)}, f32[16,768]{1,0:T(8,128)S(1)}, u32[]{:S(2)}, u32[]{:S(2)}) collective-permute-start(f32[16,768]{1,0:T(8,128)S(1)} %constant_dynamic-update-slice_fusion.pair_ref), channel_id=1, source_target_pairs={{0,2},{2,0},{1,3},{3,1},{4,6},{6,4},{5,7},{7,5},{8,10},{10,8},{9,1... | collective-permute-start | bytes 147464 | tf_op jit(solution)/shard_map/ppermute | solution.py:596
  151.3 38.8 %all-to-all-start.3 = ((bf16[32,24,896]{2,1,0:T(8,128)(2,1)}), bf16[32,24,896]{2,1,0:T(8,128)(2,1)S(1)}, u32[]{:S(2)}, u32[]{:S(2)}) async-start(bf16[32,24,896]{2,1,0:T(8,128)(2,1)} %bitcast.16), calls=%async_computation.3 | async-start | bytes 2752512 | tf_op jit(solution)/shard_map/all_to_all | solution.py:699
  157.8 21.6 %collective-permute-start.10 = (bf16[256,768]{1,0:T(8,128)(2,1)S(1)}, bf16[256,768]{1,0:T(8,128)(2,1)S(1)}, u32[]{:S(2)}, u32[]{:S(2)}) collective-permute-start(bf16[256,768]{1,0:T(8,128)(2,1)S(1)} %add_convert_fusion.2), channel_id=1, source_target_pairs={{0,2},{2,0},{1,3},{3,1},{4,6},{6,4},{5,7},{7,5},{8,10},{10,8},{9,1... | collective-permute-start | bytes 1179656 | tf_op jit(solution)/shard_map/ppermute | solution.py:596
  179.6 8.1 %collective-permute-start.11 = (bf16[256,768]{1,0:T(8,128)(2,1)S(1)}, bf16[256,768]{1,0:T(8,128)(2,1)S(1)}, u32[]{:S(2)}, u32[]{:S(2)}) collective-permute-start(bf16[256,768]{1,0:T(8,128)(2,1)S(1)} %add_convert_fusion.1.own_ref), channel_id=1, source_target_pairs={{0,1},{1,0},{2,3},{3,2},{4,5},{5,4},{6,7},{7,6},{8,9},{9,8},{10,11... | collective-permute-start | bytes 1179656 | tf_op jit(solution)/shard_map/ppermute | solution.py:596
  (45 other events, 279.9 us)

commit v5 on v3

--- a/solution.py
+++ b/solution.py
@@ -85,7 +85,7 @@
 
 
 def call(
-    body, out_shape, args, scratch=(), scalars=0, far=(), far_out=(), limit=40, flops=0, moved=0
+    body, out_shape, args, scratch=(), scalars=0, far=(), far_out=(), alias=None, limit=40, flops=0, moved=0
 ):
     spaces = [pltpu.SMEM] * scalars + [pltpu.VMEM] * (len(args) - scalars)
     for i in far:
@@ -98,6 +98,7 @@
         in_specs=[pl.BlockSpec(memory_space=space) for space in spaces],
         out_specs=tuple(pl.BlockSpec(memory_space=space) for space in out_spaces),
         scratch_shapes=scratch,
+        input_output_aliases=alias or {},
         compiler_params=pltpu.CompilerParams(vmem_limit_bytes=limit << 20),
         cost_estimate=pl.CostEstimate(flops=flops, bytes_accessed=moved, transcendentals=0),
     )(*args)
@@ -160,7 +161,7 @@
     lines = []
     for block in (-1, 0, 1):
         buckets = lax.broadcasted_iota(jnp.int32, (BUCKETS, 256), 0)
-        hot = (buckets == line_buckets(block, BUCKETS)).astype(F32)
+        hot = (buckets == line_buckets(block, 1)).astype(F32)
         lines.append(
             jnp.dot(table, hot, precision=lax.Precision.HIGHEST, preferred_element_type=F32)
         )
@@ -271,9 +272,9 @@
         send_ref[rows, :] = out.astype(BF16)
 
 
-def expert_kernel(
+def first_expert_kernel(
     place_ref, own_ref, other_ref, in_ref, out_ref, sel_ref, back_ref,
-    mine_ref, theirs_ref, x_ref, s_ref, act_ref, pre_ref, o_s, i_s,
+    theirs_ref, x_ref, s_ref, act_ref, pre_ref, part_s,
 ):
     core = place_ref[1]
     for b in range(4):
@@ -293,42 +294,46 @@
     for e in range(2):
         x = x_ref[e]
         s = s_ref[e]
-        out = jnp.zeros((320, D), F32)
-        back = jnp.zeros((320, D), F32)
         for f in range(3):
             cols = slice(f * 256, f * 256 + 256)
-            w_in = in_ref[e, :, cols]
-            w_out = out_ref[e, cols, :]
-            pre = dot(x, w_in)
+            pre = dot(x, in_ref[e, :, cols])
             bent = jnp.tanh(GELU_C * (pre + 0.044715 * (pre * pre * pre)))
             cdf = 0.5 * (1.0 + bent)
-            act = (pre * cdf).astype(BF16)
+            act_ref[e, :, cols] = (pre * cdf).astype(BF16)
             slope = cdf + (0.5 * GELU_C) * pre * (1.0 - bent * bent) * (
                 1.0 + (3 * 0.044715) * (pre * pre)
             )
-            act_ref[e, :, cols] = act
-            out = out + dot(act, w_out)
-            act_grad = dot_nt(s, w_out)
-            pre_grad = (act_grad * slope).astype(BF16)
-            pre_ref[e, :, cols] = pre_grad
-            back = back + dot_nt(pre_grad, w_in)
-        o_s[e] = out.astype(BF16)
-        i_s[e] = back.astype(BF16)
+            act_grad = dot_nt(s, out_ref[e, cols, :])
+            pre_ref[e, :, cols] = (act_grad * slope).astype(BF16)
+    expert_sums(core == 1, act_ref, pre_ref, in_ref, out_ref, back_ref, theirs_ref, part_s)
+
+
+def expert_sums(forward, act_ref, pre_ref, in_ref, out_ref, back_ref, sum_ref, part_s):
+    @pl.when(forward)
+    def _():
+        for e in range(2):
+            part_s[e] = dot(act_ref[e], out_ref[e]).astype(BF16)
+
+    @pl.when(jnp.logical_not(forward))
+    def _():
+        for e in range(2):
+            part_s[e] = dot_nt(pre_ref[e], in_ref[e]).astype(BF16)
+
     for b in range(4):
         rows = pl.ds(b * 80, 80)
-        pieces = []
-        for src in (o_s, i_s):
-            stacked = jnp.concatenate(
-                [
-                    src[e, rows, pl.ds(half * HALF, HALF)]
-                    for half in range(2)
-                    for e in range(2)
-                ],
-                axis=0,
-            )
-            pieces.append(dot(back_ref[...], stacked).astype(BF16))
-        mine_ref[pl.ds(b * 320, 320), :] = jnp.where(core == 0, pieces[0], pieces[1])
-        theirs_ref[pl.ds(b * 320, 320), :] = jnp.where(core == 0, pieces[1], pieces[0])
+        stacked = jnp.concatenate(
+            [part_s[e, rows, pl.ds(half * HALF, HALF)] for half in range(2) for e in range(2)],
+            axis=0,
+        )
+        sum_ref[pl.ds(b * 320, 320), :] = dot(back_ref[...], stacked).astype(BF16)
+
+
+def second_expert_kernel(
+    place_ref, act_ref, pre_ref, in_ref, out_ref, back_ref, mine_ref, part_s
+):
+    expert_sums(
+        place_ref[1] == 0, act_ref, pre_ref, in_ref, out_ref, back_ref, mine_ref, part_s
+    )
 
 
 def expert_grads_kernel(x_ref, s_ref, act_ref, pre_ref, in_grad_ref, out_grad_ref):
@@ -367,7 +372,7 @@
     place_ref, table_ref, x_ref, middle_ref, mixed_ref, probs_ref, route_ref, grad_ref,
     own_ref, other_ref, router_ref, gain_ref, wo_ref, ctx_ref, q_ref, k_ref, v_ref, normed_ref,
     lse_ref, tiles_ref, wq_ref, wk_ref, wv_ref, stretch_ref,
-    output_ref, middle_grad_ref, grads_ref, mine_ref, theirs_ref,
+    output_ref, middle_grad_ref, grads_ref, mine_ref, theirs_ref, gain_one_ref,
     low_s, logit_s, normed_s,
 ):
     core = place_ref[1]
@@ -410,6 +415,8 @@
     key_grad = jnp.zeros((SEQ, WIDTH), F32)
     value_grad = jnp.zeros((SEQ, WIDTH), F32)
     query_grads = [jnp.zeros((256, WIDTH), F32), jnp.zeros((256, WIDTH), F32)]
+    buckets = lax.broadcasted_iota(jnp.int32, (BUCKETS, 256), 0)
+    line_ids = [line_buckets(block, 1) for block in (-1, 0, 1)]
     bias_grad = jnp.zeros((BUCKETS, 128), F32)
     bias_lanes = lax.broadcasted_iota(jnp.int32, (BUCKETS, 128), 1)
     turn = (
@@ -446,7 +453,6 @@
                         far_high = far_high + piece
                     else:
                         near[block + 1] = near[block + 1] + piece
-        buckets = lax.broadcasted_iota(jnp.int32, (BUCKETS, 256), 0)
         by_bucket = jnp.zeros((BUCKETS, 256), F32)
         for block in range(3):
             turned = jnp.dot(
@@ -456,7 +462,7 @@
             wide = pltpu.roll(wide, 1, 1, stride=1, stride_axis=0)
             line = jnp.sum(wide, axis=0, keepdims=True)
             by_bucket = by_bucket + jnp.where(
-                buckets == line_buckets(block - 1, BUCKETS), line, 0.0
+                buckets == line_ids[block], line, 0.0
             )
         side = lax.broadcasted_iota(jnp.int32, (BUCKETS, 128), 0)
         low_line = jnp.sum(far_low, axis=0, keepdims=True)
@@ -477,12 +483,19 @@
     column = jnp.transpose(jnp.broadcast_to(gain_grad, (128, D)))
     lanes = lax.broadcasted_iota(jnp.int32, (D, 128), 1)
     grads_ref[:, D:] = jnp.where(lanes == EXPERTS, column, rest).astype(BF16)
-    normed_part = (
-        dot(query_low, wq_ref[...])
-        + dot(key_low, wk_ref[...])
-        + dot(value_low, wv_ref[...])
-    )
-    normed_s[...] = normed_part.astype(BF16)
+    gain_one = jnp.zeros((1, D), F32)
+    for i in range(4):
+        rows = slice(i * 128, i * 128 + 128)
+        normed_part = (
+            dot(query_low[rows], wq_ref[...])
+            + dot(key_low[rows], wk_ref[...])
+            + dot(value_low[rows], wv_ref[...])
+        )
+        normed_s[rows, :] = normed_part.astype(BF16)
+        hidden = x_ref[rows, :].astype(F32)
+        scale = lax.rsqrt(jnp.mean(hidden * hidden, axis=-1, keepdims=True) + EPS)
+        gain_one = gain_one + jnp.sum(normed_part * hidden * scale, axis=0, keepdims=True)
+    gain_one_ref[...] = jnp.broadcast_to(gain_one, (8, D))
     mine_ref[...] = normed_s[pl.ds(pl.multiple_of(core * 256, 256), 256), :]
     theirs_ref[...] = normed_s[pl.ds(pl.multiple_of((1 - core) * 256, 256), 256), :]
 
@@ -492,14 +505,8 @@
     return jnp.where(core == i // 2, own_ref[local, :], other_ref[local, :]).astype(F32)
 
 
-def reduce_kernel(place_ref, parts_ref, own_ref, other_ref, x_ref, send_ref):
-    core = place_ref[1]
-    gain_grad = jnp.zeros((1, D), F32)
-    for i in range(4):
-        hidden = x_ref[pl.ds(i * 128, 128), :].astype(F32)
-        scale = lax.rsqrt(jnp.mean(hidden * hidden, axis=-1, keepdims=True) + EPS)
-        normed_grad = halves(core, own_ref, other_ref, i)
-        gain_grad = gain_grad + jnp.sum(normed_grad * hidden * scale, axis=0, keepdims=True)
+def reduce_kernel(parts_ref, pair_ref, link_ref, send_ref):
+    gain_grad = (pair_ref[0:1] + pair_ref[8:9]) + (link_ref[0:1] + link_ref[8:9])
     total = jnp.zeros((24, GRADS), F32)
     for j in range(GROUPS // 2):
         pair = parts_ref[pl.ds(j * 48, 48), :].astype(F32)
@@ -620,19 +627,26 @@
     received_other = swap(received, "c")
     select = regroup_matrix()
     low = shape((2, 320, D), BF16)
-    mine, theirs, slots, slot_grads, act, pre_grad = call(
-        expert_kernel,
-        (shape((ROWS, HALF), BF16), shape((ROWS, HALF), BF16), low, low, low, low),
+    sums = shape((ROWS, HALF), BF16)
+    back_select = jnp.asarray(select.T, BF16)
+    theirs, slots, slot_grads, act, pre_grad = call(
+        first_expert_kernel,
+        (sums, low, low, low, low),
         (place, received, received_other, expert_in, expert_out,
-         jnp.asarray(select, BF16), jnp.asarray(select.T, BF16)),
-        scratch=(pltpu.VMEM((2, 320, D), BF16), pltpu.VMEM((2, 320, D), BF16)),
-        scalars=1, limit=24, flops=5_000_000_000, moved=14_000_000,
+         jnp.asarray(select, BF16), back_select),
+        scratch=(pltpu.VMEM((2, 320, D), BF16),),
+        scalars=1, limit=24, flops=4_000_000_000, moved=14_000_000,
+    )
+    mine = call(
+        second_expert_kernel, sums,
+        (place, act, pre_grad, expert_in, expert_out, back_select),
+        scratch=(pltpu.VMEM((2, 320, D), BF16),),
+        scalars=1, limit=12, flops=1_000_000_000, moved=4_000_000,
     )
     partial = (mine.astype(F32) + swap(theirs, "c").astype(F32)).astype(BF16)
     back = lax.all_to_all(
         jnp.concatenate([partial, partial], axis=0), pair_axis, 0, 0, tiled=True
     )
-    expert_in_grad, expert_out_grad = expert_grads(slots, slot_grads, act, pre_grad)
     rows_own = call(
         tokens_kernel, shape((SEQ, D), BF16), (low_back, high_back, back),
         limit=12, flops=2_000_000_000, moved=3_000_000,
@@ -640,10 +654,10 @@
     rows_other = swap(rows_own, "c")
     stretch = np.zeros((D, BUCKETS), np.float32)
     stretch[24 * np.arange(BUCKETS), np.arange(BUCKETS)] = 1
-    layer_output, middle_grad, grads, norm_mine, norm_theirs = call(
+    layer_output, middle_grad, grads, norm_mine, norm_theirs, gain_part = call(
         backward_kernel,
         (shape((SEQ, D), BF16), shape((SEQ, D), F32), shape((D, GRADS), BF16),
-         shape((256, D), BF16), shape((256, D), BF16)),
+         shape((256, D), BF16), shape((256, D), BF16), shape((8, D), F32)),
         (place, table, layer_input, middle, mixed, probs, route, out_grad,
          rows_own, rows_other, router, gain_two, output_weight, context, queries, keys,
          values, normed, lse, tiles, wq, wk, wv, jnp.asarray(stretch, BF16)),
@@ -651,20 +665,28 @@
                  pltpu.VMEM((SEQ, D), BF16)),
         scalars=1, limit=24, flops=4_000_000_000, moved=12_000_000,
     )
+    gain_pair = jnp.concatenate([gain_part, swap(gain_part, "c")], axis=0)
+    halved = (norm_mine.astype(F32) + swap(norm_theirs, "c").astype(F32)).astype(BF16)
     scattered = lax.all_to_all(grads, experts_axis, 0, 0, tiled=True)
-    halved = (norm_mine.astype(F32) + swap(norm_theirs, "c").astype(F32)).astype(BF16)
-    halved = (halved.astype(F32) + swap(halved, "l").astype(F32)).astype(BF16)
+    gain_link, halved_link = lax.optimization_barrier(
+        (swap(gain_pair, "l"), swap(halved, "l"))
+    )
+    halved = (halved.astype(F32) + halved_link.astype(F32)).astype(BF16)
     halved_other = swap(halved, "c")
     spread = call(
         reduce_kernel, shape((D, GRADS), BF16),
-        (place, scattered, halved, halved_other, layer_input),
-        scalars=1, limit=12, flops=10_000_000, moved=5_000_000,
-    )
+        (scattered, gain_pair, gain_link),
+        limit=12, flops=10_000_000, moved=3_000_000,
+    )
+    spread, slots, slot_grads, act, pre_grad = lax.optimization_barrier(
+        (spread, slots, slot_grads, act, pre_grad)
+    )
+    expert_in_grad, expert_out_grad = expert_grads(slots, slot_grads, act, pre_grad)
     gathered = lax.all_to_all(spread, experts_axis, 0, 0, tiled=True)
     input_grad = call(
         input_kernel, shape((SEQ, D), F32),
         (place, halved, halved_other, layer_input, gain_one, middle_grad),
-        scalars=1, limit=12, flops=10_000_000, moved=5_000_000,
+        alias={5: 0}, scalars=1, limit=12, flops=10_000_000, moved=5_000_000,
     )
     out = shape((WIDTH, D), F32)
     line = shape((D,), F32)

time: 187 us -> 183 us (0.979)
  waiting for transfers between devices: 47.7 us -> 44.8 us
  local copies, waits for them, and re-layouts: 10.3 us -> 7.41 us
    unnamed x80 -> x81, local copies, waits for them, and re-layouts: 10.3 us -> 6.46 us
    ppermute x12 -> x14, waiting for transfers between devices: 37.2 us -> 34 us  [swap(): return lax.ppermute(array, axis, [(0, 1), (1, 0)])]
    ppermute x12 -> x14, starting transfers between devices: 4.48 us -> 5.47 us  [swap(): return lax.ppermute(array, axis, [(0, 1), (1, 0)])]
    pallas_call x9 -> x10, Pallas kernels: 37.9 us -> 38.3 us  [call(): pl.pallas_call(body, out_shape=outs, in_specs=[pl.BlockSpec(memory_space=...]
  transfers between devices with their start and end apart: 14 -> 16, of which waited for: 9 -> 11; matrix products, arithmetic and copies ran while one was open for 1% -> 2% of each run, Pallas kernels for 8% -> 10%
where the time goes in v5:
time: 183 us; the launch traced here: 182 us
  blocking collectives  61.4 us (34%)
  waiting for transfers between devices  44.8 us (24%)
  Pallas kernels  43.8 us (24%)
  starting transfers between devices  21.6 us (12%)
  local copies, waits for them, and re-layouts  7.41 us (4%)
    pallas_call x10, Pallas kernels, call(): pl.pallas_call(body, out_shape=outs, in_specs=[pl.BlockSpec(memory_space=...  38.3 us
    ppermute x14, waiting for transfers between devices, swap(): return lax.ppermute(array, axis, [(0, 1), (1, 0)])  34 us
    all_to_all x1, blocking collectives, shards(): lax.all_to_all(jnp.concatenate([partial, partial], axis=0), pair_axis, 0,...  32 us
    all_to_all x1, blocking collectives, shards(): received = lax.all_to_all(send, experts_axis, 0, 0, tiled=True)  29.4 us
    all_to_all x1, starting transfers between devices, shards(): gathered = lax.all_to_all(spread, experts_axis, 0, 0, tiled=True)  11 us
    all_to_all x1, waiting for transfers between devices, shards(): gathered = lax.all_to_all(spread, experts_axis, 0, 0, tiled=True)  10.8 us
    unnamed x81, local copies, waits for them, and re-layouts  6.46 us
    pallas_call x1, Pallas kernels, expert_grads(): pl.pallas_call(expert_grads_kernel, grid=(2, 3), out_shape=(shape((2, D,...  5.54 us
  transfers between devices with their start and end apart: 16, of which 11 were waited for; matrix products, arithmetic and copies ran while one was open for 2% of the time, Pallas kernels for 10%

profile of v5, /device:TPU:0, one launch (start us, length us, event | category | flops | bytes accessed | tf_op | source)
XLA Modules:
  0.0 181.9 jit_solution(813465985851733627)
XLA Ops:
  0.7 1.7 collective-permute-start.4
  2.4 5.4 %shard_map.274 = (bf16[512,768]{1,0:T(8,128)(2,1)}, bf16[512,192]{1,0:T(8,128)(2,1)}, bf16[512,192]{1,0:T(8,128)(2,1)}, bf16[512,192]{1,0:T(8,128)(2,1)}, f32[9,...) custom-call(f32[3,32]{1,0:T(4,128)} %bitcast.35, bf16[512,768]{1,0:T(8,128)(2,1)} %x_ref.5, ...), custom_call_target="tpu_custom_call" | custom-call | flops 900000000 | bytes 5000000 | tf_op jit(solution)/shard_map/pallas_call | solution.py:95
  8.3 1.4 collective-permute-done.4.wo2
  10.3 1.6 shard_map.275
  14.0 2.0 %collective-permute-done.1.ctx2 = bf16[512,192]{1,0:T(8,128)(2,1)} collective-permute-done((bf16[512,192]{1,0:T(8,128)(2,1)}, bf16[512,192]{1,0:T(8,128)(2,1)}, u32[]{:S(2)}, u32[]{:S(2)}) %collective-permute-start.1) | collective-permute-done | bytes 196640 | tf_op jit(solution)/shard_map/ppermute | solution.py:577
  20.0 5.7 %shard_map.276 = (f32[512,768]{1,0:T(8,128)S(1)}, bf16[512,768]{1,0:T(8,128)(2,1)S(1)}, f32[512,128]{1,0:T(8,128)S(1)}, bf16[1280,384]{1,0:T(8,128)(2,1)S(1)}) custom-call(s32[2]{0:T(128)S(1)} %pad_add_fusion.place_ref, bf16[512,768]{1,0:T(8,128)(2,1)S(1)} %copy-done, bf16[512,192]{1,0:T(8,128)(2,1)S(1)} %copy-done.7, ...), custom_call_target="tpu_custom_call" | custom-call | flops 1700000000 | bytes 8000000 | tf_op jit(solution)/shard_map/pallas_call | solution.py:95
  25.8 29.4 %all_to_all.44 = bf16[32,40,384]{2,1,0:T(8,128)(2,1)S(1)} all-to-all(bf16[32,40,384]{2,1,0:T(8,128)(2,1)S(1)} %bitcast.28), channel_id=1, replica_groups=mesh['z'=4,'x'=4,'h'=2,'l'=2,'c'=2] {'z','x','h'}, dimensions={0} | all-to-all | bytes 1966080 | tf_op jit(solution)/shard_map/all_to_all | solution.py:626
  55.1 2.6 %collective-permute-done.6.other_ref = bf16[1280,384]{1,0:T(8,128)(2,1)S(1)} collective-permute-done((bf16[1280,384]{1,0:T(8,128)(2,1)S(1)}, bf16[1280,384]{1,0:T(8,128)(2,1)S(1)}, u32[]{:S(2)}, u32[]{:S(2)}) %collective-permute-start.6) | collective-permute-done | bytes 983072 | tf_op jit(solution)/shard_map/ppermute | solution.py:577
  57.7 5.6 %shard_map.277 = (bf16[1280,384]{1,0:T(8,128)(2,1)S(1)}, bf16[2,320,768]{2,1,0:T(8,128)(2,1)S(1)}, bf16[2,320,768]{2,1,0:T(8,128)(2,1)S(1)}, bf16[2,320,768]{2,1,0:T(8,128)(2,1)S(1)}, bf16[2,320,768]{2,1,0:T(8,128)(2,1)S(1)}) custom-call(s32[2]{0:T(128)S(1)} %pad_add_fusion.place_ref, bf16[1280,384]{1,0:T(8,128)(2,1)S(1)} %bitcast.27, ...), custom_call_target="tpu_custom_call" | custom-call | flops 4000000000 | bytes 14000000 | tf_op jit(solution)/shard_map/pallas_call | solution.py:95
  63.5 2.2 %shard_map.278 = bf16[1280,384]{1,0:T(8,128)(2,1)S(1)} custom-call(s32[2]{0:T(128)S(1)} %pad_add_fusion.place_ref, bf16[2,320,768]{2,1,0:T(8,128)(2,1)S(1)} %get-tuple-element.98.act_ref, bf16[2,320,768]{2,1,0:T(8,128)(2,1)S(1)} %get-tuple-element.99.pre_ref, bf16[2,768,768]{2,1,0:T(8,128)(2,1)S(1)} %copy-done.1, bf16[2,768,768]{2,1,0:T(8,128)(2,1)S(1)} %copy-done.2, ...), custom_call_target="tpu_custom_call" | custom-call | flops 1000000000 | bytes 4000000 | tf_op jit(solution)/shard_map/pallas_call | solution.py:95
  66.5 32.0 %all_to_all.45 = bf16[64,40,384]{2,1,0:T(8,128)(2,1)S(1)} all-to-all(bf16[64,40,384]{2,1,0:T(8,128)(2,1)S(1)} %bitcast.37), channel_id=1, replica_groups=mesh['z'=4,'x'=4,'h'=2,'l'=2,'c'=2] {'l','z','x','h'}, dimensions={0} | all-to-all | bytes 3932160 | tf_op jit(solution)/shard_map/all_to_all | solution.py:647
  98.6 1.5 shard_map.279.own_ref
  100.5 2.3 %collective-permute-done.8.other_ref = bf16[512,768]{1,0:T(8,128)(2,1)S(1)} collective-permute-done((bf16[512,768]{1,0:T(8,128)(2,1)S(1)}, bf16[512,768]{1,0:T(8,128)(2,1)S(1)}, u32[]{:S(2)}, u32[]{:S(2)}) %collective-permute-start.8) | collective-permute-done | bytes 786464 | tf_op jit(solution)/shard_map/ppermute | solution.py:577
  102.9 9.8 %shard_map.280 = (bf16[512,768]{1,0:T(8,128)(2,1)}, f32[512,768]{1,0:T(8,128)}, bf16[768,896]{1,0:T(8,128)(2,1)}, bf16[256,768]{1,0:T(8,128)(2,1)S(1)}, bf16[256...) custom-call(s32[2]{0:T(128)S(1)} %pad_add_fusion.place_ref, f32[3,32]{1,0:T(4,128)S(1)} %bitcast.36, ...), custom_call_target="tpu_custom_call" | custom-call | flops 4000000000 | bytes 12000000 | tf_op jit(solution)/shard_map/pallas_call | solution.py:95
  114.1 5.1 %all-to-all-start.2 = ((bf16[32,24,896]{2,1,0:T(8,128)(2,1)}), bf16[32,24,896]{2,1,0:T(8,128)(2,1)S(1)}, u32[]{:S(2)}, u32[]{:S(2)}) async-start(bf16[32,24,896]{2,1,0:T(8,128)(2,1)} %bitcast.14), calls=%async_computation.2 | async-start | bytes 2752512 | tf_op jit(solution)/shard_map/all_to_all | solution.py:670
  119.3 1.9 %collective-permute-done.9 = bf16[256,768]{1,0:T(8,128)(2,1)S(1)} collective-permute-done((bf16[256,768]{1,0:T(8,128)(2,1)}, bf16[256,768]{1,0:T(8,128)(2,1)S(1)}, u32[]{:S(2)}, u32[]{:S(2)}) %collective-permute-start.9) | collective-permute-done | bytes 393248 | tf_op jit(solution)/shard_map/ppermute | solution.py:577
  124.8 20.4 %collective-permute-done.11.link_ref = f32[16,768]{1,0:T(8,128)S(1)} collective-permute-done((f32[16,768]{1,0:T(8,128)S(1)}, f32[16,768]{1,0:T(8,128)S(1)}, u32[]{:S(2)}, u32[]{:S(2)}) %collective-permute-start.11) | collective-permute-done | bytes 49184 | tf_op jit(solution)/shard_map/ppermute | solution.py:577
  145.2 1.4 shard_map.282
  146.6 11.0 %all-to-all-start.3 = ((bf16[32,24,896]{2,1,0:T(8,128)(2,1)}), bf16[32,24,896]{2,1,0:T(8,128)(2,1)S(1)}, u32[]{:S(2)}, u32[]{:S(2)}) async-start(bf16[32,24,896]{2,1,0:T(8,128)(2,1)} %bitcast.16), calls=%async_computation.3 | async-start | bytes 2752512 | tf_op jit(solution)/shard_map/all_to_all | solution.py:685
  158.9 1.7 collective-permute-done.13.other_ref
  160.6 3.4 %shard_map.281 = f32[512,768]{1,0:T(8,128)} custom-call(s32[2]{0:T(128)S(1)} %pad_add_fusion.place_ref, bf16[256,768]{1,0:T(8,128)(2,1)S(1)} %add_convert_fusion.1.own_ref, bf16[256,768]{1,0:T(8,128)(2,1)S(1)} %collective-permute-done.13.other_ref, bf16[512,768]{1,0:T(8,128)(2,1)S(1)} %copy-done, ...), custom_call_target="tpu_custom_call", output_to_operand_aliasing={{}: (5, {})} | custom-call | flops 10000000 | bytes 5000000 | tf_op jit(solution)/shard_map/pallas_call | solution.py:95
  164.0 5.5 %shard_map.284 = (f32[2,768,768]{2,1,0:T(8,128)}, f32[2,768,768]{2,1,0:T(8,128)}) custom-call(bf16[2,320,768]{2,1,0:T(8,128)(2,1)S(1)} %copy-done.24, bf16[2,320,768]{2,1,0:T(8,128)(2,1)S(1)} %copy-done.26, bf16[2,320,768]{2,1,0:T(8,128)(2,1)S(1)} %get-tuple-element.98.act_ref, bf16[2,320,768]{2,1,0:T(8,128)(2,1)S(1)} %copy-done.4), custom_call_target="tpu_custom_call" | custom-call | flops 1509949440 | bytes 14000000 | tf_op jit(solution)/shard_map/pallas_call | solution.py:347
  169.5 10.8 %all-to-all-done.3 = bf16[32,24,896]{2,1,0:T(8,128)(2,1)S(1)} async-done(((bf16[32,24,896]{2,1,0:T(8,128)(2,1)}), bf16[32,24,896]{2,1,0:T(8,128)(2,1)S(1)}, u32[]{:S(2)}, u32[]{:S(2)}) %all-to-all-start.3) | async-done | bytes 1376288 | tf_op jit(solution)/shard_map/all_to_all | solution.py:685
  180.3 1.6 shard_map.283
  (114 shorter events, 14.6 us)
Async XLA Ops:
  0.6 17.3 %copy-start = (bf16[512,768]{1,0:T(8,128)(2,1)S(1)}, bf16[512,768]{1,0:T(8,128)(2,1)}, u32[]{:S(2)}) copy-start(bf16[512,768]{1,0:T(8,128)(2,1)} %x_ref.5) | copy-start | bytes 2359300
  0.7 9.1 %collective-permute-start.4 = (bf16[192,768]{1,0:T(8,128)(2,1)}, bf16[192,768]{1,0:T(8,128)(2,1)}, u32[]{:S(2)}, u32[]{:S(2)}) collective-permute-start(bf16[192,768]{1,0:T(8,128)(2,1)} %wo_ref.1), channel_id=1, source_target_pairs={{0,2},{2,0},{1,3},{3,1},{4,6},{6,4},{5,7},{7,5},{8,10},{10,8},{9,1... | collective-permute-start | bytes 884744 | tf_op jit(solution)/shard_map/ppermute | solution.py:577
  7.9 8.2 %collective-permute-start.1 = (bf16[512,192]{1,0:T(8,128)(2,1)}, bf16[512,192]{1,0:T(8,128)(2,1)}, u32[]{:S(2)}, u32[]{:S(2)}) collective-permute-start(bf16[512,192]{1,0:T(8,128)(2,1)} %get-tuple-element.57.ctx0.ctx_ref), channel_id=1, source_target_pairs={{0,2},{2,0},{1,3},{3,1},{4,6},{6,4},{5,7},{7,5},{8,10},{10,8},{9,1... | collective-permute-start | bytes 589832 | tf_op jit(solution)/shard_map/ppermute | solution.py:577
  8.3 8.7 %collective-permute-start.3 = (bf16[192,768]{1,0:T(8,128)(2,1)}, bf16[192,768]{1,0:T(8,128)(2,1)}, u32[]{:S(2)}, u32[]{:S(2)}) collective-permute-start(bf16[192,768]{1,0:T(8,128)(2,1)} %wo_ref.1), channel_id=1, source_target_pairs={{0,1},{1,0},{2,3},{3,2},{4,5},{5,4},{6,7},{7,6},{8,9},{9,8},{10,11... | collective-permute-start | bytes 884744 | tf_op jit(solution)/shard_map/ppermute | solution.py:577
  9.8 8.2 %collective-permute-start.5 = (bf16[192,768]{1,0:T(8,128)(2,1)}, bf16[192,768]{1,0:T(8,128)(2,1)}, u32[]{:S(2)}, u32[]{:S(2)}) collective-permute-start(bf16[192,768]{1,0:T(8,128)(2,1)} %collective-permute-done.4.wo2), channel_id=1, source_target_pairs={{0,1},{1,0},{2,3},{3,2},{4,5},{5,4},{6,7},{7,6},{8,9},{9,8},{10,11... | collective-permute-start | bytes 884744 | tf_op jit(solution)/shard_map/ppermute | solution.py:577
  9.8 7.3 %collective-permute-start = (bf16[512,192]{1,0:T(8,128)(2,1)}, bf16[512,192]{1,0:T(8,128)(2,1)}, u32[]{:S(2)}, u32[]{:S(2)}) collective-permute-start(bf16[512,192]{1,0:T(8,128)(2,1)} %get-tuple-element.57.ctx0.ctx_ref), channel_id=1, source_target_pairs={{0,1},{1,0},{2,3},{3,2},{4,5},{5,4},{6,7},{7,6},{8,9},{9,8},{10,11... | collective-permute-start | bytes 589832 | tf_op jit(solution)/shard_map/ppermute | solution.py:577
  16.0 1.9 %collective-permute-start.2 = (bf16[512,192]{1,0:T(8,128)(2,1)}, bf16[512,192]{1,0:T(8,128)(2,1)}, u32[]{:S(2)}, u32[]{:S(2)}) collective-permute-start(bf16[512,192]{1,0:T(8,128)(2,1)} %collective-permute-done.1.ctx2), channel_id=1, source_target_pairs={{0,1},{1,0},{2,3},{3,2},{4,5},{5,4},{6,7},{7,6},{8,9},{9,8},{10,11... | collective-permute-start | bytes 589832 | tf_op jit(solution)/shard_map/ppermute | solution.py:577
  20.0 37.7 %copy-start.1 = (bf16[2,768,768]{2,1,0:T(8,128)(2,1)S(1)}, bf16[2,768,768]{2,1,0:T(8,128)(2,1)}, u32[]{:S(2)}) copy-start(bf16[2,768,768]{2,1,0:T(8,128)(2,1)} %in_ref.3) | copy-start | bytes 7077892
  20.0 37.7 %copy-start.2 = (bf16[2,768,768]{2,1,0:T(8,128)(2,1)S(1)}, bf16[2,768,768]{2,1,0:T(8,128)(2,1)}, u32[]{:S(2)}) copy-start(bf16[2,768,768]{2,1,0:T(8,128)(2,1)} %out_ref.3) | copy-start | bytes 7077892
  25.7 32.0 %copy-start.9 = (bf16[320,320]{1,0:T(8,128)(2,1)S(1)}, bf16[320,320]{1,0:T(8,128)(2,1)}, u32[]{:S(2)}) copy-start(bf16[320,320]{1,0:T(8,128)(2,1)} %constant.20.clone.back_ref) | copy-start | bytes 614404
  25.7 32.0 %copy-start.18 = (bf16[320,320]{1,0:T(8,128)(2,1)S(1)}, bf16[320,320]{1,0:T(8,128)(2,1)}, u32[]{:S(2)}) copy-start(bf16[320,320]{1,0:T(8,128)(2,1)} %constant.21.clone.sel_ref) | copy-start | bytes 614404
  55.1 2.6 %collective-permute-start.6 = (bf16[1280,384]{1,0:T(8,128)(2,1)S(1)}, bf16[1280,384]{1,0:T(8,128)(2,1)S(1)}, u32[]{:S(2)}, u32[]{:S(2)}) collective-permute-start(bf16[1280,384]{1,0:T(8,128)(2,1)S(1)} %bitcast.26), channel_id=1, source_target_pairs={{0,1},{1,0},{2,3},{3,2},{4,5},{5,4},{6,7},{7,6},{8,9},{9,8},{10,11... | collective-permute-start | bytes 2949128 | tf_op jit(solution)/shard_map/ppermute | solution.py:577
  63.3 2.6 %collective-permute-start.7 = (bf16[1280,384]{1,0:T(8,128)(2,1)S(1)}, bf16[1280,384]{1,0:T(8,128)(2,1)S(1)}, u32[]{:S(2)}, u32[]{:S(2)}) collective-permute-start(bf16[1280,384]{1,0:T(8,128)(2,1)S(1)} %get-tuple-element.70), channel_id=1, source_target_pairs={{0,1},{1,0},{2,3},{3,2},{4,5},{5,4},{6,7},{7,6},{8,9},{9,8},{10,11... | collective-permute-start | bytes 2949128 | tf_op jit(solution)/shard_map/ppermute | solution.py:577
  66.4 32.0 %copy-start.20 = (bf16[512,1280]{1,0:T(8,128)(2,1)S(1)}, bf16[512,1280]{1,0:T(8,128)(2,1)}, u32[]{:S(2)}) copy-start(bf16[512,1280]{1,0:T(8,128)(2,1)} %copy-done.19) | copy-start | bytes 3932164
  66.5 32.0 %copy-start.22 = (bf16[512,1280]{1,0:T(8,128)(2,1)S(1)}, bf16[512,1280]{1,0:T(8,128)(2,1)}, u32[]{:S(2)}) copy-start(bf16[512,1280]{1,0:T(8,128)(2,1)} %copy-done.21) | copy-start | bytes 3932164
  100.2 2.6 %collective-permute-start.8 = (bf16[512,768]{1,0:T(8,128)(2,1)S(1)}, bf16[512,768]{1,0:T(8,128)(2,1)S(1)}, u32[]{:S(2)}, u32[]{:S(2)}) collective-permute-start(bf16[512,768]{1,0:T(8,128)(2,1)S(1)} %shard_map.279.own_ref), channel_id=1, source_target_pairs={{0,1},{1,0},{2,3},{3,2},{4,5},{5,4},{6,7},{7,6},{8,9},{9,8},{10,11... | collective-permute-start | bytes 2359304 | tf_op jit(solution)/shard_map/ppermute | solution.py:577
  114.1 31.2 %all-to-all-start.2 = ((bf16[32,24,896]{2,1,0:T(8,128)(2,1)}), bf16[32,24,896]{2,1,0:T(8,128)(2,1)S(1)}, u32[]{:S(2)}, u32[]{:S(2)}) async-start(bf16[32,24,896]{2,1,0:T(8,128)(2,1)} %bitcast.14), calls=%async_computation.2 | async-start | bytes 2752512 | tf_op jit(solution)/shard_map/all_to_all | solution.py:670
  119.2 2.0 %collective-permute-start.9 = (bf16[256,768]{1,0:T(8,128)(2,1)}, bf16[256,768]{1,0:T(8,128)(2,1)S(1)}, u32[]{:S(2)}, u32[]{:S(2)}) collective-permute-start(bf16[256,768]{1,0:T(8,128)(2,1)} %copy-done.13), channel_id=1, source_target_pairs={{0,1},{1,0},{2,3},{3,2},{4,5},{5,4},{6,7},{7,6},{8,9},{9,8},{10,11... | collective-permute-start | bytes 1179656 | tf_op jit(solution)/shard_map/ppermute | solution.py:577
  121.3 23.9 %copy-start.33 = (bf16[256,768]{1,0:T(8,128)(2,1)}, bf16[256,768]{1,0:T(8,128)(2,1)S(1)}, u32[]{:S(2)}) copy-start(bf16[256,768]{1,0:T(8,128)(2,1)S(1)} %add_convert_fusion.2) | copy-start | bytes 1179652
  121.3 23.9 %collective-permute-start.12 = (bf16[256,768]{1,0:T(8,128)(2,1)S(1)}, bf16[256,768]{1,0:T(8,128)(2,1)}, u32[]{:S(2)}, u32[]{:S(2)}) collective-permute-start(bf16[256,768]{1,0:T(8,128)(2,1)S(1)} %add_convert_fusion.2), channel_id=1, source_target_pairs={{0,2},{2,0},{1,3},{3,1},{4,6},{6,4},{5,7},{7,5},{8,10},{10,8},{9,1... | collective-permute-start | bytes 1179656 | tf_op jit(solution)/shard_map/ppermute | solution.py:577
  122.5 1.4 collective-permute-start.10
  123.9 21.3 %collective-permute-start.11 = (f32[16,768]{1,0:T(8,128)S(1)}, f32[16,768]{1,0:T(8,128)S(1)}, u32[]{:S(2)}, u32[]{:S(2)}) collective-permute-start(f32[16,768]{1,0:T(8,128)S(1)} %constant_dynamic-update-slice_fusion.pair_ref), channel_id=1, source_target_pairs={{0,2},{2,0},{1,3},{3,1},{4,6},{6,4},{5,7},{7,5},{8,10},{10,8},{9,1... | collective-permute-start | bytes 147464 | tf_op jit(solution)/shard_map/ppermute | solution.py:577
  146.6 33.7 %all-to-all-start.3 = ((bf16[32,24,896]{2,1,0:T(8,128)(2,1)}), bf16[32,24,896]{2,1,0:T(8,128)(2,1)S(1)}, u32[]{:S(2)}, u32[]{:S(2)}) async-start(bf16[32,24,896]{2,1,0:T(8,128)(2,1)} %bitcast.16), calls=%async_computation.3 | async-start | bytes 2752512 | tf_op jit(solution)/shard_map/all_to_all | solution.py:685
  158.8 1.8 collective-permute-start.13
  (32 other events, 162.4 us)

commit v6 on v5

--- a/solution.py
+++ b/solution.py
@@ -219,44 +219,57 @@
     return jnp.where(drop > 0, -1000, row)
 
 
-def place_kernel(route_ref, low_ref, high_ref, low_t_ref, high_t_ref):
+def near_kernel(
+    place_ref, route_ref, ctx0, ctx1, wo0, wo1, grad_ref, low_ref, high_ref, base_ref, raw_ref
+):
     target = row_of(route_ref[0:1, :], route_ref[1:2, :], route_ref[2:3, :])
     for i in range(4):
         rows = pl.ds(i * 320, 320)
         index = lax.broadcasted_iota(jnp.int32, (320, SEQ), 0) + 320 * i
-        low_ref[rows, :] = (index == target).astype(F32).astype(BF16)
-        high_ref[rows, :] = (index == target + 20).astype(F32).astype(BF16)
+        low = (index == target).astype(F32).astype(BF16)
+        high = (index == target + 20).astype(F32).astype(BF16)
+        low_ref[rows, :] = low
+        high_ref[rows, :] = high
+        raw = dot(low, grad_ref[:, :HALF]) + dot(high, grad_ref[:, HALF:])
+        raw_ref[rows, :] = raw.astype(BF16)
+    pair_of_heads(place_ref[1], ctx0, ctx1, wo0, wo1, base_ref)
+
+
+def pair_of_heads(core, ctx0, ctx1, wo0, wo1, sum_ref):
+    @pl.when(core == 0)
+    def _():
+        sum_ref[...] = dot(ctx0[...], wo0[...]) + dot(ctx1[...], wo1[...])
+
+    @pl.when(core == 1)
+    def _():
+        sum_ref[...] = dot(ctx1[...], wo1[...]) + dot(ctx0[...], wo0[...])
+
+
+def back_place_kernel(route_ref, low_ref, high_ref):
     columns = route_columns(route_ref).astype(jnp.int32)
     target = row_of(columns[:, 0:1], columns[:, 1:2], columns[:, 2:3])
     for i in range(4):
         rows = slice(i * 128, i * 128 + 128)
         index = lax.broadcasted_iota(jnp.int32, (128, ROWS), 1)
-        low_t_ref[rows, :] = (index == target[rows]).astype(F32).astype(BF16)
-        high_t_ref[rows, :] = (index == target[rows] + 20).astype(F32).astype(BF16)
+        low_ref[rows, :] = (index == target[rows]).astype(F32).astype(BF16)
+        high_ref[rows, :] = (index == target[rows] + 20).astype(F32).astype(BF16)
 
 
 def middle_kernel(
-    place_ref, x_ref, ctx0, ctx1, ctx2, ctx3, wo0, wo1, wo2, wo3, gain_ref, router_ref,
-    route_ref, low_ref, high_ref, grad_ref, middle_ref, mixed_ref, probs_ref, send_ref,
-    ctx_s, wo_s, rows_s,
-):
-    me = place_ref[0]
+    place_ref, x_ref, base_ref, ctx2, ctx3, wo2, wo3, gain_ref, router_ref, route_ref,
+    low_ref, high_ref, raw_ref, middle_ref, mixed_ref, probs_ref, send_ref, far_s, gate_s,
+):
     core = place_ref[1]
-    for step, (c, w) in enumerate(((ctx0, wo0), (ctx1, wo1), (ctx2, wo2), (ctx3, wo3))):
-        ctx_s[me ^ step] = c[...]
-        wo_s[me ^ step] = w[...]
     columns = route_columns(route_ref)
-    for i in range(2):
-        rows = slice(i * 256, i * 256 + 256)
-        attended = dot(ctx_s[0, rows, :], wo_s[0])
-        for t in range(1, 4):
-            attended = attended + dot(ctx_s[t, rows, :], wo_s[t])
-        middle = x_ref[rows, :].astype(F32) + attended
+    pair_of_heads(core, ctx2, ctx3, wo2, wo3, far_s)
+    for i in range(4):
+        rows = slice(i * 128, i * 128 + 128)
+        middle = x_ref[rows, :].astype(F32) + (base_ref[rows, :] + far_s[rows, :])
         scale = lax.rsqrt(jnp.mean(middle * middle, axis=-1, keepdims=True) + EPS)
         mixed = (middle * scale * gain_ref[...]).astype(BF16)
         middle_ref[rows, :] = middle
         mixed_ref[rows, :] = mixed
-        lanes = lax.broadcasted_iota(jnp.int32, (256, 128), 1)
+        lanes = lax.broadcasted_iota(jnp.int32, (128, 128), 1)
         logits = jnp.where(lanes < EXPERTS, dot_nt(mixed, router_ref[...]), -jnp.inf)
         grown = jnp.exp(logits - jnp.max(logits, axis=-1, keepdims=True))
         probs = grown / jnp.sum(grown, axis=-1, keepdims=True)
@@ -264,12 +277,27 @@
         expert = columns[rows, 0:1].astype(jnp.int32)
         chosen = jnp.sum(jnp.where(lanes == expert, probs, 0.0), axis=-1, keepdims=True)
         gate = chosen * (1.0 - columns[rows, 2:3])
-        grads = (grad_ref[rows, :].astype(F32) * gate).astype(BF16)
-        rows_s[rows, :] = jnp.where(core == 0, mixed, grads)
-    for i in range(4):
-        rows = pl.ds(i * 320, 320)
-        out = dot(low_ref[rows, :], rows_s[:, :HALF]) + dot(high_ref[rows, :], rows_s[:, HALF:])
-        send_ref[rows, :] = out.astype(BF16)
+        first = gate.astype(BF16).astype(F32)
+        second = (gate - first).astype(BF16).astype(F32)
+        third = gate - first - second
+        pieces = jnp.where(lanes == 0, first, jnp.where(lanes == 1, second, third))
+        gate_s[rows, :] = jnp.where(lanes < 3, pieces, 0.0).astype(BF16)
+
+    @pl.when(core == 0)
+    def _():
+        for i in range(4):
+            rows = pl.ds(i * 320, 320)
+            out = dot(low_ref[rows, :], mixed_ref[:, :HALF])
+            out = out + dot(high_ref[rows, :], mixed_ref[:, HALF:])
+            send_ref[rows, :] = out.astype(BF16)
+
+    @pl.when(core == 1)
+    def _():
+        for i in range(4):
+            rows = pl.ds(i * 320, 320)
+            gate = dot(low_ref[rows, :], gate_s[...]) + dot(high_ref[rows, :], gate_s[...])
+            gate = jnp.sum(gate, axis=-1, keepdims=True)
+            send_ref[rows, :] = (raw_ref[rows, :].astype(F32) * gate).astype(BF16)
 
 
 def first_expert_kernel(
@@ -369,11 +397,10 @@
 
 
 def backward_kernel(
-    place_ref, table_ref, x_ref, middle_ref, mixed_ref, probs_ref, route_ref, grad_ref,
+    place_ref, table_ref, middle_ref, mixed_ref, probs_ref, route_ref, grad_ref,
     own_ref, other_ref, router_ref, gain_ref, wo_ref, ctx_ref, q_ref, k_ref, v_ref, normed_ref,
-    lse_ref, tiles_ref, wq_ref, wk_ref, wv_ref, stretch_ref,
-    output_ref, middle_grad_ref, grads_ref, mine_ref, theirs_ref, gain_one_ref,
-    low_s, logit_s, normed_s,
+    lse_ref, tiles_ref, stretch_ref,
+    output_ref, middle_grad_ref, grads_ref, query_out, key_out, value_out, low_s, logit_s,
 ):
     core = place_ref[1]
     columns = route_columns(route_ref)
@@ -483,13 +510,23 @@
     column = jnp.transpose(jnp.broadcast_to(gain_grad, (128, D)))
     lanes = lax.broadcasted_iota(jnp.int32, (D, 128), 1)
     grads_ref[:, D:] = jnp.where(lanes == EXPERTS, column, rest).astype(BF16)
+    query_out[...] = query_low
+    key_out[...] = key_low
+    value_out[...] = value_low
+
+
+def normed_kernel(
+    place_ref, x_ref, q_ref, k_ref, v_ref, wq_ref, wk_ref, wv_ref,
+    mine_ref, theirs_ref, gain_one_ref, normed_s,
+):
+    core = place_ref[1]
     gain_one = jnp.zeros((1, D), F32)
     for i in range(4):
         rows = slice(i * 128, i * 128 + 128)
         normed_part = (
-            dot(query_low[rows], wq_ref[...])
-            + dot(key_low[rows], wk_ref[...])
-            + dot(value_low[rows], wv_ref[...])
+            dot(q_ref[rows, :], wq_ref[...])
+            + dot(k_ref[rows, :], wk_ref[...])
+            + dot(v_ref[rows, :], wv_ref[...])
         )
         normed_s[rows, :] = normed_part.astype(BF16)
         hidden = x_ref[rows, :].astype(F32)
@@ -604,30 +641,35 @@
         limit=60, flops=900_000_000, moved=5_000_000,
     )
     flat, flat_t = shape((ROWS, SEQ), BF16), shape((SEQ, ROWS), BF16)
-    low_place, high_place, low_back, high_back = call(
-        place_kernel, (flat, flat, flat_t, flat_t), (route,),
-        limit=12, flops=10_000_000, moved=5_500_000,
-    )
+    sums = shape((ROWS, HALF), BF16)
     ctx_link = swap(context, "l")
     ctx_core = swap(context, "c")
+    low_place, high_place, base, raw = call(
+        near_kernel, (flat, flat, shape((SEQ, D), F32), sums),
+        (place, route, context, ctx_core, output_weight, wo_core, out_grad),
+        scalars=1, limit=16, flops=1_500_000_000, moved=7_000_000,
+    )
     ctx_link_late, low_place = lax.optimization_barrier((ctx_link, low_place))
     ctx_far = swap(ctx_link_late, "c")
     middle, mixed, probs, send = call(
         middle_kernel,
-        (shape((SEQ, D), F32), shape((SEQ, D), BF16), shape((SEQ, 128), F32),
-         shape((ROWS, HALF), BF16)),
-        (place, layer_input, context, ctx_core, ctx_link, ctx_far,
-         output_weight, wo_core, wo_link, wo_far, gain_two, router, route, low_place, high_place,
-         out_grad),
-        scratch=(pltpu.VMEM((4, SEQ, WIDTH), BF16), pltpu.VMEM((4, WIDTH, D), BF16),
-                 pltpu.VMEM((SEQ, D), BF16)),
+        (shape((SEQ, D), F32), wide, shape((SEQ, 128), F32), sums),
+        (place, layer_input, base, ctx_link, ctx_far, wo_link, wo_far, gain_two, router, route,
+         low_place, high_place, raw),
+        scratch=(pltpu.VMEM((SEQ, D), F32), pltpu.VMEM((SEQ, 128), BF16)),
         scalars=1, limit=16, flops=1_700_000_000, moved=8_000_000,
     )
     received = lax.all_to_all(send, experts_axis, 0, 0, tiled=True)
-    received_other = swap(received, "c")
+    received, route_late = lax.optimization_barrier((received, route))
+    low_back, high_back = call(
+        back_place_kernel, (flat_t, flat_t), (route_late,),
+        limit=12, flops=10_000_000, moved=2_700_000,
+    )
+    received_other, low_back, high_back = lax.optimization_barrier(
+        (swap(received, "c"), low_back, high_back)
+    )
     select = regroup_matrix()
     low = shape((2, 320, D), BF16)
-    sums = shape((ROWS, HALF), BF16)
     back_select = jnp.asarray(select.T, BF16)
     theirs, slots, slot_grads, act, pre_grad = call(
         first_expert_kernel,
@@ -654,16 +696,21 @@
     rows_other = swap(rows_own, "c")
     stretch = np.zeros((D, BUCKETS), np.float32)
     stretch[24 * np.arange(BUCKETS), np.arange(BUCKETS)] = 1
-    layer_output, middle_grad, grads, norm_mine, norm_theirs, gain_part = call(
+    layer_output, middle_grad, grads, query_low, key_low, value_low = call(
         backward_kernel,
-        (shape((SEQ, D), BF16), shape((SEQ, D), F32), shape((D, GRADS), BF16),
-         shape((256, D), BF16), shape((256, D), BF16), shape((8, D), F32)),
-        (place, table, layer_input, middle, mixed, probs, route, out_grad,
+        (wide, shape((SEQ, D), F32), shape((D, GRADS), BF16), tall, tall, tall),
+        (place, table, middle, mixed, probs, route, out_grad,
          rows_own, rows_other, router, gain_two, output_weight, context, queries, keys,
-         values, normed, lse, tiles, wq, wk, wv, jnp.asarray(stretch, BF16)),
-        scratch=(pltpu.VMEM((SEQ, D), BF16), pltpu.VMEM((SEQ, 128), BF16),
-                 pltpu.VMEM((SEQ, D), BF16)),
+         values, normed, lse, tiles, jnp.asarray(stretch, BF16)),
+        scratch=(pltpu.VMEM((SEQ, D), BF16), pltpu.VMEM((SEQ, 128), BF16)),
         scalars=1, limit=24, flops=4_000_000_000, moved=12_000_000,
+    )
+    half = shape((256, D), BF16)
+    norm_mine, norm_theirs, gain_part = call(
+        normed_kernel, (half, half, shape((8, D), F32)),
+        (place, layer_input, query_low, key_low, value_low, wq, wk, wv),
+        scratch=(pltpu.VMEM((SEQ, D), BF16),),
+        scalars=1, limit=12, flops=500_000_000, moved=3_500_000,
     )
     gain_pair = jnp.concatenate([gain_part, swap(gain_part, "c")], axis=0)
     halved = (norm_mine.astype(F32) + swap(norm_theirs, "c").astype(F32)).astype(BF16)

time: 183 us -> 179 us (0.978)
  waiting for transfers between devices: 44.8 us -> 40.5 us
    ppermute x14, waiting for transfers between devices: 34 us -> 29.8 us  [swap(): return lax.ppermute(array, axis, [(0, 1), (1, 0)])]
    pallas_call x10 -> x12, Pallas kernels: 38.3 us -> 39.8 us  [call(): pl.pallas_call(body, out_shape=outs, in_specs=[pl.BlockSpec(memory_space=...]
  transfers between devices with their start and end apart: 16 -> 16, of which waited for: 11 -> 12; matrix products, arithmetic and copies ran while one was open for 2% -> 1% of each run, Pallas kernels for 10% -> 12%
where the time goes in v6:
time: 179 us
  blocking collectives  60.7 us (34%)
  Pallas kernels  45.4 us (25%)
  waiting for transfers between devices  40.5 us (23%)
  starting transfers between devices  20.4 us (11%)
  local copies, waits for them, and re-layouts  8.04 us (4%)
  other arithmetic  2.57 us (1%)
    pallas_call x12, Pallas kernels, call(): pl.pallas_call(body, out_shape=outs, in_specs=[pl.BlockSpec(memory_space=...  39.8 us
    all_to_all x1, blocking collectives, shards(): lax.all_to_all(jnp.concatenate([partial, partial], axis=0), pair_axis, 0,...  31.9 us
    ppermute x14, waiting for transfers between devices, swap(): return lax.ppermute(array, axis, [(0, 1), (1, 0)])  29.8 us
    all_to_all x1, blocking collectives, shards(): received = lax.all_to_all(send, experts_axis, 0, 0, tiled=True)  28.8 us
    all_to_all x1, waiting for transfers between devices, shards(): gathered = lax.all_to_all(spread, experts_axis, 0, 0, tiled=True)  10.7 us
    all_to_all x1, starting transfers between devices, shards(): gathered = lax.all_to_all(spread, experts_axis, 0, 0, tiled=True)  9.77 us
    unnamed x81, local copies, waits for them, and re-layouts  7.98 us
    pallas_call x1, Pallas kernels, expert_grads(): pl.pallas_call(expert_grads_kernel, grid=(2, 3), out_shape=(shape((2, D,...  5.54 us
  transfers between devices with their start and end apart: 16, of which 12 were waited for; matrix products, arithmetic and copies ran while one was open for 1% of the time, Pallas kernels for 12%

profile of v6, /device:TPU:0, one launch (start us, length us, event | category | flops | bytes accessed | tf_op | source)
XLA Modules:
  0.0 178.7 jit_solution(3341372854018073570)
XLA Ops:
  0.7 1.7 collective-permute-start.4
  2.4 5.4 %shard_map.274 = (bf16[512,768]{1,0:T(8,128)(2,1)}, bf16[512,192]{1,0:T(8,128)(2,1)}, bf16[512,192]{1,0:T(8,128)(2,1)}, bf16[512,192]{1,0:T(8,128)(2,1)}, f32[9,...) custom-call(f32[3,32]{1,0:T(4,128)} %bitcast.35, bf16[512,768]{1,0:T(8,128)(2,1)} %x_ref.5, ...), custom_call_target="tpu_custom_call" | custom-call | flops 900000000 | bytes 5000000 | tf_op jit(solution)/shard_map/pallas_call | solution.py:95
  10.8 2.6 %shard_map.275 = (bf16[1280,512]{1,0:T(8,128)(2,1)S(1)}, bf16[1280,512]{1,0:T(8,128)(2,1)S(1)}, f32[512,768]{1,0:T(8,128)S(1)}, bf16[1280,384]{1,0:T(8,128)(2,1)S(1)}) custom-call(s32[2]{0:T(128)S(1)} %pad_add_fusion.place_ref, s32[8,512]{1,0:T(8,128)S(1)} %stack.31.route_ref, bf16[512,192]{1,0:T(8,128)(2,1)S(1)} %copy-done.20, ...), custom_call_target="tpu_custom_call" | custom-call | flops 1500000000 | bytes 7000000 | tf_op jit(solution)/shard_map/pallas_call | solution.py:95
  13.4 3.5 %collective-permute-done.2.ctx2 = bf16[512,192]{1,0:T(8,128)(2,1)S(1)} collective-permute-done((bf16[512,192]{1,0:T(8,128)(2,1)}, bf16[512,192]{1,0:T(8,128)(2,1)S(1)}, u32[]{:S(2)}, u32[]{:S(2)}) %collective-permute-start.2) | collective-permute-done | bytes 196640 | tf_op jit(solution)/shard_map/ppermute | solution.py:614
  17.0 1.5 collective-permute-done.3.ctx3
  18.5 3.9 %shard_map.276 = (f32[512,768]{1,0:T(8,128)S(1)}, bf16[512,768]{1,0:T(8,128)(2,1)S(1)}, f32[512,128]{1,0:T(8,128)S(1)}, bf16[1280,384]{1,0:T(8,128)(2,1)S(1)}) custom-call(s32[2]{0:T(128)S(1)} %pad_add_fusion.place_ref, bf16[512,768]{1,0:T(8,128)(2,1)S(1)} %copy-done, f32[512,768]{1,0:T(8,128)S(1)} %get-tuple-element.68.base_ref, ...), custom_call_target="tpu_custom_call" | custom-call | flops 1700000000 | bytes 8000000 | tf_op jit(solution)/shard_map/pallas_call | solution.py:95
  22.5 28.8 %all_to_all.45 = bf16[32,40,384]{2,1,0:T(8,128)(2,1)S(1)} all-to-all(bf16[32,40,384]{2,1,0:T(8,128)(2,1)S(1)} %bitcast.28), channel_id=1, replica_groups=mesh['z'=4,'x'=4,'h'=2,'l'=2,'c'=2] {'z','x','h'}, dimensions={0} | all-to-all | bytes 1966080 | tf_op jit(solution)/shard_map/all_to_all | solution.py:662
  52.2 1.7 collective-permute-done.6.other_ref
  53.9 5.6 %shard_map.278 = (bf16[1280,384]{1,0:T(8,128)(2,1)S(1)}, bf16[2,320,768]{2,1,0:T(8,128)(2,1)S(1)}, bf16[2,320,768]{2,1,0:T(8,128)(2,1)S(1)}, bf16[2,320,768]{2,1,0:T(8,128)(2,1)S(1)}, bf16[2,320,768]{2,1,0:T(8,128)(2,1)S(1)}) custom-call(s32[2]{0:T(128)S(1)} %pad_add_fusion.place_ref, bf16[1280,384]{1,0:T(8,128)(2,1)S(1)} %bitcast.27, ...), custom_call_target="tpu_custom_call" | custom-call | flops 4000000000 | bytes 14000000 | tf_op jit(solution)/shard_map/pallas_call | solution.py:95
  59.7 2.2 %shard_map.279 = bf16[1280,384]{1,0:T(8,128)(2,1)S(1)} custom-call(s32[2]{0:T(128)S(1)} %pad_add_fusion.place_ref, bf16[2,320,768]{2,1,0:T(8,128)(2,1)S(1)} %get-tuple-element.118.act_ref, bf16[2,320,768]{2,1,0:T(8,128)(2,1)S(1)} %get-tuple-element.119.pre_ref, bf16[2,768,768]{2,1,0:T(8,128)(2,1)S(1)} %copy-done.1, bf16[2,768,768]{2,1,0:T(8,128)(2,1)S(1)} %copy-done.2, ...), custom_call_target="tpu_custom_call" | custom-call | flops 1000000000 | bytes 4000000 | tf_op jit(solution)/shard_map/pallas_call | solution.py:95
  62.6 31.9 %all_to_all.46 = bf16[64,40,384]{2,1,0:T(8,128)(2,1)S(1)} all-to-all(bf16[64,40,384]{2,1,0:T(8,128)(2,1)S(1)} %bitcast.37), channel_id=1, replica_groups=mesh['z'=4,'x'=4,'h'=2,'l'=2,'c'=2] {'l','z','x','h'}, dimensions={0} | all-to-all | bytes 3932160 | tf_op jit(solution)/shard_map/all_to_all | solution.py:689
  94.7 1.6 shard_map.280.own_ref
  96.5 2.3 %collective-permute-done.8.other_ref = bf16[512,768]{1,0:T(8,128)(2,1)S(1)} collective-permute-done((bf16[512,768]{1,0:T(8,128)(2,1)S(1)}, bf16[512,768]{1,0:T(8,128)(2,1)S(1)}, u32[]{:S(2)}, u32[]{:S(2)}) %collective-permute-start.8) | collective-permute-done | bytes 786464 | tf_op jit(solution)/shard_map/ppermute | solution.py:614
  98.9 9.8 %shard_map.281 = (bf16[512,768]{1,0:T(8,128)(2,1)}, f32[512,768]{1,0:T(8,128)}, bf16[768,896]{1,0:T(8,128)(2,1)}, bf16[512,192]{1,0:T(8,128)(2,1)S(1)}, bf16[512...) custom-call(s32[2]{0:T(128)S(1)} %pad_add_fusion.place_ref, f32[3,32]{1,0:T(4,128)S(1)} %bitcast.36, ...), custom_call_target="tpu_custom_call" | custom-call | flops 4000000000 | bytes 12000000 | tf_op jit(solution)/shard_map/pallas_call | solution.py:95
  110.8 5.3 %all-to-all-start.2 = ((bf16[32,24,896]{2,1,0:T(8,128)(2,1)}), bf16[32,24,896]{2,1,0:T(8,128)(2,1)S(1)}, u32[]{:S(2)}, u32[]{:S(2)}) async-start(bf16[32,24,896]{2,1,0:T(8,128)(2,1)} %bitcast.14), calls=%async_computation.2 | async-start | bytes 2752512 | tf_op jit(solution)/shard_map/all_to_all | solution.py:717
  120.8 1.4 shard_map.282
  122.3 1.7 collective-permute-done.9
  128.1 15.2 %collective-permute-done.11.link_ref = f32[16,768]{1,0:T(8,128)S(1)} collective-permute-done((f32[16,768]{1,0:T(8,128)S(1)}, f32[16,768]{1,0:T(8,128)S(1)}, u32[]{:S(2)}, u32[]{:S(2)}) %collective-permute-start.11) | collective-permute-done | bytes 49184 | tf_op jit(solution)/shard_map/ppermute | solution.py:614
  144.7 9.8 %all-to-all-start.3 = ((bf16[32,24,896]{2,1,0:T(8,128)(2,1)}), bf16[32,24,896]{2,1,0:T(8,128)(2,1)S(1)}, u32[]{:S(2)}, u32[]{:S(2)}) async-start(bf16[32,24,896]{2,1,0:T(8,128)(2,1)} %bitcast.16), calls=%async_computation.3 | async-start | bytes 2752512 | tf_op jit(solution)/shard_map/all_to_all | solution.py:732
  155.8 1.7 collective-permute-done.13.other_ref
  157.5 3.4 %shard_map.283 = f32[512,768]{1,0:T(8,128)} custom-call(s32[2]{0:T(128)S(1)} %pad_add_fusion.place_ref, bf16[256,768]{1,0:T(8,128)(2,1)S(1)} %add_convert_fusion.1.own_ref, bf16[256,768]{1,0:T(8,128)(2,1)S(1)} %collective-permute-done.13.other_ref, bf16[512,768]{1,0:T(8,128)(2,1)S(1)} %copy-done, ...), custom_call_target="tpu_custom_call", output_to_operand_aliasing={{}: (5, {})} | custom-call | flops 10000000 | bytes 5000000 | tf_op jit(solution)/shard_map/pallas_call | solution.py:95
  160.9 5.5 %shard_map.286 = (f32[2,768,768]{2,1,0:T(8,128)}, f32[2,768,768]{2,1,0:T(8,128)}) custom-call(bf16[2,320,768]{2,1,0:T(8,128)(2,1)S(1)} %copy-done.25, bf16[2,320,768]{2,1,0:T(8,128)(2,1)S(1)} %copy-done.27, bf16[2,320,768]{2,1,0:T(8,128)(2,1)S(1)} %get-tuple-element.118.act_ref, bf16[2,320,768]{2,1,0:T(8,128)(2,1)S(1)} %copy-done.4), custom_call_target="tpu_custom_call" | custom-call | flops 1509949440 | bytes 14000000 | tf_op jit(solution)/shard_map/pallas_call | solution.py:375
  166.4 10.7 %all-to-all-done.3 = bf16[32,24,896]{2,1,0:T(8,128)(2,1)S(1)} async-done(((bf16[32,24,896]{2,1,0:T(8,128)(2,1)}), bf16[32,24,896]{2,1,0:T(8,128)(2,1)S(1)}, u32[]{:S(2)}, u32[]{:S(2)}) %all-to-all-start.3) | async-done | bytes 1376288 | tf_op jit(solution)/shard_map/all_to_all | solution.py:732
  177.1 1.6 shard_map.285
  (116 shorter events, 18.8 us)
Async XLA Ops:
  0.6 9.2 %copy-start.19 = (bf16[192,768]{1,0:T(8,128)(2,1)S(1)}, bf16[192,768]{1,0:T(8,128)(2,1)}, u32[]{:S(2)}) copy-start(bf16[192,768]{1,0:T(8,128)(2,1)} %wo_ref.1) | copy-start | bytes 884740
  0.7 9.0 %collective-permute-start.4 = (bf16[192,768]{1,0:T(8,128)(2,1)}, bf16[192,768]{1,0:T(8,128)(2,1)S(1)}, u32[]{:S(2)}, u32[]{:S(2)}) collective-permute-start(bf16[192,768]{1,0:T(8,128)(2,1)} %wo_ref.1), channel_id=1, source_target_pairs={{0,2},{2,0},{1,3},{3,1},{4,6},{6,4},{5,7},{7,5},{8,10},{10,8},{9,1... | collective-permute-start | bytes 884744 | tf_op jit(solution)/shard_map/ppermute | solution.py:614
  2.4 7.4 %collective-permute-start.1 = (bf16[192,768]{1,0:T(8,128)(2,1)}, bf16[192,768]{1,0:T(8,128)(2,1)S(1)}, u32[]{:S(2)}, u32[]{:S(2)}) collective-permute-start(bf16[192,768]{1,0:T(8,128)(2,1)} %wo_ref.1), channel_id=1, source_target_pairs={{0,1},{1,0},{2,3},{3,2},{4,5},{5,4},{6,7},{7,6},{8,9},{9,8},{10,11... | collective-permute-start | bytes 884744 | tf_op jit(solution)/shard_map/ppermute | solution.py:614
  7.9 2.0 %collective-permute-start = (bf16[512,192]{1,0:T(8,128)(2,1)}, bf16[512,192]{1,0:T(8,128)(2,1)S(1)}, u32[]{:S(2)}, u32[]{:S(2)}) collective-permute-start(bf16[512,192]{1,0:T(8,128)(2,1)} %get-tuple-element.67.ctx0.ctx_ref), channel_id=1, source_target_pairs={{0,1},{1,0},{2,3},{3,2},{4,5},{5,4},{6,7},{7,6},{8,9},{9,8},{10,11... | collective-permute-start | bytes 589832 | tf_op jit(solution)/shard_map/ppermute | solution.py:614
  8.5 8.5 %collective-permute-start.2 = (bf16[512,192]{1,0:T(8,128)(2,1)}, bf16[512,192]{1,0:T(8,128)(2,1)S(1)}, u32[]{:S(2)}, u32[]{:S(2)}) collective-permute-start(bf16[512,192]{1,0:T(8,128)(2,1)} %get-tuple-element.67.ctx0.ctx_ref), channel_id=1, source_target_pairs={{0,2},{2,0},{1,3},{3,1},{4,6},{6,4},{5,7},{7,5},{8,10},{10,8},{9,1... | collective-permute-start | bytes 589832 | tf_op jit(solution)/shard_map/ppermute | solution.py:614
  9.0 9.5 %copy-start = (bf16[512,768]{1,0:T(8,128)(2,1)S(1)}, bf16[512,768]{1,0:T(8,128)(2,1)}, u32[]{:S(2)}) copy-start(bf16[512,768]{1,0:T(8,128)(2,1)} %x_ref.5) | copy-start | bytes 2359300
  9.7 8.9 %collective-permute-start.5 = (bf16[192,768]{1,0:T(8,128)(2,1)S(1)}, bf16[192,768]{1,0:T(8,128)(2,1)S(1)}, u32[]{:S(2)}, u32[]{:S(2)}) collective-permute-start(bf16[192,768]{1,0:T(8,128)(2,1)S(1)} %collective-permute-done.4.wo2), channel_id=1, source_target_pairs={{0,1},{1,0},{2,3},{3,2},{4,5},{5,4},{6,7},{7,6},{8,9},{9,8},{10,11... | collective-permute-start | bytes 884744 | tf_op jit(solution)/shard_map/ppermute | solution.py:614
  17.0 1.5 collective-permute-start.3
  18.5 35.3 %copy-start.1 = (bf16[2,768,768]{2,1,0:T(8,128)(2,1)S(1)}, bf16[2,768,768]{2,1,0:T(8,128)(2,1)}, u32[]{:S(2)}) copy-start(bf16[2,768,768]{2,1,0:T(8,128)(2,1)} %in_ref.3) | copy-start | bytes 7077892
  18.5 35.3 %copy-start.2 = (bf16[2,768,768]{2,1,0:T(8,128)(2,1)S(1)}, bf16[2,768,768]{2,1,0:T(8,128)(2,1)}, u32[]{:S(2)}) copy-start(bf16[2,768,768]{2,1,0:T(8,128)(2,1)} %out_ref.3) | copy-start | bytes 7077892
  22.5 31.4 %copy-start.14 = (bf16[320,320]{1,0:T(8,128)(2,1)S(1)}, bf16[320,320]{1,0:T(8,128)(2,1)}, u32[]{:S(2)}) copy-start(bf16[320,320]{1,0:T(8,128)(2,1)} %constant.20.clone.back_ref) | copy-start | bytes 614404
  22.5 31.4 %copy-start.23 = (bf16[320,320]{1,0:T(8,128)(2,1)S(1)}, bf16[320,320]{1,0:T(8,128)(2,1)}, u32[]{:S(2)}) copy-start(bf16[320,320]{1,0:T(8,128)(2,1)} %constant.21.clone.sel_ref) | copy-start | bytes 614404
  51.3 2.6 %collective-permute-start.6 = (bf16[1280,384]{1,0:T(8,128)(2,1)S(1)}, bf16[1280,384]{1,0:T(8,128)(2,1)S(1)}, u32[]{:S(2)}, u32[]{:S(2)}) collective-permute-start(bf16[1280,384]{1,0:T(8,128)(2,1)S(1)} %bitcast.26), channel_id=1, source_target_pairs={{0,1},{1,0},{2,3},{3,2},{4,5},{5,4},{6,7},{7,6},{8,9},{9,8},{10,11... | collective-permute-start | bytes 2949128 | tf_op jit(solution)/shard_map/ppermute | solution.py:614
  59.5 2.6 %collective-permute-start.7 = (bf16[1280,384]{1,0:T(8,128)(2,1)S(1)}, bf16[1280,384]{1,0:T(8,128)(2,1)S(1)}, u32[]{:S(2)}, u32[]{:S(2)}) collective-permute-start(bf16[1280,384]{1,0:T(8,128)(2,1)S(1)} %get-tuple-element.87), channel_id=1, source_target_pairs={{0,1},{1,0},{2,3},{3,2},{4,5},{5,4},{6,7},{7,6},{8,9},{9,8},{10,11... | collective-permute-start | bytes 2949128 | tf_op jit(solution)/shard_map/ppermute | solution.py:614
  96.2 2.6 %collective-permute-start.8 = (bf16[512,768]{1,0:T(8,128)(2,1)S(1)}, bf16[512,768]{1,0:T(8,128)(2,1)S(1)}, u32[]{:S(2)}, u32[]{:S(2)}) collective-permute-start(bf16[512,768]{1,0:T(8,128)(2,1)S(1)} %shard_map.280.own_ref), channel_id=1, source_target_pairs={{0,1},{1,0},{2,3},{3,2},{4,5},{5,4},{6,7},{7,6},{8,9},{9,8},{10,11... | collective-permute-start | bytes 2359304 | tf_op jit(solution)/shard_map/ppermute | solution.py:614
  110.8 32.5 %all-to-all-start.2 = ((bf16[32,24,896]{2,1,0:T(8,128)(2,1)}), bf16[32,24,896]{2,1,0:T(8,128)(2,1)S(1)}, u32[]{:S(2)}, u32[]{:S(2)}) async-start(bf16[32,24,896]{2,1,0:T(8,128)(2,1)} %bitcast.14), calls=%async_computation.2 | async-start | bytes 2752512 | tf_op jit(solution)/shard_map/all_to_all | solution.py:717
  122.2 1.8 %collective-permute-start.9 = (bf16[256,768]{1,0:T(8,128)(2,1)S(1)}, bf16[256,768]{1,0:T(8,128)(2,1)S(1)}, u32[]{:S(2)}, u32[]{:S(2)}) collective-permute-start(bf16[256,768]{1,0:T(8,128)(2,1)S(1)} %get-tuple-element.99), channel_id=1, source_target_pairs={{0,1},{1,0},{2,3},{3,2},{4,5},{5,4},{6,7},{7,6},{8,9},{9,8},{10,11... | collective-permute-start | bytes 1179656 | tf_op jit(solution)/shard_map/ppermute | solution.py:614
  124.9 18.4 %collective-permute-start.12 = (bf16[256,768]{1,0:T(8,128)(2,1)}, bf16[256,768]{1,0:T(8,128)(2,1)}, u32[]{:S(2)}, u32[]{:S(2)}) collective-permute-start(bf16[256,768]{1,0:T(8,128)(2,1)} %add_convert_fusion.2), channel_id=1, source_target_pairs={{0,2},{2,0},{1,3},{3,1},{4,6},{6,4},{5,7},{7,5},{8,10},{10,8},{9,1... | collective-permute-start | bytes 1179656 | tf_op jit(solution)/shard_map/ppermute | solution.py:614
  125.9 1.2 collective-permute-start.10
  127.1 16.1 %collective-permute-start.11 = (f32[16,768]{1,0:T(8,128)S(1)}, f32[16,768]{1,0:T(8,128)S(1)}, u32[]{:S(2)}, u32[]{:S(2)}) collective-permute-start(f32[16,768]{1,0:T(8,128)S(1)} %constant_dynamic-update-slice_fusion.pair_ref), channel_id=1, source_target_pairs={{0,2},{2,0},{1,3},{3,1},{4,6},{6,4},{5,7},{7,5},{8,10},{10,8},{9,1... | collective-permute-start | bytes 147464 | tf_op jit(solution)/shard_map/ppermute | solution.py:614
  144.7 11.1 %copy-start.36 = (f32[768]{0:T(1024)S(1)}, f32[768]{0:T(1024)}, u32[]{:S(2)}) copy-start(f32[768]{0:T(1024)} %gain_hbm.1) | copy-start | bytes 9220
  144.7 32.4 %all-to-all-start.3 = ((bf16[32,24,896]{2,1,0:T(8,128)(2,1)}), bf16[32,24,896]{2,1,0:T(8,128)(2,1)S(1)}, u32[]{:S(2)}, u32[]{:S(2)}) async-start(bf16[32,24,896]{2,1,0:T(8,128)(2,1)} %bitcast.16), calls=%async_computation.3 | async-start | bytes 2752512 | tf_op jit(solution)/shard_map/all_to_all | solution.py:732
  155.7 1.8 %collective-permute-start.13 = (bf16[256,768]{1,0:T(8,128)(2,1)S(1)}, bf16[256,768]{1,0:T(8,128)(2,1)S(1)}, u32[]{:S(2)}, u32[]{:S(2)}) collective-permute-start(bf16[256,768]{1,0:T(8,128)(2,1)S(1)} %add_convert_fusion.1.own_ref), channel_id=1, source_target_pairs={{0,1},{1,0},{2,3},{3,2},{4,5},{5,4},{6,7},{7,6},{8,9},{9,8},{10,11... | collective-permute-start | bytes 1179656 | tf_op jit(solution)/shard_map/ppermute | solution.py:614
  160.9 16.2 %copy-start.16 = (bf16[768,32]{1,0:T(8,128)(2,1)S(1)}, bf16[768,32]{1,0:T(8,128)(2,1)}, u32[]{:S(2)}) copy-start(bf16[768,32]{1,0:T(8,128)(2,1)} %constant.22.clone.stretch_ref) | copy-start | bytes 147460
  (32 other events, 121.2 us)

commit v7 on v6

--- a/solution.py
+++ b/solution.py
@@ -176,8 +176,8 @@
     loads[1].wait()
     loads[5].wait()
     gain = gain_ref[...].reshape(1, D)
-    for i in range(4):
-        rows = pl.ds(i * 128, 128)
+    for i in range(SEQ // 32):
+        rows = pl.ds(i * 32, 32)
         x = x_ref[rows, :].astype(F32)
         scale = lax.rsqrt(jnp.mean(x * x, axis=-1, keepdims=True) + EPS)
         normed_ref[rows, :] = (x * scale * gain).astype(BF16)
@@ -262,15 +262,17 @@
     core = place_ref[1]
     columns = route_columns(route_ref)
     pair_of_heads(core, ctx2, ctx3, wo2, wo3, far_s)
+    for i in range(SEQ // 32):
+        rows = slice(i * 32, i * 32 + 32)
+        middle = x_ref[rows, :].astype(F32) + (base_ref[rows, :] + far_s[rows, :])
+        scale = lax.rsqrt(jnp.mean(middle * middle, axis=-1, keepdims=True) + EPS)
+        middle_ref[rows, :] = middle
+        mixed_ref[rows, :] = (middle * scale * gain_ref[...]).astype(BF16)
     for i in range(4):
         rows = slice(i * 128, i * 128 + 128)
-        middle = x_ref[rows, :].astype(F32) + (base_ref[rows, :] + far_s[rows, :])
-        scale = lax.rsqrt(jnp.mean(middle * middle, axis=-1, keepdims=True) + EPS)
-        mixed = (middle * scale * gain_ref[...]).astype(BF16)
-        middle_ref[rows, :] = middle
-        mixed_ref[rows, :] = mixed
         lanes = lax.broadcasted_iota(jnp.int32, (128, 128), 1)
-        logits = jnp.where(lanes < EXPERTS, dot_nt(mixed, router_ref[...]), -jnp.inf)
+        logits = dot_nt(mixed_ref[rows, :], router_ref[...])
+        logits = jnp.where(lanes < EXPERTS, logits, -jnp.inf)
         grown = jnp.exp(logits - jnp.max(logits, axis=-1, keepdims=True))
         probs = grown / jnp.sum(grown, axis=-1, keepdims=True)
         probs_ref[rows, :] = probs
@@ -397,40 +399,52 @@
 
 
 def backward_kernel(
-    place_ref, table_ref, middle_ref, mixed_ref, probs_ref, route_ref, grad_ref,
+    place_ref, x_ref, table_ref, middle_ref, mixed_ref, probs_ref, route_ref, grad_ref,
     own_ref, other_ref, router_ref, gain_ref, wo_ref, ctx_ref, q_ref, k_ref, v_ref, normed_ref,
-    lse_ref, tiles_ref, stretch_ref,
-    output_ref, middle_grad_ref, grads_ref, query_out, key_out, value_out, low_s, logit_s,
+    lse_ref, tiles_ref, wq_ref, wk_ref, wv_ref, stretch_ref,
+    output_hbm, middle_grad_hbm, grads_ref, mine_ref, theirs_ref,
+    low_s, logit_s, normed_s, wide_s, output_ref, middle_grad_ref, sems,
 ):
     core = place_ref[1]
     columns = route_columns(route_ref)
     gain = gain_ref[...]
-    gain_grad = jnp.zeros((1, D), F32)
-    for i in range(4):
-        rows = slice(i * 128, i * 128 + 128)
-        own = own_ref[rows, :]
-        other = other_ref[rows, :]
-        expert_rows = jnp.where(core == 0, own, other).astype(F32)
-        mixed_grad = jnp.where(core == 0, other, own).astype(F32)
+    for i in range(SEQ // 32):
+        rows = slice(i * 32, i * 32 + 32)
+        expert_rows = jnp.where(core == 0, own_ref[rows, :], other_ref[rows, :]).astype(F32)
         probs = probs_ref[rows, :]
         kept = 1.0 - columns[rows, 2:3]
-        lanes = lax.broadcasted_iota(jnp.int32, (128, 128), 1)
+        lanes = lax.broadcasted_iota(jnp.int32, (32, 128), 1)
         hot = (lanes == columns[rows, 0:1].astype(jnp.int32)).astype(F32)
         chosen = jnp.sum(probs * hot, axis=-1, keepdims=True)
+        upstream = grad_ref[rows, :].astype(F32)
+        output_ref[rows, :] = (
+            middle_ref[rows, :] + (chosen * kept) * expert_rows
+        ).astype(BF16)
+        gate_grad = jnp.sum(upstream * expert_rows, axis=-1, keepdims=True) * kept
+        logit_s[rows, :] = (probs * (hot - chosen) * gate_grad).astype(BF16)
+    output_copy = pltpu.make_async_copy(output_ref, output_hbm, sems.at[0])
+    output_copy.start()
+    wide_s[...] = dot(logit_s[...], router_ref[...])
+    gain_grad = jnp.zeros((8, D), F32)
+    for i in range(SEQ // 32):
+        rows = slice(i * 32, i * 32 + 32)
+        mixed_grad = jnp.where(core == 0, other_ref[rows, :], own_ref[rows, :]).astype(F32)
+        mixed_grad = mixed_grad + wide_s[rows, :]
         middle = middle_ref[rows, :]
-        upstream = grad_ref[rows, :].astype(F32)
-        output_ref[rows, :] = (middle + (chosen * kept) * expert_rows).astype(BF16)
-        gate_grad = jnp.sum(upstream * expert_rows, axis=-1, keepdims=True) * kept
-        logit_grad = (probs * (hot - chosen) * gate_grad).astype(BF16)
-        logit_s[rows, :] = logit_grad
-        mixed_grad = mixed_grad + dot(logit_grad, router_ref[...])
         scale = lax.rsqrt(jnp.mean(middle * middle, axis=-1, keepdims=True) + EPS)
-        weighted = mixed_grad * gain
-        inner = jnp.mean(weighted * middle, axis=-1, keepdims=True)
-        gain_grad = gain_grad + jnp.sum(mixed_grad * middle * scale, axis=0, keepdims=True)
-        middle_grad = upstream + scale * weighted - middle * (scale * scale * scale * inner)
+        along = mixed_grad * middle
+        inner = jnp.mean(along * gain, axis=-1, keepdims=True)
+        gain_grad = gain_grad + jnp.sum((along * scale).reshape(4, 8, D), axis=0)
+        middle_grad = (
+            grad_ref[rows, :].astype(F32)
+            + scale * (mixed_grad * gain)
+            - middle * (scale * scale * scale * inner)
+        )
         middle_grad_ref[rows, :] = middle_grad
         low_s[rows, :] = middle_grad.astype(BF16)
+    gain_grad = jnp.sum(gain_grad, axis=0, keepdims=True)
+    middle_copy = pltpu.make_async_copy(middle_grad_ref, middle_grad_hbm, sems.at[1])
+    middle_copy.start()
     middle_low = low_s[...]
     grads_ref[pl.ds(3 * WIDTH, WIDTH), :D] = dot_tn(ctx_ref[...], middle_low).astype(BF16)
     ctx_grad = dot_nt(middle_low, wo_ref[...]).astype(BF16)
@@ -510,31 +524,23 @@
     column = jnp.transpose(jnp.broadcast_to(gain_grad, (128, D)))
     lanes = lax.broadcasted_iota(jnp.int32, (D, 128), 1)
     grads_ref[:, D:] = jnp.where(lanes == EXPERTS, column, rest).astype(BF16)
-    query_out[...] = query_low
-    key_out[...] = key_low
-    value_out[...] = value_low
-
-
-def normed_kernel(
-    place_ref, x_ref, q_ref, k_ref, v_ref, wq_ref, wk_ref, wv_ref,
-    mine_ref, theirs_ref, gain_one_ref, normed_s,
-):
-    core = place_ref[1]
-    gain_one = jnp.zeros((1, D), F32)
-    for i in range(4):
-        rows = slice(i * 128, i * 128 + 128)
-        normed_part = (
-            dot(q_ref[rows, :], wq_ref[...])
-            + dot(k_ref[rows, :], wk_ref[...])
-            + dot(v_ref[rows, :], wv_ref[...])
-        )
+    wide_s[...] = (
+        dot(query_low, wq_ref[...]) + dot(key_low, wk_ref[...]) + dot(value_low, wv_ref[...])
+    )
+    gain_one = jnp.zeros((8, D), F32)
+    for i in range(SEQ // 32):
+        rows = slice(i * 32, i * 32 + 32)
+        normed_part = wide_s[rows, :]
         normed_s[rows, :] = normed_part.astype(BF16)
         hidden = x_ref[rows, :].astype(F32)
         scale = lax.rsqrt(jnp.mean(hidden * hidden, axis=-1, keepdims=True) + EPS)
-        gain_one = gain_one + jnp.sum(normed_part * hidden * scale, axis=0, keepdims=True)
-    gain_one_ref[...] = jnp.broadcast_to(gain_one, (8, D))
-    mine_ref[...] = normed_s[pl.ds(pl.multiple_of(core * 256, 256), 256), :]
-    theirs_ref[...] = normed_s[pl.ds(pl.multiple_of((1 - core) * 256, 256), 256), :]
+        gain_one = gain_one + jnp.sum((normed_part * hidden * scale).reshape(4, 8, D), axis=0)
+    gain_rows = jnp.broadcast_to(jnp.sum(gain_one, axis=0, keepdims=True), (16, D)).astype(BF16)
+    for out, start in ((mine_ref, core * 256), (theirs_ref, (1 - core) * 256)):
+        out[:256, :] = normed_s[pl.ds(pl.multiple_of(start, 256), 256), :]
+        out[256:, :] = gain_rows
+    output_copy.wait()
+    middle_copy.wait()
 
 
 def halves(core, own_ref, other_ref, i):
@@ -542,8 +548,9 @@
     return jnp.where(core == i // 2, own_ref[local, :], other_ref[local, :]).astype(F32)
 
 
-def reduce_kernel(parts_ref, pair_ref, link_ref, send_ref):
-    gain_grad = (pair_ref[0:1] + pair_ref[8:9]) + (link_ref[0:1] + link_ref[8:9])
+def reduce_kernel(parts_ref, halved_ref, link_ref, send_ref):
+    extra = pl.ds(256, 16)
+    gain_grad = (halved_ref[extra, :].astype(F32) + link_ref[extra, :].astype(F32))[0:1]
     total = jnp.zeros((24, GRADS), F32)
     for j in range(GROUPS // 2):
         pair = parts_ref[pl.ds(j * 48, 48), :].astype(F32)
@@ -696,33 +703,28 @@
     rows_other = swap(rows_own, "c")
     stretch = np.zeros((D, BUCKETS), np.float32)
     stretch[24 * np.arange(BUCKETS), np.arange(BUCKETS)] = 1
-    layer_output, middle_grad, grads, query_low, key_low, value_low = call(
+    half = shape((256 + 16, D), BF16)
+    layer_output, middle_grad, grads, norm_mine, norm_theirs = call(
         backward_kernel,
-        (wide, shape((SEQ, D), F32), shape((D, GRADS), BF16), tall, tall, tall),
-        (place, table, middle, mixed, probs, route, out_grad,
+        (wide, shape((SEQ, D), F32), shape((D, GRADS), BF16), half, half),
+        (place, layer_input, table, middle, mixed, probs, route, out_grad,
          rows_own, rows_other, router, gain_two, output_weight, context, queries, keys,
-         values, normed, lse, tiles, jnp.asarray(stretch, BF16)),
-        scratch=(pltpu.VMEM((SEQ, D), BF16), pltpu.VMEM((SEQ, 128), BF16)),
+         values, normed, lse, tiles, wq, wk, wv, jnp.asarray(stretch, BF16)),
+        scratch=(pltpu.VMEM((SEQ, D), BF16), pltpu.VMEM((SEQ, 128), BF16),
+                 pltpu.VMEM((SEQ, D), BF16), pltpu.VMEM((SEQ, D), F32),
+                 pltpu.VMEM((SEQ, D), BF16), pltpu.VMEM((SEQ, D), F32),
+                 pltpu.SemaphoreType.DMA((2,))),
+        far_out=(0, 1),
         scalars=1, limit=24, flops=4_000_000_000, moved=12_000_000,
     )
-    half = shape((256, D), BF16)
-    norm_mine, norm_theirs, gain_part = call(
-        normed_kernel, (half, half, shape((8, D), F32)),
-        (place, layer_input, query_low, key_low, value_low, wq, wk, wv),
-        scratch=(pltpu.VMEM((SEQ, D), BF16),),
-        scalars=1, limit=12, flops=500_000_000, moved=3_500_000,
-    )
-    gain_pair = jnp.concatenate([gain_part, swap(gain_part, "c")], axis=0)
     halved = (norm_mine.astype(F32) + swap(norm_theirs, "c").astype(F32)).astype(BF16)
     scattered = lax.all_to_all(grads, experts_axis, 0, 0, tiled=True)
-    gain_link, halved_link = lax.optimization_barrier(
-        (swap(gain_pair, "l"), swap(halved, "l"))
-    )
-    halved = (halved.astype(F32) + halved_link.astype(F32)).astype(BF16)
-    halved_other = swap(halved, "c")
+    halved_link = swap(halved, "l")
+    reduced = (halved.astype(F32) + halved_link.astype(F32)).astype(BF16)
+    reduced_other = swap(reduced, "c")
     spread = call(
         reduce_kernel, shape((D, GRADS), BF16),
-        (scattered, gain_pair, gain_link),
+        (scattered, halved, halved_link),
         limit=12, flops=10_000_000, moved=3_000_000,
     )
     spread, slots, slot_grads, act, pre_grad = lax.optimization_barrier(
@@ -732,7 +734,7 @@
     gathered = lax.all_to_all(spread, experts_axis, 0, 0, tiled=True)
     input_grad = call(
         input_kernel, shape((SEQ, D), F32),
-        (place, halved, halved_other, layer_input, gain_one, middle_grad),
+        (place, reduced, reduced_other, layer_input, gain_one, middle_grad),
         alias={5: 0}, scalars=1, limit=12, flops=10_000_000, moved=5_000_000,
     )
     out = shape((WIDTH, D), F32)

time: 179 us -> 177 us (0.989)
  waiting for transfers between devices: 40.5 us -> 47.6 us
  local copies, waits for them, and re-layouts: 8.04 us -> 2.25 us
  Pallas kernels: 45.4 us -> 43.1 us
  other arithmetic: 2.57 us -> 0.74 us
    ppermute x14 -> x12, waiting for transfers between devices: 29.8 us -> 35.9 us  [swap(): return lax.ppermute(array, axis, [(0, 1), (1, 0)])]
    unnamed x81 -> x72, local copies, waits for them, and re-layouts: 7.98 us -> 2.19 us
    pallas_call x12 -> x11, Pallas kernels: 39.8 us -> 37.6 us  [call(): pl.pallas_call(body, out_shape=outs, in_specs=[pl.BlockSpec(memory_space=...]
    ppermute x14 -> x12, starting transfers between devices: 5.38 us -> 4.53 us  [swap(): return lax.ppermute(array, axis, [(0, 1), (1, 0)])]
  transfers between devices with their start and end apart: 16 -> 14, of which waited for: 12 -> 11; matrix products, arithmetic and copies ran while one was open for 1% -> 0% of each run, Pallas kernels for 12% -> 11%
where the time goes in v7:
time: 177 us; the launch traced here: 176 us
  blocking collectives  60.7 us (34%)
  waiting for transfers between devices  47.6 us (27%)
  Pallas kernels  43.1 us (24%)
  starting transfers between devices  20.7 us (12%)
  local copies, waits for them, and re-layouts  2.25 us (1%)
    pallas_call x11, Pallas kernels, call(): pl.pallas_call(body, out_shape=outs, in_specs=[pl.BlockSpec(memory_space=...  37.6 us
    ppermute x12, waiting for transfers between devices, swap(): return lax.ppermute(array, axis, [(0, 1), (1, 0)])  35.9 us
    all_to_all x1, blocking collectives, shards(): lax.all_to_all(jnp.concatenate([partial, partial], axis=0), pair_axis, 0,...  31.9 us
    all_to_all x1, blocking collectives, shards(): received = lax.all_to_all(send, experts_axis, 0, 0, tiled=True)  28.8 us
    all_to_all x1, waiting for transfers between devices, shards(): gathered = lax.all_to_all(spread, experts_axis, 0, 0, tiled=True)  11.8 us
    all_to_all x1, starting transfers between devices, shards(): gathered = lax.all_to_all(spread, experts_axis, 0, 0, tiled=True)  11 us
    pallas_call x1, Pallas kernels, expert_grads(): pl.pallas_call(expert_grads_kernel, grid=(2, 3), out_shape=(shape((2, D,...  5.54 us
    all_to_all x1, starting transfers between devices, shards(): scattered = lax.all_to_all(grads, experts_axis, 0, 0, tiled=True)  5.12 us
  transfers between devices with their start and end apart: 14, of which 11 were waited for; matrix products, arithmetic and copies ran while one was open for 0% of the time, Pallas kernels for 11%

profile of v7, /device:TPU:0, one launch (start us, length us, event | category | flops | bytes accessed | tf_op | source)
XLA Modules:
  0.0 176.3 jit_solution(5429386179954348095)
XLA Ops:
  0.7 1.7 collective-permute-start.4
  2.4 5.4 %shard_map.274 = (bf16[512,768]{1,0:T(8,128)(2,1)}, bf16[512,192]{1,0:T(8,128)(2,1)}, bf16[512,192]{1,0:T(8,128)(2,1)}, bf16[512,192]{1,0:T(8,128)(2,1)}, f32[9,...) custom-call(f32[3,32]{1,0:T(4,128)} %bitcast.36, bf16[512,768]{1,0:T(8,128)(2,1)} %x_ref.5, ...), custom_call_target="tpu_custom_call" | custom-call | flops 900000000 | bytes 5000000 | tf_op jit(solution)/shard_map/pallas_call | solution.py:95
  10.8 2.6 %shard_map.275 = (bf16[1280,512]{1,0:T(8,128)(2,1)S(1)}, bf16[1280,512]{1,0:T(8,128)(2,1)S(1)}, f32[512,768]{1,0:T(8,128)S(1)}, bf16[1280,384]{1,0:T(8,128)(2,1)S(1)}) custom-call(s32[2]{0:T(128)S(1)} %pad_add_fusion.place_ref, s32[8,512]{1,0:T(8,128)S(1)} %stack.31.route_ref, bf16[512,192]{1,0:T(8,128)(2,1)S(1)} %copy-done.16, ...), custom_call_target="tpu_custom_call" | custom-call | flops 1500000000 | bytes 7000000 | tf_op jit(solution)/shard_map/pallas_call | solution.py:95
  13.4 3.5 %collective-permute-done.2.ctx2 = bf16[512,192]{1,0:T(8,128)(2,1)S(1)} collective-permute-done((bf16[512,192]{1,0:T(8,128)(2,1)}, bf16[512,192]{1,0:T(8,128)(2,1)S(1)}, u32[]{:S(2)}, u32[]{:S(2)}) %collective-permute-start.2) | collective-permute-done | bytes 196640 | tf_op jit(solution)/shard_map/ppermute | solution.py:621
  17.0 1.5 collective-permute-done.3.ctx3
  18.5 3.9 %shard_map.276 = (f32[512,768]{1,0:T(8,128)S(1)}, bf16[512,768]{1,0:T(8,128)(2,1)S(1)}, f32[512,128]{1,0:T(8,128)S(1)}, bf16[1280,384]{1,0:T(8,128)(2,1)S(1)}) custom-call(s32[2]{0:T(128)S(1)} %pad_add_fusion.place_ref, bf16[512,768]{1,0:T(8,128)(2,1)S(1)} %copy-done, f32[512,768]{1,0:T(8,128)S(1)} %get-tuple-element.62.base_ref, ...), custom_call_target="tpu_custom_call" | custom-call | flops 1700000000 | bytes 8000000 | tf_op jit(solution)/shard_map/pallas_call | solution.py:95
  22.5 28.8 %all_to_all.45 = bf16[32,40,384]{2,1,0:T(8,128)(2,1)S(1)} all-to-all(bf16[32,40,384]{2,1,0:T(8,128)(2,1)S(1)} %bitcast.29), channel_id=1, replica_groups=mesh['z'=4,'x'=4,'h'=2,'l'=2,'c'=2] {'z','x','h'}, dimensions={0} | all-to-all | bytes 1966080 | tf_op jit(solution)/shard_map/all_to_all | solution.py:669
  52.1 1.7 collective-permute-done.6.other_ref
  53.8 5.5 %shard_map.278 = (bf16[1280,384]{1,0:T(8,128)(2,1)S(1)}, bf16[2,320,768]{2,1,0:T(8,128)(2,1)S(1)}, bf16[2,320,768]{2,1,0:T(8,128)(2,1)S(1)}, bf16[2,320,768]{2,1,0:T(8,128)(2,1)S(1)}, bf16[2,320,768]{2,1,0:T(8,128)(2,1)S(1)}) custom-call(s32[2]{0:T(128)S(1)} %pad_add_fusion.place_ref, bf16[1280,384]{1,0:T(8,128)(2,1)S(1)} %bitcast.28, ...), custom_call_target="tpu_custom_call" | custom-call | flops 4000000000 | bytes 14000000 | tf_op jit(solution)/shard_map/pallas_call | solution.py:95
  59.6 2.2 %shard_map.279 = bf16[1280,384]{1,0:T(8,128)(2,1)S(1)} custom-call(s32[2]{0:T(128)S(1)} %pad_add_fusion.place_ref, bf16[2,320,768]{2,1,0:T(8,128)(2,1)S(1)} %get-tuple-element.106.act_ref, bf16[2,320,768]{2,1,0:T(8,128)(2,1)S(1)} %get-tuple-element.107.pre_ref, bf16[2,768,768]{2,1,0:T(8,128)(2,1)S(1)} %copy-done.1, bf16[2,768,768]{2,1,0:T(8,128)(2,1)S(1)} %copy-done.2, ...), custom_call_target="tpu_custom_call" | custom-call | flops 1000000000 | bytes 4000000 | tf_op jit(solution)/shard_map/pallas_call | solution.py:95
  62.5 31.9 %all_to_all.46 = bf16[64,40,384]{2,1,0:T(8,128)(2,1)S(1)} all-to-all(bf16[64,40,384]{2,1,0:T(8,128)(2,1)S(1)} %bitcast.38), channel_id=1, replica_groups=mesh['z'=4,'x'=4,'h'=2,'l'=2,'c'=2] {'l','z','x','h'}, dimensions={0} | all-to-all | bytes 3932160 | tf_op jit(solution)/shard_map/all_to_all | solution.py:696
  94.6 1.6 shard_map.280.own_ref
  96.5 2.3 %collective-permute-done.8.other_ref = bf16[512,768]{1,0:T(8,128)(2,1)S(1)} collective-permute-done((bf16[512,768]{1,0:T(8,128)(2,1)S(1)}, bf16[512,768]{1,0:T(8,128)(2,1)S(1)}, u32[]{:S(2)}, u32[]{:S(2)}) %collective-permute-start.8) | collective-permute-done | bytes 786464 | tf_op jit(solution)/shard_map/ppermute | solution.py:621
  98.8 9.1 %shard_map.281 = (bf16[512,768]{1,0:T(8,128)(2,1)}, f32[512,768]{1,0:T(8,128)}, bf16[768,896]{1,0:T(8,128)(2,1)S(1)}, bf16[272,768]{1,0:T(8,128)(2,1)S(1)}, bf16[272,768]{1,0:T(8,128)(2,1)S(1)}) custom-call(s32[2]{0:T(128)S(1)} %pad_add_fusion.place_ref, bf16[512,768]{1,0:T(8,128)(2,1)S(1)} %copy-done, f32[3,32]{1,0:T(4,128)S(1)} %bitcast.37, ...), custom_call_target="tpu_custom_call" | custom-call | flops 4000000000 | bytes 12000000 | tf_op jit(solution)/shard_map/pallas_call | solution.py:95
  109.0 5.1 %all-to-all-start.2 = ((bf16[32,24,896]{2,1,0:T(8,128)(2,1)}), bf16[32,24,896]{2,1,0:T(8,128)(2,1)S(1)}, u32[]{:S(2)}, u32[]{:S(2)}) async-start(bf16[32,24,896]{2,1,0:T(8,128)(2,1)} %bitcast.26), calls=%async_computation.2 | async-start | bytes 2752512 | tf_op jit(solution)/shard_map/all_to_all | solution.py:721
  114.2 1.7 collective-permute-done.9
  117.2 22.4 %collective-permute-done.10.link_ref = bf16[272,768]{1,0:T(8,128)(2,1)S(1)} collective-permute-done((bf16[272,768]{1,0:T(8,128)(2,1)S(1)}, bf16[272,768]{1,0:T(8,128)(2,1)S(1)}, u32[]{:S(2)}, u32[]{:S(2)}) %collective-permute-start.10) | collective-permute-done | bytes 417824 | tf_op jit(solution)/shard_map/ppermute | solution.py:621
  139.6 1.4 shard_map.283
  141.0 11.0 %all-to-all-start.3 = ((bf16[32,24,896]{2,1,0:T(8,128)(2,1)}), bf16[32,24,896]{2,1,0:T(8,128)(2,1)S(1)}, u32[]{:S(2)}, u32[]{:S(2)}) async-start(bf16[32,24,896]{2,1,0:T(8,128)(2,1)} %bitcast.16), calls=%async_computation.3 | async-start | bytes 2752512 | tf_op jit(solution)/shard_map/all_to_all | solution.py:734
  152.3 1.7 collective-permute-done.11.other_ref
  154.0 3.4 %shard_map.282 = f32[512,768]{1,0:T(8,128)} custom-call(s32[2]{0:T(128)S(1)} %pad_add_fusion.place_ref, bf16[272,768]{1,0:T(8,128)(2,1)S(1)} %add_convert_fusion.1.own_ref, bf16[272,768]{1,0:T(8,128)(2,1)S(1)} %collective-permute-done.11.other_ref, bf16[512,768]{1,0:T(8,128)(2,1)S(1)} %copy-done, ...), custom_call_target="tpu_custom_call", output_to_operand_aliasing={{}: (5, {})} | custom-call | flops 10000000 | bytes 5000000 | tf_op jit(solution)/shard_map/pallas_call | solution.py:95
  157.4 5.5 %shard_map.285 = (f32[2,768,768]{2,1,0:T(8,128)}, f32[2,768,768]{2,1,0:T(8,128)}) custom-call(bf16[2,320,768]{2,1,0:T(8,128)(2,1)S(1)} %copy-done.21, bf16[2,320,768]{2,1,0:T(8,128)(2,1)S(1)} %copy-done.23, bf16[2,320,768]{2,1,0:T(8,128)(2,1)S(1)} %copy-done.5, bf16[2,320,768]{2,1,0:T(8,128)(2,1)S(1)} %copy-done.7), custom_call_target="tpu_custom_call" | custom-call | flops 1509949440 | bytes 14000000 | tf_op jit(solution)/shard_map/pallas_call | solution.py:377
  162.9 11.8 %all-to-all-done.3 = bf16[32,24,896]{2,1,0:T(8,128)(2,1)S(1)} async-done(((bf16[32,24,896]{2,1,0:T(8,128)(2,1)}), bf16[32,24,896]{2,1,0:T(8,128)(2,1)S(1)}, u32[]{:S(2)}, u32[]{:S(2)}) %all-to-all-start.3) | async-done | bytes 1376288 | tf_op jit(solution)/shard_map/all_to_all | solution.py:734
  174.7 1.6 shard_map.284
  (101 shorter events, 7.7 us)
Async XLA Ops:
  0.6 9.2 %copy-start.15 = (bf16[192,768]{1,0:T(8,128)(2,1)S(1)}, bf16[192,768]{1,0:T(8,128)(2,1)}, u32[]{:S(2)}) copy-start(bf16[192,768]{1,0:T(8,128)(2,1)} %wo_ref.1) | copy-start | bytes 884740
  0.7 8.3 %copy-start.33 = (s32[512]{0:T(512)S(1)}, s32[512]{0:T(512)}, u32[]{:S(2)}) copy-start(s32[512]{0:T(512)} %param.30) | copy-start | bytes 6148
  0.7 8.3 %copy-start.34 = (s32[512]{0:T(512)S(1)}, s32[512]{0:T(512)}, u32[]{:S(2)}) copy-start(s32[512]{0:T(512)} %param.31) | copy-start | bytes 6148
  0.7 9.2 %copy-start.10 = (bf16[512,768]{1,0:T(8,128)(2,1)S(1)}, bf16[512,768]{1,0:T(8,128)(2,1)}, u32[]{:S(2)}) copy-start(bf16[512,768]{1,0:T(8,128)(2,1)} %grad_ref.3) | copy-start | bytes 2359300
  0.7 9.0 %collective-permute-start.4 = (bf16[192,768]{1,0:T(8,128)(2,1)}, bf16[192,768]{1,0:T(8,128)(2,1)S(1)}, u32[]{:S(2)}, u32[]{:S(2)}) collective-permute-start(bf16[192,768]{1,0:T(8,128)(2,1)} %wo_ref.1), channel_id=1, source_target_pairs={{0,2},{2,0},{1,3},{3,1},{4,6},{6,4},{5,7},{7,5},{8,10},{10,8},{9,1... | collective-permute-start | bytes 884744 | tf_op jit(solution)/shard_map/ppermute | solution.py:621
  2.4 7.4 %collective-permute-start.1 = (bf16[192,768]{1,0:T(8,128)(2,1)}, bf16[192,768]{1,0:T(8,128)(2,1)S(1)}, u32[]{:S(2)}, u32[]{:S(2)}) collective-permute-start(bf16[192,768]{1,0:T(8,128)(2,1)} %wo_ref.1), channel_id=1, source_target_pairs={{0,1},{1,0},{2,3},{3,2},{4,5},{5,4},{6,7},{7,6},{8,9},{9,8},{10,11... | collective-permute-start | bytes 884744 | tf_op jit(solution)/shard_map/ppermute | solution.py:621
  7.9 2.0 %collective-permute-start = (bf16[512,192]{1,0:T(8,128)(2,1)}, bf16[512,192]{1,0:T(8,128)(2,1)S(1)}, u32[]{:S(2)}, u32[]{:S(2)}) collective-permute-start(bf16[512,192]{1,0:T(8,128)(2,1)} %get-tuple-element.61.ctx0.ctx_ref), channel_id=1, source_target_pairs={{0,1},{1,0},{2,3},{3,2},{4,5},{5,4},{6,7},{7,6},{8,9},{9,8},{10,11... | collective-permute-start | bytes 589832 | tf_op jit(solution)/shard_map/ppermute | solution.py:621
  8.5 8.5 %collective-permute-start.2 = (bf16[512,192]{1,0:T(8,128)(2,1)}, bf16[512,192]{1,0:T(8,128)(2,1)S(1)}, u32[]{:S(2)}, u32[]{:S(2)}) collective-permute-start(bf16[512,192]{1,0:T(8,128)(2,1)} %get-tuple-element.61.ctx0.ctx_ref), channel_id=1, source_target_pairs={{0,2},{2,0},{1,3},{3,1},{4,6},{6,4},{5,7},{7,5},{8,10},{10,8},{9,1... | collective-permute-start | bytes 589832 | tf_op jit(solution)/shard_map/ppermute | solution.py:621
  9.0 9.5 %copy-start = (bf16[512,768]{1,0:T(8,128)(2,1)S(1)}, bf16[512,768]{1,0:T(8,128)(2,1)}, u32[]{:S(2)}) copy-start(bf16[512,768]{1,0:T(8,128)(2,1)} %x_ref.5) | copy-start | bytes 2359300
  9.7 8.9 %collective-permute-start.5 = (bf16[192,768]{1,0:T(8,128)(2,1)S(1)}, bf16[192,768]{1,0:T(8,128)(2,1)S(1)}, u32[]{:S(2)}, u32[]{:S(2)}) collective-permute-start(bf16[192,768]{1,0:T(8,128)(2,1)S(1)} %collective-permute-done.4.wo2), channel_id=1, source_target_pairs={{0,1},{1,0},{2,3},{3,2},{4,5},{5,4},{6,7},{7,6},{8,9},{9,8},{10,11... | collective-permute-start | bytes 884744 | tf_op jit(solution)/shard_map/ppermute | solution.py:621
  17.0 1.5 collective-permute-start.3
  18.5 35.3 %copy-start.1 = (bf16[2,768,768]{2,1,0:T(8,128)(2,1)S(1)}, bf16[2,768,768]{2,1,0:T(8,128)(2,1)}, u32[]{:S(2)}) copy-start(bf16[2,768,768]{2,1,0:T(8,128)(2,1)} %in_ref.3) | copy-start | bytes 7077892
  18.5 35.3 %copy-start.2 = (bf16[2,768,768]{2,1,0:T(8,128)(2,1)S(1)}, bf16[2,768,768]{2,1,0:T(8,128)(2,1)}, u32[]{:S(2)}) copy-start(bf16[2,768,768]{2,1,0:T(8,128)(2,1)} %out_ref.3) | copy-start | bytes 7077892
  22.4 31.4 %copy-start.8 = (bf16[320,320]{1,0:T(8,128)(2,1)S(1)}, bf16[320,320]{1,0:T(8,128)(2,1)}, u32[]{:S(2)}) copy-start(bf16[320,320]{1,0:T(8,128)(2,1)} %constant.20.clone.back_ref) | copy-start | bytes 614404
  22.5 31.4 %copy-start.19 = (bf16[320,320]{1,0:T(8,128)(2,1)S(1)}, bf16[320,320]{1,0:T(8,128)(2,1)}, u32[]{:S(2)}) copy-start(bf16[320,320]{1,0:T(8,128)(2,1)} %constant.21.clone.sel_ref) | copy-start | bytes 614404
  51.3 2.6 %collective-permute-start.6 = (bf16[1280,384]{1,0:T(8,128)(2,1)S(1)}, bf16[1280,384]{1,0:T(8,128)(2,1)S(1)}, u32[]{:S(2)}, u32[]{:S(2)}) collective-permute-start(bf16[1280,384]{1,0:T(8,128)(2,1)S(1)} %bitcast.27), channel_id=1, source_target_pairs={{0,1},{1,0},{2,3},{3,2},{4,5},{5,4},{6,7},{7,6},{8,9},{9,8},{10,11... | collective-permute-start | bytes 2949128 | tf_op jit(solution)/shard_map/ppermute | solution.py:621
  59.4 2.6 %collective-permute-start.7 = (bf16[1280,384]{1,0:T(8,128)(2,1)S(1)}, bf16[1280,384]{1,0:T(8,128)(2,1)S(1)}, u32[]{:S(2)}, u32[]{:S(2)}) collective-permute-start(bf16[1280,384]{1,0:T(8,128)(2,1)S(1)} %get-tuple-element.81), channel_id=1, source_target_pairs={{0,1},{1,0},{2,3},{3,2},{4,5},{5,4},{6,7},{7,6},{8,9},{9,8},{10,11... | collective-permute-start | bytes 2949128 | tf_op jit(solution)/shard_map/ppermute | solution.py:621
  96.1 2.6 %collective-permute-start.8 = (bf16[512,768]{1,0:T(8,128)(2,1)S(1)}, bf16[512,768]{1,0:T(8,128)(2,1)S(1)}, u32[]{:S(2)}, u32[]{:S(2)}) collective-permute-start(bf16[512,768]{1,0:T(8,128)(2,1)S(1)} %shard_map.280.own_ref), channel_id=1, source_target_pairs={{0,1},{1,0},{2,3},{3,2},{4,5},{5,4},{6,7},{7,6},{8,9},{9,8},{10,11... | collective-permute-start | bytes 2359304 | tf_op jit(solution)/shard_map/ppermute | solution.py:621
  109.0 30.6 %all-to-all-start.2 = ((bf16[32,24,896]{2,1,0:T(8,128)(2,1)}), bf16[32,24,896]{2,1,0:T(8,128)(2,1)S(1)}, u32[]{:S(2)}, u32[]{:S(2)}) async-start(bf16[32,24,896]{2,1,0:T(8,128)(2,1)} %bitcast.26), calls=%async_computation.2 | async-start | bytes 2752512 | tf_op jit(solution)/shard_map/all_to_all | solution.py:721
  114.1 1.8 %collective-permute-start.9 = (bf16[272,768]{1,0:T(8,128)(2,1)S(1)}, bf16[272,768]{1,0:T(8,128)(2,1)S(1)}, u32[]{:S(2)}, u32[]{:S(2)}) collective-permute-start(bf16[272,768]{1,0:T(8,128)(2,1)S(1)} %get-tuple-element.90), channel_id=1, source_target_pairs={{0,1},{1,0},{2,3},{3,2},{4,5},{5,4},{6,7},{7,6},{8,9},{9,8},{10,11... | collective-permute-start | bytes 1253384 | tf_op jit(solution)/shard_map/ppermute | solution.py:621
  116.1 23.5 %collective-permute-start.10 = (bf16[272,768]{1,0:T(8,128)(2,1)S(1)}, bf16[272,768]{1,0:T(8,128)(2,1)S(1)}, u32[]{:S(2)}, u32[]{:S(2)}) collective-permute-start(bf16[272,768]{1,0:T(8,128)(2,1)S(1)} %add_convert_fusion.2.halved_ref), channel_id=1, source_target_pairs={{0,2},{2,0},{1,3},{3,1},{4,6},{6,4},{5,7},{7,5},{8,10},{10,8},{9,1... | collective-permute-start | bytes 1253384 | tf_op jit(solution)/shard_map/ppermute | solution.py:621
  141.0 11.2 %copy-start.32 = (f32[768]{0:T(1024)S(1)}, f32[768]{0:T(1024)}, u32[]{:S(2)}) copy-start(f32[768]{0:T(1024)} %gain_hbm.1) | copy-start | bytes 9220
  141.0 33.7 %all-to-all-start.3 = ((bf16[32,24,896]{2,1,0:T(8,128)(2,1)}), bf16[32,24,896]{2,1,0:T(8,128)(2,1)S(1)}, u32[]{:S(2)}, u32[]{:S(2)}) async-start(bf16[32,24,896]{2,1,0:T(8,128)(2,1)} %bitcast.16), calls=%async_computation.3 | async-start | bytes 2752512 | tf_op jit(solution)/shard_map/all_to_all | solution.py:734
  152.2 1.8 %collective-permute-start.11 = (bf16[272,768]{1,0:T(8,128)(2,1)S(1)}, bf16[272,768]{1,0:T(8,128)(2,1)S(1)}, u32[]{:S(2)}, u32[]{:S(2)}) collective-permute-start(bf16[272,768]{1,0:T(8,128)(2,1)S(1)} %add_convert_fusion.1.own_ref), channel_id=1, source_target_pairs={{0,1},{1,0},{2,3},{3,2},{4,5},{5,4},{6,7},{7,6},{8,9},{9,8},{10,11... | collective-permute-start | bytes 1253384 | tf_op jit(solution)/shard_map/ppermute | solution.py:621
  (26 other events, 103.4 us)

commit v8 on v7

--- a/solution.py
+++ b/solution.py
@@ -398,12 +398,40 @@
     out_ref[:, pl.ds(HALF, HALF)] = dot(high_ref[...], slots).astype(BF16)
 
 
+def window_kernel(
+    table_ref, q_ref, k_ref, lse_ref, tiles_ref, x_ref, middle_ref, probs_ref, route_ref,
+    weights_ref, stats_ref,
+):
+    scaled = q_ref[...] * jnp.asarray(HEAD**-0.5, BF16)
+    keys = k_ref[...]
+    for head in range(HEADS_HERE):
+        for part in range(2):
+            rows = slice(part * 256, part * 256 + 256)
+            scores = scores_t(
+                keys, only_head(scaled[rows], head), tiles_ref, table_ref[...], head, part
+            )
+            weights_ref[head, part] = jnp.exp(scores - lse_ref[head : head + 1, rows]).astype(BF16)
+    columns = route_columns(route_ref)
+    for i in range(SEQ // 32):
+        rows = slice(i * 32, i * 32 + 32)
+        lanes = lax.broadcasted_iota(jnp.int32, (32, 128), 1)
+        middle = middle_ref[rows, :]
+        scale_two = lax.rsqrt(jnp.mean(middle * middle, axis=-1, keepdims=True) + EPS)
+        hidden = x_ref[rows, :].astype(F32)
+        scale_one = lax.rsqrt(jnp.mean(hidden * hidden, axis=-1, keepdims=True) + EPS)
+        hot = lanes == columns[rows, 0:1].astype(jnp.int32)
+        chosen = jnp.sum(jnp.where(hot, probs_ref[rows, :], 0.0), axis=-1, keepdims=True)
+        stats_ref[rows, :] = jnp.where(
+            lanes == 0, scale_one, jnp.where(lanes == 1, scale_two, chosen)
+        )
+
+
 def backward_kernel(
-    place_ref, x_ref, table_ref, middle_ref, mixed_ref, probs_ref, route_ref, grad_ref,
+    place_ref, x_ref, middle_ref, mixed_ref, probs_ref, route_ref, grad_ref,
     own_ref, other_ref, router_ref, gain_ref, wo_ref, ctx_ref, q_ref, k_ref, v_ref, normed_ref,
-    lse_ref, tiles_ref, wq_ref, wk_ref, wv_ref, stretch_ref,
-    output_hbm, middle_grad_hbm, grads_ref, mine_ref, theirs_ref,
-    low_s, logit_s, normed_s, wide_s, output_ref, middle_grad_ref, sems,
+    weights_ref, stats_ref, wq_ref, wk_ref, wv_ref, stretch_ref,
+    output_hbm, middle_grad_hbm, grads_hbm, mine_ref, theirs_ref, gain_one_ref,
+    low_s, logit_s, normed_s, wide_s, output_ref, middle_grad_ref, grads_ref, sems,
 ):
     core = place_ref[1]
     columns = route_columns(route_ref)
@@ -415,7 +443,7 @@
         kept = 1.0 - columns[rows, 2:3]
         lanes = lax.broadcasted_iota(jnp.int32, (32, 128), 1)
         hot = (lanes == columns[rows, 0:1].astype(jnp.int32)).astype(F32)
-        chosen = jnp.sum(probs * hot, axis=-1, keepdims=True)
+        chosen = stats_ref[rows, 2:3]
         upstream = grad_ref[rows, :].astype(F32)
         output_ref[rows, :] = (
             middle_ref[rows, :] + (chosen * kept) * expert_rows
@@ -431,7 +459,7 @@
         mixed_grad = jnp.where(core == 0, other_ref[rows, :], own_ref[rows, :]).astype(F32)
         mixed_grad = mixed_grad + wide_s[rows, :]
         middle = middle_ref[rows, :]
-        scale = lax.rsqrt(jnp.mean(middle * middle, axis=-1, keepdims=True) + EPS)
+        scale = stats_ref[rows, 1:2]
         along = mixed_grad * middle
         inner = jnp.mean(along * gain, axis=-1, keepdims=True)
         gain_grad = gain_grad + jnp.sum((along * scale).reshape(4, 8, D), axis=0)
@@ -449,9 +477,8 @@
     grads_ref[pl.ds(3 * WIDTH, WIDTH), :D] = dot_tn(ctx_ref[...], middle_low).astype(BF16)
     ctx_grad = dot_nt(middle_low, wo_ref[...]).astype(BF16)
 
-    keys = k_ref[...]
     values = v_ref[...]
-    key_scaled = keys * jnp.asarray(HEAD**-0.5, BF16)
+    key_scaled = k_ref[...] * jnp.asarray(HEAD**-0.5, BF16)
     query_scaled = q_ref[...] * jnp.asarray(HEAD**-0.5, BF16)
     key_grad = jnp.zeros((SEQ, WIDTH), F32)
     value_grad = jnp.zeros((SEQ, WIDTH), F32)
@@ -474,9 +501,9 @@
             rows = slice(part * 256, part * 256 + 256)
             query_head = only_head(query_scaled[rows], head)
             ctx_head = only_head(ctx_grad[rows], head)
-            scores = scores_t(keys, query_head, tiles_ref, table_ref[...], head, part)
-            probs = jnp.exp(scores - lse_ref[head : head + 1, rows])
-            value_grad = value_grad + dot(probs.astype(BF16), ctx_head)
+            probs_low = weights_ref[head, part]
+            probs = probs_low.astype(F32)
+            value_grad = value_grad + dot(probs_low, ctx_head)
             prob_grad = dot_nt(values, ctx_head)
             inner = jnp.sum(probs * prob_grad, axis=0, keepdims=True)
             score_grad = (probs * (prob_grad - inner)).astype(BF16)
@@ -517,13 +544,20 @@
     query_low = jnp.concatenate(query_grads, axis=0).astype(BF16)
     key_low = key_grad.astype(BF16)
     value_low = value_grad.astype(BF16)
-    normed = normed_ref[...]
-    for i, low in enumerate((query_low, key_low, value_low)):
-        grads_ref[pl.ds(i * WIDTH, WIDTH), :D] = dot_tn(low, normed).astype(BF16)
     rest = dot_tn(mixed_ref[...], logit_s[...]) + dot(stretch_ref[...], bias_grad.astype(BF16))
     column = jnp.transpose(jnp.broadcast_to(gain_grad, (128, D)))
     lanes = lax.broadcasted_iota(jnp.int32, (D, 128), 1)
     grads_ref[:, D:] = jnp.where(lanes == EXPERTS, column, rest).astype(BF16)
+    normed = normed_ref[...]
+    copies = []
+    for i, low in ((3, None), (0, query_low), (1, key_low), (2, value_low)):
+        part = pl.ds(i * WIDTH, WIDTH)
+        if low is not None:
+            grads_ref[part, :D] = dot_tn(low, normed).astype(BF16)
+        copies.append(
+            pltpu.make_async_copy(grads_ref.at[part], grads_hbm.at[part], sems.at[2 + i])
+        )
+        copies[-1].start()
     wide_s[...] = (
         dot(query_low, wq_ref[...]) + dot(key_low, wk_ref[...]) + dot(value_low, wv_ref[...])
     )
@@ -533,12 +567,13 @@
         normed_part = wide_s[rows, :]
         normed_s[rows, :] = normed_part.astype(BF16)
         hidden = x_ref[rows, :].astype(F32)
-        scale = lax.rsqrt(jnp.mean(hidden * hidden, axis=-1, keepdims=True) + EPS)
+        scale = stats_ref[rows, 0:1]
         gain_one = gain_one + jnp.sum((normed_part * hidden * scale).reshape(4, 8, D), axis=0)
-    gain_rows = jnp.broadcast_to(jnp.sum(gain_one, axis=0, keepdims=True), (16, D)).astype(BF16)
+    gain_one_ref[...] = jnp.broadcast_to(jnp.sum(gain_one, axis=0, keepdims=True), (8, D))
     for out, start in ((mine_ref, core * 256), (theirs_ref, (1 - core) * 256)):
-        out[:256, :] = normed_s[pl.ds(pl.multiple_of(start, 256), 256), :]
-        out[256:, :] = gain_rows
+        out[...] = normed_s[pl.ds(pl.multiple_of(start, 256), 256), :]
+    for copy in copies:
+        copy.wait()
     output_copy.wait()
     middle_copy.wait()
 
@@ -548,9 +583,8 @@
     return jnp.where(core == i // 2, own_ref[local, :], other_ref[local, :]).astype(F32)
 
 
-def reduce_kernel(parts_ref, halved_ref, link_ref, send_ref):
-    extra = pl.ds(256, 16)
-    gain_grad = (halved_ref[extra, :].astype(F32) + link_ref[extra, :].astype(F32))[0:1]
+def reduce_kernel(parts_ref, pair_ref, link_ref, old_hbm, send_ref):
+    gain_grad = (pair_ref[0:1] + pair_ref[8:9]) + (link_ref[0:1] + link_ref[8:9])
     total = jnp.zeros((24, GRADS), F32)
     for j in range(GROUPS // 2):
         pair = parts_ref[pl.ds(j * 48, 48), :].astype(F32)
@@ -700,37 +734,46 @@
         tokens_kernel, shape((SEQ, D), BF16), (low_back, high_back, back),
         limit=12, flops=2_000_000_000, moved=3_000_000,
     )
-    rows_other = swap(rows_own, "c")
+    rows_own, queries_late, middle_late = lax.optimization_barrier((rows_own, queries, middle))
+    weights, stats = call(
+        window_kernel, (shape((HEADS_HERE, 2, SEQ, 256), BF16), shape((SEQ, 128), F32)),
+        (table, queries_late, keys, lse, tiles, layer_input, middle_late, probs, route),
+        limit=14, flops=300_000_000, moved=6_000_000,
+    )
+    rows_other, stats = lax.optimization_barrier((swap(rows_own, "c"), stats))
     stretch = np.zeros((D, BUCKETS), np.float32)
     stretch[24 * np.arange(BUCKETS), np.arange(BUCKETS)] = 1
-    half = shape((256 + 16, D), BF16)
-    layer_output, middle_grad, grads, norm_mine, norm_theirs = call(
+    half = shape((256, D), BF16)
+    layer_output, middle_grad, grads, norm_mine, norm_theirs, gain_part = call(
         backward_kernel,
-        (wide, shape((SEQ, D), F32), shape((D, GRADS), BF16), half, half),
-        (place, layer_input, table, middle, mixed, probs, route, out_grad,
+        (wide, shape((SEQ, D), F32), shape((D, GRADS), BF16), half, half, shape((8, D), F32)),
+        (place, layer_input, middle, mixed, probs, route, out_grad,
          rows_own, rows_other, router, gain_two, output_weight, context, queries, keys,
-         values, normed, lse, tiles, wq, wk, wv, jnp.asarray(stretch, BF16)),
+         values, normed, weights, stats, wq, wk, wv, jnp.asarray(stretch, BF16)),
         scratch=(pltpu.VMEM((SEQ, D), BF16), pltpu.VMEM((SEQ, 128), BF16),
                  pltpu.VMEM((SEQ, D), BF16), pltpu.VMEM((SEQ, D), F32),
                  pltpu.VMEM((SEQ, D), BF16), pltpu.VMEM((SEQ, D), F32),
-                 pltpu.SemaphoreType.DMA((2,))),
-        far_out=(0, 1),
+                 pltpu.VMEM((D, GRADS), BF16), pltpu.SemaphoreType.DMA((6,))),
+        far_out=(0, 1, 2),
         scalars=1, limit=24, flops=4_000_000_000, moved=12_000_000,
     )
     halved = (norm_mine.astype(F32) + swap(norm_theirs, "c").astype(F32)).astype(BF16)
+    gain_pair = jnp.concatenate([gain_part, swap(gain_part, "c")], axis=0)
+    gain_pair, halved = lax.optimization_barrier((gain_pair, halved))
     scattered = lax.all_to_all(grads, experts_axis, 0, 0, tiled=True)
+    gain_link = swap(gain_pair, "l")
     halved_link = swap(halved, "l")
+    spread = call(
+        reduce_kernel, shape((D, GRADS), BF16),
+        (scattered, gain_pair, gain_link, grads),
+        far=(3,), alias={3: 0}, limit=12, flops=10_000_000, moved=3_000_000,
+    )
+    halved_link, slots, slot_grads, act, pre_grad = lax.optimization_barrier(
+        (halved_link, slots, slot_grads, act, pre_grad)
+    )
+    expert_in_grad, expert_out_grad = expert_grads(slots, slot_grads, act, pre_grad)
     reduced = (halved.astype(F32) + halved_link.astype(F32)).astype(BF16)
     reduced_other = swap(reduced, "c")
-    spread = call(
-        reduce_kernel, shape((D, GRADS), BF16),
-        (scattered, halved, halved_link),
-        limit=12, flops=10_000_000, moved=3_000_000,
-    )
-    spread, slots, slot_grads, act, pre_grad = lax.optimization_barrier(
-        (spread, slots, slot_grads, act, pre_grad)
-    )
-    expert_in_grad, expert_out_grad = expert_grads(slots, slot_grads, act, pre_grad)
     gathered = lax.all_to_all(spread, experts_axis, 0, 0, tiled=True)
     input_grad = call(
         input_kernel, shape((SEQ, D), F32),

time: 177 us -> 185 us (1.045); the launches traced: 176 us -> 182 us
  starting transfers between devices: 20.7 us -> 15.4 us
  local copies, waits for them, and re-layouts: 2.25 us -> 6.92 us
  waiting for transfers between devices: 47.6 us -> 51.1 us
    all_to_all x1, waiting for transfers between devices: 11.8 us -> 0.01 us  [shards(): gathered = lax.all_to_all(spread, experts_axis, 0, 0, tiled=True)]
    all_to_all x1, waiting for transfers between devices: 0.01 us -> 11.7 us  [shards(): scattered = lax.all_to_all(grads, experts_axis, 0, 0, tiled=True)]
    all_to_all x1, starting transfers between devices: 11 us -> 5.29 us  [shards(): gathered = lax.all_to_all(spread, experts_axis, 0, 0, tiled=True)]
    unnamed x72 -> x80, local copies, waits for them, and re-layouts: 2.19 us -> 6.86 us
    ppermute x12 -> x14, waiting for transfers between devices: 35.9 us -> 39.3 us  [swap(): return lax.ppermute(array, axis, [(0, 1), (1, 0)])]
    pallas_call x11 -> x12, Pallas kernels: 37.6 us -> 39.3 us  [call(): pl.pallas_call(body, out_shape=outs, in_specs=[pl.BlockSpec(memory_space=...]
    ppermute x12 -> x14, starting transfers between devices: 4.53 us -> 4.99 us  [swap(): return lax.ppermute(array, axis, [(0, 1), (1, 0)])]
  transfers between devices with their start and end apart: 14 -> 16, of which waited for: 11 -> 11; matrix products, arithmetic and copies ran while one was open for 0% -> 1% of each run, Pallas kernels for 11% -> 12%
where the time goes in v8:
time: 185 us; the launch traced here: 182 us
  blocking collectives  60.7 us (33%)
  waiting for transfers between devices  51.1 us (28%)
  Pallas kernels  44.9 us (24%)
  starting transfers between devices  15.4 us (8%)
  local copies, waits for them, and re-layouts  6.92 us (4%)
  other arithmetic  2.2 us (1%)
    ppermute x14, waiting for transfers between devices, swap(): return lax.ppermute(array, axis, [(0, 1), (1, 0)])  39.3 us
    pallas_call x12, Pallas kernels, call(): pl.pallas_call(body, out_shape=outs, in_specs=[pl.BlockSpec(memory_space=...  39.3 us
    all_to_all x1, blocking collectives, shards(): lax.all_to_all(jnp.concatenate([partial, partial], axis=0), pair_axis, 0,...  31.9 us
    all_to_all x1, blocking collectives, shards(): received = lax.all_to_all(send, experts_axis, 0, 0, tiled=True)  28.8 us
    all_to_all x1, waiting for transfers between devices, shards(): scattered = lax.all_to_all(grads, experts_axis, 0, 0, tiled=True)  11.7 us
    unnamed x80, local copies, waits for them, and re-layouts  6.86 us
    pallas_call x1, Pallas kernels, expert_grads(): pl.pallas_call(expert_grads_kernel, grid=(2, 3), out_shape=(shape((2, D,...  5.55 us
    all_to_all x1, starting transfers between devices, shards(): gathered = lax.all_to_all(spread, experts_axis, 0, 0, tiled=True)  5.29 us
  transfers between devices with their start and end apart: 16, of which 11 were waited for; matrix products, arithmetic and copies ran while one was open for 1% of the time, Pallas kernels for 12%

profile of v8, /device:TPU:0, one launch (start us, length us, event | category | flops | bytes accessed | tf_op | source)
XLA Modules:
  0.0 182.4 jit_solution(10812917877106265453)
XLA Ops:
  0.7 1.7 collective-permute-start.4
  2.4 5.4 %shard_map.274 = (bf16[512,768]{1,0:T(8,128)(2,1)}, bf16[512,192]{1,0:T(8,128)(2,1)}, bf16[512,192]{1,0:T(8,128)(2,1)}, bf16[512,192]{1,0:T(8,128)(2,1)}, f32[9,...) custom-call(f32[3,32]{1,0:T(4,128)} %bitcast.29, bf16[512,768]{1,0:T(8,128)(2,1)} %x_ref.7, ...), custom_call_target="tpu_custom_call" | custom-call | flops 900000000 | bytes 5000000 | tf_op jit(solution)/shard_map/pallas_call | solution.py:95
  10.8 2.6 %shard_map.275 = (bf16[1280,512]{1,0:T(8,128)(2,1)S(1)}, bf16[1280,512]{1,0:T(8,128)(2,1)S(1)}, f32[512,768]{1,0:T(8,128)S(1)}, bf16[1280,384]{1,0:T(8,128)(2,1)S(1)}) custom-call(s32[2]{0:T(128)S(1)} %pad_add_fusion.place_ref, s32[8,512]{1,0:T(8,128)S(1)} %stack.31.route_ref, bf16[512,192]{1,0:T(8,128)(2,1)S(1)} %copy-done.24, ...), custom_call_target="tpu_custom_call" | custom-call | flops 1500000000 | bytes 7000000 | tf_op jit(solution)/shard_map/pallas_call | solution.py:95
  13.5 3.5 %collective-permute-done.2.ctx2 = bf16[512,192]{1,0:T(8,128)(2,1)S(1)} collective-permute-done((bf16[512,192]{1,0:T(8,128)(2,1)}, bf16[512,192]{1,0:T(8,128)(2,1)S(1)}, u32[]{:S(2)}, u32[]{:S(2)}) %collective-permute-start.2) | collective-permute-done | bytes 196640 | tf_op jit(solution)/shard_map/ppermute | solution.py:655
  17.0 1.5 collective-permute-done.3.ctx3
  18.5 3.9 %shard_map.276 = (f32[512,768]{1,0:T(8,128)S(1)}, bf16[512,768]{1,0:T(8,128)(2,1)S(1)}, f32[512,128]{1,0:T(8,128)S(1)}, bf16[1280,384]{1,0:T(8,128)(2,1)S(1)}) custom-call(s32[2]{0:T(128)S(1)} %pad_add_fusion.place_ref, bf16[512,768]{1,0:T(8,128)(2,1)S(1)} %copy-done, f32[512,768]{1,0:T(8,128)S(1)} %get-tuple-element.72.base_ref, ...), custom_call_target="tpu_custom_call" | custom-call | flops 1700000000 | bytes 8000000 | tf_op jit(solution)/shard_map/pallas_call | solution.py:95
  22.5 28.8 %all_to_all.45 = bf16[32,40,384]{2,1,0:T(8,128)(2,1)S(1)} all-to-all(bf16[32,40,384]{2,1,0:T(8,128)(2,1)S(1)} %bitcast.28), channel_id=1, replica_groups=mesh['z'=4,'x'=4,'h'=2,'l'=2,'c'=2] {'z','x','h'}, dimensions={0} | all-to-all | bytes 1966080 | tf_op jit(solution)/shard_map/all_to_all | solution.py:703
  52.2 1.7 collective-permute-done.6.other_ref
  53.9 5.5 %shard_map.278 = (bf16[1280,384]{1,0:T(8,128)(2,1)S(1)}, bf16[2,320,768]{2,1,0:T(8,128)(2,1)S(1)}, bf16[2,320,768]{2,1,0:T(8,128)(2,1)S(1)}, bf16[2,320,768]{2,1,0:T(8,128)(2,1)S(1)}, bf16[2,320,768]{2,1,0:T(8,128)(2,1)S(1)}) custom-call(s32[2]{0:T(128)S(1)} %pad_add_fusion.place_ref, bf16[1280,384]{1,0:T(8,128)(2,1)S(1)} %bitcast.27, ...), custom_call_target="tpu_custom_call" | custom-call | flops 4000000000 | bytes 14000000 | tf_op jit(solution)/shard_map/pallas_call | solution.py:95
  59.6 2.2 %shard_map.279 = bf16[1280,384]{1,0:T(8,128)(2,1)S(1)} custom-call(s32[2]{0:T(128)S(1)} %pad_add_fusion.place_ref, bf16[2,320,768]{2,1,0:T(8,128)(2,1)S(1)} %get-tuple-element.126.act_ref, bf16[2,320,768]{2,1,0:T(8,128)(2,1)S(1)} %get-tuple-element.127.pre_ref, bf16[2,768,768]{2,1,0:T(8,128)(2,1)S(1)} %copy-done.1, bf16[2,768,768]{2,1,0:T(8,128)(2,1)S(1)} %copy-done.2, ...), custom_call_target="tpu_custom_call" | custom-call | flops 1000000000 | bytes 4000000 | tf_op jit(solution)/shard_map/pallas_call | solution.py:95
  62.5 31.9 %all_to_all.46 = bf16[64,40,384]{2,1,0:T(8,128)(2,1)S(1)} all-to-all(bf16[64,40,384]{2,1,0:T(8,128)(2,1)S(1)} %bitcast.37), channel_id=1, replica_groups=mesh['z'=4,'x'=4,'h'=2,'l'=2,'c'=2] {'l','z','x','h'}, dimensions={0} | all-to-all | bytes 3932160 | tf_op jit(solution)/shard_map/all_to_all | solution.py:730
  94.5 1.6 shard_map.280.own_ref
  96.5 1.8 shard_map.281
  98.8 9.1 %shard_map.282 = (bf16[512,768]{1,0:T(8,128)(2,1)}, f32[512,768]{1,0:T(8,128)}, bf16[768,896]{1,0:T(8,128)(2,1)}, bf16[256,768]{1,0:T(8,128)(2,1)S(1)}, bf16[256...) custom-call(s32[2]{0:T(128)S(1)} %pad_add_fusion.place_ref, bf16[512,768]{1,0:T(8,128)(2,1)S(1)} %copy-done, ...), custom_call_target="tpu_custom_call" | custom-call | flops 4000000000 | bytes 12000000 | tf_op jit(solution)/shard_map/pallas_call | solution.py:95
  109.3 5.1 %all-to-all-start.2 = ((bf16[32,24,896]{2,1,0:T(8,128)(2,1)}), bf16[32,24,896]{2,1,0:T(8,128)(2,1)S(1)}, u32[]{:S(2)}, u32[]{:S(2)}) async-start(bf16[32,24,896]{2,1,0:T(8,128)(2,1)} %bitcast.14), calls=%async_computation.2 | async-start | bytes 2752512 | tf_op jit(solution)/shard_map/all_to_all | solution.py:763
  115.0 1.5 collective-permute-done.9
  119.2 6.9 %collective-permute-done.13.link_ref = f32[16,768]{1,0:T(8,128)S(1)} collective-permute-done((f32[16,768]{1,0:T(8,128)S(1)}, f32[16,768]{1,0:T(8,128)S(1)}, u32[]{:S(2)}, u32[]{:S(2)}) %collective-permute-start.13) | collective-permute-done | bytes 49184 | tf_op jit(solution)/shard_map/ppermute | solution.py:655
  126.0 11.7 %all-to-all-done.2 = bf16[32,24,896]{2,1,0:T(8,128)(2,1)S(1)} async-done(((bf16[32,24,896]{2,1,0:T(8,128)(2,1)}), bf16[32,24,896]{2,1,0:T(8,128)(2,1)S(1)}, u32[]{:S(2)}, u32[]{:S(2)}) %all-to-all-start.2) | async-done | bytes 1376288 | tf_op jit(solution)/shard_map/all_to_all | solution.py:763
  138.6 1.4 shard_map.284
  140.0 5.3 %all-to-all-start.3 = ((bf16[32,24,896]{2,1,0:T(8,128)(2,1)}), bf16[32,24,896]{2,1,0:T(8,128)(2,1)S(1)}, u32[]{:S(2)}, u32[]{:S(2)}) async-start(bf16[32,24,896]{2,1,0:T(8,128)(2,1)} %bitcast.16), calls=%async_computation.3 | async-start | bytes 2752512 | tf_op jit(solution)/shard_map/all_to_all | solution.py:777
  145.4 22.8 %collective-permute-done.11 = bf16[256,768]{1,0:T(8,128)(2,1)S(1)} collective-permute-done((bf16[256,768]{1,0:T(8,128)(2,1)S(1)}, bf16[256,768]{1,0:T(8,128)(2,1)S(1)}, u32[]{:S(2)}, u32[]{:S(2)}) %collective-permute-start.11) | collective-permute-done | bytes 393248 | tf_op jit(solution)/shard_map/ppermute | solution.py:655
  172.0 5.5 %shard_map.286 = (f32[2,768,768]{2,1,0:T(8,128)}, f32[2,768,768]{2,1,0:T(8,128)}) custom-call(bf16[2,320,768]{2,1,0:T(8,128)(2,1)S(1)} %copy-done.28, bf16[2,320,768]{2,1,0:T(8,128)(2,1)S(1)} %copy-done.30, bf16[2,320,768]{2,1,0:T(8,128)(2,1)S(1)} %get-tuple-element.126.act_ref, bf16[2,320,768]{2,1,0:T(8,128)(2,1)S(1)} %copy-done.4), custom_call_target="tpu_custom_call" | custom-call | flops 1509949440 | bytes 14000000 | tf_op jit(solution)/shard_map/pallas_call | solution.py:377
  177.6 3.3 %shard_map.283 = f32[512,768]{1,0:T(8,128)} custom-call(s32[2]{0:T(128)S(1)} %pad_add_fusion.place_ref, bf16[256,768]{1,0:T(8,128)(2,1)S(1)} %add_convert_fusion.1.own_ref, bf16[256,768]{1,0:T(8,128)(2,1)S(1)} %collective-permute-done.12.other_ref, bf16[512,768]{1,0:T(8,128)(2,1)S(1)} %copy-done, ...), custom_call_target="tpu_custom_call", output_to_operand_aliasing={{}: (5, {})} | custom-call | flops 10000000 | bytes 5000000 | tf_op jit(solution)/shard_map/pallas_call | solution.py:95
  180.8 1.6 shard_map.285
  (115 shorter events, 14.8 us)
Async XLA Ops:
  0.6 9.2 %copy-start.22 = (bf16[192,768]{1,0:T(8,128)(2,1)S(1)}, bf16[192,768]{1,0:T(8,128)(2,1)}, u32[]{:S(2)}) copy-start(bf16[192,768]{1,0:T(8,128)(2,1)} %wo_ref.1) | copy-start | bytes 884740
  0.7 9.2 %copy-start.16 = (bf16[512,768]{1,0:T(8,128)(2,1)S(1)}, bf16[512,768]{1,0:T(8,128)(2,1)}, u32[]{:S(2)}) copy-start(bf16[512,768]{1,0:T(8,128)(2,1)} %grad_ref.3) | copy-start | bytes 2359300
  0.7 9.0 %collective-permute-start.4 = (bf16[192,768]{1,0:T(8,128)(2,1)}, bf16[192,768]{1,0:T(8,128)(2,1)S(1)}, u32[]{:S(2)}, u32[]{:S(2)}) collective-permute-start(bf16[192,768]{1,0:T(8,128)(2,1)} %wo_ref.1), channel_id=1, source_target_pairs={{0,2},{2,0},{1,3},{3,1},{4,6},{6,4},{5,7},{7,5},{8,10},{10,8},{9,1... | collective-permute-start | bytes 884744 | tf_op jit(solution)/shard_map/ppermute | solution.py:655
  2.4 7.4 %collective-permute-start.1 = (bf16[192,768]{1,0:T(8,128)(2,1)}, bf16[192,768]{1,0:T(8,128)(2,1)S(1)}, u32[]{:S(2)}, u32[]{:S(2)}) collective-permute-start(bf16[192,768]{1,0:T(8,128)(2,1)} %wo_ref.1), channel_id=1, source_target_pairs={{0,1},{1,0},{2,3},{3,2},{4,5},{5,4},{6,7},{7,6},{8,9},{9,8},{10,11... | collective-permute-start | bytes 884744 | tf_op jit(solution)/shard_map/ppermute | solution.py:655
  7.9 2.0 %collective-permute-start = (bf16[512,192]{1,0:T(8,128)(2,1)}, bf16[512,192]{1,0:T(8,128)(2,1)S(1)}, u32[]{:S(2)}, u32[]{:S(2)}) collective-permute-start(bf16[512,192]{1,0:T(8,128)(2,1)} %get-tuple-element.71.ctx0.ctx_ref), channel_id=1, source_target_pairs={{0,1},{1,0},{2,3},{3,2},{4,5},{5,4},{6,7},{7,6},{8,9},{9,8},{10,11... | collective-permute-start | bytes 589832 | tf_op jit(solution)/shard_map/ppermute | solution.py:655
  8.5 8.5 %collective-permute-start.2 = (bf16[512,192]{1,0:T(8,128)(2,1)}, bf16[512,192]{1,0:T(8,128)(2,1)S(1)}, u32[]{:S(2)}, u32[]{:S(2)}) collective-permute-start(bf16[512,192]{1,0:T(8,128)(2,1)} %get-tuple-element.71.ctx0.ctx_ref), channel_id=1, source_target_pairs={{0,2},{2,0},{1,3},{3,1},{4,6},{6,4},{5,7},{7,5},{8,10},{10,8},{9,1... | collective-permute-start | bytes 589832 | tf_op jit(solution)/shard_map/ppermute | solution.py:655
  9.0 9.6 %copy-start = (bf16[512,768]{1,0:T(8,128)(2,1)S(1)}, bf16[512,768]{1,0:T(8,128)(2,1)}, u32[]{:S(2)}) copy-start(bf16[512,768]{1,0:T(8,128)(2,1)} %x_ref.7) | copy-start | bytes 2359300
  9.7 8.9 %collective-permute-start.5 = (bf16[192,768]{1,0:T(8,128)(2,1)S(1)}, bf16[192,768]{1,0:T(8,128)(2,1)S(1)}, u32[]{:S(2)}, u32[]{:S(2)}) collective-permute-start(bf16[192,768]{1,0:T(8,128)(2,1)S(1)} %collective-permute-done.4.wo2), channel_id=1, source_target_pairs={{0,1},{1,0},{2,3},{3,2},{4,5},{5,4},{6,7},{7,6},{8,9},{9,8},{10,11... | collective-permute-start | bytes 884744 | tf_op jit(solution)/shard_map/ppermute | solution.py:655
  17.0 1.5 collective-permute-start.3
  18.5 35.3 %copy-start.1 = (bf16[2,768,768]{2,1,0:T(8,128)(2,1)S(1)}, bf16[2,768,768]{2,1,0:T(8,128)(2,1)}, u32[]{:S(2)}) copy-start(bf16[2,768,768]{2,1,0:T(8,128)(2,1)} %in_ref.3) | copy-start | bytes 7077892
  18.5 35.3 %copy-start.2 = (bf16[2,768,768]{2,1,0:T(8,128)(2,1)S(1)}, bf16[2,768,768]{2,1,0:T(8,128)(2,1)}, u32[]{:S(2)}) copy-start(bf16[2,768,768]{2,1,0:T(8,128)(2,1)} %out_ref.3) | copy-start | bytes 7077892
  22.5 31.4 %copy-start.8 = (bf16[320,320]{1,0:T(8,128)(2,1)S(1)}, bf16[320,320]{1,0:T(8,128)(2,1)}, u32[]{:S(2)}) copy-start(bf16[320,320]{1,0:T(8,128)(2,1)} %constant.20.clone.back_ref) | copy-start | bytes 614404
  22.5 31.4 %copy-start.26 = (bf16[320,320]{1,0:T(8,128)(2,1)S(1)}, bf16[320,320]{1,0:T(8,128)(2,1)}, u32[]{:S(2)}) copy-start(bf16[320,320]{1,0:T(8,128)(2,1)} %constant.21.clone.sel_ref) | copy-start | bytes 614404
  51.3 2.6 %collective-permute-start.6 = (bf16[1280,384]{1,0:T(8,128)(2,1)S(1)}, bf16[1280,384]{1,0:T(8,128)(2,1)S(1)}, u32[]{:S(2)}, u32[]{:S(2)}) collective-permute-start(bf16[1280,384]{1,0:T(8,128)(2,1)S(1)} %bitcast.26), channel_id=1, source_target_pairs={{0,1},{1,0},{2,3},{3,2},{4,5},{5,4},{6,7},{7,6},{8,9},{9,8},{10,11... | collective-permute-start | bytes 2949128 | tf_op jit(solution)/shard_map/ppermute | solution.py:655
  59.4 2.6 %collective-permute-start.7 = (bf16[1280,384]{1,0:T(8,128)(2,1)S(1)}, bf16[1280,384]{1,0:T(8,128)(2,1)S(1)}, u32[]{:S(2)}, u32[]{:S(2)}) collective-permute-start(bf16[1280,384]{1,0:T(8,128)(2,1)S(1)} %get-tuple-element.91), channel_id=1, source_target_pairs={{0,1},{1,0},{2,3},{3,2},{4,5},{5,4},{6,7},{7,6},{8,9},{9,8},{10,11... | collective-permute-start | bytes 2949128 | tf_op jit(solution)/shard_map/ppermute | solution.py:655
  96.1 2.6 %collective-permute-start.8 = (bf16[512,768]{1,0:T(8,128)(2,1)S(1)}, bf16[512,768]{1,0:T(8,128)(2,1)S(1)}, u32[]{:S(2)}, u32[]{:S(2)}) collective-permute-start(bf16[512,768]{1,0:T(8,128)(2,1)S(1)} %shard_map.280.own_ref), channel_id=1, source_target_pairs={{0,1},{1,0},{2,3},{3,2},{4,5},{5,4},{6,7},{7,6},{8,9},{9,8},{10,11... | collective-permute-start | bytes 2359304 | tf_op jit(solution)/shard_map/ppermute | solution.py:655
  109.3 28.5 %all-to-all-start.2 = ((bf16[32,24,896]{2,1,0:T(8,128)(2,1)}), bf16[32,24,896]{2,1,0:T(8,128)(2,1)S(1)}, u32[]{:S(2)}, u32[]{:S(2)}) async-start(bf16[32,24,896]{2,1,0:T(8,128)(2,1)} %bitcast.14), calls=%async_computation.2 | async-start | bytes 2752512 | tf_op jit(solution)/shard_map/all_to_all | solution.py:763
  114.4 2.8 %collective-permute-start.10 = (bf16[256,768]{1,0:T(8,128)(2,1)}, bf16[256,768]{1,0:T(8,128)(2,1)S(1)}, u32[]{:S(2)}, u32[]{:S(2)}) collective-permute-start(bf16[256,768]{1,0:T(8,128)(2,1)} %copy-done.18), channel_id=1, source_target_pairs={{0,1},{1,0},{2,3},{3,2},{4,5},{5,4},{6,7},{7,6},{8,9},{9,8},{10,11... | collective-permute-start | bytes 1179656 | tf_op jit(solution)/shard_map/ppermute | solution.py:655
  114.5 2.0 %collective-permute-start.9 = (f32[8,768]{1,0:T(8,128)}, f32[8,768]{1,0:T(8,128)S(1)}, u32[]{:S(2)}, u32[]{:S(2)}) collective-permute-start(f32[8,768]{1,0:T(8,128)} %copy-done.13), channel_id=1, source_target_pairs={{0,1},{1,0},{2,3},{3,2},{4,5},{5,4},{6,7},{7,6},{8,9},{9,8},{10,11... | collective-permute-start | bytes 73736 | tf_op jit(solution)/shard_map/ppermute | solution.py:655
  118.1 7.9 %collective-permute-start.13 = (f32[16,768]{1,0:T(8,128)S(1)}, f32[16,768]{1,0:T(8,128)S(1)}, u32[]{:S(2)}, u32[]{:S(2)}) collective-permute-start(f32[16,768]{1,0:T(8,128)S(1)} %pad_maximum_fusion.1.pair_ref), channel_id=1, source_target_pairs={{0,2},{2,0},{1,3},{3,1},{4,6},{6,4},{5,7},{7,5},{8,10},{10,8},{9,1... | collective-permute-start | bytes 147464 | tf_op jit(solution)/shard_map/ppermute | solution.py:655
  140.0 28.4 %copy-start.36 = (f32[768]{0:T(1024)S(1)}, f32[768]{0:T(1024)}, u32[]{:S(2)}) copy-start(f32[768]{0:T(1024)} %gain_hbm.1) | copy-start | bytes 9220
  140.0 40.9 %all-to-all-start.3 = ((bf16[32,24,896]{2,1,0:T(8,128)(2,1)}), bf16[32,24,896]{2,1,0:T(8,128)(2,1)S(1)}, u32[]{:S(2)}, u32[]{:S(2)}) async-start(bf16[32,24,896]{2,1,0:T(8,128)(2,1)} %bitcast.16), calls=%async_computation.3 | async-start | bytes 2752512 | tf_op jit(solution)/shard_map/all_to_all | solution.py:777
  145.3 22.9 %collective-permute-start.11 = (bf16[256,768]{1,0:T(8,128)(2,1)S(1)}, bf16[256,768]{1,0:T(8,128)(2,1)S(1)}, u32[]{:S(2)}, u32[]{:S(2)}) collective-permute-start(bf16[256,768]{1,0:T(8,128)(2,1)S(1)} %copy-done.33), channel_id=1, source_target_pairs={{0,2},{2,0},{1,3},{3,1},{4,6},{6,4},{5,7},{7,5},{8,10},{10,8},{9,1... | collective-permute-start | bytes 1179656 | tf_op jit(solution)/shard_map/ppermute | solution.py:655
  168.3 9.3 %collective-permute-start.12 = (bf16[256,768]{1,0:T(8,128)(2,1)S(1)}, bf16[256,768]{1,0:T(8,128)(2,1)S(1)}, u32[]{:S(2)}, u32[]{:S(2)}) collective-permute-start(bf16[256,768]{1,0:T(8,128)(2,1)S(1)} %add_convert_fusion.1.own_ref), channel_id=1, source_target_pairs={{0,1},{1,0},{2,3},{3,2},{4,5},{5,4},{6,7},{7,6},{8,9},{9,8},{10,11... | collective-permute-start | bytes 1179656 | tf_op jit(solution)/shard_map/ppermute | solution.py:655
  (32 other events, 97.7 us)

commit v9 on v8

--- a/solution.py
+++ b/solution.py
@@ -191,12 +191,13 @@
         load.wait()
         out[...] = dot_nt(normed, weight[...]).astype(BF16)
         store(out, out_hbm)
-    queries, keys, values = q_ref[...], k_ref[...], v_ref[...]
+    queries, keys = q_ref[...], k_ref[...]
+    values_t = jnp.transpose(v_ref[...])
     lse_ref[...] = jnp.zeros((8, SEQ), F32)
     scaled = queries * jnp.asarray(HEAD**-0.5, BF16)
     for part in range(2):
         rows = slice(part * 256, part * 256 + 256)
-        context = jnp.zeros((256, WIDTH), F32)
+        context = []
         for head in range(HEADS_HERE):
             scores = scores_t(keys, only_head(scaled[rows], head), tiles_ref, table, head, part)
             top = jnp.max(scores, axis=0, keepdims=True)
@@ -204,8 +205,9 @@
             total = jnp.sum(grown, axis=0, keepdims=True)
             probs = (grown * (1.0 / total)).astype(BF16)
             lse_ref[head : head + 1, rows] = top + jnp.log(total)
-            context = context + dot_tn(probs, only_head(values, head))
-        ctx_ref[rows, :] = context.astype(BF16)
+            context.append(dot(values_t[head * HEAD : (head + 1) * HEAD], probs))
+        context = jnp.concatenate(context, axis=0).astype(BF16)
+        ctx_ref[rows, :] = jnp.transpose(context)
     for copy in stores:
         copy.wait()
 
@@ -429,9 +431,9 @@
 def backward_kernel(
     place_ref, x_ref, middle_ref, mixed_ref, probs_ref, route_ref, grad_ref,
     own_ref, other_ref, router_ref, gain_ref, wo_ref, ctx_ref, q_ref, k_ref, v_ref, normed_ref,
-    weights_ref, stats_ref, wq_ref, wk_ref, wv_ref, stretch_ref,
-    output_hbm, middle_grad_hbm, grads_hbm, mine_ref, theirs_ref, gain_one_ref,
-    low_s, logit_s, normed_s, wide_s, output_ref, middle_grad_ref, grads_ref, sems,
+    weights_ref, stats_ref, wq_ref, wk_ref, wv_ref,
+    output_hbm, middle_grad_hbm, grads_ref, mine_ref, theirs_ref,
+    low_s, logit_s, normed_s, wide_s, output_ref, middle_grad_ref, sems,
 ):
     core = place_ref[1]
     columns = route_columns(route_ref)
@@ -478,15 +480,14 @@
     ctx_grad = dot_nt(middle_low, wo_ref[...]).astype(BF16)
 
     values = v_ref[...]
-    key_scaled = k_ref[...] * jnp.asarray(HEAD**-0.5, BF16)
+    keys_t = jnp.transpose(k_ref[...] * jnp.asarray(HEAD**-0.5, BF16))
     query_scaled = q_ref[...] * jnp.asarray(HEAD**-0.5, BF16)
     key_grad = jnp.zeros((SEQ, WIDTH), F32)
     value_grad = jnp.zeros((SEQ, WIDTH), F32)
-    query_grads = [jnp.zeros((256, WIDTH), F32), jnp.zeros((256, WIDTH), F32)]
+    query_grads = []
     buckets = lax.broadcasted_iota(jnp.int32, (BUCKETS, 256), 0)
     line_ids = [line_buckets(block, 1) for block in (-1, 0, 1)]
-    bias_grad = jnp.zeros((BUCKETS, 128), F32)
-    bias_lanes = lax.broadcasted_iota(jnp.int32, (BUCKETS, 128), 1)
+    bias_columns = []
     turn = (
         lax.broadcasted_iota(jnp.int32, (128, 128), 0)
         + lax.broadcasted_iota(jnp.int32, (128, 128), 1)
@@ -496,7 +497,8 @@
         near = [jnp.zeros((128, 128), F32) for _ in range(3)]
         far_low = jnp.zeros((128, 128), F32)
         far_high = jnp.zeros((128, 128), F32)
-        key_head = only_head(key_scaled, head)
+        key_head = keys_t[head * HEAD : (head + 1) * HEAD]
+        query_parts = []
         for part in range(2):
             rows = slice(part * 256, part * 256 + 256)
             query_head = only_head(query_scaled[rows], head)
@@ -508,7 +510,7 @@
             inner = jnp.sum(probs * prob_grad, axis=0, keepdims=True)
             score_grad = (probs * (prob_grad - inner)).astype(BF16)
             key_grad = key_grad + dot(score_grad, query_head)
-            query_grads[part] = query_grads[part] + dot_tn(score_grad, key_head)
+            query_parts.append(dot(key_head, score_grad))
             for key_block in range(4):
                 for i in range(2):
                     piece = score_grad[
@@ -521,6 +523,7 @@
                         far_high = far_high + piece
                     else:
                         near[block + 1] = near[block + 1] + piece
+        query_grads.append(jnp.concatenate(query_parts, axis=1))
         by_bucket = jnp.zeros((BUCKETS, 256), F32)
         for block in range(3):
             turned = jnp.dot(
@@ -539,27 +542,26 @@
             side == BUCKETS - 1, high_line, 0.0
         )
         by_bucket = by_bucket[:, :128] + by_bucket[:, 128:] + ends
-        total = jnp.sum(by_bucket, axis=1, keepdims=True)
-        bias_grad = bias_grad + jnp.where(bias_lanes == EXPERTS + 1 + head, total, 0.0)
-    query_low = jnp.concatenate(query_grads, axis=0).astype(BF16)
+        bias_columns.append(jnp.sum(by_bucket, axis=1, keepdims=True))
+    query_t = jnp.concatenate(query_grads, axis=0).astype(BF16)
     key_low = key_grad.astype(BF16)
     value_low = value_grad.astype(BF16)
-    rest = dot_tn(mixed_ref[...], logit_s[...]) + dot(stretch_ref[...], bias_grad.astype(BF16))
-    column = jnp.transpose(jnp.broadcast_to(gain_grad, (128, D)))
-    lanes = lax.broadcasted_iota(jnp.int32, (D, 128), 1)
-    grads_ref[:, D:] = jnp.where(lanes == EXPERTS, column, rest).astype(BF16)
     normed = normed_ref[...]
-    copies = []
-    for i, low in ((3, None), (0, query_low), (1, key_low), (2, value_low)):
-        part = pl.ds(i * WIDTH, WIDTH)
-        if low is not None:
-            grads_ref[part, :D] = dot_tn(low, normed).astype(BF16)
-        copies.append(
-            pltpu.make_async_copy(grads_ref.at[part], grads_hbm.at[part], sems.at[2 + i])
-        )
-        copies[-1].start()
+    grads_ref[pl.ds(0, WIDTH), :D] = dot(query_t, normed).astype(BF16)
+    for i, low in ((1, key_low), (2, value_low)):
+        grads_ref[pl.ds(i * WIDTH, WIDTH), :D] = dot_tn(low, normed).astype(BF16)
+    lanes = lax.broadcasted_iota(jnp.int32, (BUCKETS, 128), 1)
+    bias = sum(jnp.where(lanes == h, bias_columns[h], 0.0) for h in range(HEADS_HERE))
+    bias = jnp.concatenate([bias, jnp.zeros((128 - BUCKETS, 128), F32)], axis=0)
+    bias = jnp.transpose(bias)[:8]
+    bias = jnp.concatenate([bias, jnp.zeros((8, D - 128), F32)], axis=1)
+    rest = dot_tn(logit_s[...], mixed_ref[...])
+    index = lax.broadcasted_iota(jnp.int32, (8, D), 0)
+    tail = jnp.where(index == 0, gain_grad, pltpu.roll(bias, 1, 0))
+    rest = jnp.concatenate([rest[:EXPERTS], tail, rest[EXPERTS + 8 :]], axis=0)
+    grads_ref[:, D:] = jnp.transpose(rest).astype(BF16)
     wide_s[...] = (
-        dot(query_low, wq_ref[...]) + dot(key_low, wk_ref[...]) + dot(value_low, wv_ref[...])
+        dot_tn(query_t, wq_ref[...]) + dot(key_low, wk_ref[...]) + dot(value_low, wv_ref[...])
     )
     gain_one = jnp.zeros((8, D), F32)
     for i in range(SEQ // 32):
@@ -569,11 +571,10 @@
         hidden = x_ref[rows, :].astype(F32)
         scale = stats_ref[rows, 0:1]
         gain_one = gain_one + jnp.sum((normed_part * hidden * scale).reshape(4, 8, D), axis=0)
-    gain_one_ref[...] = jnp.broadcast_to(jnp.sum(gain_one, axis=0, keepdims=True), (8, D))
+    gain_rows = jnp.broadcast_to(jnp.sum(gain_one, axis=0, keepdims=True), (16, D)).astype(BF16)
     for out, start in ((mine_ref, core * 256), (theirs_ref, (1 - core) * 256)):
-        out[...] = normed_s[pl.ds(pl.multiple_of(start, 256), 256), :]
-    for copy in copies:
-        copy.wait()
+        out[:256, :] = normed_s[pl.ds(pl.multiple_of(start, 256), 256), :]
+        out[256:, :] = gain_rows
     output_copy.wait()
     middle_copy.wait()
 
@@ -583,8 +584,9 @@
     return jnp.where(core == i // 2, own_ref[local, :], other_ref[local, :]).astype(F32)
 
 
-def reduce_kernel(parts_ref, pair_ref, link_ref, old_hbm, send_ref):
-    gain_grad = (pair_ref[0:1] + pair_ref[8:9]) + (link_ref[0:1] + link_ref[8:9])
+def reduce_kernel(parts_ref, halved_ref, link_ref, send_ref):
+    extra = pl.ds(256, 16)
+    gain_grad = (halved_ref[extra, :].astype(F32) + link_ref[extra, :].astype(F32))[0:1]
     total = jnp.zeros((24, GRADS), F32)
     for j in range(GROUPS // 2):
         pair = parts_ref[pl.ds(j * 48, 48), :].astype(F32)
@@ -618,7 +620,7 @@
 
 
 def finish_kernel(
-    recv_ref, stretch_ref, gain_one_ref, gain_two_ref, bias_ref,
+    recv_ref, gain_one_ref, gain_two_ref, bias_ref,
     q_ref, k_ref, v_ref, o_ref, router_ref,
 ):
     for i, out in enumerate((q_ref, k_ref, v_ref, o_ref)):
@@ -639,7 +641,7 @@
     router_ref[...] = turned[:EXPERTS]
     tail = turned[EXPERTS : EXPERTS + 8]
     gain_two_ref[...] = tail[0]
-    bias_ref[...] = dot(tail.astype(BF16), stretch_ref[...])[1 : 1 + HEADS_HERE]
+    bias_ref[...] = tail[1 : 1 + HEADS_HERE, :BUCKETS]
 
 
 def shards(
@@ -741,39 +743,34 @@
         limit=14, flops=300_000_000, moved=6_000_000,
     )
     rows_other, stats = lax.optimization_barrier((swap(rows_own, "c"), stats))
-    stretch = np.zeros((D, BUCKETS), np.float32)
-    stretch[24 * np.arange(BUCKETS), np.arange(BUCKETS)] = 1
-    half = shape((256, D), BF16)
-    layer_output, middle_grad, grads, norm_mine, norm_theirs, gain_part = call(
+    half = shape((256 + 16, D), BF16)
+    layer_output, middle_grad, grads, norm_mine, norm_theirs = call(
         backward_kernel,
-        (wide, shape((SEQ, D), F32), shape((D, GRADS), BF16), half, half, shape((8, D), F32)),
+        (wide, shape((SEQ, D), F32), shape((D, GRADS), BF16), half, half),
         (place, layer_input, middle, mixed, probs, route, out_grad,
          rows_own, rows_other, router, gain_two, output_weight, context, queries, keys,
-         values, normed, weights, stats, wq, wk, wv, jnp.asarray(stretch, BF16)),
+         values, normed, weights, stats, wq, wk, wv),
         scratch=(pltpu.VMEM((SEQ, D), BF16), pltpu.VMEM((SEQ, 128), BF16),
                  pltpu.VMEM((SEQ, D), BF16), pltpu.VMEM((SEQ, D), F32),
                  pltpu.VMEM((SEQ, D), BF16), pltpu.VMEM((SEQ, D), F32),
-                 pltpu.VMEM((D, GRADS), BF16), pltpu.SemaphoreType.DMA((6,))),
-        far_out=(0, 1, 2),
+                 pltpu.SemaphoreType.DMA((2,))),
+        far_out=(0, 1),
         scalars=1, limit=24, flops=4_000_000_000, moved=12_000_000,
     )
     halved = (norm_mine.astype(F32) + swap(norm_theirs, "c").astype(F32)).astype(BF16)
-    gain_pair = jnp.concatenate([gain_part, swap(gain_part, "c")], axis=0)
-    gain_pair, halved = lax.optimization_barrier((gain_pair, halved))
     scattered = lax.all_to_all(grads, experts_axis, 0, 0, tiled=True)
-    gain_link = swap(gain_pair, "l")
     halved_link = swap(halved, "l")
+    reduced = (halved.astype(F32) + halved_link.astype(F32)).astype(BF16)
+    reduced_other = swap(reduced, "c")
     spread = call(
         reduce_kernel, shape((D, GRADS), BF16),
-        (scattered, gain_pair, gain_link, grads),
-        far=(3,), alias={3: 0}, limit=12, flops=10_000_000, moved=3_000_000,
-    )
-    halved_link, slots, slot_grads, act, pre_grad = lax.optimization_barrier(
-        (halved_link, slots, slot_grads, act, pre_grad)
+        (scattered, halved, halved_link),
+        limit=12, flops=10_000_000, moved=3_000_000,
+    )
+    spread, slots, slot_grads, act, pre_grad = lax.optimization_barrier(
+        (spread, slots, slot_grads, act, pre_grad)
     )
     expert_in_grad, expert_out_grad = expert_grads(slots, slot_grads, act, pre_grad)
-    reduced = (halved.astype(F32) + halved_link.astype(F32)).astype(BF16)
-    reduced_other = swap(reduced, "c")
     gathered = lax.all_to_all(spread, experts_axis, 0, 0, tiled=True)
     input_grad = call(
         input_kernel, shape((SEQ, D), F32),
@@ -787,7 +784,7 @@
             finish_kernel,
             (line, line, shape((HEADS_HERE, BUCKETS), F32), out, out, out, out,
              shape((EXPERTS, D), F32)),
-            (gathered, jnp.asarray(stretch, BF16)),
+            (gathered,),
             limit=12, flops=10_000_000, moved=6_000_000,
         )
     return (

time: 185 us -> 177 us (0.957)
  local copies, waits for them, and re-layouts: 6.92 us -> 1.17 us
  waiting for transfers between devices: 51.1 us -> 45.7 us
  starting transfers between devices: 15.4 us -> 20.7 us
    all_to_all x1, waiting for transfers between devices: 11.7 us -> 0.01 us  [shards(): scattered = lax.all_to_all(grads, experts_axis, 0, 0, tiled=True)]
    all_to_all x1, waiting for transfers between devices: 0.01 us -> 11.7 us  [shards(): gathered = lax.all_to_all(spread, experts_axis, 0, 0, tiled=True)]
    unnamed x80 -> x68, local copies, waits for them, and re-layouts: 6.86 us -> 1.11 us
    all_to_all x1, starting transfers between devices: 5.29 us -> 11 us  [shards(): gathered = lax.all_to_all(spread, experts_axis, 0, 0, tiled=True)]
    ppermute x14 -> x12, waiting for transfers between devices: 39.3 us -> 34 us  [swap(): return lax.ppermute(array, axis, [(0, 1), (1, 0)])]
    ppermute x14 -> x12, starting transfers between devices: 4.99 us -> 4.5 us  [swap(): return lax.ppermute(array, axis, [(0, 1), (1, 0)])]
  transfers between devices with their start and end apart: 16 -> 14, of which waited for: 11 -> 11; matrix products, arithmetic and copies ran while one was open for 1% -> 0% of each run, Pallas kernels for 12% -> 13%
where the time goes in v9:
time: 177 us; the launch traced here: 176 us
  blocking collectives  60.7 us (34%)
  Pallas kernels  46 us (26%)
  waiting for transfers between devices  45.7 us (26%)
  starting transfers between devices  20.7 us (12%)
    pallas_call x12, Pallas kernels, call(): pl.pallas_call(body, out_shape=outs, in_specs=[pl.BlockSpec(memory_space=...  40.4 us
    ppermute x12, waiting for transfers between devices, swap(): return lax.ppermute(array, axis, [(0, 1), (1, 0)])  34 us
    all_to_all x1, blocking collectives, shards(): lax.all_to_all(jnp.concatenate([partial, partial], axis=0), pair_axis, 0,...  31.9 us
    all_to_all x1, blocking collectives, shards(): received = lax.all_to_all(send, experts_axis, 0, 0, tiled=True)  28.8 us
    all_to_all x1, waiting for transfers between devices, shards(): gathered = lax.all_to_all(spread, experts_axis, 0, 0, tiled=True)  11.7 us
    all_to_all x1, starting transfers between devices, shards(): gathered = lax.all_to_all(spread, experts_axis, 0, 0, tiled=True)  11 us
    pallas_call x1, Pallas kernels, expert_grads(): pl.pallas_call(expert_grads_kernel, grid=(2, 3), out_shape=(shape((2, D,...  5.54 us
    all_to_all x1, starting transfers between devices, shards(): scattered = lax.all_to_all(grads, experts_axis, 0, 0, tiled=True)  5.15 us
  transfers between devices with their start and end apart: 14, of which 11 were waited for; matrix products, arithmetic and copies ran while one was open for 0% of the time, Pallas kernels for 13%

profile of v9, /device:TPU:0, one launch (start us, length us, event | category | flops | bytes accessed | tf_op | source)
XLA Modules:
  0.0 176.2 jit_solution(16007231611261118641)
XLA Ops:
  0.7 1.7 collective-permute-start.4
  2.4 5.8 %shard_map.256 = (bf16[512,768]{1,0:T(8,128)(2,1)}, bf16[512,192]{1,0:T(8,128)(2,1)}, bf16[512,192]{1,0:T(8,128)(2,1)}, bf16[512,192]{1,0:T(8,128)(2,1)}, f32[9,...) custom-call(f32[3,32]{1,0:T(4,128)} %bitcast.29, bf16[512,768]{1,0:T(8,128)(2,1)} %x_ref.7, ...), custom_call_target="tpu_custom_call" | custom-call | flops 900000000 | bytes 5000000 | tf_op jit(solution)/shard_map/pallas_call | solution.py:95
  11.2 2.6 %shard_map.257 = (bf16[1280,512]{1,0:T(8,128)(2,1)S(1)}, bf16[1280,512]{1,0:T(8,128)(2,1)S(1)}, f32[512,768]{1,0:T(8,128)S(1)}, bf16[1280,384]{1,0:T(8,128)(2,1)S(1)}) custom-call(s32[2]{0:T(128)S(1)} %pad_add_fusion.place_ref, s32[8,512]{1,0:T(8,128)S(1)} %stack.31.route_ref, bf16[512,192]{1,0:T(8,128)(2,1)S(1)} %copy-done.19, ...), custom_call_target="tpu_custom_call" | custom-call | flops 1500000000 | bytes 7000000 | tf_op jit(solution)/shard_map/pallas_call | solution.py:95
  13.8 3.5 %collective-permute-done.2.ctx2 = bf16[512,192]{1,0:T(8,128)(2,1)S(1)} collective-permute-done((bf16[512,192]{1,0:T(8,128)(2,1)}, bf16[512,192]{1,0:T(8,128)(2,1)S(1)}, u32[]{:S(2)}, u32[]{:S(2)}) %collective-permute-start.2) | collective-permute-done | bytes 196640 | tf_op jit(solution)/shard_map/ppermute | solution.py:657
  17.4 1.5 collective-permute-done.3.ctx3
  18.9 3.9 %shard_map.258 = (f32[512,768]{1,0:T(8,128)S(1)}, bf16[512,768]{1,0:T(8,128)(2,1)S(1)}, f32[512,128]{1,0:T(8,128)S(1)}, bf16[1280,384]{1,0:T(8,128)(2,1)S(1)}) custom-call(s32[2]{0:T(128)S(1)} %pad_add_fusion.place_ref, bf16[512,768]{1,0:T(8,128)(2,1)S(1)} %copy-done, f32[512,768]{1,0:T(8,128)S(1)} %get-tuple-element.69.base_ref, ...), custom_call_target="tpu_custom_call" | custom-call | flops 1700000000 | bytes 8000000 | tf_op jit(solution)/shard_map/pallas_call | solution.py:95
  22.9 28.8 %all_to_all.45 = bf16[32,40,384]{2,1,0:T(8,128)(2,1)S(1)} all-to-all(bf16[32,40,384]{2,1,0:T(8,128)(2,1)S(1)} %bitcast.28), channel_id=1, replica_groups=mesh['z'=4,'x'=4,'h'=2,'l'=2,'c'=2] {'z','x','h'}, dimensions={0} | all-to-all | bytes 1966080 | tf_op jit(solution)/shard_map/all_to_all | solution.py:705
  52.6 1.7 collective-permute-done.6.other_ref
  54.3 5.6 %shard_map.260 = (bf16[1280,384]{1,0:T(8,128)(2,1)S(1)}, bf16[2,320,768]{2,1,0:T(8,128)(2,1)S(1)}, bf16[2,320,768]{2,1,0:T(8,128)(2,1)S(1)}, bf16[2,320,768]{2,1,0:T(8,128)(2,1)S(1)}, bf16[2,320,768]{2,1,0:T(8,128)(2,1)S(1)}) custom-call(s32[2]{0:T(128)S(1)} %pad_add_fusion.place_ref, bf16[1280,384]{1,0:T(8,128)(2,1)S(1)} %bitcast.27, ...), custom_call_target="tpu_custom_call" | custom-call | flops 4000000000 | bytes 14000000 | tf_op jit(solution)/shard_map/pallas_call | solution.py:95
  60.1 2.2 %shard_map.261 = bf16[1280,384]{1,0:T(8,128)(2,1)S(1)} custom-call(s32[2]{0:T(128)S(1)} %pad_add_fusion.place_ref, bf16[2,320,768]{2,1,0:T(8,128)(2,1)S(1)} %get-tuple-element.120.act_ref, bf16[2,320,768]{2,1,0:T(8,128)(2,1)S(1)} %get-tuple-element.121.pre_ref, bf16[2,768,768]{2,1,0:T(8,128)(2,1)S(1)} %copy-done.1, bf16[2,768,768]{2,1,0:T(8,128)(2,1)S(1)} %copy-done.2, ...), custom_call_target="tpu_custom_call" | custom-call | flops 1000000000 | bytes 4000000 | tf_op jit(solution)/shard_map/pallas_call | solution.py:95
  63.0 31.9 %all_to_all.46 = bf16[64,40,384]{2,1,0:T(8,128)(2,1)S(1)} all-to-all(bf16[64,40,384]{2,1,0:T(8,128)(2,1)S(1)} %bitcast.37), channel_id=1, replica_groups=mesh['z'=4,'x'=4,'h'=2,'l'=2,'c'=2] {'l','z','x','h'}, dimensions={0} | all-to-all | bytes 3932160 | tf_op jit(solution)/shard_map/all_to_all | solution.py:732
  95.0 1.5 shard_map.262.own_ref
  97.0 1.8 %shard_map.263 = (bf16[3,2,512,256]{3,2,1,0:T(8,128)(2,1)S(1)}, f32[512,128]{1,0:T(8,128)S(1)}) custom-call(f32[3,32]{1,0:T(4,128)S(1)} %bitcast.30, bf16[512,192]{1,0:T(8,128)(2,1)S(1)} %copy-done.8, bf16[512,192]{1,0:T(8,128)(2,1)S(1)} %copy-done.9, f32[8,512]{1,0:T(8,128)S(1)} %copy-done.11, f32[9,128,128]{2,1,0:T(8,128)S(1)} %copy-done.7, ...), custom_call_target="tpu_custom_call" | custom-call | flops 300000000 | bytes 6000000 | tf_op jit(solution)/shard_map/pallas_call | solution.py:95
  99.3 9.5 %shard_map.264 = (bf16[512,768]{1,0:T(8,128)(2,1)}, f32[512,768]{1,0:T(8,128)}, bf16[768,896]{1,0:T(8,128)(2,1)}, bf16[272,768]{1,0:T(8,128)(2,1)S(1)}, bf16[272,768]{1,0:T(8,128)(2,1)S(1)}) custom-call(s32[2]{0:T(128)S(1)} %pad_add_fusion.place_ref, bf16[512,768]{1,0:T(8,128)(2,1)S(1)} %copy-done, f32[512,768]{1,0:T(8,128)S(1)} %get-tuple-element.95.middle_ref, ...), custom_call_target="tpu_custom_call" | custom-call | flops 4000000000 | bytes 12000000 | tf_op jit(solution)/shard_map/pallas_call | solution.py:95
  108.8 5.2 %all-to-all-start.2 = ((bf16[32,24,896]{2,1,0:T(8,128)(2,1)}), bf16[32,24,896]{2,1,0:T(8,128)(2,1)S(1)}, u32[]{:S(2)}, u32[]{:S(2)}) async-start(bf16[32,24,896]{2,1,0:T(8,128)(2,1)} %bitcast.14), calls=%async_computation.2 | async-start | bytes 2752512 | tf_op jit(solution)/shard_map/all_to_all | solution.py:761
  114.0 1.7 collective-permute-done.9
  117.0 22.4 %collective-permute-done.10.link_ref = bf16[272,768]{1,0:T(8,128)(2,1)S(1)} collective-permute-done((bf16[272,768]{1,0:T(8,128)(2,1)S(1)}, bf16[272,768]{1,0:T(8,128)(2,1)S(1)}, u32[]{:S(2)}, u32[]{:S(2)}) %collective-permute-start.10) | collective-permute-done | bytes 417824 | tf_op jit(solution)/shard_map/ppermute | solution.py:657
  139.4 1.4 shard_map.266
  140.8 11.0 %all-to-all-start.3 = ((bf16[32,24,896]{2,1,0:T(8,128)(2,1)}), bf16[32,24,896]{2,1,0:T(8,128)(2,1)S(1)}, u32[]{:S(2)}, u32[]{:S(2)}) async-start(bf16[32,24,896]{2,1,0:T(8,128)(2,1)} %bitcast.16), calls=%async_computation.3 | async-start | bytes 2752512 | tf_op jit(solution)/shard_map/all_to_all | solution.py:774
  152.1 1.7 collective-permute-done.11.other_ref
  153.8 3.4 %shard_map.265 = f32[512,768]{1,0:T(8,128)} custom-call(s32[2]{0:T(128)S(1)} %pad_add_fusion.place_ref, bf16[272,768]{1,0:T(8,128)(2,1)S(1)} %add_convert_fusion.1.own_ref, bf16[272,768]{1,0:T(8,128)(2,1)S(1)} %collective-permute-done.11.other_ref, bf16[512,768]{1,0:T(8,128)(2,1)S(1)} %copy-done, ...), custom_call_target="tpu_custom_call", output_to_operand_aliasing={{}: (5, {})} | custom-call | flops 10000000 | bytes 5000000 | tf_op jit(solution)/shard_map/pallas_call | solution.py:95
  157.3 5.5 %shard_map.268 = (f32[2,768,768]{2,1,0:T(8,128)}, f32[2,768,768]{2,1,0:T(8,128)}) custom-call(bf16[2,320,768]{2,1,0:T(8,128)(2,1)S(1)} %copy-done.23, bf16[2,320,768]{2,1,0:T(8,128)(2,1)S(1)} %copy-done.25, bf16[2,320,768]{2,1,0:T(8,128)(2,1)S(1)} %copy-done.4, bf16[2,320,768]{2,1,0:T(8,128)(2,1)S(1)} %copy-done.6), custom_call_target="tpu_custom_call" | custom-call | flops 1509949440 | bytes 14000000 | tf_op jit(solution)/shard_map/pallas_call | solution.py:379
  162.8 11.7 %all-to-all-done.3 = bf16[32,24,896]{2,1,0:T(8,128)(2,1)S(1)} async-done(((bf16[32,24,896]{2,1,0:T(8,128)(2,1)}), bf16[32,24,896]{2,1,0:T(8,128)(2,1)S(1)}, u32[]{:S(2)}, u32[]{:S(2)}) %all-to-all-start.3) | async-done | bytes 1376288 | tf_op jit(solution)/shard_map/all_to_all | solution.py:774
  174.5 1.6 shard_map.267
  (98 shorter events, 7.0 us)
Async XLA Ops:
  0.6 9.6 %copy-start.17 = (bf16[192,768]{1,0:T(8,128)(2,1)S(1)}, bf16[192,768]{1,0:T(8,128)(2,1)}, u32[]{:S(2)}) copy-start(bf16[192,768]{1,0:T(8,128)(2,1)} %wo_ref.1) | copy-start | bytes 884740
  0.7 8.6 %copy-start.31 = (s32[512]{0:T(512)S(1)}, s32[512]{0:T(512)}, u32[]{:S(2)}) copy-start(s32[512]{0:T(512)} %param.28) | copy-start | bytes 6148
  0.7 8.6 %copy-start.32 = (s32[512]{0:T(512)S(1)}, s32[512]{0:T(512)}, u32[]{:S(2)}) copy-start(s32[512]{0:T(512)} %param.29) | copy-start | bytes 6148
  0.7 9.5 %copy-start.13 = (bf16[512,768]{1,0:T(8,128)(2,1)S(1)}, bf16[512,768]{1,0:T(8,128)(2,1)}, u32[]{:S(2)}) copy-start(bf16[512,768]{1,0:T(8,128)(2,1)} %grad_ref.3) | copy-start | bytes 2359300
  0.7 9.0 %collective-permute-start.4 = (bf16[192,768]{1,0:T(8,128)(2,1)}, bf16[192,768]{1,0:T(8,128)(2,1)S(1)}, u32[]{:S(2)}, u32[]{:S(2)}) collective-permute-start(bf16[192,768]{1,0:T(8,128)(2,1)} %wo_ref.1), channel_id=1, source_target_pairs={{0,2},{2,0},{1,3},{3,1},{4,6},{6,4},{5,7},{7,5},{8,10},{10,8},{9,1... | collective-permute-start | bytes 884744 | tf_op jit(solution)/shard_map/ppermute | solution.py:657
  2.4 7.8 %collective-permute-start.1 = (bf16[192,768]{1,0:T(8,128)(2,1)}, bf16[192,768]{1,0:T(8,128)(2,1)S(1)}, u32[]{:S(2)}, u32[]{:S(2)}) collective-permute-start(bf16[192,768]{1,0:T(8,128)(2,1)} %wo_ref.1), channel_id=1, source_target_pairs={{0,1},{1,0},{2,3},{3,2},{4,5},{5,4},{6,7},{7,6},{8,9},{9,8},{10,11... | collective-permute-start | bytes 884744 | tf_op jit(solution)/shard_map/ppermute | solution.py:657
  8.2 2.0 %collective-permute-start = (bf16[512,192]{1,0:T(8,128)(2,1)}, bf16[512,192]{1,0:T(8,128)(2,1)S(1)}, u32[]{:S(2)}, u32[]{:S(2)}) collective-permute-start(bf16[512,192]{1,0:T(8,128)(2,1)} %get-tuple-element.68.ctx0.ctx_ref), channel_id=1, source_target_pairs={{0,1},{1,0},{2,3},{3,2},{4,5},{5,4},{6,7},{7,6},{8,9},{9,8},{10,11... | collective-permute-start | bytes 589832 | tf_op jit(solution)/shard_map/ppermute | solution.py:657
  8.8 8.5 %collective-permute-start.2 = (bf16[512,192]{1,0:T(8,128)(2,1)}, bf16[512,192]{1,0:T(8,128)(2,1)S(1)}, u32[]{:S(2)}, u32[]{:S(2)}) collective-permute-start(bf16[512,192]{1,0:T(8,128)(2,1)} %get-tuple-element.68.ctx0.ctx_ref), channel_id=1, source_target_pairs={{0,2},{2,0},{1,3},{3,1},{4,6},{6,4},{5,7},{7,5},{8,10},{10,8},{9,1... | collective-permute-start | bytes 589832 | tf_op jit(solution)/shard_map/ppermute | solution.py:657
  9.3 9.5 %copy-start = (bf16[512,768]{1,0:T(8,128)(2,1)S(1)}, bf16[512,768]{1,0:T(8,128)(2,1)}, u32[]{:S(2)}) copy-start(bf16[512,768]{1,0:T(8,128)(2,1)} %x_ref.7) | copy-start | bytes 2359300
  9.7 9.2 %collective-permute-start.5 = (bf16[192,768]{1,0:T(8,128)(2,1)S(1)}, bf16[192,768]{1,0:T(8,128)(2,1)S(1)}, u32[]{:S(2)}, u32[]{:S(2)}) collective-permute-start(bf16[192,768]{1,0:T(8,128)(2,1)S(1)} %collective-permute-done.4.wo2), channel_id=1, source_target_pairs={{0,1},{1,0},{2,3},{3,2},{4,5},{5,4},{6,7},{7,6},{8,9},{9,8},{10,11... | collective-permute-start | bytes 884744 | tf_op jit(solution)/shard_map/ppermute | solution.py:657
  17.4 1.5 collective-permute-start.3
  18.9 35.4 %copy-start.1 = (bf16[2,768,768]{2,1,0:T(8,128)(2,1)S(1)}, bf16[2,768,768]{2,1,0:T(8,128)(2,1)}, u32[]{:S(2)}) copy-start(bf16[2,768,768]{2,1,0:T(8,128)(2,1)} %in_ref.3) | copy-start | bytes 7077892
  18.9 35.3 %copy-start.2 = (bf16[2,768,768]{2,1,0:T(8,128)(2,1)S(1)}, bf16[2,768,768]{2,1,0:T(8,128)(2,1)}, u32[]{:S(2)}) copy-start(bf16[2,768,768]{2,1,0:T(8,128)(2,1)} %out_ref.3) | copy-start | bytes 7077892
  22.9 31.4 %copy-start.10 = (bf16[320,320]{1,0:T(8,128)(2,1)S(1)}, bf16[320,320]{1,0:T(8,128)(2,1)}, u32[]{:S(2)}) copy-start(bf16[320,320]{1,0:T(8,128)(2,1)} %constant.18.clone.back_ref) | copy-start | bytes 614404
  22.9 31.4 %copy-start.21 = (bf16[320,320]{1,0:T(8,128)(2,1)S(1)}, bf16[320,320]{1,0:T(8,128)(2,1)}, u32[]{:S(2)}) copy-start(bf16[320,320]{1,0:T(8,128)(2,1)} %constant.19.clone.sel_ref) | copy-start | bytes 614404
  51.7 2.6 %collective-permute-start.6 = (bf16[1280,384]{1,0:T(8,128)(2,1)S(1)}, bf16[1280,384]{1,0:T(8,128)(2,1)S(1)}, u32[]{:S(2)}, u32[]{:S(2)}) collective-permute-start(bf16[1280,384]{1,0:T(8,128)(2,1)S(1)} %bitcast.26), channel_id=1, source_target_pairs={{0,1},{1,0},{2,3},{3,2},{4,5},{5,4},{6,7},{7,6},{8,9},{9,8},{10,11... | collective-permute-start | bytes 2949128 | tf_op jit(solution)/shard_map/ppermute | solution.py:657
  59.9 2.6 %collective-permute-start.7 = (bf16[1280,384]{1,0:T(8,128)(2,1)S(1)}, bf16[1280,384]{1,0:T(8,128)(2,1)S(1)}, u32[]{:S(2)}, u32[]{:S(2)}) collective-permute-start(bf16[1280,384]{1,0:T(8,128)(2,1)S(1)} %get-tuple-element.88), channel_id=1, source_target_pairs={{0,1},{1,0},{2,3},{3,2},{4,5},{5,4},{6,7},{7,6},{8,9},{9,8},{10,11... | collective-permute-start | bytes 2949128 | tf_op jit(solution)/shard_map/ppermute | solution.py:657
  96.6 2.6 %collective-permute-start.8 = (bf16[512,768]{1,0:T(8,128)(2,1)S(1)}, bf16[512,768]{1,0:T(8,128)(2,1)S(1)}, u32[]{:S(2)}, u32[]{:S(2)}) collective-permute-start(bf16[512,768]{1,0:T(8,128)(2,1)S(1)} %shard_map.262.own_ref), channel_id=1, source_target_pairs={{0,1},{1,0},{2,3},{3,2},{4,5},{5,4},{6,7},{7,6},{8,9},{9,8},{10,11... | collective-permute-start | bytes 2359304 | tf_op jit(solution)/shard_map/ppermute | solution.py:657
  108.8 30.6 %all-to-all-start.2 = ((bf16[32,24,896]{2,1,0:T(8,128)(2,1)}), bf16[32,24,896]{2,1,0:T(8,128)(2,1)S(1)}, u32[]{:S(2)}, u32[]{:S(2)}) async-start(bf16[32,24,896]{2,1,0:T(8,128)(2,1)} %bitcast.14), calls=%async_computation.2 | async-start | bytes 2752512 | tf_op jit(solution)/shard_map/all_to_all | solution.py:761
  114.0 1.8 %collective-permute-start.9 = (bf16[272,768]{1,0:T(8,128)(2,1)S(1)}, bf16[272,768]{1,0:T(8,128)(2,1)S(1)}, u32[]{:S(2)}, u32[]{:S(2)}) collective-permute-start(bf16[272,768]{1,0:T(8,128)(2,1)S(1)} %get-tuple-element.104), channel_id=1, source_target_pairs={{0,1},{1,0},{2,3},{3,2},{4,5},{5,4},{6,7},{7,6},{8,9},{9,8},{10,11... | collective-permute-start | bytes 1253384 | tf_op jit(solution)/shard_map/ppermute | solution.py:657
  115.9 23.5 %collective-permute-start.10 = (bf16[272,768]{1,0:T(8,128)(2,1)S(1)}, bf16[272,768]{1,0:T(8,128)(2,1)S(1)}, u32[]{:S(2)}, u32[]{:S(2)}) collective-permute-start(bf16[272,768]{1,0:T(8,128)(2,1)S(1)} %add_convert_fusion.2.halved_ref), channel_id=1, source_target_pairs={{0,2},{2,0},{1,3},{3,1},{4,6},{6,4},{5,7},{7,5},{8,10},{10,8},{9,1... | collective-permute-start | bytes 1253384 | tf_op jit(solution)/shard_map/ppermute | solution.py:657
  140.8 11.2 %copy-start.30 = (f32[768]{0:T(1024)S(1)}, f32[768]{0:T(1024)}, u32[]{:S(2)}) copy-start(f32[768]{0:T(1024)} %gain_hbm.1) | copy-start | bytes 9220
  140.8 33.7 %all-to-all-start.3 = ((bf16[32,24,896]{2,1,0:T(8,128)(2,1)}), bf16[32,24,896]{2,1,0:T(8,128)(2,1)S(1)}, u32[]{:S(2)}, u32[]{:S(2)}) async-start(bf16[32,24,896]{2,1,0:T(8,128)(2,1)} %bitcast.16), calls=%async_computation.3 | async-start | bytes 2752512 | tf_op jit(solution)/shard_map/all_to_all | solution.py:774
  152.0 1.8 %collective-permute-start.11 = (bf16[272,768]{1,0:T(8,128)(2,1)S(1)}, bf16[272,768]{1,0:T(8,128)(2,1)S(1)}, u32[]{:S(2)}, u32[]{:S(2)}) collective-permute-start(bf16[272,768]{1,0:T(8,128)(2,1)S(1)} %add_convert_fusion.1.own_ref), channel_id=1, source_target_pairs={{0,1},{1,0},{2,3},{3,2},{4,5},{5,4},{6,7},{7,6},{8,9},{9,8},{10,11... | collective-permute-start | bytes 1253384 | tf_op jit(solution)/shard_map/ppermute | solution.py:657
  (24 other events, 75.8 us)

commit v10 on v9

--- a/solution.py
+++ b/solution.py
@@ -134,9 +134,9 @@
 
 def attention_forward(
     table_hbm, x_hbm, gain_hbm, wq_hbm, wk_hbm, wv_hbm,
-    normed_hbm, q_hbm, k_hbm, v_hbm, tiles_hbm, ctx_ref, lse_ref,
+    normed_hbm, q_hbm, k_hbm, v_hbm, tiles_hbm, ctx_hbm, lse_ref,
     table_ref, x_ref, gain_ref, wq_ref, wk_ref, wv_ref, normed_ref, q_ref, k_ref, v_ref,
-    tiles_ref, sems,
+    ctx_ref, tiles_ref, sems,
 ):
     loads = [
         pltpu.make_async_copy(src, dst, sems.at[i])
@@ -191,13 +191,12 @@
         load.wait()
         out[...] = dot_nt(normed, weight[...]).astype(BF16)
         store(out, out_hbm)
-    queries, keys = q_ref[...], k_ref[...]
-    values_t = jnp.transpose(v_ref[...])
+    queries, keys, values = q_ref[...], k_ref[...], v_ref[...]
     lse_ref[...] = jnp.zeros((8, SEQ), F32)
     scaled = queries * jnp.asarray(HEAD**-0.5, BF16)
     for part in range(2):
         rows = slice(part * 256, part * 256 + 256)
-        context = []
+        context = jnp.zeros((256, WIDTH), F32)
         for head in range(HEADS_HERE):
             scores = scores_t(keys, only_head(scaled[rows], head), tiles_ref, table, head, part)
             top = jnp.max(scores, axis=0, keepdims=True)
@@ -205,9 +204,9 @@
             total = jnp.sum(grown, axis=0, keepdims=True)
             probs = (grown * (1.0 / total)).astype(BF16)
             lse_ref[head : head + 1, rows] = top + jnp.log(total)
-            context.append(dot(values_t[head * HEAD : (head + 1) * HEAD], probs))
-        context = jnp.concatenate(context, axis=0).astype(BF16)
-        ctx_ref[rows, :] = jnp.transpose(context)
+            context = context + dot_tn(probs, only_head(values, head))
+        ctx_ref[rows, :] = context.astype(BF16)
+        store(ctx_ref.at[pl.ds(part * 256, 256)], ctx_hbm.at[pl.ds(part * 256, 256)])
     for copy in stores:
         copy.wait()
 
@@ -432,8 +431,8 @@
     place_ref, x_ref, middle_ref, mixed_ref, probs_ref, route_ref, grad_ref,
     own_ref, other_ref, router_ref, gain_ref, wo_ref, ctx_ref, q_ref, k_ref, v_ref, normed_ref,
     weights_ref, stats_ref, wq_ref, wk_ref, wv_ref,
-    output_hbm, middle_grad_hbm, grads_ref, mine_ref, theirs_ref,
-    low_s, logit_s, normed_s, wide_s, output_ref, middle_grad_ref, sems,
+    output_hbm, middle_grad_hbm, grads_hbm, mine_ref, theirs_ref,
+    low_s, logit_s, normed_s, wide_s, output_ref, middle_grad_ref, grads_ref, sems,
 ):
     core = place_ref[1]
     columns = route_columns(route_ref)
@@ -546,10 +545,6 @@
     query_t = jnp.concatenate(query_grads, axis=0).astype(BF16)
     key_low = key_grad.astype(BF16)
     value_low = value_grad.astype(BF16)
-    normed = normed_ref[...]
-    grads_ref[pl.ds(0, WIDTH), :D] = dot(query_t, normed).astype(BF16)
-    for i, low in ((1, key_low), (2, value_low)):
-        grads_ref[pl.ds(i * WIDTH, WIDTH), :D] = dot_tn(low, normed).astype(BF16)
     lanes = lax.broadcasted_iota(jnp.int32, (BUCKETS, 128), 1)
     bias = sum(jnp.where(lanes == h, bias_columns[h], 0.0) for h in range(HEADS_HERE))
     bias = jnp.concatenate([bias, jnp.zeros((128 - BUCKETS, 128), F32)], axis=0)
@@ -560,6 +555,18 @@
     tail = jnp.where(index == 0, gain_grad, pltpu.roll(bias, 1, 0))
     rest = jnp.concatenate([rest[:EXPERTS], tail, rest[EXPERTS + 8 :]], axis=0)
     grads_ref[:, D:] = jnp.transpose(rest).astype(BF16)
+    normed = normed_ref[...]
+    copies = []
+    for i in (3, 0, 1, 2):
+        part = pl.ds(i * WIDTH, WIDTH)
+        if i == 0:
+            grads_ref[part, :D] = dot(query_t, normed).astype(BF16)
+        elif i < 3:
+            grads_ref[part, :D] = dot_tn((key_low, value_low)[i - 1], normed).astype(BF16)
+        copies.append(
+            pltpu.make_async_copy(grads_ref.at[part], grads_hbm.at[part], sems.at[2 + i])
+        )
+        copies[-1].start()
     wide_s[...] = (
         dot_tn(query_t, wq_ref[...]) + dot(key_low, wk_ref[...]) + dot(value_low, wv_ref[...])
     )
@@ -575,6 +582,8 @@
     for out, start in ((mine_ref, core * 256), (theirs_ref, (1 - core) * 256)):
         out[:256, :] = normed_s[pl.ds(pl.multiple_of(start, 256), 256), :]
         out[256:, :] = gain_rows
+    for copy in copies:
+        copy.wait()
     output_copy.wait()
     middle_copy.wait()
 
@@ -584,7 +593,7 @@
     return jnp.where(core == i // 2, own_ref[local, :], other_ref[local, :]).astype(F32)
 
 
-def reduce_kernel(parts_ref, halved_ref, link_ref, send_ref):
+def reduce_kernel(parts_ref, halved_ref, link_ref, old_hbm, send_ref):
     extra = pl.ds(256, 16)
     gain_grad = (halved_ref[extra, :].astype(F32) + link_ref[extra, :].astype(F32))[0:1]
     total = jnp.zeros((24, GRADS), F32)
@@ -621,10 +630,13 @@
 
 def finish_kernel(
     recv_ref, gain_one_ref, gain_two_ref, bias_ref,
-    q_ref, k_ref, v_ref, o_ref, router_ref,
-):
-    for i, out in enumerate((q_ref, k_ref, v_ref, o_ref)):
-        out[...] = recv_ref[pl.ds(i * WIDTH, WIDTH), :D].astype(F32)
+    q_hbm, k_hbm, v_hbm, o_hbm, router_ref, wide_s, sems,
+):
+    copies = []
+    for i, out in enumerate((q_hbm, k_hbm, v_hbm, o_hbm)):
+        wide_s[i] = recv_ref[pl.ds(i * WIDTH, WIDTH), :D].astype(F32)
+        copies.append(pltpu.make_async_copy(wide_s.at[i], out, sems.at[i]))
+        copies[-1].start()
     last = recv_ref[:, D:].astype(F32)
     summed = jnp.zeros((24, 128), F32)
     for j in range(GROUPS):
@@ -642,6 +654,8 @@
     tail = turned[EXPERTS : EXPERTS + 8]
     gain_two_ref[...] = tail[0]
     bias_ref[...] = tail[1 : 1 + HEADS_HERE, :BUCKETS]
+    for copy in copies:
+        copy.wait()
 
 
 def shards(
@@ -676,11 +690,11 @@
         attention_forward,
         (wide, tall, tall, tall, shape(tile_shape, F32), tall, shape((8, SEQ), F32)),
         (table, layer_input, attn_gain, wq, wk, wv),
-        far=(0, 1, 2, 3, 4, 5), far_out=(0, 1, 2, 3, 4),
+        far=(0, 1, 2, 3, 4, 5), far_out=(0, 1, 2, 3, 4, 5),
         scratch=(pltpu.VMEM((HEADS_HERE, BUCKETS), F32), pltpu.VMEM((SEQ, D), BF16),
                  pltpu.VMEM((D,), F32), weight_vmem, weight_vmem, weight_vmem, pltpu.VMEM((SEQ, D), BF16),
-                 tall_vmem, tall_vmem, tall_vmem, pltpu.VMEM(tile_shape, F32),
-                 pltpu.SemaphoreType.DMA((11,))),
+                 tall_vmem, tall_vmem, tall_vmem, tall_vmem, pltpu.VMEM(tile_shape, F32),
+                 pltpu.SemaphoreType.DMA((13,))),
         limit=60, flops=900_000_000, moved=5_000_000,
     )
     flat, flat_t = shape((ROWS, SEQ), BF16), shape((SEQ, ROWS), BF16)
@@ -753,8 +767,8 @@
         scratch=(pltpu.VMEM((SEQ, D), BF16), pltpu.VMEM((SEQ, 128), BF16),
                  pltpu.VMEM((SEQ, D), BF16), pltpu.VMEM((SEQ, D), F32),
                  pltpu.VMEM((SEQ, D), BF16), pltpu.VMEM((SEQ, D), F32),
-                 pltpu.SemaphoreType.DMA((2,))),
-        far_out=(0, 1),
+                 pltpu.VMEM((D, GRADS), BF16), pltpu.SemaphoreType.DMA((6,))),
+        far_out=(0, 1, 2),
         scalars=1, limit=24, flops=4_000_000_000, moved=12_000_000,
     )
     halved = (norm_mine.astype(F32) + swap(norm_theirs, "c").astype(F32)).astype(BF16)
@@ -764,8 +778,8 @@
     reduced_other = swap(reduced, "c")
     spread = call(
         reduce_kernel, shape((D, GRADS), BF16),
-        (scattered, halved, halved_link),
-        limit=12, flops=10_000_000, moved=3_000_000,
+        (scattered, halved, halved_link, grads),
+        far=(3,), alias={3: 0}, limit=12, flops=10_000_000, moved=3_000_000,
     )
     spread, slots, slot_grads, act, pre_grad = lax.optimization_barrier(
         (spread, slots, slot_grads, act, pre_grad)
@@ -785,7 +799,8 @@
             (line, line, shape((HEADS_HERE, BUCKETS), F32), out, out, out, out,
              shape((EXPERTS, D), F32)),
             (gathered,),
-            limit=12, flops=10_000_000, moved=6_000_000,
+            scratch=(pltpu.VMEM((4, WIDTH, D), F32), pltpu.SemaphoreType.DMA((4,))),
+            far_out=(3, 4, 5, 6), limit=16, flops=10_000_000, moved=6_000_000,
         )
     return (
         layer_output,

time: 177 us -> 177 us (level)
  no operation moved by 1% of the time
where the time goes in v10:
time: 177 us
  blocking collectives  60.7 us (34%)
  Pallas kernels  46.3 us (26%)
  waiting for transfers between devices  45.7 us (26%)
  starting transfers between devices  20.7 us (12%)
    pallas_call x12, Pallas kernels, call(): pl.pallas_call(body, out_shape=outs, in_specs=[pl.BlockSpec(memory_space=...  40.7 us
    ppermute x12, waiting for transfers between devices, swap(): return lax.ppermute(array, axis, [(0, 1), (1, 0)])  33.9 us
    all_to_all x1, blocking collectives, shards(): lax.all_to_all(jnp.concatenate([partial, partial], axis=0), pair_axis, 0,...  31.9 us
    all_to_all x1, blocking collectives, shards(): received = lax.all_to_all(send, experts_axis, 0, 0, tiled=True)  28.8 us
    all_to_all x1, waiting for transfers between devices, shards(): gathered = lax.all_to_all(spread, experts_axis, 0, 0, tiled=True)  11.7 us
    all_to_all x1, starting transfers between devices, shards(): gathered = lax.all_to_all(spread, experts_axis, 0, 0, tiled=True)  11 us
    pallas_call x1, Pallas kernels, expert_grads(): pl.pallas_call(expert_grads_kernel, grid=(2, 3), out_shape=(shape((2, D,...  5.54 us
    all_to_all x1, starting transfers between devices, shards(): scattered = lax.all_to_all(grads, experts_axis, 0, 0, tiled=True)  5.15 us
  transfers between devices with their start and end apart: 14, of which 11 were waited for; matrix products, arithmetic and copies ran while one was open for 0% of the time, Pallas kernels for 13%

profile of v10, /device:TPU:0, one launch (start us, length us, event | category | flops | bytes accessed | tf_op | source)
XLA Modules:
  0.0 176.6 jit_solution(6078328100713509695)
XLA Ops:
  0.7 1.7 collective-permute-start.4
  2.4 6.0 %shard_map.256 = (bf16[512,768]{1,0:T(8,128)(2,1)}, bf16[512,192]{1,0:T(8,128)(2,1)}, bf16[512,192]{1,0:T(8,128)(2,1)}, bf16[512,192]{1,0:T(8,128)(2,1)}, f32[9,...) custom-call(f32[3,32]{1,0:T(4,128)} %bitcast.29, bf16[512,768]{1,0:T(8,128)(2,1)} %x_ref.7, ...), custom_call_target="tpu_custom_call" | custom-call | flops 900000000 | bytes 5000000 | tf_op jit(solution)/shard_map/pallas_call | solution.py:95
  11.4 2.6 %shard_map.257 = (bf16[1280,512]{1,0:T(8,128)(2,1)S(1)}, bf16[1280,512]{1,0:T(8,128)(2,1)S(1)}, f32[512,768]{1,0:T(8,128)S(1)}, bf16[1280,384]{1,0:T(8,128)(2,1)S(1)}) custom-call(s32[2]{0:T(128)S(1)} %pad_add_fusion.place_ref, s32[8,512]{1,0:T(8,128)S(1)} %stack.31.route_ref, bf16[512,192]{1,0:T(8,128)(2,1)S(1)} %copy-done.19, ...), custom_call_target="tpu_custom_call" | custom-call | flops 1500000000 | bytes 7000000 | tf_op jit(solution)/shard_map/pallas_call | solution.py:95
  14.0 3.5 %collective-permute-done.2.ctx2 = bf16[512,192]{1,0:T(8,128)(2,1)S(1)} collective-permute-done((bf16[512,192]{1,0:T(8,128)(2,1)}, bf16[512,192]{1,0:T(8,128)(2,1)S(1)}, u32[]{:S(2)}, u32[]{:S(2)}) %collective-permute-start.2) | collective-permute-done | bytes 196640 | tf_op jit(solution)/shard_map/ppermute | solution.py:671
  17.6 1.5 collective-permute-done.3.ctx3
  19.1 3.9 %shard_map.258 = (f32[512,768]{1,0:T(8,128)S(1)}, bf16[512,768]{1,0:T(8,128)(2,1)S(1)}, f32[512,128]{1,0:T(8,128)S(1)}, bf16[1280,384]{1,0:T(8,128)(2,1)S(1)}) custom-call(s32[2]{0:T(128)S(1)} %pad_add_fusion.place_ref, bf16[512,768]{1,0:T(8,128)(2,1)S(1)} %copy-done, f32[512,768]{1,0:T(8,128)S(1)} %get-tuple-element.69.base_ref, ...), custom_call_target="tpu_custom_call" | custom-call | flops 1700000000 | bytes 8000000 | tf_op jit(solution)/shard_map/pallas_call | solution.py:95
  23.1 28.8 %all_to_all.45 = bf16[32,40,384]{2,1,0:T(8,128)(2,1)S(1)} all-to-all(bf16[32,40,384]{2,1,0:T(8,128)(2,1)S(1)} %bitcast.28), channel_id=1, replica_groups=mesh['z'=4,'x'=4,'h'=2,'l'=2,'c'=2] {'z','x','h'}, dimensions={0} | all-to-all | bytes 1966080 | tf_op jit(solution)/shard_map/all_to_all | solution.py:719
  52.8 1.7 collective-permute-done.6.other_ref
  54.5 5.6 %shard_map.260 = (bf16[1280,384]{1,0:T(8,128)(2,1)S(1)}, bf16[2,320,768]{2,1,0:T(8,128)(2,1)S(1)}, bf16[2,320,768]{2,1,0:T(8,128)(2,1)S(1)}, bf16[2,320,768]{2,1,0:T(8,128)(2,1)S(1)}, bf16[2,320,768]{2,1,0:T(8,128)(2,1)S(1)}) custom-call(s32[2]{0:T(128)S(1)} %pad_add_fusion.place_ref, bf16[1280,384]{1,0:T(8,128)(2,1)S(1)} %bitcast.27, ...), custom_call_target="tpu_custom_call" | custom-call | flops 4000000000 | bytes 14000000 | tf_op jit(solution)/shard_map/pallas_call | solution.py:95
  60.3 2.2 %shard_map.261 = bf16[1280,384]{1,0:T(8,128)(2,1)S(1)} custom-call(s32[2]{0:T(128)S(1)} %pad_add_fusion.place_ref, bf16[2,320,768]{2,1,0:T(8,128)(2,1)S(1)} %get-tuple-element.120.act_ref, bf16[2,320,768]{2,1,0:T(8,128)(2,1)S(1)} %get-tuple-element.121.pre_ref, bf16[2,768,768]{2,1,0:T(8,128)(2,1)S(1)} %copy-done.1, bf16[2,768,768]{2,1,0:T(8,128)(2,1)S(1)} %copy-done.2, ...), custom_call_target="tpu_custom_call" | custom-call | flops 1000000000 | bytes 4000000 | tf_op jit(solution)/shard_map/pallas_call | solution.py:95
  63.2 31.9 %all_to_all.46 = bf16[64,40,384]{2,1,0:T(8,128)(2,1)S(1)} all-to-all(bf16[64,40,384]{2,1,0:T(8,128)(2,1)S(1)} %bitcast.37), channel_id=1, replica_groups=mesh['z'=4,'x'=4,'h'=2,'l'=2,'c'=2] {'l','z','x','h'}, dimensions={0} | all-to-all | bytes 3932160 | tf_op jit(solution)/shard_map/all_to_all | solution.py:746
  95.2 1.5 shard_map.262.own_ref
  97.2 1.8 %shard_map.263 = (bf16[3,2,512,256]{3,2,1,0:T(8,128)(2,1)S(1)}, f32[512,128]{1,0:T(8,128)S(1)}) custom-call(f32[3,32]{1,0:T(4,128)S(1)} %bitcast.30, bf16[512,192]{1,0:T(8,128)(2,1)S(1)} %copy-done.8, bf16[512,192]{1,0:T(8,128)(2,1)S(1)} %copy-done.9, f32[8,512]{1,0:T(8,128)S(1)} %copy-done.11, f32[9,128,128]{2,1,0:T(8,128)S(1)} %copy-done.7, ...), custom_call_target="tpu_custom_call" | custom-call | flops 300000000 | bytes 6000000 | tf_op jit(solution)/shard_map/pallas_call | solution.py:95
  99.4 9.0 %shard_map.264 = (bf16[512,768]{1,0:T(8,128)(2,1)}, f32[512,768]{1,0:T(8,128)}, bf16[768,896]{1,0:T(8,128)(2,1)}, bf16[272,768]{1,0:T(8,128)(2,1)S(1)}, bf16[272,768]{1,0:T(8,128)(2,1)S(1)}) custom-call(s32[2]{0:T(128)S(1)} %pad_add_fusion.place_ref, bf16[512,768]{1,0:T(8,128)(2,1)S(1)} %copy-done, f32[512,768]{1,0:T(8,128)S(1)} %get-tuple-element.95.middle_ref, ...), custom_call_target="tpu_custom_call" | custom-call | flops 4000000000 | bytes 12000000 | tf_op jit(solution)/shard_map/pallas_call | solution.py:95
  108.4 5.2 %all-to-all-start.2 = ((bf16[32,24,896]{2,1,0:T(8,128)(2,1)}), bf16[32,24,896]{2,1,0:T(8,128)(2,1)S(1)}, u32[]{:S(2)}, u32[]{:S(2)}) async-start(bf16[32,24,896]{2,1,0:T(8,128)(2,1)} %bitcast.14), calls=%async_computation.2 | async-start | bytes 2752512 | tf_op jit(solution)/shard_map/all_to_all | solution.py:775
  113.7 1.7 collective-permute-done.9
  116.7 22.4 %collective-permute-done.10.link_ref = bf16[272,768]{1,0:T(8,128)(2,1)S(1)} collective-permute-done((bf16[272,768]{1,0:T(8,128)(2,1)S(1)}, bf16[272,768]{1,0:T(8,128)(2,1)S(1)}, u32[]{:S(2)}, u32[]{:S(2)}) %collective-permute-start.10) | collective-permute-done | bytes 417824 | tf_op jit(solution)/shard_map/ppermute | solution.py:671
  139.0 1.4 shard_map.266
  140.5 11.0 %all-to-all-start.3 = ((bf16[32,24,896]{2,1,0:T(8,128)(2,1)}), bf16[32,24,896]{2,1,0:T(8,128)(2,1)S(1)}, u32[]{:S(2)}, u32[]{:S(2)}) async-start(bf16[32,24,896]{2,1,0:T(8,128)(2,1)} %bitcast.16), calls=%async_computation.3 | async-start | bytes 2752512 | tf_op jit(solution)/shard_map/all_to_all | solution.py:788
  151.7 1.7 collective-permute-done.11.other_ref
  153.4 3.4 %shard_map.265 = f32[512,768]{1,0:T(8,128)} custom-call(s32[2]{0:T(128)S(1)} %pad_add_fusion.place_ref, bf16[272,768]{1,0:T(8,128)(2,1)S(1)} %add_convert_fusion.1.own_ref, bf16[272,768]{1,0:T(8,128)(2,1)S(1)} %collective-permute-done.11.other_ref, bf16[512,768]{1,0:T(8,128)(2,1)S(1)} %copy-done, ...), custom_call_target="tpu_custom_call", output_to_operand_aliasing={{}: (5, {})} | custom-call | flops 10000000 | bytes 5000000 | tf_op jit(solution)/shard_map/pallas_call | solution.py:95
  156.9 5.5 %shard_map.268 = (f32[2,768,768]{2,1,0:T(8,128)}, f32[2,768,768]{2,1,0:T(8,128)}) custom-call(bf16[2,320,768]{2,1,0:T(8,128)(2,1)S(1)} %copy-done.23, bf16[2,320,768]{2,1,0:T(8,128)(2,1)S(1)} %copy-done.25, bf16[2,320,768]{2,1,0:T(8,128)(2,1)S(1)} %copy-done.4, bf16[2,320,768]{2,1,0:T(8,128)(2,1)S(1)} %copy-done.6), custom_call_target="tpu_custom_call" | custom-call | flops 1509949440 | bytes 14000000 | tf_op jit(solution)/shard_map/pallas_call | solution.py:378
  162.4 11.7 %all-to-all-done.3 = bf16[32,24,896]{2,1,0:T(8,128)(2,1)S(1)} async-done(((bf16[32,24,896]{2,1,0:T(8,128)(2,1)}), bf16[32,24,896]{2,1,0:T(8,128)(2,1)S(1)}, u32[]{:S(2)}, u32[]{:S(2)}) %all-to-all-start.3) | async-done | bytes 1376288 | tf_op jit(solution)/shard_map/all_to_all | solution.py:788
  174.1 2.3 %shard_map.267 = (f32[768]{0:T(1024)}, f32[768]{0:T(1024)}, f32[3,32]{1,0:T(4,128)}, f32[192,768]{1,0:T(8,128)}, f32[192,768]{1,0:T(8,128)}, /*index=5*/f32[192,...) custom-call(bf16[768,896]{1,0:T(8,128)(2,1)S(1)} %bitcast.23), custom_call_target="tpu_custom_call" | custom-call | flops 10000000 | bytes 6000000 | tf_op jit(solution)/shard_map/pallas_call | solution.py:95
  (98 shorter events, 7.0 us)
Async XLA Ops:
  0.6 9.8 %copy-start.17 = (bf16[192,768]{1,0:T(8,128)(2,1)S(1)}, bf16[192,768]{1,0:T(8,128)(2,1)}, u32[]{:S(2)}) copy-start(bf16[192,768]{1,0:T(8,128)(2,1)} %wo_ref.1) | copy-start | bytes 884740
  0.7 8.8 %copy-start.31 = (s32[512]{0:T(512)S(1)}, s32[512]{0:T(512)}, u32[]{:S(2)}) copy-start(s32[512]{0:T(512)} %param.28) | copy-start | bytes 6148
  0.7 8.8 %copy-start.32 = (s32[512]{0:T(512)S(1)}, s32[512]{0:T(512)}, u32[]{:S(2)}) copy-start(s32[512]{0:T(512)} %param.29) | copy-start | bytes 6148
  0.7 9.7 %copy-start.13 = (bf16[512,768]{1,0:T(8,128)(2,1)S(1)}, bf16[512,768]{1,0:T(8,128)(2,1)}, u32[]{:S(2)}) copy-start(bf16[512,768]{1,0:T(8,128)(2,1)} %grad_ref.3) | copy-start | bytes 2359300
  0.7 9.0 %collective-permute-start.4 = (bf16[192,768]{1,0:T(8,128)(2,1)}, bf16[192,768]{1,0:T(8,128)(2,1)S(1)}, u32[]{:S(2)}, u32[]{:S(2)}) collective-permute-start(bf16[192,768]{1,0:T(8,128)(2,1)} %wo_ref.1), channel_id=1, source_target_pairs={{0,2},{2,0},{1,3},{3,1},{4,6},{6,4},{5,7},{7,5},{8,10},{10,8},{9,1... | collective-permute-start | bytes 884744 | tf_op jit(solution)/shard_map/ppermute | solution.py:671
  2.4 8.0 %collective-permute-start.1 = (bf16[192,768]{1,0:T(8,128)(2,1)}, bf16[192,768]{1,0:T(8,128)(2,1)S(1)}, u32[]{:S(2)}, u32[]{:S(2)}) collective-permute-start(bf16[192,768]{1,0:T(8,128)(2,1)} %wo_ref.1), channel_id=1, source_target_pairs={{0,1},{1,0},{2,3},{3,2},{4,5},{5,4},{6,7},{7,6},{8,9},{9,8},{10,11... | collective-permute-start | bytes 884744 | tf_op jit(solution)/shard_map/ppermute | solution.py:671
  8.4 2.0 %collective-permute-start = (bf16[512,192]{1,0:T(8,128)(2,1)}, bf16[512,192]{1,0:T(8,128)(2,1)S(1)}, u32[]{:S(2)}, u32[]{:S(2)}) collective-permute-start(bf16[512,192]{1,0:T(8,128)(2,1)} %get-tuple-element.68.ctx0.ctx_ref), channel_id=1, source_target_pairs={{0,1},{1,0},{2,3},{3,2},{4,5},{5,4},{6,7},{7,6},{8,9},{9,8},{10,11... | collective-permute-start | bytes 589832 | tf_op jit(solution)/shard_map/ppermute | solution.py:671
  9.0 8.5 %collective-permute-start.2 = (bf16[512,192]{1,0:T(8,128)(2,1)}, bf16[512,192]{1,0:T(8,128)(2,1)S(1)}, u32[]{:S(2)}, u32[]{:S(2)}) collective-permute-start(bf16[512,192]{1,0:T(8,128)(2,1)} %get-tuple-element.68.ctx0.ctx_ref), channel_id=1, source_target_pairs={{0,2},{2,0},{1,3},{3,1},{4,6},{6,4},{5,7},{7,5},{8,10},{10,8},{9,1... | collective-permute-start | bytes 589832 | tf_op jit(solution)/shard_map/ppermute | solution.py:671
  9.5 9.5 %copy-start = (bf16[512,768]{1,0:T(8,128)(2,1)S(1)}, bf16[512,768]{1,0:T(8,128)(2,1)}, u32[]{:S(2)}) copy-start(bf16[512,768]{1,0:T(8,128)(2,1)} %x_ref.7) | copy-start | bytes 2359300
  9.7 9.4 %collective-permute-start.5 = (bf16[192,768]{1,0:T(8,128)(2,1)S(1)}, bf16[192,768]{1,0:T(8,128)(2,1)S(1)}, u32[]{:S(2)}, u32[]{:S(2)}) collective-permute-start(bf16[192,768]{1,0:T(8,128)(2,1)S(1)} %collective-permute-done.4.wo2), channel_id=1, source_target_pairs={{0,1},{1,0},{2,3},{3,2},{4,5},{5,4},{6,7},{7,6},{8,9},{9,8},{10,11... | collective-permute-start | bytes 884744 | tf_op jit(solution)/shard_map/ppermute | solution.py:671
  17.5 1.5 collective-permute-start.3
  19.1 35.3 %copy-start.1 = (bf16[2,768,768]{2,1,0:T(8,128)(2,1)S(1)}, bf16[2,768,768]{2,1,0:T(8,128)(2,1)}, u32[]{:S(2)}) copy-start(bf16[2,768,768]{2,1,0:T(8,128)(2,1)} %in_ref.3) | copy-start | bytes 7077892
  19.1 35.3 %copy-start.2 = (bf16[2,768,768]{2,1,0:T(8,128)(2,1)S(1)}, bf16[2,768,768]{2,1,0:T(8,128)(2,1)}, u32[]{:S(2)}) copy-start(bf16[2,768,768]{2,1,0:T(8,128)(2,1)} %out_ref.3) | copy-start | bytes 7077892
  23.0 31.4 %copy-start.10 = (bf16[320,320]{1,0:T(8,128)(2,1)S(1)}, bf16[320,320]{1,0:T(8,128)(2,1)}, u32[]{:S(2)}) copy-start(bf16[320,320]{1,0:T(8,128)(2,1)} %constant.18.clone.back_ref) | copy-start | bytes 614404
  23.1 31.4 %copy-start.21 = (bf16[320,320]{1,0:T(8,128)(2,1)S(1)}, bf16[320,320]{1,0:T(8,128)(2,1)}, u32[]{:S(2)}) copy-start(bf16[320,320]{1,0:T(8,128)(2,1)} %constant.19.clone.sel_ref) | copy-start | bytes 614404
  51.9 2.6 %collective-permute-start.6 = (bf16[1280,384]{1,0:T(8,128)(2,1)S(1)}, bf16[1280,384]{1,0:T(8,128)(2,1)S(1)}, u32[]{:S(2)}, u32[]{:S(2)}) collective-permute-start(bf16[1280,384]{1,0:T(8,128)(2,1)S(1)} %bitcast.26), channel_id=1, source_target_pairs={{0,1},{1,0},{2,3},{3,2},{4,5},{5,4},{6,7},{7,6},{8,9},{9,8},{10,11... | collective-permute-start | bytes 2949128 | tf_op jit(solution)/shard_map/ppermute | solution.py:671
  60.1 2.6 %collective-permute-start.7 = (bf16[1280,384]{1,0:T(8,128)(2,1)S(1)}, bf16[1280,384]{1,0:T(8,128)(2,1)S(1)}, u32[]{:S(2)}, u32[]{:S(2)}) collective-permute-start(bf16[1280,384]{1,0:T(8,128)(2,1)S(1)} %get-tuple-element.88), channel_id=1, source_target_pairs={{0,1},{1,0},{2,3},{3,2},{4,5},{5,4},{6,7},{7,6},{8,9},{9,8},{10,11... | collective-permute-start | bytes 2949128 | tf_op jit(solution)/shard_map/ppermute | solution.py:671
  96.8 2.6 %collective-permute-start.8 = (bf16[512,768]{1,0:T(8,128)(2,1)S(1)}, bf16[512,768]{1,0:T(8,128)(2,1)S(1)}, u32[]{:S(2)}, u32[]{:S(2)}) collective-permute-start(bf16[512,768]{1,0:T(8,128)(2,1)S(1)} %shard_map.262.own_ref), channel_id=1, source_target_pairs={{0,1},{1,0},{2,3},{3,2},{4,5},{5,4},{6,7},{7,6},{8,9},{9,8},{10,11... | collective-permute-start | bytes 2359304 | tf_op jit(solution)/shard_map/ppermute | solution.py:671
  108.4 30.6 %all-to-all-start.2 = ((bf16[32,24,896]{2,1,0:T(8,128)(2,1)}), bf16[32,24,896]{2,1,0:T(8,128)(2,1)S(1)}, u32[]{:S(2)}, u32[]{:S(2)}) async-start(bf16[32,24,896]{2,1,0:T(8,128)(2,1)} %bitcast.14), calls=%async_computation.2 | async-start | bytes 2752512 | tf_op jit(solution)/shard_map/all_to_all | solution.py:775
  113.6 1.8 %collective-permute-start.9 = (bf16[272,768]{1,0:T(8,128)(2,1)S(1)}, bf16[272,768]{1,0:T(8,128)(2,1)S(1)}, u32[]{:S(2)}, u32[]{:S(2)}) collective-permute-start(bf16[272,768]{1,0:T(8,128)(2,1)S(1)} %get-tuple-element.104), channel_id=1, source_target_pairs={{0,1},{1,0},{2,3},{3,2},{4,5},{5,4},{6,7},{7,6},{8,9},{9,8},{10,11... | collective-permute-start | bytes 1253384 | tf_op jit(solution)/shard_map/ppermute | solution.py:671
  115.5 23.5 %collective-permute-start.10 = (bf16[272,768]{1,0:T(8,128)(2,1)S(1)}, bf16[272,768]{1,0:T(8,128)(2,1)S(1)}, u32[]{:S(2)}, u32[]{:S(2)}) collective-permute-start(bf16[272,768]{1,0:T(8,128)(2,1)S(1)} %add_convert_fusion.2.halved_ref), channel_id=1, source_target_pairs={{0,2},{2,0},{1,3},{3,1},{4,6},{6,4},{5,7},{7,5},{8,10},{10,8},{9,1... | collective-permute-start | bytes 1253384 | tf_op jit(solution)/shard_map/ppermute | solution.py:671
  140.5 11.2 %copy-start.30 = (f32[768]{0:T(1024)S(1)}, f32[768]{0:T(1024)}, u32[]{:S(2)}) copy-start(f32[768]{0:T(1024)} %gain_hbm.1) | copy-start | bytes 9220
  140.5 33.7 %all-to-all-start.3 = ((bf16[32,24,896]{2,1,0:T(8,128)(2,1)}), bf16[32,24,896]{2,1,0:T(8,128)(2,1)S(1)}, u32[]{:S(2)}, u32[]{:S(2)}) async-start(bf16[32,24,896]{2,1,0:T(8,128)(2,1)} %bitcast.16), calls=%async_computation.3 | async-start | bytes 2752512 | tf_op jit(solution)/shard_map/all_to_all | solution.py:788
  151.6 1.8 %collective-permute-start.11 = (bf16[272,768]{1,0:T(8,128)(2,1)S(1)}, bf16[272,768]{1,0:T(8,128)(2,1)S(1)}, u32[]{:S(2)}, u32[]{:S(2)}) collective-permute-start(bf16[272,768]{1,0:T(8,128)(2,1)S(1)} %add_convert_fusion.1.own_ref), channel_id=1, source_target_pairs={{0,1},{1,0},{2,3},{3,2},{4,5},{5,4},{6,7},{7,6},{8,9},{9,8},{10,11... | collective-permute-start | bytes 1253384 | tf_op jit(solution)/shard_map/ppermute | solution.py:671
  (24 other events, 76.1 us)
